TPU v7x, 32 devices: a whole 2x2x4 slice. The times are simulated.
32 devices in a mesh: pop: 2 (over y), section: 2 (over core), tensor: 4 (over z), rep: 2 (over x).
Axes of the slice: x: 2, y: 2, z: 4, core: 2. Of those that a mesh axis runs over, the one named last changes fastest.
Arguments:
- tokens: bfloat16 [768, 4096], P(('pop', 'rep'), 'tensor'), parts along dimension 0, may hold values from -6 to 6
- norm_gain: bfloat16 [2, 4096], P('section'), may hold values from 0.099609375 to 1.8984375
- gate_tiles: bfloat16 [2, 2048, 128, 128], P('section', ('tensor', 'rep')), may hold values from -0.125 to 0.125
- up_tiles: bfloat16 [2, 2048, 128, 128], P('section', ('tensor', 'rep')), may hold values from -0.125 to 0.125
- down_tiles: bfloat16 [2, 2048, 128, 128], P('section', ('tensor', 'rep')), may hold values from -0.0625 to 0.0625
- gate_slot: int32 [2, 2048], P('section', 'tensor'), may hold values from -1 to 1023, as said below
- up_slot: int32 [2, 2048], P('section', 'tensor'), may hold values from -1 to 1023, as said below
- down_slot: int32 [2, 2048], P('section', 'tensor'), may hold values from -1 to 1023, as said below
- owned_columns: int32 [2, 128], P('section'), may hold values from 0 to 127, each once within a row
- gate_left: bfloat16 [2, 8, 4096], P('section'), may hold values from -0.09375 to 0.09375
- gate_right: bfloat16 [2, 8, 16384], P('section'), may hold values from -6 to 6
- up_left: bfloat16 [2, 8, 4096], P('section'), may hold values from -0.09375 to 0.09375
- up_right: bfloat16 [2, 8, 16384], P('section'), may hold values from -6 to 6
- down_left: bfloat16 [2, 8, 16384], P('section'), may hold values from -0.046875 to 0.046875
- down_right: bfloat16 [2, 8, 4096], P('section'), may hold values from -6 to 6
- row_member: int32 [768], P(('pop', 'rep')), parts along dimension 0, may hold values from 0 to 63
- member_seed: int32 [128], P('pop'), parts along dimension 0, may hold values from 0 to 7
Outputs:
- layer_outputs: bfloat16 [2, 768, 4096], P('section', ('pop', 'rep'), 'tensor'), parts along dimension 1
There are 2 independent parts, one for each index of `pop`. A program takes and returns all parts, laid end to end along the dimension named above; an argument that names none is the same for every part. Nothing has to cross between parts.
Inputs may be any that keep to these rules, and one draw needn't show every extreme that they name: `gate_slot`: each entry is -1 (an empty slot) or c * 32 + d, placing a tile at the owner's c-th hidden block column and block row d of the features; the codes of one owner in one layer are distinct, and in every layer some owner has all 512 slots in use. `up_slot`: as for gate_slot. `down_slot`: each entry is -1 (an empty slot) or c * 32 + d, placing a tile at the owner's c-th hidden block column (its rows) and block d of the output features (its columns); the codes of one owner in one layer are distinct, and in every layer some owner has all 512 slots in use.
All inputs are finite; a program needn't handle non-finite values.
Results may differ from a plain program's by a relative error of at most 0.015.
Values may be sent and summed in bfloat16 or wider, within the bound.
No kernel may reach another device: no remote copies, remote signals or barrier semaphores. Data moves between devices by JAX's collectives and lax.ppermute only.
A program may use at most 384 MiB of HBM per device.

v0:
```python
import jax
import jax.numpy as jnp
from jax import lax
from jax.sharding import PartitionSpec as P

BLOCK = 128
MICRO = 1


perturb_scale = 0.5
epsilon = 1e-05


def shifted(value, axis, steps):
    count = lax.axis_size(axis)
    leading, last = (max(0, -steps), min(count, count - steps))
    return lax.ppermute(value, axis, [(source, source + steps) for source in range(leading, last)])


def pick_matrix(row_member, member_seed, noise_count):
    member_ids = jnp.arange(member_seed.shape[0], dtype=jnp.int32)
    matched = row_member[:, None] == member_ids[None, :]
    seed_of = jnp.sum(jnp.where(matched, member_seed[None, :], 0), axis=1)
    sign_values = (1 - 2 * (row_member % 2)).astype(jnp.float32) * perturb_scale
    noise_ids = jnp.arange(noise_count, dtype=jnp.int32)
    return jnp.where(seed_of[:, None] == noise_ids[None, :], sign_values[:, None], jnp.float32(0.0))


def place_tiles(tile_set, slot_codes, own_cols, block_rows, hidden_first):
    active = slot_codes >= 0
    cleared = jnp.where(active, slot_codes, 0)
    hidden_index = cleared // block_rows
    feature_index = jnp.where(active, cleared % block_rows, block_rows)
    side = tile_set.shape[1]
    if hidden_first:
        empty = jnp.zeros((own_cols, side, block_rows, side), tile_set.dtype)
        placed = empty.at[hidden_index, :, feature_index, :].set(tile_set, mode="drop")
        return placed.reshape(own_cols * side, block_rows * side)
    empty = jnp.zeros((block_rows, side, own_cols, side), tile_set.dtype)
    placed = empty.at[feature_index, :, hidden_index, :].set(tile_set, mode="drop")
    return placed.reshape(block_rows * side, own_cols * side)


def column_select(noise_table, columns):
    noise_count = noise_table.shape[0]
    blocked = noise_table.reshape(noise_count, -1, BLOCK)
    return jnp.take(blocked, columns, axis=1).reshape(noise_count, -1)


def per_device(
    tokens,
    norm_gain,
    gate_tiles,
    up_tiles,
    down_tiles,
    gate_slot,
    up_slot,
    down_slot,
    owned_columns,
    gate_left,
    gate_right,
    up_left,
    up_right,
    down_left,
    down_right,
    row_member,
    member_seed,
):
    section_index = lax.axis_index("section")
    owner_index = lax.axis_index("tensor")
    row_count, local_width = tokens.shape
    micro_rows = row_count // MICRO
    own_cols = owned_columns.shape[1] // lax.axis_size("tensor")
    block_rows = gate_left.shape[2] // BLOCK
    gate_full, up_full, down_full = (
        lax.all_gather(gate_tiles[0], "rep", axis=0, tiled=True),
        lax.all_gather(up_tiles[0], "rep", axis=0, tiled=True),
        lax.all_gather(down_tiles[0], "rep", axis=0, tiled=True),
    )
    gate_dense = place_tiles(gate_full, gate_slot[0], own_cols, block_rows, False)
    up_dense = place_tiles(up_full, up_slot[0], own_cols, block_rows, False)
    down_dense = place_tiles(down_full, down_slot[0], own_cols, block_rows, True)
    columns = lax.dynamic_slice_in_dim(owned_columns[0], owner_index * own_cols, own_cols)
    gate_cols = column_select(gate_right[0], columns)
    up_cols = column_select(up_right[0], columns)
    down_cols = column_select(down_left[0], columns)
    down_wide = down_right[0].astype(jnp.float32)
    gain_row = norm_gain[0].astype(jnp.float32)
    picks = pick_matrix(row_member, member_seed, gate_left.shape[1])
    carried = jnp.zeros((micro_rows, local_width), jnp.bfloat16)
    results = []
    for tick_index in range(MICRO + 1):
        current = jnp.where(section_index == 0, tokens, carried)
        whole_rows = lax.all_gather(current, "tensor", axis=1, tiled=True)
        values = whole_rows.astype(jnp.float32)
        inverse_rms = lax.rsqrt(jnp.mean(values * values, axis=1, keepdims=True) + epsilon)
        normed = (values * inverse_rms * gain_row).astype(jnp.bfloat16)
        gate_coef = (
            picks * jnp.dot(normed, gate_left[0].T, preferred_element_type=jnp.float32)
        ).astype(jnp.bfloat16)
        up_coef = (
            picks * jnp.dot(normed, up_left[0].T, preferred_element_type=jnp.float32)
        ).astype(jnp.bfloat16)
        gate_value = jnp.dot(normed, gate_dense, preferred_element_type=jnp.float32) + jnp.dot(
            gate_coef, gate_cols, preferred_element_type=jnp.float32
        )
        up_value = jnp.dot(normed, up_dense, preferred_element_type=jnp.float32) + jnp.dot(
            up_coef, up_cols, preferred_element_type=jnp.float32
        )
        hidden = (jax.nn.silu(gate_value) * up_value).astype(jnp.bfloat16)
        partial_value = jnp.dot(hidden, down_dense, preferred_element_type=jnp.float32)
        down_coef = picks * jnp.dot(hidden, down_cols.T, preferred_element_type=jnp.float32)
        partial_value = partial_value + jnp.dot(
            down_coef, down_wide, precision=lax.Precision.HIGHEST
        )
        summed = lax.psum_scatter(
            partial_value.astype(jnp.bfloat16), "tensor", scatter_dimension=1, tiled=True
        ).astype(jnp.float32)
        updated = (current.astype(jnp.float32) + summed).astype(jnp.bfloat16)
        results.append(updated)
        if tick_index < MICRO:
            carried = shifted(updated, "section", 1)
    first_out = jnp.concatenate(results[:MICRO], axis=0)
    second_out = jnp.concatenate(results[1:], axis=0)
    return jnp.where(section_index == 0, first_out, second_out)[None]


def solution(mesh):
    placed = (
        P(("pop", "rep"), "tensor"),
        P("section", None),
        P("section", ("tensor", "rep"), None, None),
        P("section", ("tensor", "rep"), None, None),
        P("section", ("tensor", "rep"), None, None),
        P("section", "tensor"),
        P("section", "tensor"),
        P("section", "tensor"),
        P("section", None),
        P("section", None, None),
        P("section", None, None),
        P("section", None, None),
        P("section", None, None),
        P("section", None, None),
        P("section", None, None),
        P(("pop", "rep")),
        P("pop"),
    )
    return jax.shard_map(
        per_device,
        mesh=mesh,
        in_specs=placed,
        out_specs=P("section", ("pop", "rep"), "tensor"),
        check_vma=False,
    )
```

profile of v0, /device:TPU:1, one launch (start us, length us, event | category | flops | bytes accessed | tf_op | source)
XLA Modules:
  0.0 1067.3 jit_solution(2535243118481960410)
XLA Ops:
  11.5 2.1 gather_fusion.1
  13.6 2.2 gather_fusion.2
  17.2 30.8 %all-gather.9.cloned.1.call-done = bf16[192,4096]{1,0:T(8,128)(2,1)} async-done(((bf16[192,1024]{1,0:T(8,128)(2,1)}), bf16[192,4096]{1,0:T(8,128)(2,1)}) %all-gather.9.cloned.1.call-update) | async-done | bytes 1572880 | tf_op jit(solution)/shard_map/all_gather | solution.py:94
  49.8 197.6 %all-gather.13.cloned.1.call-done = bf16[1,512,128,128]{3,2,0,1:T(8,128)(2,1)} async-done(((bf16[1,256,128,128]{3,2,0,1:T(8,128)(2,1)}), bf16[1,512,128,128]{3,2,0,1:T(8,128)(2,1)}) %all-gather.13.cloned.1.call-update) | async-done | bytes 16777232 | tf_op jit(solution)/shard_map/all_gather | solution.py:76
  247.4 14.4 %broadcast.464.clone.1 = bf16[32,128,32,128]{3,1,2,0:T(8,128)(2,1)} broadcast(bf16[]{:T(256)} %constant.96.clone.1), dimensions={} | broadcast | bytes 33554432 | tf_op jit(solution)/shard_map/broadcast.14
  261.8 81.5 %scatter_fusion = bf16[32,128,32,128]{3,1,2,0:T(8,128)(2,1)} fusion(bf16[32,128,32,128]{3,1,2,0:T(8,128)(2,1)} %broadcast.464.clone.1, s32[512]{0:T(512)S(1)} %bitcast.109, bf16[512,128,128]{2,1,0:T(8,128)(2,1)} %bitcast.117), kind=kCustom, calls=%fused_computation.3 | custom fusion | bytes 50335744 | tf_op jit(solution)/shard_map/scatter | solution.py:40
  343.3 29.2 %copy.28 = bf16[32,128,32,128]{3,2,1,0:T(8,128)(2,1)} copy(bf16[32,128,32,128]{3,1,2,0:T(8,128)(2,1)} %scatter_fusion) | data formatting | bytes 67108864 | tf_op jit(solution)/shard_map/scatter | solution.py:40
  372.5 75.3 %all-gather.15.cloned.1.call-done = bf16[1,512,128,128]{3,2,0,1:T(8,128)(2,1)} async-done(((bf16[1,256,128,128]{3,2,0,1:T(8,128)(2,1)}), bf16[1,512,128,128]{3,2,0,1:T(8,128)(2,1)}) %all-gather.15.cloned.1.call-update) | async-done | bytes 16777232 | tf_op jit(solution)/shard_map/all_gather | solution.py:77
  447.9 14.5 %broadcast.464.clone = bf16[32,128,32,128]{3,1,2,0:T(8,128)(2,1)} broadcast(bf16[]{:T(256)} %constant.96.clone.1), dimensions={} | broadcast | bytes 33554432 | tf_op jit(solution)/shard_map/broadcast.14
  462.4 80.6 %scatter_fusion.1 = bf16[32,128,32,128]{3,1,2,0:T(8,128)(2,1)} fusion(bf16[32,128,32,128]{3,1,2,0:T(8,128)(2,1)} %broadcast.464.clone, s32[512]{0:T(512)S(1)} %bitcast.108, bf16[512,128,128]{2,1,0:T(8,128)(2,1)} %bitcast.118), kind=kCustom, calls=%fused_computation.4 | custom fusion | bytes 50335744 | tf_op jit(solution)/shard_map/scatter | solution.py:40
  543.0 29.2 %copy.30 = bf16[32,128,32,128]{3,2,1,0:T(8,128)(2,1)} copy(bf16[32,128,32,128]{3,1,2,0:T(8,128)(2,1)} %scatter_fusion.1) | data formatting | bytes 67108864 | tf_op jit(solution)/shard_map/scatter | solution.py:40
  572.2 75.9 %all-gather.17.cloned.1.call-done = bf16[1,512,128,128]{3,2,0,1:T(8,128)(2,1)} async-done(((bf16[1,256,128,128]{3,2,0,1:T(8,128)(2,1)}), bf16[1,512,128,128]{3,2,0,1:T(8,128)(2,1)}) %all-gather.17.cloned.1.call-update) | async-done | bytes 16777232 | tf_op jit(solution)/shard_map/all_gather | solution.py:78
  648.2 11.2 %broadcast.464.clone.2 = bf16[32,128,32,128]{3,1,2,0:T(8,128)(2,1)} broadcast(bf16[]{:T(256)} %constant.96.clone.1), dimensions={} | broadcast | bytes 33554432 | tf_op jit(solution)/shard_map/broadcast.14
  659.4 80.6 %scatter_fusion.2 = bf16[32,128,32,128]{3,1,2,0:T(8,128)(2,1)} fusion(bf16[32,128,32,128]{3,1,2,0:T(8,128)(2,1)} %broadcast.464.clone.2, s32[512]{0:T(512)S(1)} %bitcast.107, bf16[512,128,128]{2,1,0:T(8,128)(2,1)} %bitcast.116), kind=kCustom, calls=%fused_computation.5 | custom fusion | bytes 50335744 | tf_op jit(solution)/shard_map/scatter | solution.py:37
  740.0 29.4 %copy.32 = bf16[32,128,32,128]{3,2,1,0:T(8,128)(2,1)} copy(bf16[32,128,32,128]{3,1,2,0:T(8,128)(2,1)} %scatter_fusion.2) | data formatting | bytes 67108864 | tf_op jit(solution)/shard_map/scatter | solution.py:37
  769.4 23.4 %fusion.10 = f32[192,4096]{1,0:T(8,128)} fusion(bf16[512,8,32,128]{3,2,1,0:T(8,128)(2,1)} %bitcast.110, bf16[192,4096]{1,0:T(8,128)(2,1)S(1)} %copy-done.2, f32[4096]{0:T(1024)S(1)} %bitcast.122, f32[192]{0:T(256)S(1)} %add_rsqrt_fusion.1), kind=kOutput, calls=%fused_computation.16 | convolution fusion | flops 6445596672 | bytes 38290176 | tf_op jit(solution)/shard_map/dot_general | solution.py:104
  792.9 23.1 %fusion.6 = f32[192,4096]{1,0:T(8,128)} fusion(bf16[512,8,32,128]{3,2,1,0:T(8,128)(2,1)} %bitcast.114, bf16[192,4096]{1,0:T(8,128)(2,1)S(1)} %copy-done.2, f32[4096]{0:T(1024)S(1)} %bitcast.123, f32[192]{0:T(256)S(1)} %add_rsqrt_fusion.1), kind=kOutput, calls=%fused_computation.12 | convolution fusion | flops 6445596672 | bytes 38290176 | tf_op jit(solution)/shard_map/dot_general | solution.py:107
  816.0 5.6 convolution_add_fusion.3
  821.6 4.8 fusion.22
  826.5 23.1 %fusion.2 = f32[192,4096]{1,0:T(8,128)} fusion(bf16[192,4096]{1,0:T(8,128)(2,1)S(1)} %fusion.22, bf16[512,8,32,128]{3,2,1,0:T(8,128)(2,1)} %bitcast.112), kind=kOutput, calls=%fused_computation.8 | convolution fusion | flops 6442450944 | bytes 38273024 | tf_op jit(solution)/shard_map/dot_general | solution.py:111
  850.1 4.6 fusion.20
  854.8 35.4 %reduce-scatter.3.cloned.1.call-done = bf16[192,1024]{1,0:T(8,128)(2,1)} async-done(((bf16[192,4096]{1,0:T(8,128)(2,1)}), bf16[192,1024]{1,0:T(8,128)(2,1)}) %reduce-scatter.3.cloned.1.call-update) | async-done | bytes 393232 | tf_op jit(solution)/shard_map/reduce_scatter | solution.py:116
  893.3 2.3 collective-permute-done
  896.5 35.7 %all-gather.11.cloned.1.call-done = bf16[192,4096]{1,0:T(8,128)(2,1)} async-done(((bf16[192,1024]{1,0:T(8,128)(2,1)}), bf16[192,4096]{1,0:T(8,128)(2,1)}) %all-gather.11.cloned.1.call-update) | async-done | bytes 1572880 | tf_op jit(solution)/shard_map/all_gather | solution.py:94
  934.1 28.3 %fusion.8 = f32[192,4096]{1,0:T(8,128)} fusion(bf16[512,8,32,128]{3,2,1,0:T(8,128)(2,1)} %bitcast.111, bf16[192,4096]{1,0:T(8,128)(2,1)} %all-gather.11.cloned.1.call-done, f32[192]{0:T(256)S(1)} %add_rsqrt_fusion, f32[4096]{0:T(1024)S(1)} %bitcast.126), kind=kOutput, calls=%fused_computation.14 | convolution fusion | flops 6445596672 | bytes 38290176 | tf_op jit(solution)/shard_map/dot_general | solution.py:104
  962.4 23.0 %fusion.4 = f32[192,4096]{1,0:T(8,128)} fusion(bf16[512,8,32,128]{3,2,1,0:T(8,128)(2,1)} %bitcast.115, bf16[192,4096]{1,0:T(8,128)(2,1)S(1)} %copy-done.3, f32[192]{0:T(256)S(1)} %add_rsqrt_fusion, f32[4096]{0:T(1024)S(1)} %bitcast.127), kind=kOutput, calls=%fused_computation.10 | convolution fusion | flops 6445596672 | bytes 38290176 | tf_op jit(solution)/shard_map/dot_general | solution.py:107
  985.3 5.5 convolution_add_fusion.1
  990.8 4.9 fusion.23
  995.7 23.0 %fusion = f32[192,4096]{1,0:T(8,128)} fusion(bf16[192,4096]{1,0:T(8,128)(2,1)S(1)} %fusion.23, bf16[512,8,32,128]{3,2,1,0:T(8,128)(2,1)} %bitcast.113), kind=kOutput, calls=%fused_computation.6 | convolution fusion | flops 6442450944 | bytes 38273024 | tf_op jit(solution)/shard_map/dot_general | solution.py:111
  1019.3 4.6 fusion.21
  1024.0 34.3 %reduce-scatter.5.cloned.1.call-done = bf16[192,1024]{1,0:T(8,128)(2,1)} async-done(((bf16[192,4096]{1,0:T(8,128)(2,1)}), bf16[192,1024]{1,0:T(8,128)(2,1)}) %reduce-scatter.5.cloned.1.call-update) | async-done | bytes 393232 | tf_op jit(solution)/shard_map/reduce_scatter | solution.py:116
  1058.3 1.9 fusion.35
  (87 shorter events, 15.0 us)
Async XLA Ops:
  6.5 3.7 copy-start
  6.5 41.4 %all-gather.9.cloned.1.call-start = ((), (), s32[]{:S(2)}) async-start(), calls=%async_computation.2 | async-start | bytes 1966080 | tf_op jit(solution)/shard_map/all_gather | solution.py:94
  7.3 240.1 %all-gather.13.cloned.1.call-start = ((), (), s32[]{:S(2)}) async-start(), calls=%async_computation.6 | async-start | bytes 25165824 | tf_op jit(solution)/shard_map/all_gather | solution.py:76
  8.1 439.8 %all-gather.15.cloned.1.call-start = ((), (), s32[]{:S(2)}) async-start(), calls=%async_computation.7 | async-start | bytes 25165824 | tf_op jit(solution)/shard_map/all_gather | solution.py:77
  8.8 639.4 %all-gather.17.cloned.1.call-start = ((), (), s32[]{:S(2)}) async-start(), calls=%async_computation.8 | async-start | bytes 25165824 | tf_op jit(solution)/shard_map/all_gather | solution.py:78
  8.9 6.9 copy-start.20
  8.9 6.9 copy-start.24
  8.9 8.1 copy-start.21
  8.9 8.1 copy-start.22
  8.9 8.2 copy-start.23
  9.4 880.7 %reduce-scatter.3.cloned.1.call-start = ((), (), s32[]{:S(2)}) async-start(), calls=%async_computation.3 | async-start | bytes 1966080 | tf_op jit(solution)/shard_map/reduce_scatter | solution.py:116
  740.0 29.4 %copy-start.2 = (bf16[192,4096]{1,0:T(8,128)(2,1)S(1)}, bf16[192,4096]{1,0:T(8,128)(2,1)}, u32[]{:S(2)}) copy-start(bf16[192,4096]{1,0:T(8,128)(2,1)} %all-gather.9.cloned.1.call-done) | copy-start | bytes 4718596
  792.8 23.1 %copy-start.8 = (bf16[32,8,128]{2,1,0:T(8,128)(2,1)S(1)}, bf16[32,8,128]{2,1,0:T(8,128)(2,1)}, u32[]{:S(2)}) copy-start(bf16[32,8,128]{2,1,0:T(8,128)(2,1)} %gather_fusion) | copy-start | bytes 196612
  792.8 23.1 %copy-start.10 = (bf16[1,8,4096]{2,1,0:T(8,128)(2,1)S(1)}, bf16[1,8,4096]{2,1,0:T(8,128)(2,1)}, u32[]{:S(2)}) copy-start(bf16[1,8,4096]{2,1,0:T(8,128)(2,1)} %param.28) | copy-start | bytes 196612
  792.8 23.1 %copy-start.13 = (s32[192]{0:T(256)S(1)}, s32[192]{0:T(256)}, u32[]{:S(2)}) copy-start(s32[192]{0:T(256)} %select_reduce_fusion) | copy-start | bytes 2308
  792.8 23.1 %copy-start.15 = (f32[192]{0:T(256)S(1)}, f32[192]{0:T(256)}, u32[]{:S(2)}) copy-start(f32[192]{0:T(256)} %fusion.74) | copy-start | bytes 2308
  792.8 23.1 %copy-start.18 = (pred[32]{0:T(512)(128)(4,1)S(1)}, pred[32]{0:T(512)(128)(4,1)}, u32[]{:S(2)}) copy-start(pred[32]{0:T(512)(128)(4,1)} %get-tuple-element.6) | copy-start | bytes 100
  816.0 5.6 copy-start.12
  816.0 5.6 copy-start.26
  826.5 23.1 %copy-start.9 = (bf16[32,8,128]{2,1,0:T(8,128)(2,1)S(1)}, bf16[32,8,128]{2,1,0:T(8,128)(2,1)}, u32[]{:S(2)}) copy-start(bf16[32,8,128]{2,1,0:T(8,128)(2,1)} %gather_fusion.2) | copy-start | bytes 196612
  826.5 23.6 %copy-start.11 = (bf16[1,8,4096]{2,1,0:T(8,128)(2,1)S(1)}, bf16[1,8,4096]{2,1,0:T(8,128)(2,1)}, u32[]{:S(2)}) copy-start(bf16[1,8,4096]{2,1,0:T(8,128)(2,1)} %param.33) | copy-start | bytes 196612
  850.1 40.0 %copy-start.5 = (bf16[192,1024]{1,0:T(8,128)(2,1)S(1)}, bf16[192,1024]{1,0:T(8,128)(2,1)}, u32[]{:S(2)}) copy-start(bf16[192,1024]{1,0:T(8,128)(2,1)} %param.19) | copy-start | bytes 1179652
  854.7 77.5 %all-gather.11.cloned.1.call-start = ((), (), s32[]{:S(2)}) async-start(), calls=%async_computation.4 | async-start | bytes 1966080 | tf_op jit(solution)/shard_map/all_gather | solution.py:94
  892.0 3.6 collective-permute-start
  896.5 161.8 %reduce-scatter.5.cloned.1.call-start = ((), (), s32[]{:S(2)}) async-start(), calls=%async_computation.5 | async-start | bytes 1966080 | tf_op jit(solution)/shard_map/reduce_scatter | solution.py:116
  934.1 28.3 %copy-start.3 = (bf16[192,4096]{1,0:T(8,128)(2,1)S(1)}, bf16[192,4096]{1,0:T(8,128)(2,1)}, u32[]{:S(2)}) copy-start(bf16[192,4096]{1,0:T(8,128)(2,1)} %all-gather.11.cloned.1.call-done) | copy-start | bytes 4718596
  995.7 23.1 %copy-start.14 = (s32[192]{0:T(256)S(1)}, s32[192]{0:T(256)}, u32[]{:S(2)}) copy-start(s32[192]{0:T(256)} %select_reduce_fusion) | copy-start | bytes 2308
  995.7 23.1 %copy-start.16 = (f32[192]{0:T(256)S(1)}, f32[192]{0:T(256)}, u32[]{:S(2)}) copy-start(f32[192]{0:T(256)} %fusion.74) | copy-start | bytes 2308
  995.7 23.1 %copy-start.19 = (pred[32]{0:T(512)(128)(4,1)S(1)}, pred[32]{0:T(512)(128)(4,1)}, u32[]{:S(2)}) copy-start(pred[32]{0:T(512)(128)(4,1)} %get-tuple-element.6) | copy-start | bytes 100
  1018.8 41.5 %copy-start.1 = (bf16[1,8,16384]{2,1,0:T(8,128)(2,1)S(1)}, bf16[1,8,16384]{2,1,0:T(8,128)(2,1)}, u32[]{:S(2)}) copy-start(bf16[1,8,16384]{2,1,0:T(8,128)(2,1)} %param.29) | copy-start | bytes 786436
  1019.3 39.0 %copy-start.4 = (bf16[192,1024]{1,0:T(8,128)(2,1)S(1)}, bf16[192,1024]{1,0:T(8,128)(2,1)}, u32[]{:S(2)}) copy-start(bf16[192,1024]{1,0:T(8,128)(2,1)} %broadcast_select_fusion) | copy-start | bytes 1179652
  1019.3 39.0 %copy-start.7 = (bf16[192,1024]{1,0:T(8,128)(2,1)S(1)}, bf16[192,1024]{1,0:T(8,128)(2,1)}, u32[]{:S(2)}) copy-start(bf16[192,1024]{1,0:T(8,128)(2,1)} %copy-done.6) | copy-start | bytes 1179652
  (3 other events, 2.2 us)
Sparse Core Ops, SparseCore 0:
  8.9 39.0 all-gather.8
  49.5 197.8 all-gather.12
  249.0 198.8 all-gather.14
  449.3 198.8 all-gather.16
  854.8 35.2 reduce-scatter.2
  896.6 35.6 all-gather.10
  1024.1 34.1 reduce-scatter.4
where the time goes:
time: 1080 us; the launch traced here: 1070 us
  waiting for transfers between devices  489 us (45%)
  local copies, waits for them, and re-layouts  377 us (35%)
  matrix products  175 us (16%)
  between operations  14 us (1%)
    scatter x4, local copies, waits for them, and re-layouts, place_tiles(): empty.at[feature_index, :, hidden_index, :].set(tile_set, mode='drop')  221 us
    all_gather x1, waiting for transfers between devices, per_device(): lax.all_gather(gate_tiles[0], 'rep', axis=0, tiled=True)  198 us
    scatter x2, local copies, waits for them, and re-layouts, place_tiles(): empty.at[hidden_index, :, feature_index, :].set(tile_set, mode='drop')  110 us
    all_gather x1, waiting for transfers between devices, per_device(): lax.all_gather(down_tiles[0], 'rep', axis=0, tiled=True)  75.9 us
    all_gather x1, waiting for transfers between devices, per_device(): lax.all_gather(up_tiles[0], 'rep', axis=0, tiled=True)  75.3 us
    reduce_scatter x2, waiting for transfers between devices, per_device(): lax.psum_scatter(partial_value.astype(jnp.bfloat16), 'tensor', scatter_di...  69.7 us
    all_gather x2, waiting for transfers between devices, per_device(): whole_rows = lax.all_gather(current, 'tensor', axis=1, tiled=True)  66.5 us
    dot_general x2, matrix products, per_device(): jnp.dot(normed, gate_dense, preferred_element_type=jnp.float32)  51.7 us
  transfers between devices with their start and end apart: 8, of which 8 were waited for; matrix products, arithmetic and copies ran while one was open for 24% of the time, Pallas kernels for 0%

commit v1 on v0

v1 whole, which is shorter than its diff:
```python
import functools

import jax
import jax.numpy as jnp
from jax import lax
from jax.experimental import pallas as pl
from jax.experimental.pallas import tpu as pltpu
from jax.sharding import PartitionSpec as P

BLOCK = 128
UNROLL = 4
VMEM_LIMIT = 56 * 1024 * 1024

perturb_scale = 0.5
epsilon = 1e-05


def hop(value, axis, steps, source, target):
    count = lax.axis_size(axis)
    pairs = [(source * count + i, target * count + (i + steps) % count) for i in range(count)]
    return lax.ppermute(value, ("section", axis), pairs)


def pick_matrix(row_member, member_seed, noise_count):
    member_ids = jnp.arange(member_seed.shape[0], dtype=jnp.int32)
    matched = row_member[:, None] == member_ids[None, :]
    seed_of = jnp.sum(jnp.where(matched, member_seed[None, :], 0), axis=1)
    sign_values = (1 - 2 * (row_member % 2)).astype(jnp.float32) * perturb_scale
    noise_ids = jnp.arange(noise_count, dtype=jnp.int32)
    return jnp.where(seed_of[:, None] == noise_ids[None, :], sign_values[:, None], jnp.float32(0.0))


def tile_plan(codes, block_rows, own_cols, owner_index, owners):
    tile_count = codes.shape[1]
    active = codes >= 0
    cleared = jnp.where(active, codes, 0)
    column = cleared // block_rows
    feature = cleared % block_rows
    per_owner = block_rows // owners
    feature = lax.rem(owner_index - feature // per_owner + owners, owners) * per_owner + feature % per_owner
    is_down = jnp.arange(3)[:, None] == 2
    major = jnp.where(is_down, feature, column)
    minor = jnp.where(is_down, column, feature)
    major_count = max(block_rows, own_cols)
    majors = jnp.arange(major_count, dtype=jnp.int32)
    filled = jnp.sum(
        jnp.where(active[:, None, :] & (major[:, None, :] == majors[None, :, None]), 1, 0), axis=2
    )
    padded = 2 * ((filled + 1) // 2)
    before = jnp.sum(jnp.where(majors[None, None, :] < major[:, :, None], padded[:, None, :], 0), axis=2)
    rank = jnp.sum(
        jnp.where(
            active[:, None, :]
            & (major[:, None, :] == major[:, :, None])
            & (minor[:, None, :] < minor[:, :, None]),
            1,
            0,
        ),
        axis=2,
    )
    place = jnp.where(active, before + rank, -1)
    length = tile_count + min(tile_count, major_count)
    group = 2 * UNROLL
    length = -(-length // group) * group
    tile_ids = jnp.arange(tile_count, dtype=jnp.int32)
    words = (tile_ids[None, :] - tile_count) + minor * 4096 + major * 1048576
    spots = jnp.arange(length, dtype=jnp.int32)
    packed = tile_count + jnp.sum(
        jnp.where(place[:, None, :] == spots[None, :, None], words[:, None, :], 0), axis=2
    )
    groups = (jnp.sum(padded, axis=1) + group - 1) // group
    return packed.astype(jnp.int32), groups.astype(jnp.int32)


def multiply_tiles(words_ref, groups_ref, which, length, read, tiles_ref, add):
    def group(i, carry):
        for u in range(UNROLL):
            at = which * length + (i * UNROLL + u) * 2
            first, second = words_ref[at], words_ref[at + 1]
            left = jnp.concatenate([read((first >> 12) & 255), read((second >> 12) & 255)], axis=1)
            right = jnp.concatenate([tiles_ref[first & 4095], tiles_ref[second & 4095]], axis=0)
            add(first >> 20, jnp.dot(left, right, preferred_element_type=jnp.float32))
        return carry

    lax.fori_loop(0, groups_ref[which], group, 0)


def expand_kernel(owners, reps, length, words_ref, groups_ref, *refs):
    blocks = refs[: owners * reps]
    gain_ref, left_ref, gate_hbm, up_hbm = refs[owners * reps : owners * reps + 4]
    own_ref, raw_ref = refs[owners * reps + 4 : owners * reps + 6]
    peer_refs = refs[owners * reps + 6 : owners * reps + 6 + reps - 1]
    x_ref, other_ref, gate_tiles, up_tiles, sems = refs[owners * reps + 6 + reps - 1 :]
    tile_count = gate_hbm.shape[0]
    copies = [
        pltpu.make_async_copy(gate_hbm, gate_tiles.at[pl.ds(0, tile_count)], sems.at[0]),
        pltpu.make_async_copy(up_hbm, up_tiles.at[pl.ds(0, tile_count)], sems.at[1]),
    ]
    for copy in copies:
        copy.start()
    gate_tiles[tile_count] = jnp.zeros((BLOCK, BLOCK), gate_tiles.dtype)
    up_tiles[tile_count] = jnp.zeros((BLOCK, BLOCK), up_tiles.dtype)
    rows, width = blocks[0].shape
    strip = 16
    for rep in range(reps):

        def norm_rows(i, carry, rep=rep):
            at = pl.multiple_of(i * strip, strip)
            total = jnp.zeros((strip, 1), jnp.float32)
            for owner in range(owners):
                values = blocks[owner * reps + rep][pl.ds(at, strip), :].astype(jnp.float32)
                total = total + jnp.sum(values * values, axis=1, keepdims=True)
            inverse = lax.rsqrt(total / (owners * width) + epsilon)
            for owner in range(owners):
                for part in range(width // BLOCK):
                    lanes = pl.ds(part * BLOCK, BLOCK)
                    values = blocks[owner * reps + rep][pl.ds(at, strip), lanes].astype(jnp.float32)
                    gain = gain_ref[:, pl.ds(owner * width + part * BLOCK, BLOCK)].astype(jnp.float32)
                    normed = (values * inverse * gain).astype(jnp.bfloat16)
                    x_ref[owner * (width // BLOCK) + part, pl.ds(rep * rows + at, strip), :] = normed
            return carry

        lax.fori_loop(0, rows // strip, norm_rows, 0)

    raw = jnp.zeros(raw_ref.shape, jnp.float32)
    for d in range(x_ref.shape[0]):
        raw = raw + lax.dot_general(
            x_ref[d, pl.ds(0, rows), :],
            left_ref[:, pl.ds(d * BLOCK, BLOCK)],
            (((1,), (1,)), ((), ())),
            preferred_element_type=jnp.float32,
        )
    raw_ref[...] = raw

    def read(block):
        return x_ref[block]

    for which, tiles in ((0, gate_tiles), (1, up_tiles)):
        own_ref[which] = jnp.zeros(own_ref.shape[1:], jnp.float32)
        other_ref[...] = jnp.zeros(other_ref.shape, jnp.float32)
        copies[which].wait()

        def add(block, product, which=which):
            own_ref[which, block] += product[:rows]
            if reps > 1:
                other_ref[block] += product[rows:]

        multiply_tiles(words_ref, groups_ref, which, length, read, tiles, add)
        for rep in range(1, reps):

            def narrow(c, carry, which=which, rep=rep):
                peer_refs[rep - 1][which, c] = other_ref[c, pl.ds((rep - 1) * rows, rows), :].astype(jnp.bfloat16)
                return carry

            lax.fori_loop(0, other_ref.shape[0], narrow, 0)


def expand(words, groups, blocks, gain, left, gate_tiles, up_tiles, own_cols):
    owners, reps = len(blocks), len(blocks[0])
    rows, width = blocks[0][0].shape
    tile_count = gate_tiles.shape[0]
    feature_blocks = owners * width // BLOCK
    length = words.shape[0] // 3
    smem = pl.BlockSpec(memory_space=pltpu.SMEM)
    vmem = pl.BlockSpec(memory_space=pltpu.VMEM)
    hbm = pl.BlockSpec(memory_space=pl.ANY)
    flat = [block for group in blocks for block in group]
    out = pl.pallas_call(
        functools.partial(expand_kernel, owners, reps, length),
        out_shape=[
            jax.ShapeDtypeStruct((2, own_cols, rows, BLOCK), jnp.float32),
            jax.ShapeDtypeStruct((rows, left.shape[0]), jnp.float32),
        ]
        + [jax.ShapeDtypeStruct((2, own_cols, rows, BLOCK), jnp.bfloat16)] * (reps - 1),
        in_specs=[smem, smem] + [vmem] * (len(flat) + 2) + [hbm, hbm],
        out_specs=[vmem] * (2 + reps - 1),
        scratch_shapes=[
            pltpu.VMEM((feature_blocks, reps * rows, BLOCK), jnp.bfloat16),
            pltpu.VMEM((own_cols, max(reps - 1, 1) * rows, BLOCK), jnp.float32),
            pltpu.VMEM((tile_count + 1, BLOCK, BLOCK), jnp.bfloat16),
            pltpu.VMEM((tile_count + 1, BLOCK, BLOCK), jnp.bfloat16),
            pltpu.SemaphoreType.DMA((2,)),
        ],
        compiler_params=pltpu.CompilerParams(vmem_limit_bytes=VMEM_LIMIT),
        cost_estimate=pl.CostEstimate(
            flops=2 * 2 * tile_count * reps * rows * BLOCK * BLOCK,
            bytes_accessed=4 * tile_count * BLOCK * BLOCK,
            transcendentals=0,
        ),
        name="expand",
    )(words, groups, *flat, gain, left, gate_tiles, up_tiles)
    return out[0], out[1], out[2:]


def activate_kernel(reps, own_ref, *refs):
    peers = refs[: reps - 1]
    raw_ref, picks_ref, gate_cols, up_cols, down_cols, hidden_ref, coef_ref = refs[reps - 1 :]
    noise = picks_ref.shape[1]

    @pl.when(pl.program_id(0) == 0)
    def _():
        coef_ref[...] = jnp.zeros_like(coef_ref)

    picks = picks_ref[...]
    coefs = [
        (picks * raw_ref[:, :noise]).astype(jnp.bfloat16),
        (picks * raw_ref[:, noise:]).astype(jnp.bfloat16),
    ]
    down = jnp.zeros(coef_ref.shape, jnp.float32)
    for c in range(own_ref.shape[1]):
        values = []
        for which, cols in ((0, gate_cols), (1, up_cols)):
            value = own_ref[which, c]
            for peer in peers:
                value = value + peer[which, c].astype(jnp.float32)
            values.append(value + jnp.dot(coefs[which], cols[c], preferred_element_type=jnp.float32))
        gate, up = values
        hidden = (gate / (1.0 + jnp.exp(-gate)) * up).astype(jnp.bfloat16)
        hidden_ref[c] = hidden
        down = down + lax.dot_general(
            hidden, down_cols[c], (((1,), (1,)), ((), ())), preferred_element_type=jnp.float32
        )
    coef_ref[...] += picks * down


def activate(own, peers, raw, picks, gate_cols, up_cols, down_cols):
    own_cols, rows = own.shape[1:3]
    noise = picks.shape[1]
    chunk = min(4, own_cols)
    wide = pl.BlockSpec((2, chunk, rows, BLOCK), lambda i: (0, i, 0, 0))
    cols = pl.BlockSpec((chunk, noise, BLOCK), lambda i: (i, 0, 0))
    return pl.pallas_call(
        functools.partial(activate_kernel, len(peers) + 1),
        grid=(own_cols // chunk,),
        out_shape=[
            jax.ShapeDtypeStruct((own_cols, rows, BLOCK), jnp.bfloat16),
            jax.ShapeDtypeStruct((rows, noise), jnp.float32),
        ],
        in_specs=[wide] * (len(peers) + 1)
        + [pl.BlockSpec(raw.shape, lambda i: (0, 0)), pl.BlockSpec(picks.shape, lambda i: (0, 0))]
        + [cols] * 3,
        out_specs=[
            pl.BlockSpec((chunk, rows, BLOCK), lambda i: (i, 0, 0)),
            pl.BlockSpec((rows, noise), lambda i: (0, 0)),
        ],
        compiler_params=pltpu.CompilerParams(vmem_limit_bytes=VMEM_LIMIT),
        name="activate",
    )(own, *peers, raw, picks, gate_cols, up_cols, down_cols)


def contract_kernel(owners, reps, length, words_ref, groups_ref, *refs):
    hiddens = refs[:reps]
    coef_ref, right_ref, tiles_hbm = refs[reps : reps + 3]
    outs = refs[reps + 3 : reps + 3 + owners]
    total_ref, tiles_ref, sem = refs[reps + 3 + owners :]
    tile_count = tiles_hbm.shape[0]
    copy = pltpu.make_async_copy(tiles_hbm, tiles_ref.at[pl.ds(0, tile_count)], sem)
    copy.start()
    tiles_ref[tile_count] = jnp.zeros((BLOCK, BLOCK), tiles_ref.dtype)
    rows = hiddens[0].shape[1]
    width = outs[0].shape[1]
    coef = coef_ref[...]
    high = coef.astype(jnp.bfloat16)
    low = (coef - high.astype(jnp.float32)).astype(jnp.bfloat16)
    for d in range(total_ref.shape[0]):
        right = right_ref[:, pl.ds(d * BLOCK, BLOCK)]
        total_ref[d, pl.ds(0, rows), :] = jnp.dot(high, right, preferred_element_type=jnp.float32) + jnp.dot(
            low, right, preferred_element_type=jnp.float32
        )
        if reps > 1:
            total_ref[d, pl.ds(rows, (reps - 1) * rows), :] = jnp.zeros(((reps - 1) * rows, BLOCK), jnp.float32)
    copy.wait()

    def read(block):
        return jnp.concatenate([hidden[block] for hidden in hiddens], axis=0)

    def add(block, product):
        total_ref[block] += product

    multiply_tiles(words_ref, groups_ref, 2, length, read, tiles_ref, add)
    for owner in range(owners):
        for part in range(width // BLOCK):
            outs[owner][:, pl.ds(part * BLOCK, BLOCK)] = total_ref[owner * (width // BLOCK) + part].astype(
                jnp.bfloat16
            )


def contract(words, groups, hiddens, coef, right, tiles, owners):
    own_cols, rows = hiddens[0].shape[:2]
    reps = len(hiddens)
    features = right.shape[1]
    tile_count = tiles.shape[0]
    smem = pl.BlockSpec(memory_space=pltpu.SMEM)
    vmem = pl.BlockSpec(memory_space=pltpu.VMEM)
    return pl.pallas_call(
        functools.partial(contract_kernel, owners, reps, words.shape[0] // 3),
        out_shape=[jax.ShapeDtypeStruct((reps * rows, features // owners), jnp.bfloat16)] * owners,
        in_specs=[smem, smem] + [vmem] * (reps + 2) + [pl.BlockSpec(memory_space=pl.ANY)],
        out_specs=[vmem] * owners,
        scratch_shapes=[
            pltpu.VMEM((features // BLOCK, reps * rows, BLOCK), jnp.float32),
            pltpu.VMEM((tile_count + 1, BLOCK, BLOCK), jnp.bfloat16),
            pltpu.SemaphoreType.DMA,
        ],
        compiler_params=pltpu.CompilerParams(vmem_limit_bytes=VMEM_LIMIT),
        cost_estimate=pl.CostEstimate(
            flops=2 * tile_count * reps * rows * BLOCK * BLOCK,
            bytes_accessed=2 * tile_count * BLOCK * BLOCK,
            transcendentals=0,
        ),
        name="contract",
    )(words, groups, *hiddens, coef, right, tiles)


def per_device(
    tokens,
    norm_gain,
    gate_tiles,
    up_tiles,
    down_tiles,
    gate_slot,
    up_slot,
    down_slot,
    owned_columns,
    gate_left,
    gate_right,
    up_left,
    up_right,
    down_left,
    down_right,
    row_member,
    member_seed,
):
    section_index = lax.axis_index("section")
    owner_index = lax.axis_index("tensor")
    rep_index = lax.axis_index("rep")
    owners, reps = lax.axis_size("tensor"), lax.axis_size("rep")
    rows, width = tokens.shape
    own_cols = owned_columns.shape[1] // owners
    block_rows = gate_left.shape[2] // BLOCK
    tile_count = gate_tiles.shape[1]

    codes = jnp.stack([gate_slot[0], up_slot[0], down_slot[0]])
    codes = lax.dynamic_slice_in_dim(codes, rep_index * tile_count, tile_count, axis=1)
    words, groups = tile_plan(codes, block_rows, own_cols, owner_index, owners)
    words = words.reshape(-1)

    rotation = lax.rem(owner_index - jnp.arange(owners, dtype=jnp.int32) + owners, owners)

    def rotated(table):
        parts = table.reshape(table.shape[0], owners, width)
        return jnp.take(parts, rotation, axis=1).reshape(table.shape)

    gain = rotated(norm_gain)
    left = rotated(jnp.concatenate([gate_left[0], up_left[0]], axis=0))
    right = rotated(down_right[0])
    columns = lax.dynamic_slice_in_dim(owned_columns[0], owner_index * own_cols, own_cols)

    def owned(table):
        blocked = table.reshape(table.shape[0], -1, BLOCK)
        return jnp.take(blocked, columns, axis=1).transpose(1, 0, 2)

    gate_cols, up_cols, down_cols = owned(gate_right[0]), owned(up_right[0]), owned(down_left[0])
    picks = pick_matrix(row_member, member_seed, gate_left.shape[1])

    def layer(streams, section, target):
        blocks = [streams] + [[hop(s, "tensor", step, section, section) for s in streams] for step in range(1, owners)]
        own, raw, partials = expand(
            words, groups, blocks, gain, left, gate_tiles[0], up_tiles[0], own_cols
        )
        received = [hop(p, "rep", -(g + 1), section, section) for g, p in enumerate(partials)]
        hidden, coef = activate(own, received, raw, picks, gate_cols, up_cols, down_cols)
        hiddens = [hidden] + [hop(hidden, "rep", g, section, section) for g in range(1, reps)]
        outs = contract(words, groups, hiddens, coef, right, down_tiles[0], owners)
        if section == target:
            summed = outs[0].astype(jnp.float32)
        else:
            summed = hop(outs[0], "tensor", 0, section, target).astype(jnp.float32)
        for step in range(1, owners):
            summed = summed + hop(outs[step], "tensor", -step, section, target).astype(jnp.float32)
        return summed

    streams = [tokens] + [hop(tokens, "rep", g, 0, 0) for g in range(1, reps)]
    residuals = [tokens] + [hop(tokens, "rep", g, 1, 1) for g in range(1, reps)]
    summed = layer(streams, 0, 1).astype(jnp.bfloat16)
    arrived = [summed] + [hop(summed, "rep", g, 1, 1) for g in range(1, reps)]
    streams = []
    for g in range(reps):
        value = residuals[g].astype(jnp.float32)
        for step in range(reps):
            at = (g - step) % reps
            value = value + arrived[step][at * rows : (at + 1) * rows].astype(jnp.float32)
        streams.append(value.astype(jnp.bfloat16))
    first = lax.ppermute(streams[0], "section", [(1, 0)])
    summed = layer(streams, 1, 1)
    value = streams[0].astype(jnp.float32) + summed[:rows]
    for g in range(1, reps):
        sent = summed[g * rows : (g + 1) * rows].astype(jnp.bfloat16)
        value = value + hop(sent, "rep", -g, 1, 1).astype(jnp.float32)
    second = value.astype(jnp.bfloat16)
    return jnp.where(section_index == 0, first, second)[None]


def solution(mesh):
    placed = (
        P(("pop", "rep"), "tensor"),
        P("section", None),
        P("section", ("tensor", "rep"), None, None),
        P("section", ("tensor", "rep"), None, None),
        P("section", ("tensor", "rep"), None, None),
        P("section", "tensor"),
        P("section", "tensor"),
        P("section", "tensor"),
        P("section", None),
        P("section", None, None),
        P("section", None, None),
        P("section", None, None),
        P("section", None, None),
        P("section", None, None),
        P("section", None, None),
        P(("pop", "rep")),
        P("pop"),
    )
    return jax.shard_map(
        per_device,
        mesh=mesh,
        in_specs=placed,
        out_specs=P("section", ("pop", "rep"), "tensor"),
        check_vma=False,
    )
```

time: 1080 us -> 441 us (0.41); the launches traced: 1070 us -> 440 us
  local copies, waits for them, and re-layouts: 377 us -> 14.1 us
  waiting for transfers between devices: 489 us -> 234 us
  matrix products: 175 us -> 0 us
  Pallas kernels: 0 us -> 118 us
  starting transfers between devices: 1.52 us -> 62.6 us
  between operations: 14 us -> 0.68 us
    all_gather x5 -> x0, waiting for transfers between devices: 415 us -> none  [the longest x1 198 us: per_device(): lax.all_gather(gate_tiles[0], 'rep', axis=0, tiled=True)]
    scatter x6 -> x0, local copies, waits for them, and re-layouts: 331 us -> none  [the longest x4 221 us: place_tiles(): empty.at[feature_index, :, hidden_index, :].set(tile_set, mode='drop')]
    ppermute x1 -> x28, waiting for transfers between devices: 2.32 us -> 234 us  [the longest x27 234 us: hop(): return lax.ppermute(value, ('section', axis), pairs)]
    dot_general x14 -> x0, matrix products: 175 us -> none  [the longest x2 51.7 us: per_device(): jnp.dot(normed, gate_dense, preferred_element_type=jnp.float32)]
    pallas_call x0 -> x6, Pallas kernels: none -> 118 us  [the longest x2 58.1 us: expand(): pl.pallas_call(functools.partial(expand_kernel, owners, reps, length), ou...]
    reduce_scatter x2 -> x0, waiting for transfers between devices: 69.7 us -> none  [per_device(): lax.psum_scatter(partial_value.astype(jnp.bfloat16), 'tensor', scatter_di...]
    ppermute x1 -> x28, starting transfers between devices: 1.28 us -> 62.6 us  [the longest x27 61.3 us: hop(): return lax.ppermute(value, ('section', axis), pairs)]
    another operation x3 -> x0, local copies, waits for them, and re-layouts: 40.2 us -> none
  transfers between devices with their start and end apart: 8 -> 28, of which waited for: 8 -> 11; matrix products, arithmetic and copies ran while one was open for 24% -> 4% of each run, Pallas kernels for 0% -> 0%
where the time goes in v1:
time: 441 us; the launch traced here: 440 us
  waiting for transfers between devices  234 us (53%)
  Pallas kernels  118 us (27%)
  starting transfers between devices  62.6 us (14%)
  local copies, waits for them, and re-layouts  14.1 us (3%)
  other arithmetic  11.7 us (3%)
    ppermute x27, waiting for transfers between devices, hop(): return lax.ppermute(value, ('section', axis), pairs)  234 us
    ppermute x27, starting transfers between devices, hop(): return lax.ppermute(value, ('section', axis), pairs)  61.3 us
    pallas_call x2, Pallas kernels, expand(): pl.pallas_call(functools.partial(expand_kernel, owners, reps, length), ou...  58.1 us
    pallas_call x2, Pallas kernels, contract(): pl.pallas_call(functools.partial(contract_kernel, owners, reps, words.sha...  41.7 us
    pallas_call x2, Pallas kernels, activate(): pl.pallas_call(functools.partial(activate_kernel, len(peers) + 1), grid=(...  17.9 us
  transfers between devices with their start and end apart: 28, of which 11 were waited for; matrix products, arithmetic and copies ran while one was open for 4% of the time, Pallas kernels for 0%

profile of v1, /device:TPU:1, one launch (start us, length us, event | category | flops | bytes accessed | tf_op | source)
XLA Modules:
  0.0 440.3 jit_solution(644793825679551430)
XLA Ops:
  13.9 29.1 %expand.2 = (f32[2,32,192,128]{3,2,1,0:T(8,128)}, f32[192,16]{1,0:T(8,128)}, bf16[2,32,192,128]{3,2,1,0:T(8,128)(2,1)}) custom-call(s32[864]{0:T(1024)} %add.168.words_ref, s32[3]{0:T(128)} %and_select_fusion.1.groups_ref, bf16[192,1024]{1,0:T(8,128)(2,1)} %refs_0_.1, bf16[192,1024]{1,0:T(8,128)(2,1)} %copy-done.14, bf16[192,1024]{1,0:T(8,128)(2,1)} %copy-done.15, ...), custom_call_target="tpu_custom_call" | custom-call | flops 6442450944 | bytes 16777216 | tf_op jit(solution)/shard_map/expand/pallas_call | solution.py:168
  49.4 1.7 copy-done.2
  51.1 9.0 %activate.2 = (bf16[32,192,128]{2,1,0:T(8,128)(2,1)}, f32[192,8]{1,0:T(8,128)}) custom-call(f32[2,32,192,128]{3,2,1,0:T(8,128)} %get-tuple-element.24.own_ref, bf16[2,32,192,128]{3,2,1,0:T(8,128)(2,1)} %copy-done.2, f32[192,16]{1,0:T(8,128)} %get-tuple-element.26.refs_1_, f32[192,8]{1,0:T(8,128)} %fusion.5.refs_2_, ...), custom_call_target="tpu_custom_call" | custom-call | tf_op jit(solution)/shard_map/activate/pallas_call | solution.py:232
  63.2 20.8 %contract.2 = (bf16[384,1024]{1,0:T(8,128)(2,1)}, bf16[384,1024]{1,0:T(8,128)(2,1)}, bf16[384,1024]{1,0:T(8,128)(2,1)}, bf16[384,1024]{1,0:T(8,128)(2,1)}) custom-call(s32[864]{0:T(1024)} %add.168.words_ref, s32[3]{0:T(128)} %and_select_fusion.1.groups_ref, bf16[32,192,128]{2,1,0:T(8,128)(2,1)} %get-tuple-element.27.refs_0_, ...), custom_call_target="tpu_custom_call" | custom-call | flops 3221225472 | bytes 8388608 | tf_op jit(solution)/shard_map/contract/pallas_call | solution.py:295
  89.4 100.0 %collective-permute-done.10 = bf16[384,1024]{1,0:T(8,128)(2,1)S(1)} collective-permute-done((bf16[384,1024]{1,0:T(8,128)(2,1)}, bf16[384,1024]{1,0:T(8,128)(2,1)S(1)}, u32[]{:S(2)}, u32[]{:S(2)}) %collective-permute-start.10) | collective-permute-done | bytes 786464 | tf_op jit(solution)/shard_map/ppermute | solution.py:21
  189.4 18.7 %collective-permute-done.12 = bf16[384,1024]{1,0:T(8,128)(2,1)S(1)} collective-permute-done((bf16[384,1024]{1,0:T(8,128)(2,1)}, bf16[384,1024]{1,0:T(8,128)(2,1)S(1)}, u32[]{:S(2)}, u32[]{:S(2)}) %collective-permute-start.12) | collective-permute-done | bytes 786464 | tf_op jit(solution)/shard_map/ppermute | solution.py:21
  208.8 2.9 collective-permute-start.13
  211.7 2.3 collective-permute-start.15
  214.1 11.6 %collective-permute-done.15 = bf16[192,1024]{1,0:T(8,128)(2,1)S(1)} collective-permute-done((bf16[192,1024]{1,0:T(8,128)(2,1)S(1)}, bf16[192,1024]{1,0:T(8,128)(2,1)S(1)}, u32[]{:S(2)}, u32[]{:S(2)}) %collective-permute-start.15) | collective-permute-done | bytes 393248 | tf_op jit(solution)/shard_map/ppermute | solution.py:21
  226.2 1.9 collective-permute-start.16
  228.1 1.9 collective-permute-start.18
  230.1 5.4 %collective-permute-start.17 = (bf16[192,1024]{1,0:T(8,128)(2,1)S(1)}, bf16[192,1024]{1,0:T(8,128)(2,1)S(1)}, u32[]{:S(2)}, u32[]{:S(2)}) collective-permute-start(bf16[192,1024]{1,0:T(8,128)(2,1)S(1)} %get-tuple-element.51.refs_1_), channel_id=1, source_target_pairs={{8,10},{10,12},{12,14},{14,8},{9,11},{11,13},{13,15},{15,9},{24,26... | collective-permute-start | bytes 1179656 | tf_op jit(solution)/shard_map/ppermute | solution.py:21
  235.5 1.9 collective-permute-start.19
  237.4 4.0 collective-permute-start.20
  241.5 3.4 collective-permute-start.21
  245.2 8.4 %collective-permute-done.18.refs_4_ = bf16[192,1024]{1,0:T(8,128)(2,1)S(1)} collective-permute-done((bf16[192,1024]{1,0:T(8,128)(2,1)S(1)}, bf16[192,1024]{1,0:T(8,128)(2,1)S(1)}, u32[]{:S(2)}, u32[]{:S(2)}) %collective-permute-start.18) | collective-permute-done | bytes 393248 | tf_op jit(solution)/shard_map/ppermute | solution.py:21
  253.5 4.2 collective-permute-done.19.refs_5_
  257.8 4.1 collective-permute-done.21.refs_7_
  262.6 29.0 %expand.3 = (f32[2,32,192,128]{3,2,1,0:T(8,128)}, f32[192,16]{1,0:T(8,128)}, bf16[2,32,192,128]{3,2,1,0:T(8,128)(2,1)}) custom-call(s32[864]{0:T(1024)} %add.168.words_ref, s32[3]{0:T(128)} %and_select_fusion.1.groups_ref, bf16[192,1024]{1,0:T(8,128)(2,1)} %copy-done.4, bf16[192,1024]{1,0:T(8,128)(2,1)} %copy-done.7, bf16[192,1024]{1,0:T(8,128)(2,1)} %copy-done.18, ...), custom_call_target="tpu_custom_call" | custom-call | flops 6442450944 | bytes 16777216 | tf_op jit(solution)/shard_map/expand/pallas_call | solution.py:168
  291.6 4.9 %collective-permute-start.22 = (bf16[2,32,192,128]{3,2,1,0:T(8,128)(2,1)}, bf16[2,32,192,128]{3,2,1,0:T(8,128)(2,1)S(1)}, u32[]{:S(2)}, u32[]{:S(2)}) collective-permute-start(bf16[2,32,192,128]{3,2,1,0:T(8,128)(2,1)} %get-tuple-element.34), channel_id=1, source_target_pairs={{8,9},{9,8},{10,11},{11,10},{12,13},{13,12},{14,15},{15,14},{24,25... | collective-permute-start | bytes 9437192 | tf_op jit(solution)/shard_map/ppermute | solution.py:21
  296.6 34.9 %collective-permute-done.22.refs_0_ = bf16[2,32,192,128]{3,2,1,0:T(8,128)(2,1)S(1)} collective-permute-done((bf16[2,32,192,128]{3,2,1,0:T(8,128)(2,1)}, bf16[2,32,192,128]{3,2,1,0:T(8,128)(2,1)S(1)}, u32[]{:S(2)}, u32[]{:S(2)}) %collective-permute-start.22) | collective-permute-done | bytes 3145760 | tf_op jit(solution)/shard_map/ppermute | solution.py:21
  333.1 8.9 %activate.3 = (bf16[32,192,128]{2,1,0:T(8,128)(2,1)}, f32[192,8]{1,0:T(8,128)}) custom-call(f32[2,32,192,128]{3,2,1,0:T(8,128)} %get-tuple-element.33.own_ref, bf16[2,32,192,128]{3,2,1,0:T(8,128)(2,1)} %copy-done.3, f32[192,16]{1,0:T(8,128)} %get-tuple-element.35.refs_1_, f32[192,8]{1,0:T(8,128)} %fusion.5.refs_2_, ...), custom_call_target="tpu_custom_call" | custom-call | tf_op jit(solution)/shard_map/activate/pallas_call | solution.py:232
  342.0 3.5 collective-permute-start.23
  345.6 18.0 %collective-permute-done.23.refs_1_ = bf16[32,192,128]{2,1,0:T(8,128)(2,1)S(1)} collective-permute-done((bf16[32,192,128]{2,1,0:T(8,128)(2,1)}, bf16[32,192,128]{2,1,0:T(8,128)(2,1)S(1)}, u32[]{:S(2)}, u32[]{:S(2)}) %collective-permute-start.23) | collective-permute-done | bytes 1572896 | tf_op jit(solution)/shard_map/ppermute | solution.py:21
  364.8 20.9 %contract.3 = (bf16[384,1024]{1,0:T(8,128)(2,1)}, bf16[384,1024]{1,0:T(8,128)(2,1)}, bf16[384,1024]{1,0:T(8,128)(2,1)}, bf16[384,1024]{1,0:T(8,128)(2,1)}) custom-call(s32[864]{0:T(1024)} %add.168.words_ref, s32[3]{0:T(128)} %and_select_fusion.1.groups_ref, bf16[32,192,128]{2,1,0:T(8,128)(2,1)} %get-tuple-element.36.refs_0_, ...), custom_call_target="tpu_custom_call" | custom-call | flops 3221225472 | bytes 8388608 | tf_op jit(solution)/shard_map/contract/pallas_call | solution.py:295
  385.6 3.8 collective-permute-start.24
  389.5 6.2 %collective-permute-start.25 = (bf16[384,1024]{1,0:T(8,128)(2,1)}, bf16[384,1024]{1,0:T(8,128)(2,1)S(1)}, u32[]{:S(2)}, u32[]{:S(2)}) collective-permute-start(bf16[384,1024]{1,0:T(8,128)(2,1)} %get-tuple-element.40), channel_id=1, source_target_pairs={{8,12},{10,14},{12,8},{14,10},{9,13},{11,15},{13,9},{15,11},{24,28... | collective-permute-start | bytes 2359304 | tf_op jit(solution)/shard_map/ppermute | solution.py:21
  395.7 3.4 collective-permute-start.26
  400.4 28.2 %collective-permute-done.25 = bf16[384,1024]{1,0:T(8,128)(2,1)S(1)} collective-permute-done((bf16[384,1024]{1,0:T(8,128)(2,1)}, bf16[384,1024]{1,0:T(8,128)(2,1)S(1)}, u32[]{:S(2)}, u32[]{:S(2)}) %collective-permute-start.25) | collective-permute-done | bytes 786464 | tf_op jit(solution)/shard_map/ppermute | solution.py:21
  428.6 1.7 convert_add_fusion
  430.4 3.8 collective-permute-start.27
  434.2 5.1 %collective-permute-done.27 = bf16[192,1024]{1,0:T(8,128)(2,1)S(1)} collective-permute-done((bf16[192,1024]{1,0:T(8,128)(2,1)S(1)}, bf16[192,1024]{1,0:T(8,128)(2,1)S(1)}, u32[]{:S(2)}, u32[]{:S(2)}) %collective-permute-start.27) | collective-permute-done | bytes 393248 | tf_op jit(solution)/shard_map/ppermute | solution.py:21
  (129 shorter events, 35.9 us)
Async XLA Ops:
  0.0 44.0 %copy-start = (bf16[1,8,16384]{2,1,0:T(8,128)(2,1)S(1)}, bf16[1,8,16384]{2,1,0:T(8,128)(2,1)}, u32[]{:S(2)}) copy-start(bf16[1,8,16384]{2,1,0:T(8,128)(2,1)} %param.29) | copy-start | bytes 786436
  0.0 9.3 %collective-permute-start = (bf16[192,1024]{1,0:T(8,128)(2,1)}, bf16[192,1024]{1,0:T(8,128)(2,1)S(1)}, u32[]{:S(2)}, u32[]{:S(2)}) collective-permute-start(bf16[192,1024]{1,0:T(8,128)(2,1)} %refs_0_.1), channel_id=1, source_target_pairs={{0,1},{1,0},{2,3},{3,2},{4,5},{5,4},{6,7},{7,6},{16,17},{17,16},{1... | collective-permute-start | bytes 1179656 | tf_op jit(solution)/shard_map/ppermute | solution.py:21
  0.8 9.9 %collective-permute-start.1 = (bf16[192,1024]{1,0:T(8,128)(2,1)}, bf16[192,1024]{1,0:T(8,128)(2,1)S(1)}, u32[]{:S(2)}, u32[]{:S(2)}) collective-permute-start(bf16[192,1024]{1,0:T(8,128)(2,1)} %refs_0_.1), channel_id=1, source_target_pairs={{0,2},{2,4},{4,6},{6,0},{1,3},{3,5},{5,7},{7,1},{16,18},{18,20},{2... | collective-permute-start | bytes 1179656 | tf_op jit(solution)/shard_map/ppermute | solution.py:21
  1.5 11.1 %collective-permute-start.3 = (bf16[192,1024]{1,0:T(8,128)(2,1)}, bf16[192,1024]{1,0:T(8,128)(2,1)S(1)}, u32[]{:S(2)}, u32[]{:S(2)}) collective-permute-start(bf16[192,1024]{1,0:T(8,128)(2,1)} %refs_0_.1), channel_id=1, source_target_pairs={{0,4},{2,6},{4,0},{6,2},{1,5},{3,7},{5,1},{7,3},{16,20},{18,22},{2... | collective-permute-start | bytes 1179656 | tf_op jit(solution)/shard_map/ppermute | solution.py:21
  2.2 10.4 %collective-permute-start.5 = (bf16[192,1024]{1,0:T(8,128)(2,1)}, bf16[192,1024]{1,0:T(8,128)(2,1)S(1)}, u32[]{:S(2)}, u32[]{:S(2)}) collective-permute-start(bf16[192,1024]{1,0:T(8,128)(2,1)} %refs_0_.1), channel_id=1, source_target_pairs={{0,6},{2,0},{4,2},{6,4},{1,7},{3,1},{5,3},{7,5},{16,22},{18,16},{2... | collective-permute-start | bytes 1179656 | tf_op jit(solution)/shard_map/ppermute | solution.py:21
  9.3 3.4 collective-permute-start.2
  10.0 2.7 collective-permute-start.4
  10.7 2.0 collective-permute-start.6
  43.0 6.4 %collective-permute-start.7 = (bf16[2,32,192,128]{3,2,1,0:T(8,128)(2,1)}, bf16[2,32,192,128]{3,2,1,0:T(8,128)(2,1)S(1)}, u32[]{:S(2)}, u32[]{:S(2)}) collective-permute-start(bf16[2,32,192,128]{3,2,1,0:T(8,128)(2,1)} %get-tuple-element.25), channel_id=1, source_target_pairs={{0,1},{1,0},{2,3},{3,2},{4,5},{5,4},{6,7},{7,6},{16,17},{17,16},{1... | collective-permute-start | bytes 9437192 | tf_op jit(solution)/shard_map/ppermute | solution.py:21
  60.1 2.0 collective-permute-start.8
  84.0 105.4 %collective-permute-start.10 = (bf16[384,1024]{1,0:T(8,128)(2,1)}, bf16[384,1024]{1,0:T(8,128)(2,1)S(1)}, u32[]{:S(2)}, u32[]{:S(2)}) collective-permute-start(bf16[384,1024]{1,0:T(8,128)(2,1)} %get-tuple-element.30), channel_id=1, source_target_pairs={{0,14},{2,8},{4,10},{6,12},{1,15},{3,9},{5,11},{7,13},{16,30},{18,... | collective-permute-start | bytes 2359304 | tf_op jit(solution)/shard_map/ppermute | solution.py:21
  85.3 104.1 %collective-permute-start.11 = (bf16[384,1024]{1,0:T(8,128)(2,1)}, bf16[384,1024]{1,0:T(8,128)(2,1)S(1)}, u32[]{:S(2)}, u32[]{:S(2)}) collective-permute-start(bf16[384,1024]{1,0:T(8,128)(2,1)} %get-tuple-element.31), channel_id=1, source_target_pairs={{0,12},{2,14},{4,8},{6,10},{1,13},{3,15},{5,9},{7,11},{16,28},{18,... | collective-permute-start | bytes 2359304 | tf_op jit(solution)/shard_map/ppermute | solution.py:21
  86.6 121.5 %collective-permute-start.12 = (bf16[384,1024]{1,0:T(8,128)(2,1)}, bf16[384,1024]{1,0:T(8,128)(2,1)S(1)}, u32[]{:S(2)}, u32[]{:S(2)}) collective-permute-start(bf16[384,1024]{1,0:T(8,128)(2,1)} %get-tuple-element.32), channel_id=1, source_target_pairs={{0,10},{2,12},{4,14},{6,8},{1,11},{3,13},{5,15},{7,9},{16,26},{18,... | collective-permute-start | bytes 2359304 | tf_op jit(solution)/shard_map/ppermute | solution.py:21
  87.9 123.8 %copy-start.6 = (bf16[192,1024]{1,0:T(8,128)(2,1)S(1)}, bf16[192,1024]{1,0:T(8,128)(2,1)}, u32[]{:S(2)}) copy-start(bf16[192,1024]{1,0:T(8,128)(2,1)} %refs_0_.1) | copy-start | bytes 1179652
  88.0 120.2 %collective-permute-start.9 = (bf16[384,1024]{1,0:T(8,128)(2,1)}, bf16[384,1024]{1,0:T(8,128)(2,1)S(1)}, u32[]{:S(2)}, u32[]{:S(2)}) collective-permute-start(bf16[384,1024]{1,0:T(8,128)(2,1)} %get-tuple-element.29), channel_id=1, source_target_pairs={{0,8},{2,10},{4,12},{6,14},{1,9},{3,11},{5,13},{7,15},{16,24},{18,... | collective-permute-start | bytes 2359304 | tf_op jit(solution)/shard_map/ppermute | solution.py:21
  208.8 17.0 %collective-permute-start.13 = (bf16[384,1024]{1,0:T(8,128)(2,1)S(1)}, bf16[384,1024]{1,0:T(8,128)(2,1)S(1)}, u32[]{:S(2)}, u32[]{:S(2)}) collective-permute-start(bf16[384,1024]{1,0:T(8,128)(2,1)S(1)} %add_convert_fusion), channel_id=1, source_target_pairs={{8,9},{9,8},{10,11},{11,10},{12,13},{13,12},{14,15},{15,14},{24,25... | collective-permute-start | bytes 2359304 | tf_op jit(solution)/shard_map/ppermute | solution.py:21
  211.7 14.0 %collective-permute-start.15 = (bf16[192,1024]{1,0:T(8,128)(2,1)S(1)}, bf16[192,1024]{1,0:T(8,128)(2,1)S(1)}, u32[]{:S(2)}, u32[]{:S(2)}) collective-permute-start(bf16[192,1024]{1,0:T(8,128)(2,1)S(1)} %copy-done.6), channel_id=1, source_target_pairs={{8,9},{9,8},{10,11},{11,10},{12,13},{13,12},{14,15},{15,14},{24,25... | collective-permute-start | bytes 1179656 | tf_op jit(solution)/shard_map/ppermute | solution.py:21
  226.2 35.6 %copy-start.4 = (bf16[192,1024]{1,0:T(8,128)(2,1)}, bf16[192,1024]{1,0:T(8,128)(2,1)S(1)}, u32[]{:S(2)}) copy-start(bf16[192,1024]{1,0:T(8,128)(2,1)S(1)} %get-tuple-element.52.refs_0_) | copy-start | bytes 1179652
  226.2 35.6 %copy-start.7 = (bf16[192,1024]{1,0:T(8,128)(2,1)}, bf16[192,1024]{1,0:T(8,128)(2,1)S(1)}, u32[]{:S(2)}) copy-start(bf16[192,1024]{1,0:T(8,128)(2,1)S(1)} %get-tuple-element.51.refs_1_) | copy-start | bytes 1179652
  226.2 15.2 %collective-permute-start.16 = (bf16[192,1024]{1,0:T(8,128)(2,1)S(1)}, bf16[192,1024]{1,0:T(8,128)(2,1)S(1)}, u32[]{:S(2)}, u32[]{:S(2)}) collective-permute-start(bf16[192,1024]{1,0:T(8,128)(2,1)S(1)} %get-tuple-element.52.refs_0_), channel_id=1, source_target_pairs={{8,10},{10,12},{12,14},{14,8},{9,11},{11,13},{13,15},{15,9},{24,26... | collective-permute-start | bytes 1179656 | tf_op jit(solution)/shard_map/ppermute | solution.py:21
  228.1 25.4 %collective-permute-start.18 = (bf16[192,1024]{1,0:T(8,128)(2,1)S(1)}, bf16[192,1024]{1,0:T(8,128)(2,1)S(1)}, u32[]{:S(2)}, u32[]{:S(2)}) collective-permute-start(bf16[192,1024]{1,0:T(8,128)(2,1)S(1)} %get-tuple-element.52.refs_0_), channel_id=1, source_target_pairs={{8,12},{10,14},{12,8},{14,10},{9,13},{11,15},{13,9},{15,11},{24,28... | collective-permute-start | bytes 1179656 | tf_op jit(solution)/shard_map/ppermute | solution.py:21
  230.1 15.1 %collective-permute-start.17 = (bf16[192,1024]{1,0:T(8,128)(2,1)S(1)}, bf16[192,1024]{1,0:T(8,128)(2,1)S(1)}, u32[]{:S(2)}, u32[]{:S(2)}) collective-permute-start(bf16[192,1024]{1,0:T(8,128)(2,1)S(1)} %get-tuple-element.51.refs_1_), channel_id=1, source_target_pairs={{8,10},{10,12},{12,14},{14,8},{9,11},{11,13},{13,15},{15,9},{24,26... | collective-permute-start | bytes 1179656 | tf_op jit(solution)/shard_map/ppermute | solution.py:21
  235.5 22.2 %collective-permute-start.19 = (bf16[192,1024]{1,0:T(8,128)(2,1)S(1)}, bf16[192,1024]{1,0:T(8,128)(2,1)S(1)}, u32[]{:S(2)}, u32[]{:S(2)}) collective-permute-start(bf16[192,1024]{1,0:T(8,128)(2,1)S(1)} %get-tuple-element.51.refs_1_), channel_id=1, source_target_pairs={{8,12},{10,14},{12,8},{14,10},{9,13},{11,15},{13,9},{15,11},{24,28... | collective-permute-start | bytes 1179656 | tf_op jit(solution)/shard_map/ppermute | solution.py:21
  237.4 20.3 %collective-permute-start.20 = (bf16[192,1024]{1,0:T(8,128)(2,1)S(1)}, bf16[192,1024]{1,0:T(8,128)(2,1)S(1)}, u32[]{:S(2)}, u32[]{:S(2)}) collective-permute-start(bf16[192,1024]{1,0:T(8,128)(2,1)S(1)} %get-tuple-element.52.refs_0_), channel_id=1, source_target_pairs={{8,14},{10,8},{12,10},{14,12},{9,15},{11,9},{13,11},{15,13},{24,30... | collective-permute-start | bytes 1179656 | tf_op jit(solution)/shard_map/ppermute | solution.py:21
  241.5 20.4 %collective-permute-start.21 = (bf16[192,1024]{1,0:T(8,128)(2,1)S(1)}, bf16[192,1024]{1,0:T(8,128)(2,1)S(1)}, u32[]{:S(2)}, u32[]{:S(2)}) collective-permute-start(bf16[192,1024]{1,0:T(8,128)(2,1)S(1)} %get-tuple-element.51.refs_1_), channel_id=1, source_target_pairs={{8,14},{10,8},{12,10},{14,12},{9,15},{11,9},{13,11},{15,13},{24,30... | collective-permute-start | bytes 1179656 | tf_op jit(solution)/shard_map/ppermute | solution.py:21
  291.6 39.8 %collective-permute-start.22 = (bf16[2,32,192,128]{3,2,1,0:T(8,128)(2,1)}, bf16[2,32,192,128]{3,2,1,0:T(8,128)(2,1)S(1)}, u32[]{:S(2)}, u32[]{:S(2)}) collective-permute-start(bf16[2,32,192,128]{3,2,1,0:T(8,128)(2,1)} %get-tuple-element.34), channel_id=1, source_target_pairs={{8,9},{9,8},{10,11},{11,10},{12,13},{13,12},{14,15},{15,14},{24,25... | collective-permute-start | bytes 9437192 | tf_op jit(solution)/shard_map/ppermute | solution.py:21
  342.0 21.5 %collective-permute-start.23 = (bf16[32,192,128]{2,1,0:T(8,128)(2,1)}, bf16[32,192,128]{2,1,0:T(8,128)(2,1)S(1)}, u32[]{:S(2)}, u32[]{:S(2)}) collective-permute-start(bf16[32,192,128]{2,1,0:T(8,128)(2,1)} %get-tuple-element.36.refs_0_), channel_id=1, source_target_pairs={{8,9},{9,8},{10,11},{11,10},{12,13},{13,12},{14,15},{15,14},{24,25... | collective-permute-start | bytes 4718600 | tf_op jit(solution)/shard_map/ppermute | solution.py:21
  385.6 14.7 %collective-permute-start.24 = (bf16[384,1024]{1,0:T(8,128)(2,1)}, bf16[384,1024]{1,0:T(8,128)(2,1)S(1)}, u32[]{:S(2)}, u32[]{:S(2)}) collective-permute-start(bf16[384,1024]{1,0:T(8,128)(2,1)} %get-tuple-element.39), channel_id=1, source_target_pairs={{8,14},{10,8},{12,10},{14,12},{9,15},{11,9},{13,11},{15,13},{24,30... | collective-permute-start | bytes 2359304 | tf_op jit(solution)/shard_map/ppermute | solution.py:21
  389.5 39.1 %collective-permute-start.25 = (bf16[384,1024]{1,0:T(8,128)(2,1)}, bf16[384,1024]{1,0:T(8,128)(2,1)S(1)}, u32[]{:S(2)}, u32[]{:S(2)}) collective-permute-start(bf16[384,1024]{1,0:T(8,128)(2,1)} %get-tuple-element.40), channel_id=1, source_target_pairs={{8,12},{10,14},{12,8},{14,10},{9,13},{11,15},{13,9},{15,11},{24,28... | collective-permute-start | bytes 2359304 | tf_op jit(solution)/shard_map/ppermute | solution.py:21
  395.7 32.9 %collective-permute-start.26 = (bf16[384,1024]{1,0:T(8,128)(2,1)}, bf16[384,1024]{1,0:T(8,128)(2,1)S(1)}, u32[]{:S(2)}, u32[]{:S(2)}) collective-permute-start(bf16[384,1024]{1,0:T(8,128)(2,1)} %get-tuple-element.41), channel_id=1, source_target_pairs={{8,10},{10,12},{12,14},{14,8},{9,11},{11,13},{13,15},{15,9},{24,26... | collective-permute-start | bytes 2359304 | tf_op jit(solution)/shard_map/ppermute | solution.py:21
  399.0 35.1 %collective-permute-start.14 = (bf16[192,1024]{1,0:T(8,128)(2,1)S(1)}, bf16[192,1024]{1,0:T(8,128)(2,1)S(1)}, u32[]{:S(2)}, u32[]{:S(2)}) collective-permute-start(bf16[192,1024]{1,0:T(8,128)(2,1)S(1)} %copy-done.5), channel_id=1, source_target_pairs={{8,0},{9,1},{10,2},{11,3},{12,4},{13,5},{14,6},{15,7},{24,16},{25,... | collective-permute-start | bytes 1179656 | tf_op jit(solution)/shard_map/ppermute | solution.py:394
  430.4 8.9 %collective-permute-start.27 = (bf16[192,1024]{1,0:T(8,128)(2,1)S(1)}, bf16[192,1024]{1,0:T(8,128)(2,1)S(1)}, u32[]{:S(2)}, u32[]{:S(2)}) collective-permute-start(bf16[192,1024]{1,0:T(8,128)(2,1)S(1)} %slice.57), channel_id=1, source_target_pairs={{8,9},{9,8},{10,11},{11,10},{12,13},{13,12},{14,15},{15,14},{24,25... | collective-permute-start | bytes 1179656 | tf_op jit(solution)/shard_map/ppermute | solution.py:21
  (23 other events, 223.9 us)

commit v2 on v1

v2 whole, which is shorter than its diff:
```python
import functools

import jax
import jax.numpy as jnp
from jax import lax
from jax.experimental import pallas as pl
from jax.experimental.pallas import tpu as pltpu
from jax.sharding import PartitionSpec as P

BLOCK = 128
UNROLL = 16
MIB = 1024 * 1024
SLOW = 4

perturb_scale = 0.5
epsilon = 1e-05


def hop(value, axis, steps, source, target):
    count = lax.axis_size(axis)
    pairs = [(source * count + i, target * count + (i + steps) % count) for i in range(count)]
    return lax.ppermute(value, ("section", axis), pairs)


def pick_matrix(row_member, member_seed, noise_count):
    member_ids = jnp.arange(member_seed.shape[0], dtype=jnp.int32)
    matched = row_member[:, None] == member_ids[None, :]
    seed_of = jnp.sum(jnp.where(matched, member_seed[None, :], 0), axis=1)
    sign_values = (1 - 2 * (row_member % 2)).astype(jnp.float32) * perturb_scale
    noise_ids = jnp.arange(noise_count, dtype=jnp.int32)
    return jnp.where(seed_of[:, None] == noise_ids[None, :], sign_values[:, None], jnp.float32(0.0))


def tile_plan(codes, block_rows, own_cols, owner_index, owners):
    tile_count = codes.shape[1]
    active = codes >= 0
    cleared = jnp.where(active, codes, 0)
    column = cleared // block_rows
    feature = cleared % block_rows
    per_owner = block_rows // owners
    feature = lax.rem(owner_index - feature // per_owner + owners, owners) * per_owner + feature % per_owner
    is_down = jnp.arange(3)[:, None] == 2
    major = jnp.where(is_down, feature, column)
    minor = jnp.where(is_down, column, feature)
    major_count = max(block_rows, own_cols)
    majors = jnp.arange(major_count, dtype=jnp.int32)
    filled = jnp.sum(
        jnp.where(active[:, None, :] & (major[:, None, :] == majors[None, :, None]), 1, 0), axis=2
    )
    padded = 2 * ((filled + 1) // 2)
    before = jnp.sum(jnp.where(majors[None, None, :] < major[:, :, None], padded[:, None, :], 0), axis=2)
    rank = jnp.sum(
        jnp.where(
            active[:, None, :]
            & (major[:, None, :] == major[:, :, None])
            & (minor[:, None, :] < minor[:, :, None]),
            1,
            0,
        ),
        axis=2,
    )
    place = jnp.where(active, before + rank, -1)
    length = tile_count + min(tile_count, major_count)
    group = 2 * UNROLL
    length = -(-length // group) * group
    tile_ids = jnp.arange(tile_count, dtype=jnp.int32)
    words = (tile_ids[None, :] - tile_count) + minor * 4096 + major * 1048576
    spots = jnp.arange(length, dtype=jnp.int32)
    packed = tile_count + jnp.sum(
        jnp.where(place[:, None, :] == spots[None, :, None], words[:, None, :], 0), axis=2
    )
    groups = (jnp.sum(padded, axis=1) + group - 1) // group
    return packed.astype(jnp.int32), groups.astype(jnp.int32)


def multiply_tiles(words_ref, groups_ref, which, length, read, tiles_ref, add):
    def group(i, carry):
        for u in range(UNROLL):
            at = which * length + (i * UNROLL + u) * 2
            first, second = words_ref[at], words_ref[at + 1]
            left = jnp.concatenate([read((first >> 12) & 255), read((second >> 12) & 255)], axis=1)
            right = jnp.concatenate([tiles_ref[first & 4095], tiles_ref[second & 4095]], axis=0)
            add(first >> 20, jnp.dot(left, right, preferred_element_type=jnp.float32))
        return carry

    lax.fori_loop(0, groups_ref[which], group, 0)


def expand_kernel(owners, reps, length, words_ref, groups_ref, *refs):
    blocks = refs[:owners]
    gain_ref, left_ref, gate_hbm, up_hbm, raw_ref = refs[owners : owners + 5]
    part_refs = refs[owners + 5 : owners + 5 + reps]
    x_ref, total_ref, gate_tiles, up_tiles, sems = refs[owners + 5 + reps :]
    tile_count = gate_hbm.shape[0]
    all_rows, width = blocks[0].shape
    rows = all_rows // reps
    per_owner = width // BLOCK
    strip = 48 if all_rows % 48 == 0 else 16

    def norm_rows(i, carry):
        at = pl.ds(pl.multiple_of(i * strip, strip), strip)
        squares = jnp.zeros((strip, BLOCK), jnp.float32)
        for owner in range(owners):
            for part in range(per_owner):
                values = blocks[owner][at, pl.ds(part * BLOCK, BLOCK)].astype(jnp.float32)
                squares = squares + values * values
        total = jnp.sum(squares, axis=1, keepdims=True)
        inverse = lax.rsqrt(total / (owners * width) + epsilon)
        for owner in range(owners):
            for part in range(per_owner):
                values = blocks[owner][at, pl.ds(part * BLOCK, BLOCK)].astype(jnp.float32)
                gain = gain_ref[:, pl.ds(owner * width + part * BLOCK, BLOCK)].astype(jnp.float32)
                x_ref[owner * per_owner + part, at, :] = (values * inverse * gain).astype(jnp.bfloat16)
        return carry

    def read(block):
        return x_ref[block]

    def add(block, product):
        total_ref[block] += product

    @pl.when(groups_ref[3] == 1)
    def _():
        copies = [
            pltpu.make_async_copy(gate_hbm, gate_tiles.at[pl.ds(0, tile_count)], sems.at[0]),
            pltpu.make_async_copy(up_hbm, up_tiles.at[pl.ds(0, tile_count)], sems.at[1]),
        ]
        for copy in copies:
            copy.start()
        gate_tiles[tile_count] = jnp.zeros((BLOCK, BLOCK), gate_tiles.dtype)
        up_tiles[tile_count] = jnp.zeros((BLOCK, BLOCK), up_tiles.dtype)
        lax.fori_loop(0, all_rows // strip, norm_rows, 0)
        raw = jnp.zeros(raw_ref.shape, jnp.float32)
        step = min(8, x_ref.shape[0])
        for d in range(0, x_ref.shape[0], step):
            raw = raw + lax.dot_general(
                jnp.concatenate([x_ref[d + i, pl.ds(0, rows), :] for i in range(step)], axis=1),
                left_ref[:, pl.ds(d * BLOCK, step * BLOCK)],
                (((1,), (1,)), ((), ())),
                preferred_element_type=jnp.float32,
            )
        raw_ref[...] = raw
        for which, tiles in ((0, gate_tiles), (1, up_tiles)):
            total_ref[...] = jnp.zeros(total_ref.shape, jnp.float32)
            copies[which].wait()
            multiply_tiles(words_ref, groups_ref, which, length, read, tiles, add)
            for rep in range(reps):

                def narrow(c, carry, which=which, rep=rep):
                    part_refs[rep][which, c] = total_ref[c, pl.ds(rep * rows, rows), :].astype(jnp.bfloat16)
                    return carry

                lax.fori_loop(0, total_ref.shape[0], narrow, 0, unroll=min(4, total_ref.shape[0]))


def expand(words, groups, blocks, gain, left, gate_tiles, up_tiles, own_cols, reps):
    owners = len(blocks)
    all_rows, width = blocks[0].shape
    rows = all_rows // reps
    tile_count = gate_tiles.shape[0]
    smem = pl.BlockSpec(memory_space=pltpu.SMEM)
    vmem = pl.BlockSpec(memory_space=pltpu.VMEM)
    hbm = pl.BlockSpec(memory_space=pl.ANY)
    out = pl.pallas_call(
        functools.partial(expand_kernel, owners, reps, words.shape[0] // 3),
        out_shape=[jax.ShapeDtypeStruct((rows, left.shape[0]), jnp.float32)]
        + [jax.ShapeDtypeStruct((2, own_cols, rows, BLOCK), jnp.bfloat16)] * reps,
        in_specs=[smem, smem] + [vmem] * (owners + 2) + [hbm, hbm],
        out_specs=[vmem] * (1 + reps),
        scratch_shapes=[
            pltpu.VMEM((owners * width // BLOCK, all_rows, BLOCK), jnp.bfloat16),
            pltpu.VMEM((own_cols, all_rows, BLOCK), jnp.float32),
            pltpu.VMEM((tile_count + 1, BLOCK, BLOCK), jnp.bfloat16),
            pltpu.VMEM((tile_count + 1, BLOCK, BLOCK), jnp.bfloat16),
            pltpu.SemaphoreType.DMA((2,)),
        ],
        compiler_params=pltpu.CompilerParams(vmem_limit_bytes=36 * MIB),
        cost_estimate=pl.CostEstimate(
            flops=SLOW * 2 * 2 * tile_count * all_rows * BLOCK * BLOCK,
            bytes_accessed=4 * tile_count * BLOCK * BLOCK,
            transcendentals=0,
        ),
        name="expand",
    )(words, groups, *blocks, gain, left, gate_tiles, up_tiles)
    return out[0], out[1:]


def activate_kernel(reps, groups_ref, *refs):
    parts = refs[:reps]
    raw_ref, picks_ref, wide_cols, down_cols, hidden_ref, coef_ref = refs[reps:]
    noise = picks_ref.shape[1]
    columns, rows = hidden_ref.shape[:2]

    @pl.when(groups_ref[3] == 1)
    def _():
        picks = picks_ref[...]
        coefs = (jnp.concatenate([picks, picks], axis=1) * raw_ref[...]).astype(jnp.bfloat16)

        def pair(i, down):
            hiddens = []
            for u in range(2):
                c = i * 2 + u
                low_rank = jnp.dot(coefs, wide_cols[c], preferred_element_type=jnp.float32)
                values = []
                for which in range(2):
                    value = low_rank[:, which * BLOCK : (which + 1) * BLOCK]
                    for part in parts:
                        value = value + part[which, c].astype(jnp.float32)
                    values.append(value)
                gate, up = values
                hidden = (gate / (1.0 + jnp.exp(-gate)) * up).astype(jnp.bfloat16)
                hidden_ref[c] = hidden
                hiddens.append(hidden)
            return down + lax.dot_general(
                jnp.concatenate(hiddens, axis=1),
                down_cols[i],
                (((1,), (1,)), ((), ())),
                preferred_element_type=jnp.float32,
            )

        down = lax.fori_loop(
            0, columns // 2, pair, jnp.zeros((rows, noise), jnp.float32), unroll=min(2, columns // 2)
        )
        coef_ref[...] = picks * down


def activate(groups, parts, raw, picks, wide_cols, down_cols):
    own_cols, rows = parts[0].shape[1:3]
    noise = picks.shape[1]
    vmem = pl.BlockSpec(memory_space=pltpu.VMEM)
    return pl.pallas_call(
        functools.partial(activate_kernel, len(parts)),
        out_shape=[
            jax.ShapeDtypeStruct((own_cols, rows, BLOCK), jnp.bfloat16),
            jax.ShapeDtypeStruct((rows, noise), jnp.float32),
        ],
        in_specs=[pl.BlockSpec(memory_space=pltpu.SMEM)] + [vmem] * (len(parts) + 4),
        out_specs=[vmem] * 2,
        compiler_params=pltpu.CompilerParams(vmem_limit_bytes=16 * MIB),
        cost_estimate=pl.CostEstimate(
            flops=100 * own_cols * rows * BLOCK,
            bytes_accessed=(len(parts) * 2 + 1) * 2 * own_cols * rows * BLOCK,
            transcendentals=own_cols * rows * BLOCK,
        ),
        name="activate",
    )(groups, *parts, raw, picks, wide_cols, down_cols)


def contract_kernel(owners, reps, length, words_ref, groups_ref, *refs):
    hiddens = refs[:reps]
    coef_ref, right_ref, tiles_hbm = refs[reps : reps + 3]
    outs = refs[reps + 3 : reps + 3 + owners]
    total_ref, tiles_ref, sem = refs[reps + 3 + owners :]
    tile_count = tiles_hbm.shape[0]
    rows = hiddens[0].shape[1]
    per_owner = outs[0].shape[1] // BLOCK
    blocks = total_ref.shape[0]

    def read(block):
        return jnp.concatenate([hidden[block] for hidden in hiddens], axis=0)

    def add(block, product):
        total_ref[block] += product

    @pl.when(groups_ref[3] == 1)
    def _():
        copy = pltpu.make_async_copy(tiles_hbm, tiles_ref.at[pl.ds(0, tile_count)], sem)
        copy.start()
        tiles_ref[tile_count] = jnp.zeros((BLOCK, BLOCK), tiles_ref.dtype)
        coef = coef_ref[...]
        high = coef.astype(jnp.bfloat16)
        low = (coef - high.astype(jnp.float32)).astype(jnp.bfloat16)
        both = jnp.concatenate([high, low], axis=1)
        for d in range(0, blocks, 2):
            right = right_ref[:, pl.ds(d * BLOCK, 2 * BLOCK)]
            start = jnp.dot(both, right, preferred_element_type=jnp.float32)
            for i in range(2):
                total_ref[d + i, pl.ds(0, rows), :] = start[:, i * BLOCK : (i + 1) * BLOCK]
                if reps > 1:
                    total_ref[d + i, pl.ds(rows, (reps - 1) * rows), :] = jnp.zeros(
                        ((reps - 1) * rows, BLOCK), jnp.float32
                    )
        copy.wait()
        multiply_tiles(words_ref, groups_ref, 2, length, read, tiles_ref, add)
        for owner in range(owners):
            for part in range(per_owner):
                outs[owner][:, pl.ds(part * BLOCK, BLOCK)] = total_ref[owner * per_owner + part].astype(jnp.bfloat16)


def contract(words, groups, hiddens, coef, right, tiles, owners):
    own_cols, rows = hiddens[0].shape[:2]
    reps = len(hiddens)
    features = right.shape[1]
    tile_count = tiles.shape[0]
    smem = pl.BlockSpec(memory_space=pltpu.SMEM)
    vmem = pl.BlockSpec(memory_space=pltpu.VMEM)
    return pl.pallas_call(
        functools.partial(contract_kernel, owners, reps, words.shape[0] // 3),
        out_shape=[jax.ShapeDtypeStruct((reps * rows, features // owners), jnp.bfloat16)] * owners,
        in_specs=[smem, smem] + [vmem] * (reps + 2) + [pl.BlockSpec(memory_space=pl.ANY)],
        out_specs=[vmem] * owners,
        scratch_shapes=[
            pltpu.VMEM((features // BLOCK, reps * rows, BLOCK), jnp.float32),
            pltpu.VMEM((tile_count + 1, BLOCK, BLOCK), jnp.bfloat16),
            pltpu.SemaphoreType.DMA,
        ],
        compiler_params=pltpu.CompilerParams(vmem_limit_bytes=24 * MIB),
        cost_estimate=pl.CostEstimate(
            flops=SLOW * 2 * tile_count * reps * rows * BLOCK * BLOCK,
            bytes_accessed=2 * tile_count * BLOCK * BLOCK,
            transcendentals=0,
        ),
        name="contract",
    )(words, groups, *hiddens, coef, right, tiles)


def per_device(
    tokens,
    norm_gain,
    gate_tiles,
    up_tiles,
    down_tiles,
    gate_slot,
    up_slot,
    down_slot,
    owned_columns,
    gate_left,
    gate_right,
    up_left,
    up_right,
    down_left,
    down_right,
    row_member,
    member_seed,
):
    section_index = lax.axis_index("section")
    owner_index = lax.axis_index("tensor")
    rep_index = lax.axis_index("rep")
    owners, reps = lax.axis_size("tensor"), lax.axis_size("rep")
    rows, width = tokens.shape
    own_cols = owned_columns.shape[1] // owners
    block_rows = gate_left.shape[2] // BLOCK
    tile_count = gate_tiles.shape[1]

    codes = jnp.stack([gate_slot[0], up_slot[0], down_slot[0]])
    codes = lax.dynamic_slice_in_dim(codes, rep_index * tile_count, tile_count, axis=1)
    words, groups = tile_plan(codes, block_rows, own_cols, owner_index, owners)
    words = words.reshape(-1)

    running = [
        jnp.concatenate([groups, (section_index == section).astype(jnp.int32)[None]]) for section in range(2)
    ]

    rotation = lax.rem(owner_index - jnp.arange(owners, dtype=jnp.int32) + owners, owners)

    def rotated(table):
        parts = table.reshape(table.shape[0], owners, width)
        return jnp.take(parts, rotation, axis=1).reshape(table.shape)

    gain = rotated(norm_gain)
    left = rotated(jnp.concatenate([gate_left[0], up_left[0]], axis=0))
    right = rotated(down_right[0])
    right = jnp.concatenate([right, right], axis=0)
    columns = lax.dynamic_slice_in_dim(owned_columns[0], owner_index * own_cols, own_cols)

    def owned(table):
        blocked = table.reshape(table.shape[0], -1, BLOCK)
        return jnp.take(blocked, columns, axis=1).transpose(1, 0, 2)

    gate_cols, up_cols, down_cols = owned(gate_right[0]), owned(up_right[0]), owned(down_left[0])
    empty = jnp.zeros_like(gate_cols)
    wide_cols = jnp.concatenate(
        [jnp.concatenate([gate_cols, empty], axis=2), jnp.concatenate([empty, up_cols], axis=2)], axis=1
    )
    noise = gate_left.shape[1]
    down_cols = down_cols.reshape(own_cols // 2, 2, noise, BLOCK).transpose(0, 2, 1, 3)
    down_cols = down_cols.reshape(own_cols // 2, noise, 2 * BLOCK)
    picks = pick_matrix(row_member, member_seed, noise)

    halves = 2 if rows % 32 == 0 else 1
    half = rows // halves

    def layer(stream, picked, section, target):
        here = running[section]
        blocks = [stream] + [hop(stream, "tensor", step, section, section) for step in range(1, owners)]
        raw, parts = expand(words, here, blocks, gain, left, gate_tiles[0], up_tiles[0], own_cols, reps)
        parts = [parts[0]] + [hop(parts[g], "rep", -g, section, section) for g in range(1, reps)]
        hidden, coef = activate(here, parts, raw, picked, wide_cols, down_cols)
        hiddens = [hidden] + [hop(hidden, "rep", g, section, section) for g in range(1, reps)]
        outs = contract(words, here, hiddens, coef, right, down_tiles[0], owners)
        summed = outs[0] if section == target else hop(outs[0], "tensor", 0, section, target)
        summed = summed.astype(jnp.float32)
        for step in range(1, owners):
            summed = summed + hop(outs[step], "tensor", -step, section, target).astype(jnp.float32)
        return summed

    others = [hop(tokens, "rep", g, 0, 0) for g in range(1, reps)]
    firsts, seconds = [], []
    for h in range(halves):
        cut = slice(h * half, (h + 1) * half)
        stream = jnp.concatenate([value[cut] for value in [tokens] + others], axis=0)
        summed = layer(stream, picks[cut], 0, 1)
        own = tokens[cut].astype(jnp.float32) + summed[:half]
        summed = jnp.concatenate([own, summed[half:]], axis=0).astype(jnp.bfloat16)
        total = summed.astype(jnp.float32)
        for g in range(1, reps):
            arrived = hop(summed, "rep", g, 1, 1).astype(jnp.float32)
            total = total + jnp.roll(arrived, g * half, axis=0)
        stream = total.astype(jnp.bfloat16)
        firsts.append(stream[:half])
        summed = layer(stream, picks[cut], 1, 1)
        value = stream[:half].astype(jnp.float32) + summed[:half]
        for g in range(1, reps):
            sent = summed[g * half : (g + 1) * half].astype(jnp.bfloat16)
            value = value + hop(sent, "rep", -g, 1, 1).astype(jnp.float32)
        seconds.append(value.astype(jnp.bfloat16))
    first = lax.ppermute(jnp.concatenate(firsts, axis=0), "section", [(1, 0)])
    second = jnp.concatenate(seconds, axis=0)
    return jnp.where(section_index == 0, first, second)[None]


def solution(mesh):
    placed = (
        P(("pop", "rep"), "tensor"),
        P("section", None),
        P("section", ("tensor", "rep"), None, None),
        P("section", ("tensor", "rep"), None, None),
        P("section", ("tensor", "rep"), None, None),
        P("section", "tensor"),
        P("section", "tensor"),
        P("section", "tensor"),
        P("section", None),
        P("section", None, None),
        P("section", None, None),
        P("section", None, None),
        P("section", None, None),
        P("section", None, None),
        P("section", None, None),
        P(("pop", "rep")),
        P("pop"),
    )
    return jax.shard_map(
        per_device,
        mesh=mesh,
        in_specs=placed,
        out_specs=P("section", ("pop", "rep"), "tensor"),
        check_vma=False,
    )
```

time: 441 us -> 308 us (0.70)
  waiting for transfers between devices: 234 us -> 141 us
  Pallas kernels: 118 us -> 47.9 us
  starting transfers between devices: 62.6 us -> 87.3 us
  local copies, waits for them, and re-layouts: 14.1 us -> 19.5 us
    ppermute x27 -> x39, waiting for transfers between devices: 234 us -> 141 us  [hop(): return lax.ppermute(value, ('section', axis), pairs)]
    pallas_call x4 -> x8, Pallas kernels: 76 us -> 33.3 us  [the longest x4 23.4 us: expand(): pl.pallas_call(functools.partial(expand_kernel, owners, reps, words.shape...]
    pallas_call x2 -> x4, Pallas kernels: 41.7 us -> 14.6 us  [contract(): pl.pallas_call(functools.partial(contract_kernel, owners, reps, words.sha...]
    ppermute x27 -> x39, starting transfers between devices: 61.3 us -> 86 us  [hop(): return lax.ppermute(value, ('section', axis), pairs)]
    unnamed x59 -> x29, local copies, waits for them, and re-layouts: 7.99 us -> 13.7 us
  transfers between devices with their start and end apart: 28 -> 40, of which waited for: 11 -> 14; matrix products, arithmetic and copies ran while one was open for 4% -> 4% of each run, Pallas kernels for 0% -> 16%
where the time goes in v2:
time: 308 us; the launch traced here: 304 us
  waiting for transfers between devices  141 us (46%)
  starting transfers between devices  87.3 us (28%)
  Pallas kernels  47.9 us (16%)
  local copies, waits for them, and re-layouts  19.5 us (6%)
  other arithmetic  7.36 us (2%)
    ppermute x39, waiting for transfers between devices, hop(): return lax.ppermute(value, ('section', axis), pairs)  141 us
    ppermute x39, starting transfers between devices, hop(): return lax.ppermute(value, ('section', axis), pairs)  86 us
    pallas_call x4, Pallas kernels, expand(): pl.pallas_call(functools.partial(expand_kernel, owners, reps, words.shape...  23.4 us
    pallas_call x4, Pallas kernels, contract(): pl.pallas_call(functools.partial(contract_kernel, owners, reps, words.sha...  14.6 us
    unnamed x29, local copies, waits for them, and re-layouts  13.7 us
    pallas_call x4, Pallas kernels, activate(): pl.pallas_call(functools.partial(activate_kernel, len(parts)), out_shape=...  9.87 us
  transfers between devices with their start and end apart: 40, of which 14 were waited for; matrix products, arithmetic and copies ran while one was open for 4% of the time, Pallas kernels for 16%

profile of v2, /device:TPU:1, one launch (start us, length us, event | category | flops | bytes accessed | tf_op | source)
XLA Modules:
  0.0 304.4 jit_solution(3022171279694471120)
XLA Ops:
  15.8 3.4 %copy-done.2 = bf16[1,256,128,128]{3,2,1,0:T(8,128)(2,1)S(1)} copy-done((bf16[1,256,128,128]{3,2,1,0:T(8,128)(2,1)S(1)}, bf16[1,256,128,128]{3,2,1,0:T(8,128)(2,1)}, u32[]{:S(2)}) %copy-start.2) | copy-done | bytes 8388632
  24.8 3.4 %copy-done.3 = bf16[1,256,128,128]{3,2,1,0:T(8,128)(2,1)S(1)} copy-done((bf16[1,256,128,128]{3,2,1,0:T(8,128)(2,1)S(1)}, bf16[1,256,128,128]{3,2,1,0:T(8,128)(2,1)}, u32[]{:S(2)}) %copy-start.3) | copy-done | bytes 8388632
  34.2 3.4 %copy-done.4 = bf16[1,256,128,128]{3,2,1,0:T(8,128)(2,1)S(1)} copy-done((bf16[1,256,128,128]{3,2,1,0:T(8,128)(2,1)S(1)}, bf16[1,256,128,128]{3,2,1,0:T(8,128)(2,1)}, u32[]{:S(2)}) %copy-start.4) | copy-done | bytes 8388632
  39.6 81.5 %collective-permute-done.19 = bf16[192,1024]{1,0:T(8,128)(2,1)S(1)} collective-permute-done((bf16[192,1024]{1,0:T(8,128)(2,1)S(1)}, bf16[192,1024]{1,0:T(8,128)(2,1)S(1)}, u32[]{:S(2)}, u32[]{:S(2)}) %collective-permute-start.19) | collective-permute-done | bytes 393248 | tf_op jit(solution)/shard_map/ppermute | solution.py:22
  122.4 7.2 %collective-permute-done.18 = bf16[192,1024]{1,0:T(8,128)(2,1)S(1)} collective-permute-done((bf16[192,1024]{1,0:T(8,128)(2,1)S(1)}, bf16[192,1024]{1,0:T(8,128)(2,1)S(1)}, u32[]{:S(2)}, u32[]{:S(2)}) %collective-permute-start.18) | collective-permute-done | bytes 393248 | tf_op jit(solution)/shard_map/ppermute | solution.py:22
  133.8 3.4 %collective-permute-done.9 = bf16[192,1024]{1,0:T(8,128)(2,1)S(1)} collective-permute-done((bf16[192,1024]{1,0:T(8,128)(2,1)S(1)}, bf16[192,1024]{1,0:T(8,128)(2,1)S(1)}, u32[]{:S(2)}, u32[]{:S(2)}) %collective-permute-start.9) | collective-permute-done | bytes 393248 | tf_op jit(solution)/shard_map/ppermute | solution.py:22
  137.2 9.3 %collective-permute-done.8 = bf16[192,1024]{1,0:T(8,128)(2,1)S(1)} collective-permute-done((bf16[192,1024]{1,0:T(8,128)(2,1)S(1)}, bf16[192,1024]{1,0:T(8,128)(2,1)S(1)}, u32[]{:S(2)}, u32[]{:S(2)}) %collective-permute-start.8) | collective-permute-done | bytes 393248 | tf_op jit(solution)/shard_map/ppermute | solution.py:22
  151.2 3.3 %collective-permute-start.10 = (bf16[192,1024]{1,0:T(8,128)(2,1)S(1)}, bf16[192,1024]{1,0:T(8,128)(2,1)S(1)}, u32[]{:S(2)}, u32[]{:S(2)}) collective-permute-start(bf16[192,1024]{1,0:T(8,128)(2,1)S(1)} %pad_maximum_fusion.1), channel_id=1, source_target_pairs={{8,9},{9,8},{10,11},{11,10},{12,13},{13,12},{14,15},{15,14},{24,25... | collective-permute-start | bytes 1179656 | tf_op jit(solution)/shard_map/ppermute | solution.py:22
  154.5 3.0 collective-permute-done.20
  157.7 4.3 %collective-permute-start.31 = (bf16[192,1024]{1,0:T(8,128)(2,1)S(1)}, bf16[192,1024]{1,0:T(8,128)(2,1)S(1)}, u32[]{:S(2)}, u32[]{:S(2)}) collective-permute-start(bf16[192,1024]{1,0:T(8,128)(2,1)S(1)} %fusion.1.refs_0_), channel_id=1, source_target_pairs={{8,10},{10,12},{12,14},{14,8},{9,11},{11,13},{13,15},{15,9},{24,26... | collective-permute-start | bytes 1179656 | tf_op jit(solution)/shard_map/ppermute | solution.py:22
  162.0 8.0 %collective-permute-start.32 = (bf16[192,1024]{1,0:T(8,128)(2,1)S(1)}, bf16[192,1024]{1,0:T(8,128)(2,1)S(1)}, u32[]{:S(2)}, u32[]{:S(2)}) collective-permute-start(bf16[192,1024]{1,0:T(8,128)(2,1)S(1)} %fusion.1.refs_0_), channel_id=1, source_target_pairs={{8,12},{10,14},{12,8},{14,10},{9,13},{11,15},{13,9},{15,11},{24,28... | collective-permute-start | bytes 1179656 | tf_op jit(solution)/shard_map/ppermute | solution.py:22
  172.1 3.4 %collective-permute-start.22 = (bf16[192,1024]{1,0:T(8,128)(2,1)S(1)}, bf16[192,1024]{1,0:T(8,128)(2,1)S(1)}, u32[]{:S(2)}, u32[]{:S(2)}) collective-permute-start(bf16[192,1024]{1,0:T(8,128)(2,1)S(1)} %fusion.refs_0_), channel_id=1, source_target_pairs={{8,10},{10,12},{12,14},{14,8},{9,11},{11,13},{13,15},{15,9},{24,26... | collective-permute-start | bytes 1179656 | tf_op jit(solution)/shard_map/ppermute | solution.py:22
  177.4 4.0 %collective-permute-start.24 = (bf16[192,1024]{1,0:T(8,128)(2,1)S(1)}, bf16[192,1024]{1,0:T(8,128)(2,1)S(1)}, u32[]{:S(2)}, u32[]{:S(2)}) collective-permute-start(bf16[192,1024]{1,0:T(8,128)(2,1)S(1)} %fusion.refs_0_), channel_id=1, source_target_pairs={{8,14},{10,8},{12,10},{14,12},{9,15},{11,9},{13,11},{15,13},{24,30... | collective-permute-start | bytes 1179656 | tf_op jit(solution)/shard_map/ppermute | solution.py:22
  181.4 5.4 %collective-permute-done.33.refs_3_ = bf16[192,1024]{1,0:T(8,128)(2,1)S(1)} collective-permute-done((bf16[192,1024]{1,0:T(8,128)(2,1)S(1)}, bf16[192,1024]{1,0:T(8,128)(2,1)S(1)}, u32[]{:S(2)}, u32[]{:S(2)}) %collective-permute-start.33) | collective-permute-done | bytes 393248 | tf_op jit(solution)/shard_map/ppermute | solution.py:22
  186.8 11.1 %expand.7 = (f32[96,16]{1,0:T(8,128)S(1)}, bf16[2,32,96,128]{3,2,1,0:T(8,128)(2,1)S(1)}, bf16[2,32,96,128]{3,2,1,0:T(8,128)(2,1)S(1)}) custom-call(s32[864]{0:T(1024)S(1)} %add.196.words_ref, s32[4]{0:T(128)S(1)} %get-tuple-element.99.groups_ref, bf16[192,1024]{1,0:T(8,128)(2,1)S(1)} %fusion.1.refs_0_, ...), custom_call_target="tpu_custom_call" | custom-call | flops 12884901888 | bytes 16777216 | tf_op jit(solution)/shard_map/expand/pallas_call | solution.py:164
  199.9 11.1 %expand.6 = (f32[96,16]{1,0:T(8,128)S(1)}, bf16[2,32,96,128]{3,2,1,0:T(8,128)(2,1)S(1)}, bf16[2,32,96,128]{3,2,1,0:T(8,128)(2,1)S(1)}) custom-call(s32[864]{0:T(1024)S(1)} %add.196.words_ref, s32[4]{0:T(128)S(1)} %get-tuple-element.99.groups_ref, bf16[192,1024]{1,0:T(8,128)(2,1)S(1)} %fusion.refs_0_, bf16[192,1024]{1,0:T(8,128)(2,1)S(1)} %collective-permute-done.22.refs_1_, ...), custom_call_target="tpu_custom_call" | custom-call | flops 12884901888 | bytes 16777216 | tf_op jit(solution)/shard_map/expand/pallas_call | solution.py:164
  211.0 2.8 collective-permute-start.25
  213.8 5.3 %collective-permute-done.34.refs_1_ = bf16[2,32,96,128]{3,2,1,0:T(8,128)(2,1)S(1)} collective-permute-done((bf16[2,32,96,128]{3,2,1,0:T(8,128)(2,1)S(1)}, bf16[2,32,96,128]{3,2,1,0:T(8,128)(2,1)S(1)}, u32[]{:S(2)}, u32[]{:S(2)}) %collective-permute-start.34) | collective-permute-done | bytes 1572896 | tf_op jit(solution)/shard_map/ppermute | solution.py:22
  219.1 4.4 %activate.7 = (bf16[32,96,128]{2,1,0:T(8,128)(2,1)S(1)}, f32[96,8]{1,0:T(8,128)S(1)}) custom-call(s32[4]{0:T(128)S(1)} %get-tuple-element.99.groups_ref, bf16[2,32,96,128]{3,2,1,0:T(8,128)(2,1)S(1)} %get-tuple-element.69.refs_0_, bf16[2,32,96,128]{3,2,1,0:T(8,128)(2,1)S(1)} %collective-permute-done.34.refs_1_, f32[96,16]{1,0:T(8,128)S(1)} %get-tuple-element.71.refs_2_, ...), custom_call_target="tpu_custom_call" | custom-call | flops 39321600 | bytes 3932160 | tf_op jit(solution)/shard_map/activate/pallas_call | solution.py:231
  225.4 10.5 %collective-permute-done.25.refs_1_ = bf16[2,32,96,128]{3,2,1,0:T(8,128)(2,1)S(1)} collective-permute-done((bf16[2,32,96,128]{3,2,1,0:T(8,128)(2,1)S(1)}, bf16[2,32,96,128]{3,2,1,0:T(8,128)(2,1)S(1)}, u32[]{:S(2)}, u32[]{:S(2)}) %collective-permute-start.25) | collective-permute-done | bytes 1572896 | tf_op jit(solution)/shard_map/ppermute | solution.py:22
  235.9 4.4 %activate.6 = (bf16[32,96,128]{2,1,0:T(8,128)(2,1)S(1)}, f32[96,8]{1,0:T(8,128)S(1)}) custom-call(s32[4]{0:T(128)S(1)} %get-tuple-element.99.groups_ref, bf16[2,32,96,128]{3,2,1,0:T(8,128)(2,1)S(1)} %get-tuple-element.60.refs_0_, bf16[2,32,96,128]{3,2,1,0:T(8,128)(2,1)S(1)} %collective-permute-done.25.refs_1_, f32[96,16]{1,0:T(8,128)S(1)} %get-tuple-element.62.refs_2_, ...), custom_call_target="tpu_custom_call" | custom-call | flops 39321600 | bytes 3932160 | tf_op jit(solution)/shard_map/activate/pallas_call | solution.py:231
  244.4 3.4 %copy-done.5 = bf16[1,256,128,128]{3,2,1,0:T(8,128)(2,1)S(1)} copy-done((bf16[1,256,128,128]{3,2,1,0:T(8,128)(2,1)S(1)}, bf16[1,256,128,128]{3,2,1,0:T(8,128)(2,1)}, u32[]{:S(2)}) %copy-start.5) | copy-done | bytes 8388632
  247.7 6.7 %contract.7 = (bf16[192,1024]{1,0:T(8,128)(2,1)S(1)}, bf16[192,1024]{1,0:T(8,128)(2,1)S(1)}, bf16[192,1024]{1,0:T(8,128)(2,1)S(1)}, bf16[192,1024]{1,0:T(8,128)(2,1)S(1)}) custom-call(s32[864]{0:T(1024)S(1)} %add.196.words_ref, s32[4]{0:T(128)S(1)} %get-tuple-element.99.groups_ref, bf16[32,96,128]{2,1,0:T(8,128)(2,1)S(1)} %get-tuple-element.72.refs_0_, ...), custom_call_target="tpu_custom_call" | custom-call | flops 6442450944 | bytes 8388608 | tf_op jit(solution)/shard_map/contract/pallas_call | solution.py:297
  254.5 9.4 %collective-permute-start.38 = (bf16[192,1024]{1,0:T(8,128)(2,1)S(1)}, bf16[192,1024]{1,0:T(8,128)(2,1)S(1)}, u32[]{:S(2)}, u32[]{:S(2)}) collective-permute-start(bf16[192,1024]{1,0:T(8,128)(2,1)S(1)} %get-tuple-element.77), channel_id=1, source_target_pairs={{8,10},{10,12},{12,14},{14,8},{9,11},{11,13},{13,15},{15,9},{24,26... | collective-permute-start | bytes 1179656 | tf_op jit(solution)/shard_map/ppermute | solution.py:22
  263.9 2.9 collective-permute-start.37
  266.8 4.3 %collective-permute-start.36 = (bf16[192,1024]{1,0:T(8,128)(2,1)S(1)}, bf16[192,1024]{1,0:T(8,128)(2,1)S(1)}, u32[]{:S(2)}, u32[]{:S(2)}) collective-permute-start(bf16[192,1024]{1,0:T(8,128)(2,1)S(1)} %get-tuple-element.75), channel_id=1, source_target_pairs={{8,14},{10,8},{12,10},{14,12},{9,15},{11,9},{13,11},{15,13},{24,30... | collective-permute-start | bytes 1179656 | tf_op jit(solution)/shard_map/ppermute | solution.py:22
  271.1 6.7 %contract.6 = (bf16[192,1024]{1,0:T(8,128)(2,1)S(1)}, bf16[192,1024]{1,0:T(8,128)(2,1)S(1)}, bf16[192,1024]{1,0:T(8,128)(2,1)S(1)}, bf16[192,1024]{1,0:T(8,128)(2,1)S(1)}) custom-call(s32[864]{0:T(1024)S(1)} %add.196.words_ref, s32[4]{0:T(128)S(1)} %get-tuple-element.99.groups_ref, bf16[32,96,128]{2,1,0:T(8,128)(2,1)S(1)} %get-tuple-element.63.refs_0_, ...), custom_call_target="tpu_custom_call" | custom-call | flops 6442450944 | bytes 8388608 | tf_op jit(solution)/shard_map/contract/pallas_call | solution.py:297
  279.7 2.4 collective-permute-start.28
  282.1 4.7 %collective-permute-start.27 = (bf16[192,1024]{1,0:T(8,128)(2,1)S(1)}, bf16[192,1024]{1,0:T(8,128)(2,1)S(1)}, u32[]{:S(2)}, u32[]{:S(2)}) collective-permute-start(bf16[192,1024]{1,0:T(8,128)(2,1)S(1)} %get-tuple-element.66), channel_id=1, source_target_pairs={{8,14},{10,8},{12,10},{14,12},{9,15},{11,9},{13,11},{15,13},{24,30... | collective-permute-start | bytes 1179656 | tf_op jit(solution)/shard_map/ppermute | solution.py:22
  290.7 5.8 %collective-permute-done.28 = bf16[192,1024]{1,0:T(8,128)(2,1)S(1)} collective-permute-done((bf16[192,1024]{1,0:T(8,128)(2,1)S(1)}, bf16[192,1024]{1,0:T(8,128)(2,1)S(1)}, u32[]{:S(2)}, u32[]{:S(2)}) %collective-permute-start.28) | collective-permute-done | bytes 393248 | tf_op jit(solution)/shard_map/ppermute | solution.py:22
  296.9 2.3 collective-permute-start.30
  299.3 4.1 %collective-permute-done.30 = bf16[96,1024]{1,0:T(8,128)(2,1)S(1)} collective-permute-done((bf16[96,1024]{1,0:T(8,128)(2,1)S(1)}, bf16[96,1024]{1,0:T(8,128)(2,1)S(1)}, u32[]{:S(2)}, u32[]{:S(2)}) %collective-permute-start.30) | collective-permute-done | bytes 196640 | tf_op jit(solution)/shard_map/ppermute | solution.py:22
  (154 shorter events, 58.1 us)
Async XLA Ops:
  0.0 10.6 %collective-permute-start = (bf16[192,1024]{1,0:T(8,128)(2,1)}, bf16[192,1024]{1,0:T(8,128)(2,1)S(1)}, u32[]{:S(2)}, u32[]{:S(2)}) collective-permute-start(bf16[192,1024]{1,0:T(8,128)(2,1)} %param.19), channel_id=1, source_target_pairs={{0,1},{1,0},{2,3},{3,2},{4,5},{5,4},{6,7},{7,6},{16,17},{17,16},{1... | collective-permute-start | bytes 1179656 | tf_op jit(solution)/shard_map/ppermute | solution.py:22
  13.7 6.9 %collective-permute-start.1 = (bf16[192,1024]{1,0:T(8,128)(2,1)S(1)}, bf16[192,1024]{1,0:T(8,128)(2,1)S(1)}, u32[]{:S(2)}, u32[]{:S(2)}) collective-permute-start(bf16[192,1024]{1,0:T(8,128)(2,1)S(1)} %pad_maximum_fusion.refs_0_), channel_id=1, source_target_pairs={{0,2},{2,4},{4,6},{6,0},{1,3},{3,5},{5,7},{7,1},{16,18},{18,20},{2... | collective-permute-start | bytes 1179656 | tf_op jit(solution)/shard_map/ppermute | solution.py:22
  24.1 10.1 %collective-permute-start.5 = (bf16[32,96,128]{2,1,0:T(8,128)(2,1)S(1)}, bf16[32,96,128]{2,1,0:T(8,128)(2,1)S(1)}, u32[]{:S(2)}, u32[]{:S(2)}) collective-permute-start(bf16[32,96,128]{2,1,0:T(8,128)(2,1)S(1)} %get-tuple-element.45.refs_0_), channel_id=1, source_target_pairs={{0,1},{1,0},{2,3},{3,2},{4,5},{5,4},{6,7},{7,6},{16,17},{17,16},{1... | collective-permute-start | bytes 2359304 | tf_op jit(solution)/shard_map/ppermute | solution.py:22
  28.8 92.3 %collective-permute-start.19 = (bf16[192,1024]{1,0:T(8,128)(2,1)S(1)}, bf16[192,1024]{1,0:T(8,128)(2,1)S(1)}, u32[]{:S(2)}, u32[]{:S(2)}) collective-permute-start(bf16[192,1024]{1,0:T(8,128)(2,1)S(1)} %get-tuple-element.59), channel_id=1, source_target_pairs={{0,10},{2,12},{4,14},{6,8},{1,11},{3,13},{5,15},{7,9},{16,26},{18,... | collective-permute-start | bytes 1179656 | tf_op jit(solution)/shard_map/ppermute | solution.py:22
  30.2 99.4 %collective-permute-start.18 = (bf16[192,1024]{1,0:T(8,128)(2,1)S(1)}, bf16[192,1024]{1,0:T(8,128)(2,1)S(1)}, u32[]{:S(2)}, u32[]{:S(2)}) collective-permute-start(bf16[192,1024]{1,0:T(8,128)(2,1)S(1)} %get-tuple-element.58), channel_id=1, source_target_pairs={{0,12},{2,14},{4,8},{6,10},{1,13},{3,15},{5,9},{7,11},{16,28},{18,... | collective-permute-start | bytes 1179656 | tf_op jit(solution)/shard_map/ppermute | solution.py:22
  31.5 100.7 %collective-permute-start.17 = (bf16[192,1024]{1,0:T(8,128)(2,1)S(1)}, bf16[192,1024]{1,0:T(8,128)(2,1)S(1)}, u32[]{:S(2)}, u32[]{:S(2)}) collective-permute-start(bf16[192,1024]{1,0:T(8,128)(2,1)S(1)} %get-tuple-element.57), channel_id=1, source_target_pairs={{0,14},{2,8},{4,10},{6,12},{1,15},{3,9},{5,11},{7,13},{16,30},{18,... | collective-permute-start | bytes 1179656 | tf_op jit(solution)/shard_map/ppermute | solution.py:22
  32.8 100.7 %collective-permute-start.16 = (bf16[192,1024]{1,0:T(8,128)(2,1)S(1)}, bf16[192,1024]{1,0:T(8,128)(2,1)S(1)}, u32[]{:S(2)}, u32[]{:S(2)}) collective-permute-start(bf16[192,1024]{1,0:T(8,128)(2,1)S(1)} %get-tuple-element.56), channel_id=1, source_target_pairs={{0,8},{2,10},{4,12},{6,14},{1,9},{3,11},{5,13},{7,15},{16,24},{18,... | collective-permute-start | bytes 1179656 | tf_op jit(solution)/shard_map/ppermute | solution.py:22
  38.2 99.0 %collective-permute-start.9 = (bf16[192,1024]{1,0:T(8,128)(2,1)S(1)}, bf16[192,1024]{1,0:T(8,128)(2,1)S(1)}, u32[]{:S(2)}, u32[]{:S(2)}) collective-permute-start(bf16[192,1024]{1,0:T(8,128)(2,1)S(1)} %get-tuple-element.50), channel_id=1, source_target_pairs={{0,10},{2,12},{4,14},{6,8},{1,11},{3,13},{5,15},{7,9},{16,26},{18,... | collective-permute-start | bytes 1179656 | tf_op jit(solution)/shard_map/ppermute | solution.py:22
  121.1 25.4 %collective-permute-start.8 = (bf16[192,1024]{1,0:T(8,128)(2,1)S(1)}, bf16[192,1024]{1,0:T(8,128)(2,1)S(1)}, u32[]{:S(2)}, u32[]{:S(2)}) collective-permute-start(bf16[192,1024]{1,0:T(8,128)(2,1)S(1)} %get-tuple-element.49), channel_id=1, source_target_pairs={{0,12},{2,14},{4,8},{6,10},{1,13},{3,15},{5,9},{7,11},{16,28},{18,... | collective-permute-start | bytes 1179656 | tf_op jit(solution)/shard_map/ppermute | solution.py:22
  129.6 18.9 %collective-permute-start.7 = (bf16[192,1024]{1,0:T(8,128)(2,1)S(1)}, bf16[192,1024]{1,0:T(8,128)(2,1)S(1)}, u32[]{:S(2)}, u32[]{:S(2)}) collective-permute-start(bf16[192,1024]{1,0:T(8,128)(2,1)S(1)} %get-tuple-element.48), channel_id=1, source_target_pairs={{0,14},{2,8},{4,10},{6,12},{1,15},{3,9},{5,11},{7,13},{16,30},{18,... | collective-permute-start | bytes 1179656 | tf_op jit(solution)/shard_map/ppermute | solution.py:22
  132.3 16.3 %collective-permute-start.6 = (bf16[192,1024]{1,0:T(8,128)(2,1)S(1)}, bf16[192,1024]{1,0:T(8,128)(2,1)S(1)}, u32[]{:S(2)}, u32[]{:S(2)}) collective-permute-start(bf16[192,1024]{1,0:T(8,128)(2,1)S(1)} %get-tuple-element.47), channel_id=1, source_target_pairs={{0,8},{2,10},{4,12},{6,14},{1,9},{3,11},{5,13},{7,15},{16,24},{18,... | collective-permute-start | bytes 1179656 | tf_op jit(solution)/shard_map/ppermute | solution.py:22
  149.0 8.5 %collective-permute-start.20 = (bf16[192,1024]{1,0:T(8,128)(2,1)S(1)}, bf16[192,1024]{1,0:T(8,128)(2,1)S(1)}, u32[]{:S(2)}, u32[]{:S(2)}) collective-permute-start(bf16[192,1024]{1,0:T(8,128)(2,1)S(1)} %pad_maximum_fusion.3), channel_id=1, source_target_pairs={{8,9},{9,8},{10,11},{11,10},{12,13},{13,12},{14,15},{15,14},{24,25... | collective-permute-start | bytes 1179656 | tf_op jit(solution)/shard_map/ppermute | solution.py:22
  151.2 20.7 %collective-permute-start.10 = (bf16[192,1024]{1,0:T(8,128)(2,1)S(1)}, bf16[192,1024]{1,0:T(8,128)(2,1)S(1)}, u32[]{:S(2)}, u32[]{:S(2)}) collective-permute-start(bf16[192,1024]{1,0:T(8,128)(2,1)S(1)} %pad_maximum_fusion.1), channel_id=1, source_target_pairs={{8,9},{9,8},{10,11},{11,10},{12,13},{13,12},{14,15},{15,14},{24,25... | collective-permute-start | bytes 1179656 | tf_op jit(solution)/shard_map/ppermute | solution.py:22
  157.7 19.7 %collective-permute-start.31 = (bf16[192,1024]{1,0:T(8,128)(2,1)S(1)}, bf16[192,1024]{1,0:T(8,128)(2,1)S(1)}, u32[]{:S(2)}, u32[]{:S(2)}) collective-permute-start(bf16[192,1024]{1,0:T(8,128)(2,1)S(1)} %fusion.1.refs_0_), channel_id=1, source_target_pairs={{8,10},{10,12},{12,14},{14,8},{9,11},{11,13},{13,15},{15,9},{24,26... | collective-permute-start | bytes 1179656 | tf_op jit(solution)/shard_map/ppermute | solution.py:22
  162.0 19.4 %collective-permute-start.32 = (bf16[192,1024]{1,0:T(8,128)(2,1)S(1)}, bf16[192,1024]{1,0:T(8,128)(2,1)S(1)}, u32[]{:S(2)}, u32[]{:S(2)}) collective-permute-start(bf16[192,1024]{1,0:T(8,128)(2,1)S(1)} %fusion.1.refs_0_), channel_id=1, source_target_pairs={{8,12},{10,14},{12,8},{14,10},{9,13},{11,15},{13,9},{15,11},{24,28... | collective-permute-start | bytes 1179656 | tf_op jit(solution)/shard_map/ppermute | solution.py:22
  170.0 16.8 %collective-permute-start.33 = (bf16[192,1024]{1,0:T(8,128)(2,1)S(1)}, bf16[192,1024]{1,0:T(8,128)(2,1)S(1)}, u32[]{:S(2)}, u32[]{:S(2)}) collective-permute-start(bf16[192,1024]{1,0:T(8,128)(2,1)S(1)} %fusion.1.refs_0_), channel_id=1, source_target_pairs={{8,14},{10,8},{12,10},{14,12},{9,15},{11,9},{13,11},{15,13},{24,30... | collective-permute-start | bytes 1179656 | tf_op jit(solution)/shard_map/ppermute | solution.py:22
  172.1 27.8 %collective-permute-start.22 = (bf16[192,1024]{1,0:T(8,128)(2,1)S(1)}, bf16[192,1024]{1,0:T(8,128)(2,1)S(1)}, u32[]{:S(2)}, u32[]{:S(2)}) collective-permute-start(bf16[192,1024]{1,0:T(8,128)(2,1)S(1)} %fusion.refs_0_), channel_id=1, source_target_pairs={{8,10},{10,12},{12,14},{14,8},{9,11},{11,13},{13,15},{15,9},{24,26... | collective-permute-start | bytes 1179656 | tf_op jit(solution)/shard_map/ppermute | solution.py:22
  175.4 24.4 %collective-permute-start.23 = (bf16[192,1024]{1,0:T(8,128)(2,1)S(1)}, bf16[192,1024]{1,0:T(8,128)(2,1)S(1)}, u32[]{:S(2)}, u32[]{:S(2)}) collective-permute-start(bf16[192,1024]{1,0:T(8,128)(2,1)S(1)} %fusion.refs_0_), channel_id=1, source_target_pairs={{8,12},{10,14},{12,8},{14,10},{9,13},{11,15},{13,9},{15,11},{24,28... | collective-permute-start | bytes 1179656 | tf_op jit(solution)/shard_map/ppermute | solution.py:22
  177.4 22.5 %collective-permute-start.24 = (bf16[192,1024]{1,0:T(8,128)(2,1)S(1)}, bf16[192,1024]{1,0:T(8,128)(2,1)S(1)}, u32[]{:S(2)}, u32[]{:S(2)}) collective-permute-start(bf16[192,1024]{1,0:T(8,128)(2,1)S(1)} %fusion.refs_0_), channel_id=1, source_target_pairs={{8,14},{10,8},{12,10},{14,12},{9,15},{11,9},{13,11},{15,13},{24,30... | collective-permute-start | bytes 1179656 | tf_op jit(solution)/shard_map/ppermute | solution.py:22
  197.9 21.2 %collective-permute-start.34 = (bf16[2,32,96,128]{3,2,1,0:T(8,128)(2,1)S(1)}, bf16[2,32,96,128]{3,2,1,0:T(8,128)(2,1)S(1)}, u32[]{:S(2)}, u32[]{:S(2)}) collective-permute-start(bf16[2,32,96,128]{3,2,1,0:T(8,128)(2,1)S(1)} %get-tuple-element.70), channel_id=1, source_target_pairs={{8,9},{9,8},{10,11},{11,10},{12,13},{13,12},{14,15},{15,14},{24,25... | collective-permute-start | bytes 4718600 | tf_op jit(solution)/shard_map/ppermute | solution.py:22
  211.0 24.9 %collective-permute-start.25 = (bf16[2,32,96,128]{3,2,1,0:T(8,128)(2,1)S(1)}, bf16[2,32,96,128]{3,2,1,0:T(8,128)(2,1)S(1)}, u32[]{:S(2)}, u32[]{:S(2)}) collective-permute-start(bf16[2,32,96,128]{3,2,1,0:T(8,128)(2,1)S(1)} %get-tuple-element.61), channel_id=1, source_target_pairs={{8,9},{9,8},{10,11},{11,10},{12,13},{13,12},{14,15},{15,14},{24,25... | collective-permute-start | bytes 4718600 | tf_op jit(solution)/shard_map/ppermute | solution.py:22
  223.5 20.9 %collective-permute-start.35 = (bf16[32,96,128]{2,1,0:T(8,128)(2,1)S(1)}, bf16[32,96,128]{2,1,0:T(8,128)(2,1)S(1)}, u32[]{:S(2)}, u32[]{:S(2)}) collective-permute-start(bf16[32,96,128]{2,1,0:T(8,128)(2,1)S(1)} %get-tuple-element.72.refs_0_), channel_id=1, source_target_pairs={{8,9},{9,8},{10,11},{11,10},{12,13},{13,12},{14,15},{15,14},{24,25... | collective-permute-start | bytes 2359304 | tf_op jit(solution)/shard_map/ppermute | solution.py:22
  240.3 30.7 %collective-permute-start.26 = (bf16[32,96,128]{2,1,0:T(8,128)(2,1)S(1)}, bf16[32,96,128]{2,1,0:T(8,128)(2,1)S(1)}, u32[]{:S(2)}, u32[]{:S(2)}) collective-permute-start(bf16[32,96,128]{2,1,0:T(8,128)(2,1)S(1)} %get-tuple-element.63.refs_0_), channel_id=1, source_target_pairs={{8,9},{9,8},{10,11},{11,10},{12,13},{13,12},{14,15},{15,14},{24,25... | collective-permute-start | bytes 2359304 | tf_op jit(solution)/shard_map/ppermute | solution.py:22
  254.5 27.7 %collective-permute-start.38 = (bf16[192,1024]{1,0:T(8,128)(2,1)S(1)}, bf16[192,1024]{1,0:T(8,128)(2,1)S(1)}, u32[]{:S(2)}, u32[]{:S(2)}) collective-permute-start(bf16[192,1024]{1,0:T(8,128)(2,1)S(1)} %get-tuple-element.77), channel_id=1, source_target_pairs={{8,10},{10,12},{12,14},{14,8},{9,11},{11,13},{13,15},{15,9},{24,26... | collective-permute-start | bytes 1179656 | tf_op jit(solution)/shard_map/ppermute | solution.py:22
  263.9 23.0 %collective-permute-start.37 = (bf16[192,1024]{1,0:T(8,128)(2,1)S(1)}, bf16[192,1024]{1,0:T(8,128)(2,1)S(1)}, u32[]{:S(2)}, u32[]{:S(2)}) collective-permute-start(bf16[192,1024]{1,0:T(8,128)(2,1)S(1)} %get-tuple-element.76), channel_id=1, source_target_pairs={{8,12},{10,14},{12,8},{14,10},{9,13},{11,15},{13,9},{15,11},{24,28... | collective-permute-start | bytes 1179656 | tf_op jit(solution)/shard_map/ppermute | solution.py:22
  266.8 21.4 %collective-permute-start.36 = (bf16[192,1024]{1,0:T(8,128)(2,1)S(1)}, bf16[192,1024]{1,0:T(8,128)(2,1)S(1)}, u32[]{:S(2)}, u32[]{:S(2)}) collective-permute-start(bf16[192,1024]{1,0:T(8,128)(2,1)S(1)} %get-tuple-element.75), channel_id=1, source_target_pairs={{8,14},{10,8},{12,10},{14,12},{9,15},{11,9},{13,11},{15,13},{24,30... | collective-permute-start | bytes 1179656 | tf_op jit(solution)/shard_map/ppermute | solution.py:22
  277.8 12.9 %collective-permute-start.29 = (bf16[192,1024]{1,0:T(8,128)(2,1)S(1)}, bf16[192,1024]{1,0:T(8,128)(2,1)S(1)}, u32[]{:S(2)}, u32[]{:S(2)}) collective-permute-start(bf16[192,1024]{1,0:T(8,128)(2,1)S(1)} %get-tuple-element.68), channel_id=1, source_target_pairs={{8,10},{10,12},{12,14},{14,8},{9,11},{11,13},{13,15},{15,9},{24,26... | collective-permute-start | bytes 1179656 | tf_op jit(solution)/shard_map/ppermute | solution.py:22
  279.7 16.8 %collective-permute-start.28 = (bf16[192,1024]{1,0:T(8,128)(2,1)S(1)}, bf16[192,1024]{1,0:T(8,128)(2,1)S(1)}, u32[]{:S(2)}, u32[]{:S(2)}) collective-permute-start(bf16[192,1024]{1,0:T(8,128)(2,1)S(1)} %get-tuple-element.67), channel_id=1, source_target_pairs={{8,12},{10,14},{12,8},{14,10},{9,13},{11,15},{13,9},{15,11},{24,28... | collective-permute-start | bytes 1179656 | tf_op jit(solution)/shard_map/ppermute | solution.py:22
  282.1 14.4 %collective-permute-start.27 = (bf16[192,1024]{1,0:T(8,128)(2,1)S(1)}, bf16[192,1024]{1,0:T(8,128)(2,1)S(1)}, u32[]{:S(2)}, u32[]{:S(2)}) collective-permute-start(bf16[192,1024]{1,0:T(8,128)(2,1)S(1)} %get-tuple-element.66), channel_id=1, source_target_pairs={{8,14},{10,8},{12,10},{14,12},{9,15},{11,9},{13,11},{15,13},{24,30... | collective-permute-start | bytes 1179656 | tf_op jit(solution)/shard_map/ppermute | solution.py:22
  286.9 16.6 %collective-permute-start.21 = (bf16[192,1024]{1,0:T(8,128)(2,1)S(1)}, bf16[192,1024]{1,0:T(8,128)(2,1)S(1)}, u32[]{:S(2)}, u32[]{:S(2)}) collective-permute-start(bf16[192,1024]{1,0:T(8,128)(2,1)S(1)} %pad_maximum_fusion.4), channel_id=1, source_target_pairs={{8,0},{9,1},{10,2},{11,3},{12,4},{13,5},{14,6},{15,7},{24,16},{25,... | collective-permute-start | bytes 1179656 | tf_op jit(solution)/shard_map/ppermute | solution.py:417
  288.5 10.7 %collective-permute-start.39 = (bf16[96,1024]{1,0:T(8,128)(2,1)S(1)}, bf16[96,1024]{1,0:T(8,128)(2,1)S(1)}, u32[]{:S(2)}, u32[]{:S(2)}) collective-permute-start(bf16[96,1024]{1,0:T(8,128)(2,1)S(1)} %slice.146), channel_id=1, source_target_pairs={{8,9},{9,8},{10,11},{11,10},{12,13},{13,12},{14,15},{15,14},{24,25... | collective-permute-start | bytes 589832 | tf_op jit(solution)/shard_map/ppermute | solution.py:22
  296.9 6.5 %collective-permute-start.30 = (bf16[96,1024]{1,0:T(8,128)(2,1)S(1)}, bf16[96,1024]{1,0:T(8,128)(2,1)S(1)}, u32[]{:S(2)}, u32[]{:S(2)}) collective-permute-start(bf16[96,1024]{1,0:T(8,128)(2,1)S(1)} %slice.147), channel_id=1, source_target_pairs={{8,9},{9,8},{10,11},{11,10},{12,13},{13,12},{14,15},{15,14},{24,25... | collective-permute-start | bytes 589832 | tf_op jit(solution)/shard_map/ppermute | solution.py:22
  (20 other events, 385.9 us)

commit v3 on v2

v3 whole, which is shorter than its diff:
```python
import functools

import jax
import jax.numpy as jnp
from jax import lax
from jax.experimental import pallas as pl
from jax.experimental.pallas import tpu as pltpu
from jax.sharding import PartitionSpec as P

BLOCK = 128
UNROLL = 16
MIB = 1024 * 1024
VMEM_LIMIT = 56 * MIB
PIECES = 1
SLOW = 4

perturb_scale = 0.5
epsilon = 1e-05


def hop(value, axis, steps):
    count = lax.axis_size(axis)
    return lax.ppermute(value, axis, [(i, (i + steps) % count) for i in range(count)])


def pick_matrix(row_member, member_seed, noise_count):
    member_ids = jnp.arange(member_seed.shape[0], dtype=jnp.int32)
    matched = row_member[:, None] == member_ids[None, :]
    seed_of = jnp.sum(jnp.where(matched, member_seed[None, :], 0), axis=1)
    sign_values = (1 - 2 * (row_member % 2)).astype(jnp.float32) * perturb_scale
    noise_ids = jnp.arange(noise_count, dtype=jnp.int32)
    return jnp.where(seed_of[:, None] == noise_ids[None, :], sign_values[:, None], jnp.float32(0.0))


def tile_plan(codes, block_rows, own_cols, owner_index, owners):
    tile_count = codes.shape[1]
    active = codes >= 0
    cleared = jnp.where(active, codes, 0)
    column = cleared // block_rows
    feature = cleared % block_rows
    per_owner = block_rows // owners
    feature = lax.rem(owner_index - feature // per_owner + owners, owners) * per_owner + feature % per_owner
    is_down = jnp.arange(3)[:, None] == 2
    major = jnp.where(is_down, feature, column)
    minor = jnp.where(is_down, column, feature)
    major_count = max(block_rows, own_cols)
    majors = jnp.arange(major_count, dtype=jnp.int32)
    filled = jnp.sum(
        jnp.where(active[:, None, :] & (major[:, None, :] == majors[None, :, None]), 1, 0), axis=2
    )
    padded = 2 * ((filled + 1) // 2)
    before = jnp.sum(jnp.where(majors[None, None, :] < major[:, :, None], padded[:, None, :], 0), axis=2)
    rank = jnp.sum(
        jnp.where(
            active[:, None, :]
            & (major[:, None, :] == major[:, :, None])
            & (minor[:, None, :] < minor[:, :, None]),
            1,
            0,
        ),
        axis=2,
    )
    place = jnp.where(active, before + rank, -1)
    length = tile_count + min(tile_count, major_count)
    group = 2 * UNROLL
    length = -(-length // group) * group
    tile_ids = jnp.arange(tile_count, dtype=jnp.int32)
    words = (tile_ids[None, :] - tile_count) + minor * 4096 + major * 1048576
    spots = jnp.arange(length, dtype=jnp.int32)
    packed = tile_count + jnp.sum(
        jnp.where(place[:, None, :] == spots[None, :, None], words[:, None, :], 0), axis=2
    )
    groups = (jnp.sum(padded, axis=1) + group - 1) // group
    return packed.astype(jnp.int32), groups.astype(jnp.int32)


def multiply_tiles(words_ref, groups_ref, which, length, read, tiles_ref, add):
    def group(i, carry):
        for u in range(UNROLL):
            at = which * length + (i * UNROLL + u) * 2
            first, second = words_ref[at], words_ref[at + 1]
            left = jnp.concatenate([read((first >> 12) & 255), read((second >> 12) & 255)], axis=1)
            right = jnp.concatenate([tiles_ref[first & 4095], tiles_ref[second & 4095]], axis=0)
            add(first >> 20, jnp.dot(left, right, preferred_element_type=jnp.float32))
        return carry

    lax.fori_loop(0, groups_ref[which], group, 0)


def load_tiles(own, choices, tiles, sem):
    copies = [pltpu.make_async_copy(tiles_hbm, tiles.at[pl.ds(0, tiles_hbm.shape[0])], sem) for tiles_hbm in choices]
    pl.when(own == 1)(copies[0].start)
    pl.when(own != 1)(copies[1].start)
    tiles[tiles.shape[0] - 1] = jnp.zeros((BLOCK, BLOCK), tiles.dtype)
    return copies[0]


def expand_into(words_ref, groups_ref, which, x_ref, tiles, total_ref, part_refs, copy):
    length = words_ref.shape[0] // 3
    rows = part_refs[0].shape[1]
    total_ref[...] = jnp.zeros(total_ref.shape, jnp.float32)
    copy.wait()

    def read(block):
        return x_ref[block]

    def add(block, product):
        total_ref[block] += product

    multiply_tiles(words_ref, groups_ref, which, length, read, tiles, add)
    for rep, part_ref in enumerate(part_refs):

        def narrow(c, carry, rep=rep, part_ref=part_ref):
            part_ref[c] = total_ref[c, pl.ds(rep * rows, rows), :].astype(jnp.bfloat16)
            return carry

        lax.fori_loop(0, total_ref.shape[0], narrow, 0, unroll=min(4, total_ref.shape[0]))


def gate_kernel(owners, reps, words_ref, groups_ref, *refs):
    blocks = refs[:owners]
    gain_ref, left_ref, own_hbm, other_hbm, raw_ref, x_ref = refs[owners : owners + 6]
    part_refs = refs[owners + 6 : owners + 6 + reps]
    total_ref, tiles, sem = refs[owners + 6 + reps :]
    all_rows, width = blocks[0].shape
    rows = all_rows // reps
    per_owner = width // BLOCK
    strip = 48 if all_rows % 48 == 0 else 16
    copy = load_tiles(groups_ref[3], (own_hbm, other_hbm), tiles, sem)

    def norm_rows(i, carry):
        at = pl.ds(pl.multiple_of(i * strip, strip), strip)
        squares = jnp.zeros((strip, BLOCK), jnp.float32)
        for owner in range(owners):
            for part in range(per_owner):
                values = blocks[owner][at, pl.ds(part * BLOCK, BLOCK)].astype(jnp.float32)
                squares = squares + values * values
        total = jnp.sum(squares, axis=1, keepdims=True)
        inverse = lax.rsqrt(total / (owners * width) + epsilon)
        for owner in range(owners):
            for part in range(per_owner):
                values = blocks[owner][at, pl.ds(part * BLOCK, BLOCK)].astype(jnp.float32)
                gain = gain_ref[:, pl.ds(owner * width + part * BLOCK, BLOCK)].astype(jnp.float32)
                x_ref[owner * per_owner + part, at, :] = (values * inverse * gain).astype(jnp.bfloat16)
        return carry

    lax.fori_loop(0, all_rows // strip, norm_rows, 0)
    raw = jnp.zeros(raw_ref.shape, jnp.float32)
    step = min(8, x_ref.shape[0])
    for d in range(0, x_ref.shape[0], step):
        raw = raw + lax.dot_general(
            jnp.concatenate([x_ref[d + i, pl.ds(0, rows), :] for i in range(step)], axis=1),
            left_ref[:, pl.ds(d * BLOCK, step * BLOCK)],
            (((1,), (1,)), ((), ())),
            preferred_element_type=jnp.float32,
        )
    raw_ref[...] = raw
    expand_into(words_ref, groups_ref, 0, x_ref, tiles, total_ref, part_refs, copy)


def up_kernel(reps, words_ref, groups_ref, x_ref, own_hbm, other_hbm, *refs):
    part_refs = refs[:reps]
    total_ref, tiles, sem = refs[reps:]
    copy = load_tiles(groups_ref[3], (own_hbm, other_hbm), tiles, sem)
    expand_into(words_ref, groups_ref, 1, x_ref, tiles, total_ref, part_refs, copy)


SMEM = pl.BlockSpec(memory_space=pltpu.SMEM)
VMEM = pl.BlockSpec(memory_space=pltpu.VMEM)
HBM = pl.BlockSpec(memory_space=pl.ANY)


def tile_cost(tile_count, all_rows):
    return pl.CostEstimate(
        flops=SLOW * 2 * tile_count * all_rows * BLOCK * BLOCK,
        bytes_accessed=2 * tile_count * BLOCK * BLOCK,
        transcendentals=0,
    )


def tile_scratch(tile_count, blocks, all_rows):
    return [
        pltpu.VMEM((blocks, all_rows, BLOCK), jnp.float32),
        pltpu.VMEM((tile_count + 1, BLOCK, BLOCK), jnp.bfloat16),
        pltpu.SemaphoreType.DMA,
    ]


def expand_gate(words, groups, blocks, gain, left, tiles, own_cols, reps):
    owners = len(blocks)
    all_rows, width = blocks[0].shape
    rows = all_rows // reps
    tile_count = tiles[0].shape[0]
    out = pl.pallas_call(
        functools.partial(gate_kernel, owners, reps),
        out_shape=[
            jax.ShapeDtypeStruct((rows, left.shape[0]), jnp.float32),
            jax.ShapeDtypeStruct((owners * width // BLOCK, all_rows, BLOCK), jnp.bfloat16),
        ]
        + [jax.ShapeDtypeStruct((own_cols, rows, BLOCK), jnp.bfloat16)] * reps,
        in_specs=[SMEM, SMEM] + [VMEM] * (owners + 2) + [HBM, HBM],
        out_specs=[VMEM] * (2 + reps),
        scratch_shapes=tile_scratch(tile_count, own_cols, all_rows),
        compiler_params=pltpu.CompilerParams(vmem_limit_bytes=VMEM_LIMIT),
        cost_estimate=tile_cost(tile_count, all_rows),
        name="gate",
    )(words, groups, *blocks, gain, left, *tiles)
    return out[0], out[1], out[2:]


def expand_up(words, groups, x, tiles, own_cols, reps):
    all_rows = x.shape[1]
    rows = all_rows // reps
    tile_count = tiles[0].shape[0]
    return pl.pallas_call(
        functools.partial(up_kernel, reps),
        out_shape=[jax.ShapeDtypeStruct((own_cols, rows, BLOCK), jnp.bfloat16)] * reps,
        in_specs=[SMEM, SMEM, VMEM, HBM, HBM],
        out_specs=[VMEM] * reps,
        scratch_shapes=tile_scratch(tile_count, own_cols, all_rows),
        compiler_params=pltpu.CompilerParams(vmem_limit_bytes=VMEM_LIMIT),
        cost_estimate=tile_cost(tile_count, all_rows),
        name="up",
    )(words, groups, x, *tiles)


def activate_kernel(reps, *refs):
    parts = (refs[:reps], refs[reps : 2 * reps])
    raw_ref, picks_ref, wide_cols, down_cols, hidden_ref, coef_ref = refs[2 * reps :]
    noise = picks_ref.shape[1]
    columns, rows = hidden_ref.shape[:2]
    picks = picks_ref[...]
    coefs = (jnp.concatenate([picks, picks], axis=1) * raw_ref[...]).astype(jnp.bfloat16)

    def pair(i, down):
        hiddens = []
        for u in range(2):
            c = i * 2 + u
            low_rank = jnp.dot(coefs, wide_cols[c], preferred_element_type=jnp.float32)
            values = []
            for which in range(2):
                value = low_rank[:, which * BLOCK : (which + 1) * BLOCK]
                for part in parts[which]:
                    value = value + part[c].astype(jnp.float32)
                values.append(value)
            gate, up = values
            hidden = (gate / (1.0 + jnp.exp(-gate)) * up).astype(jnp.bfloat16)
            hidden_ref[c] = hidden
            hiddens.append(hidden)
        return down + lax.dot_general(
            jnp.concatenate(hiddens, axis=1),
            down_cols[i],
            (((1,), (1,)), ((), ())),
            preferred_element_type=jnp.float32,
        )

    down = lax.fori_loop(
        0, columns // 2, pair, jnp.zeros((rows, noise), jnp.float32), unroll=min(4, columns // 2)
    )
    coef_ref[...] = picks * down


def activate(gates, ups, raw, picks, wide_cols, down_cols):
    own_cols, rows = gates[0].shape[:2]
    noise = picks.shape[1]
    reps = len(gates)
    return pl.pallas_call(
        functools.partial(activate_kernel, reps),
        out_shape=[
            jax.ShapeDtypeStruct((own_cols, rows, BLOCK), jnp.bfloat16),
            jax.ShapeDtypeStruct((rows, noise), jnp.float32),
        ],
        in_specs=[VMEM] * (2 * reps + 4),
        out_specs=[VMEM] * 2,
        compiler_params=pltpu.CompilerParams(vmem_limit_bytes=16 * MIB),
        cost_estimate=pl.CostEstimate(
            flops=100 * own_cols * rows * BLOCK,
            bytes_accessed=(reps * 2 + 1) * 2 * own_cols * rows * BLOCK,
            transcendentals=own_cols * rows * BLOCK,
        ),
        name="activate",
    )(*gates, *ups, raw, picks, wide_cols, down_cols)


def contract_kernel(owners, reps, words_ref, groups_ref, *refs):
    hiddens = refs[:reps]
    coef_ref, right_ref, own_hbm, other_hbm = refs[reps : reps + 4]
    outs = refs[reps + 4 : reps + 4 + owners]
    total_ref, tiles, sem = refs[reps + 4 + owners :]
    rows = hiddens[0].shape[1]
    per_owner = outs[0].shape[1] // BLOCK
    blocks = total_ref.shape[0]
    copy = load_tiles(groups_ref[3], (own_hbm, other_hbm), tiles, sem)

    def read(block):
        return jnp.concatenate([hidden[block] for hidden in hiddens], axis=0)

    def add(block, product):
        total_ref[block] += product

    coef = coef_ref[...]
    high = coef.astype(jnp.bfloat16)
    low = (coef - high.astype(jnp.float32)).astype(jnp.bfloat16)
    right = right_ref[...]
    both = jnp.concatenate([high, low], axis=1)
    twice = jnp.concatenate([right, right], axis=0)
    for d in range(0, blocks, 2):
        start = jnp.dot(both, twice[:, d * BLOCK : (d + 2) * BLOCK], preferred_element_type=jnp.float32)
        for i in range(2):
            total_ref[d + i, pl.ds(0, rows), :] = start[:, i * BLOCK : (i + 1) * BLOCK]
            if reps > 1:
                total_ref[d + i, pl.ds(rows, (reps - 1) * rows), :] = jnp.zeros(
                    ((reps - 1) * rows, BLOCK), jnp.float32
                )
    copy.wait()
    multiply_tiles(words_ref, groups_ref, 2, words_ref.shape[0] // 3, read, tiles, add)
    for owner in range(owners):
        for part in range(per_owner):
            outs[owner][:, pl.ds(part * BLOCK, BLOCK)] = total_ref[owner * per_owner + part].astype(jnp.bfloat16)


def contract(words, groups, hiddens, coef, right, tiles, owners):
    own_cols, rows = hiddens[0].shape[:2]
    reps = len(hiddens)
    features = right.shape[1]
    tile_count = tiles[0].shape[0]
    return pl.pallas_call(
        functools.partial(contract_kernel, owners, reps),
        out_shape=[jax.ShapeDtypeStruct((reps * rows, features // owners), jnp.bfloat16)] * owners,
        in_specs=[SMEM, SMEM] + [VMEM] * (reps + 2) + [HBM, HBM],
        out_specs=[VMEM] * owners,
        scratch_shapes=tile_scratch(tile_count, features // BLOCK, reps * rows),
        compiler_params=pltpu.CompilerParams(vmem_limit_bytes=VMEM_LIMIT),
        cost_estimate=tile_cost(tile_count, reps * rows),
        name="contract",
    )(words, groups, *hiddens, coef, right, *tiles)


def per_device(
    tokens,
    norm_gain,
    gate_tiles,
    up_tiles,
    down_tiles,
    gate_slot,
    up_slot,
    down_slot,
    owned_columns,
    gate_left,
    gate_right,
    up_left,
    up_right,
    down_left,
    down_right,
    row_member,
    member_seed,
):
    section_index = lax.axis_index("section")
    owner_index = lax.axis_index("tensor")
    rep_index = lax.axis_index("rep")
    owners, reps = lax.axis_size("tensor"), lax.axis_size("rep")
    rows, width = tokens.shape
    own_cols = owned_columns.shape[1] // owners
    block_rows = gate_left.shape[2] // BLOCK
    tile_count = gate_tiles.shape[1]

    codes = jnp.stack([gate_slot[0], up_slot[0], down_slot[0]])
    codes = lax.dynamic_slice_in_dim(codes, rep_index * tile_count, tile_count, axis=1)
    words, groups = tile_plan(codes, block_rows, own_cols, owner_index, owners)
    words = words.reshape(-1)

    rotation = lax.rem(owner_index - jnp.arange(owners, dtype=jnp.int32) + owners, owners)
    noise = gate_left.shape[1]

    def rotated(table):
        parts = table.reshape(table.shape[0], owners, width)
        return jnp.take(parts, rotation, axis=1).reshape(table.shape)

    columns = lax.dynamic_slice_in_dim(owned_columns[0], owner_index * own_cols, own_cols)

    def owned(table):
        return jnp.take(table.reshape(table.shape[0], -1, BLOCK), columns, axis=1)

    plan = jnp.concatenate([words, groups])
    wide = rotated(jnp.concatenate([gate_left[0], up_left[0], down_right[0], norm_gain], axis=0))
    cols = owned(jnp.concatenate([gate_right[0], up_right[0], down_left[0]], axis=0))
    mine = (plan, wide, cols)
    theirs = tuple(hop(table, "section", 1) for table in mine)
    gate_pair = (gate_tiles[0], hop(gate_tiles[0], "section", 1))
    up_pair = (up_tiles[0], hop(up_tiles[0], "section", 1))
    down_pair = (down_tiles[0], hop(down_tiles[0], "section", 1))
    picks = pick_matrix(row_member, member_seed, noise)

    def layer(stream, picked, section):
        own = section_index == section
        plan, wide, cols = (jnp.where(own, a, b) for a, b in zip(mine, theirs))
        words = plan[:-3]
        groups = jnp.concatenate([plan[-3:], own.astype(jnp.int32)[None]])
        left, right, gain = wide[: 2 * noise], wide[2 * noise : 3 * noise], wide[3 * noise :]
        gate_cols, up_cols, down_cols = cols[:noise], cols[noise : 2 * noise], cols[2 * noise :]
        empty = jnp.zeros_like(gate_cols)
        wide_cols = jnp.concatenate(
            [jnp.concatenate([gate_cols, empty], axis=2), jnp.concatenate([empty, up_cols], axis=2)], axis=0
        ).transpose(1, 0, 2)
        down_cols = down_cols.reshape(noise, own_cols // 2, 2 * BLOCK).transpose(1, 0, 2)

        blocks = [stream] + [hop(stream, "tensor", step) for step in range(1, owners)]
        raw, x, gates = expand_gate(words, groups, blocks, gain, left, gate_pair, own_cols, reps)
        gates = [gates[0]] + [hop(gates[g], "rep", -g) for g in range(1, reps)]
        ups = expand_up(words, groups, x, up_pair, own_cols, reps)
        ups = [ups[0]] + [hop(ups[g], "rep", -g) for g in range(1, reps)]
        hidden, coef = activate(gates, ups, raw, picked, wide_cols, down_cols)
        hiddens = [hidden] + [hop(hidden, "rep", g) for g in range(1, reps)]
        outs = contract(words, groups, hiddens, coef, right, down_pair, owners)
        summed = outs[0].astype(jnp.float32)
        for step in range(1, owners):
            summed = summed + hop(outs[step], "tensor", -step).astype(jnp.float32)
        return summed

    half = rows // 2
    mine_rows = lax.dynamic_slice_in_dim(tokens, section_index * half, half)
    mine_picks = lax.dynamic_slice_in_dim(picks, section_index * half, half)
    others = [hop(mine_rows, "rep", g) for g in range(1, reps)]
    piece = half // PIECES
    firsts, seconds = [], []
    for h in range(PIECES):
        cut = slice(h * piece, (h + 1) * piece)
        stream = jnp.concatenate([value[cut] for value in [mine_rows] + others], axis=0)
        summed = layer(stream, mine_picks[cut], 0)
        own = stream[:piece].astype(jnp.float32) + summed[:piece]
        summed = jnp.concatenate([own, summed[piece:]], axis=0).astype(jnp.bfloat16)
        total = summed.astype(jnp.float32)
        for g in range(1, reps):
            arrived = hop(summed, "rep", g).astype(jnp.float32)
            total = total + jnp.roll(arrived, g * piece, axis=0)
        stream = total.astype(jnp.bfloat16)
        firsts.append(stream[:piece])
        summed = layer(stream, mine_picks[cut], 1)
        value = stream[:piece].astype(jnp.float32) + summed[:piece]
        for g in range(1, reps):
            sent = summed[g * piece : (g + 1) * piece].astype(jnp.bfloat16)
            value = value + hop(sent, "rep", -g).astype(jnp.float32)
        seconds.append(value.astype(jnp.bfloat16))
    first = jnp.concatenate(firsts, axis=0)
    second = jnp.concatenate(seconds, axis=0)
    kept = jnp.where(section_index == 0, first, second)
    received = hop(jnp.where(section_index == 0, second, first), "section", 1)
    out = jnp.where(
        section_index == 0,
        jnp.concatenate([kept, received], axis=0),
        jnp.concatenate([received, kept], axis=0),
    )
    return out[None]


def solution(mesh):
    placed = (
        P(("pop", "rep"), "tensor"),
        P("section", None),
        P("section", ("tensor", "rep"), None, None),
        P("section", ("tensor", "rep"), None, None),
        P("section", ("tensor", "rep"), None, None),
        P("section", "tensor"),
        P("section", "tensor"),
        P("section", "tensor"),
        P("section", None),
        P("section", None, None),
        P("section", None, None),
        P("section", None, None),
        P("section", None, None),
        P("section", None, None),
        P("section", None, None),
        P(("pop", "rep")),
        P("pop"),
    )
    return jax.shard_map(
        per_device,
        mesh=mesh,
        in_specs=placed,
        out_specs=P("section", ("pop", "rep"), "tensor"),
        check_vma=False,
    )
```

time: 308 us -> 345 us (1.12)
  waiting for transfers between devices: 141 us -> 216 us
  starting transfers between devices: 87.3 us -> 37.4 us
  Pallas kernels: 47.9 us -> 66.7 us
  local copies, waits for them, and re-layouts: 19.5 us -> 11.5 us
    ppermute x40 -> x28, waiting for transfers between devices: 141 us -> 216 us  [hop(): lax.ppermute(value, axis, [(i, (i + steps) % count) for i in range(count)])]
    ppermute x40 -> x28, starting transfers between devices: 87.3 us -> 37.4 us  [hop(): lax.ppermute(value, axis, [(i, (i + steps) % count) for i in range(count)])]
    pallas_call x12 -> x8, Pallas kernels: 47.9 us -> 66.7 us  [the longest x2 21.9 us: expand_gate(): pl.pallas_call(functools.partial(gate_kernel, owners, reps), out_shape=[j...]
    unnamed x29 -> x64, local copies, waits for them, and re-layouts: 13.7 us -> 4.89 us
    slice x11 -> x12, local copies, waits for them, and re-layouts: 0.33 us -> 4.14 us  [the longest x2 1.32 us: layer(): wide[:2 * noise]]
  transfers between devices with their start and end apart: 40 -> 28, of which waited for: 14 -> 18; matrix products, arithmetic and copies ran while one was open for 4% -> 4% of each run, Pallas kernels for 16% -> 10%
where the time goes in v3:
time: 345 us; the launch traced here: 341 us
  waiting for transfers between devices  216 us (63%)
  Pallas kernels  66.7 us (19%)
  starting transfers between devices  37.4 us (11%)
  local copies, waits for them, and re-layouts  11.5 us (3%)
  other arithmetic  8.88 us (3%)
    ppermute x28, waiting for transfers between devices, hop(): lax.ppermute(value, axis, [(i, (i + steps) % count) for i in range(count)])  216 us
    ppermute x28, starting transfers between devices, hop(): lax.ppermute(value, axis, [(i, (i + steps) % count) for i in range(count)])  37.4 us
    pallas_call x2, Pallas kernels, expand_gate(): pl.pallas_call(functools.partial(gate_kernel, owners, reps), out_shape=[j...  21.9 us
    pallas_call x2, Pallas kernels, expand_up(): pl.pallas_call(functools.partial(up_kernel, reps), out_shape=[jax.ShapeDt...  20.5 us
    pallas_call x2, Pallas kernels, contract(): pl.pallas_call(functools.partial(contract_kernel, owners, reps), out_shap...  18.6 us
  transfers between devices with their start and end apart: 28, of which 18 were waited for; matrix products, arithmetic and copies ran while one was open for 4% of the time, Pallas kernels for 10%

profile of v3, /device:TPU:1, one launch (start us, length us, event | category | flops | bytes accessed | tf_op | source)
XLA Modules:
  0.0 341.0 jit_solution(12981955065175323824)
XLA Ops:
  4.2 2.4 collective-permute-start.1
  9.7 1.7 collective-permute-done.1
  11.5 3.3 collective-permute-start.4
  15.1 1.5 collective-permute-start.5
  17.4 8.6 %collective-permute-done.5 = bf16[25,4096]{1,0:T(8,128)(2,1)S(1)} collective-permute-done((bf16[25,4096]{1,0:T(8,128)(2,1)S(1)}, bf16[25,4096]{1,0:T(8,128)(2,1)S(1)}, u32[]{:S(2)}, u32[]{:S(2)}) %collective-permute-start.5) | collective-permute-done | bytes 204832 | tf_op jit(solution)/shard_map/ppermute | solution.py:23
  26.0 3.4 %collective-permute-start.3 = (bf16[192,1024]{1,0:T(8,128)(2,1)S(1)}, bf16[192,1024]{1,0:T(8,128)(2,1)S(1)}, u32[]{:S(2)}, u32[]{:S(2)}) collective-permute-start(bf16[192,1024]{1,0:T(8,128)(2,1)S(1)} %pad_maximum_fusion.1.refs_0_), channel_id=1, source_target_pairs={{0,4},{2,6},{4,0},{6,2},{1,5},{3,7},{5,1},{7,3},{8,12},{10,14},{12... | collective-permute-start | bytes 1179656 | tf_op jit(solution)/shard_map/ppermute | solution.py:23
  32.1 23.4 %collective-permute-done.3.refs_2_ = bf16[192,1024]{1,0:T(8,128)(2,1)S(1)} collective-permute-done((bf16[192,1024]{1,0:T(8,128)(2,1)S(1)}, bf16[192,1024]{1,0:T(8,128)(2,1)S(1)}, u32[]{:S(2)}, u32[]{:S(2)}) %collective-permute-start.3) | collective-permute-done | bytes 393248 | tf_op jit(solution)/shard_map/ppermute | solution.py:23
  57.1 11.2 %gate.2 = (f32[96,16]{1,0:T(8,128)}, bf16[32,192,128]{2,1,0:T(8,128)(2,1)}, bf16[32,96,128]{2,1,0:T(8,128)(2,1)}, bf16[32,96,128]{2,1,0:T(8,128)(2,1)}) custom-call(s32[864]{0:T(1024)} %bitcast.67, s32[4]{0:T(128)} %pad_add_fusion.1.groups_ref, bf16[192,1024]{1,0:T(8,128)(2,1)} %copy-done.12, bf16[192,1024]{1,0:T(8,128)(2,1)} %copy-done.27, ...), custom_call_target="tpu_custom_call" | custom-call | flops 6442450944 | bytes 8388608 | tf_op jit(solution)/shard_map/gate/pallas_call | solution.py:194
  69.1 10.3 %up.2 = (bf16[32,96,128]{2,1,0:T(8,128)(2,1)}, bf16[32,96,128]{2,1,0:T(8,128)(2,1)}) custom-call(s32[864]{0:T(1024)} %bitcast.68, s32[4]{0:T(128)} %pad_add_fusion.1.groups_ref, bf16[32,192,128]{2,1,0:T(8,128)(2,1)} %get-tuple-element.31.x_ref, bf16[256,128,128]{2,1,0:T(8,128)(2,1)} %bitcast.74, bf16[256,128,128]{2,1,0:T(8,128)(2,1)} %collective-permute-done.8.other_hbm), custom_call_target="tpu_custom_call" | custom-call | flops 6442450944 | bytes 8388608 | tf_op jit(solution)/shard_map/up/pallas_call | solution.py:215
  80.6 7.0 %collective-permute-done.7.refs_1_ = bf16[32,96,128]{2,1,0:T(8,128)(2,1)S(1)} collective-permute-done((bf16[32,96,128]{2,1,0:T(8,128)(2,1)}, bf16[32,96,128]{2,1,0:T(8,128)(2,1)S(1)}, u32[]{:S(2)}, u32[]{:S(2)}) %collective-permute-start.7) | collective-permute-done | bytes 786464 | tf_op jit(solution)/shard_map/ppermute | solution.py:23
  87.6 16.9 %collective-permute-done.9.refs_3_ = bf16[32,96,128]{2,1,0:T(8,128)(2,1)S(1)} collective-permute-done((bf16[32,96,128]{2,1,0:T(8,128)(2,1)}, bf16[32,96,128]{2,1,0:T(8,128)(2,1)S(1)}, u32[]{:S(2)}, u32[]{:S(2)}) %collective-permute-start.9) | collective-permute-done | bytes 786464 | tf_op jit(solution)/shard_map/ppermute | solution.py:23
  104.5 2.8 activate.2
  108.7 16.8 %collective-permute-done.11.refs_1_ = bf16[32,96,128]{2,1,0:T(8,128)(2,1)S(1)} collective-permute-done((bf16[32,96,128]{2,1,0:T(8,128)(2,1)S(1)}, bf16[32,96,128]{2,1,0:T(8,128)(2,1)S(1)}, u32[]{:S(2)}, u32[]{:S(2)}) %collective-permute-start.11) | collective-permute-done | bytes 786464 | tf_op jit(solution)/shard_map/ppermute | solution.py:23
  126.4 9.0 %contract.2 = (bf16[192,1024]{1,0:T(8,128)(2,1)}, bf16[192,1024]{1,0:T(8,128)(2,1)}, bf16[192,1024]{1,0:T(8,128)(2,1)}, bf16[192,1024]{1,0:T(8,128)(2,1)}) custom-call(s32[864]{0:T(1024)} %bitcast.69, s32[4]{0:T(128)} %pad_add_fusion.1.groups_ref, bf16[32,96,128]{2,1,0:T(8,128)(2,1)} %copy-done.6, bf16[32,96,128]{2,1,0:T(8,128)(2,1)} %copy-done.21, ...), custom_call_target="tpu_custom_call" | custom-call | flops 6442450944 | bytes 8388608 | tf_op jit(solution)/shard_map/contract/pallas_call | solution.py:327
  135.5 2.9 collective-permute-start.14
  139.8 4.6 %collective-permute-done.13 = bf16[192,1024]{1,0:T(8,128)(2,1)S(1)} collective-permute-done((bf16[192,1024]{1,0:T(8,128)(2,1)}, bf16[192,1024]{1,0:T(8,128)(2,1)S(1)}, u32[]{:S(2)}, u32[]{:S(2)}) %collective-permute-start.13) | collective-permute-done | bytes 393248 | tf_op jit(solution)/shard_map/ppermute | solution.py:23
  144.4 26.6 %collective-permute-done.14 = bf16[192,1024]{1,0:T(8,128)(2,1)S(1)} collective-permute-done((bf16[192,1024]{1,0:T(8,128)(2,1)}, bf16[192,1024]{1,0:T(8,128)(2,1)S(1)}, u32[]{:S(2)}, u32[]{:S(2)}) %collective-permute-start.14) | collective-permute-done | bytes 393248 | tf_op jit(solution)/shard_map/ppermute | solution.py:23
  173.1 7.0 %collective-permute-done.16 = bf16[192,1024]{1,0:T(8,128)(2,1)S(1)} collective-permute-done((bf16[192,1024]{1,0:T(8,128)(2,1)S(1)}, bf16[192,1024]{1,0:T(8,128)(2,1)S(1)}, u32[]{:S(2)}, u32[]{:S(2)}) %collective-permute-start.16) | collective-permute-done | bytes 393248 | tf_op jit(solution)/shard_map/ppermute | solution.py:23
  180.4 4.5 %collective-permute-start.18 = (bf16[192,1024]{1,0:T(8,128)(2,1)S(1)}, bf16[192,1024]{1,0:T(8,128)(2,1)S(1)}, u32[]{:S(2)}, u32[]{:S(2)}) collective-permute-start(bf16[192,1024]{1,0:T(8,128)(2,1)S(1)} %fusion.refs_0_), channel_id=1, source_target_pairs={{0,4},{2,6},{4,0},{6,2},{1,5},{3,7},{5,1},{7,3},{8,12},{10,14},{12... | collective-permute-start | bytes 1179656 | tf_op jit(solution)/shard_map/ppermute | solution.py:23
  189.5 28.7 %collective-permute-done.18.refs_2_ = bf16[192,1024]{1,0:T(8,128)(2,1)S(1)} collective-permute-done((bf16[192,1024]{1,0:T(8,128)(2,1)S(1)}, bf16[192,1024]{1,0:T(8,128)(2,1)S(1)}, u32[]{:S(2)}, u32[]{:S(2)}) %collective-permute-start.18) | collective-permute-done | bytes 393248 | tf_op jit(solution)/shard_map/ppermute | solution.py:23
  219.1 10.7 %gate.3 = (f32[96,16]{1,0:T(8,128)}, bf16[32,192,128]{2,1,0:T(8,128)(2,1)}, bf16[32,96,128]{2,1,0:T(8,128)(2,1)}, bf16[32,96,128]{2,1,0:T(8,128)(2,1)}) custom-call(s32[864]{0:T(1024)} %bitcast.64, s32[4]{0:T(128)} %pad_add_fusion.2.groups_ref, bf16[192,1024]{1,0:T(8,128)(2,1)} %copy-done.10, bf16[192,1024]{1,0:T(8,128)(2,1)} %copy-done.28, ...), custom_call_target="tpu_custom_call" | custom-call | flops 6442450944 | bytes 8388608 | tf_op jit(solution)/shard_map/gate/pallas_call | solution.py:194
  231.1 10.3 %up.3 = (bf16[32,96,128]{2,1,0:T(8,128)(2,1)}, bf16[32,96,128]{2,1,0:T(8,128)(2,1)}) custom-call(s32[864]{0:T(1024)} %bitcast.65, s32[4]{0:T(128)} %pad_add_fusion.2.groups_ref, bf16[32,192,128]{2,1,0:T(8,128)(2,1)} %get-tuple-element.43.x_ref, bf16[256,128,128]{2,1,0:T(8,128)(2,1)} %bitcast.75, bf16[256,128,128]{2,1,0:T(8,128)(2,1)} %collective-permute-done.8.other_hbm), custom_call_target="tpu_custom_call" | custom-call | flops 6442450944 | bytes 8388608 | tf_op jit(solution)/shard_map/up/pallas_call | solution.py:215
  241.7 5.4 %collective-permute-done.20.refs_1_ = bf16[32,96,128]{2,1,0:T(8,128)(2,1)S(1)} collective-permute-done((bf16[32,96,128]{2,1,0:T(8,128)(2,1)}, bf16[32,96,128]{2,1,0:T(8,128)(2,1)S(1)}, u32[]{:S(2)}, u32[]{:S(2)}) %collective-permute-start.20) | collective-permute-done | bytes 786464 | tf_op jit(solution)/shard_map/ppermute | solution.py:23
  247.1 16.9 %collective-permute-done.21.refs_3_ = bf16[32,96,128]{2,1,0:T(8,128)(2,1)S(1)} collective-permute-done((bf16[32,96,128]{2,1,0:T(8,128)(2,1)}, bf16[32,96,128]{2,1,0:T(8,128)(2,1)S(1)}, u32[]{:S(2)}, u32[]{:S(2)}) %collective-permute-start.21) | collective-permute-done | bytes 786464 | tf_op jit(solution)/shard_map/ppermute | solution.py:23
  265.1 2.8 activate.3
  269.9 14.2 %collective-permute-done.22.refs_1_ = bf16[32,96,128]{2,1,0:T(8,128)(2,1)S(1)} collective-permute-done((bf16[32,96,128]{2,1,0:T(8,128)(2,1)S(1)}, bf16[32,96,128]{2,1,0:T(8,128)(2,1)S(1)}, u32[]{:S(2)}, u32[]{:S(2)}) %collective-permute-start.22) | collective-permute-done | bytes 786464 | tf_op jit(solution)/shard_map/ppermute | solution.py:23
  285.0 9.6 %contract.3 = (bf16[192,1024]{1,0:T(8,128)(2,1)}, bf16[192,1024]{1,0:T(8,128)(2,1)}, bf16[192,1024]{1,0:T(8,128)(2,1)}, bf16[192,1024]{1,0:T(8,128)(2,1)}) custom-call(s32[864]{0:T(1024)} %bitcast.66, s32[4]{0:T(128)} %pad_add_fusion.2.groups_ref, bf16[32,96,128]{2,1,0:T(8,128)(2,1)} %copy-done.7, bf16[32,96,128]{2,1,0:T(8,128)(2,1)} %copy-done.22, ...), custom_call_target="tpu_custom_call" | custom-call | flops 6442450944 | bytes 8388608 | tf_op jit(solution)/shard_map/contract/pallas_call | solution.py:327
  294.7 1.7 collective-permute-start.24
  297.0 4.6 %collective-permute-done.23 = bf16[192,1024]{1,0:T(8,128)(2,1)S(1)} collective-permute-done((bf16[192,1024]{1,0:T(8,128)(2,1)}, bf16[192,1024]{1,0:T(8,128)(2,1)S(1)}, u32[]{:S(2)}, u32[]{:S(2)}) %collective-permute-start.23) | collective-permute-done | bytes 393248 | tf_op jit(solution)/shard_map/ppermute | solution.py:23
  301.5 27.0 %collective-permute-done.24 = bf16[192,1024]{1,0:T(8,128)(2,1)S(1)} collective-permute-done((bf16[192,1024]{1,0:T(8,128)(2,1)}, bf16[192,1024]{1,0:T(8,128)(2,1)S(1)}, u32[]{:S(2)}, u32[]{:S(2)}) %collective-permute-start.24) | collective-permute-done | bytes 393248 | tf_op jit(solution)/shard_map/ppermute | solution.py:23
  330.1 4.3 %collective-permute-done.26 = bf16[96,1024]{1,0:T(8,128)(2,1)S(1)} collective-permute-done((bf16[96,1024]{1,0:T(8,128)(2,1)S(1)}, bf16[96,1024]{1,0:T(8,128)(2,1)S(1)}, u32[]{:S(2)}, u32[]{:S(2)}) %collective-permute-start.26) | collective-permute-done | bytes 196640 | tf_op jit(solution)/shard_map/ppermute | solution.py:23
  334.6 4.5 %collective-permute-start.27 = (bf16[96,1024]{1,0:T(8,128)(2,1)S(1)}, bf16[96,1024]{1,0:T(8,128)(2,1)S(1)}, u32[]{:S(2)}, u32[]{:S(2)}) collective-permute-start(bf16[96,1024]{1,0:T(8,128)(2,1)S(1)} %broadcast_select_fusion.5), channel_id=1, source_target_pairs={{0,8},{8,0},{1,9},{9,1},{2,10},{10,2},{3,11},{11,3},{4,12},{12,4},... | collective-permute-start | bytes 589832 | tf_op jit(solution)/shard_map/ppermute | solution.py:23
  (157 shorter events, 35.8 us)
Async XLA Ops:
  0.0 56.3 %collective-permute-start.6 = (bf16[256,128,128]{2,1,0:T(8,128)(2,1)}, bf16[256,128,128]{2,1,0:T(8,128)(2,1)}, u32[]{:S(2)}, u32[]{:S(2)}) collective-permute-start(bf16[256,128,128]{2,1,0:T(8,128)(2,1)} %bitcast.70), channel_id=1, source_target_pairs={{0,8},{8,0},{1,9},{9,1},{2,10},{10,2},{3,11},{11,3},{4,12},{12,4},... | collective-permute-start | bytes 25165832 | tf_op jit(solution)/shard_map/ppermute | solution.py:23
  0.1 69.0 %collective-permute-start.8 = (bf16[256,128,128]{2,1,0:T(8,128)(2,1)}, bf16[256,128,128]{2,1,0:T(8,128)(2,1)}, u32[]{:S(2)}, u32[]{:S(2)}) collective-permute-start(bf16[256,128,128]{2,1,0:T(8,128)(2,1)} %bitcast.73), channel_id=1, source_target_pairs={{0,8},{8,0},{1,9},{9,1},{2,10},{10,2},{3,11},{11,3},{4,12},{12,4},... | collective-permute-start | bytes 25165832 | tf_op jit(solution)/shard_map/ppermute | solution.py:23
  0.6 108.1 %collective-permute-start.12 = (bf16[256,128,128]{2,1,0:T(8,128)(2,1)}, bf16[256,128,128]{2,1,0:T(8,128)(2,1)}, u32[]{:S(2)}, u32[]{:S(2)}) collective-permute-start(bf16[256,128,128]{2,1,0:T(8,128)(2,1)} %bitcast.76), channel_id=1, source_target_pairs={{0,8},{8,0},{1,9},{9,1},{2,10},{10,2},{3,11},{11,3},{4,12},{12,4},... | collective-permute-start | bytes 25165832 | tf_op jit(solution)/shard_map/ppermute | solution.py:23
  2.8 12.2 %collective-permute-start = (s32[867]{0:T(1024)S(1)}, s32[867]{0:T(1024)S(1)}, u32[]{:S(2)}, u32[]{:S(2)}) collective-permute-start(s32[867]{0:T(1024)S(1)} %pad_add_fusion), channel_id=1, source_target_pairs={{0,8},{8,0},{1,9},{9,1},{2,10},{10,2},{3,11},{11,3},{4,12},{12,4},... | collective-permute-start | bytes 10412 | tf_op jit(solution)/shard_map/ppermute | solution.py:23
  4.2 7.3 %collective-permute-start.1 = (bf16[96,1024]{1,0:T(8,128)(2,1)S(1)}, bf16[96,1024]{1,0:T(8,128)(2,1)S(1)}, u32[]{:S(2)}, u32[]{:S(2)}) collective-permute-start(bf16[96,1024]{1,0:T(8,128)(2,1)S(1)} %constant_dynamic-slice_fusion.1), channel_id=1, source_target_pairs={{0,1},{1,0},{2,3},{3,2},{4,5},{5,4},{6,7},{7,6},{8,9},{9,8},{10,11... | collective-permute-start | bytes 589832 | tf_op jit(solution)/shard_map/ppermute | solution.py:23
  11.5 44.9 %copy-start.12 = (bf16[192,1024]{1,0:T(8,128)(2,1)}, bf16[192,1024]{1,0:T(8,128)(2,1)S(1)}, u32[]{:S(2)}) copy-start(bf16[192,1024]{1,0:T(8,128)(2,1)S(1)} %pad_maximum_fusion.1.refs_0_) | copy-start | bytes 1179652
  11.5 17.9 %collective-permute-start.4 = (bf16[192,1024]{1,0:T(8,128)(2,1)S(1)}, bf16[192,1024]{1,0:T(8,128)(2,1)S(1)}, u32[]{:S(2)}, u32[]{:S(2)}) collective-permute-start(bf16[192,1024]{1,0:T(8,128)(2,1)S(1)} %pad_maximum_fusion.1.refs_0_), channel_id=1, source_target_pairs={{0,6},{2,0},{4,2},{6,4},{1,7},{3,1},{5,3},{7,5},{8,14},{10,8},{12,... | collective-permute-start | bytes 1179656 | tf_op jit(solution)/shard_map/ppermute | solution.py:23
  15.1 10.9 %collective-permute-start.5 = (bf16[25,4096]{1,0:T(8,128)(2,1)S(1)}, bf16[25,4096]{1,0:T(8,128)(2,1)S(1)}, u32[]{:S(2)}, u32[]{:S(2)}) collective-permute-start(bf16[25,4096]{1,0:T(8,128)(2,1)S(1)} %broadcast_select_fusion.1), channel_id=1, source_target_pairs={{0,8},{8,0},{1,9},{9,1},{2,10},{10,2},{3,11},{11,3},{4,12},{12,4},... | collective-permute-start | bytes 614408 | tf_op jit(solution)/shard_map/ppermute | solution.py:23
  16.7 39.7 %copy-start.19 = (s32[867]{0:T(1024)}, s32[867]{0:T(1024)S(1)}, u32[]{:S(2)}) copy-start(s32[867]{0:T(1024)S(1)} %get-tuple-element.75) | copy-start | bytes 10408
  16.7 169.6 %copy-start.18 = (s32[867]{0:T(1024)}, s32[867]{0:T(1024)S(1)}, u32[]{:S(2)}) copy-start(s32[867]{0:T(1024)S(1)} %get-tuple-element.74) | copy-start | bytes 10408
  26.0 29.5 %collective-permute-start.3 = (bf16[192,1024]{1,0:T(8,128)(2,1)S(1)}, bf16[192,1024]{1,0:T(8,128)(2,1)S(1)}, u32[]{:S(2)}, u32[]{:S(2)}) collective-permute-start(bf16[192,1024]{1,0:T(8,128)(2,1)S(1)} %pad_maximum_fusion.1.refs_0_), channel_id=1, source_target_pairs={{0,4},{2,6},{4,0},{6,2},{1,5},{3,7},{5,1},{7,3},{8,12},{10,14},{12... | collective-permute-start | bytes 1179656 | tf_op jit(solution)/shard_map/ppermute | solution.py:23
  29.4 26.9 %collective-permute-start.2 = (bf16[192,1024]{1,0:T(8,128)(2,1)S(1)}, bf16[192,1024]{1,0:T(8,128)(2,1)S(1)}, u32[]{:S(2)}, u32[]{:S(2)}) collective-permute-start(bf16[192,1024]{1,0:T(8,128)(2,1)S(1)} %pad_maximum_fusion.1.refs_0_), channel_id=1, source_target_pairs={{0,2},{2,4},{4,6},{6,0},{1,3},{3,5},{5,7},{7,1},{8,10},{10,12},{12... | collective-permute-start | bytes 1179656 | tf_op jit(solution)/shard_map/ppermute | solution.py:23
  55.5 24.9 %collective-permute-start.10 = (bf16[24,32,128]{2,0,1:T(8,128)(2,1)S(1)}, bf16[24,32,128]{2,0,1:T(8,128)(2,1)S(1)}, u32[]{:S(2)}, u32[]{:S(2)}) collective-permute-start(bf16[24,32,128]{2,0,1:T(8,128)(2,1)S(1)} %select_bitcast_fusion), channel_id=1, source_target_pairs={{0,8},{8,0},{1,9},{9,1},{2,10},{10,2},{3,11},{11,3},{4,12},{12,4},... | collective-permute-start | bytes 589832 | tf_op jit(solution)/shard_map/ppermute | solution.py:23
  68.4 19.3 %collective-permute-start.7 = (bf16[32,96,128]{2,1,0:T(8,128)(2,1)}, bf16[32,96,128]{2,1,0:T(8,128)(2,1)S(1)}, u32[]{:S(2)}, u32[]{:S(2)}) collective-permute-start(bf16[32,96,128]{2,1,0:T(8,128)(2,1)} %get-tuple-element.30), channel_id=1, source_target_pairs={{0,1},{1,0},{2,3},{3,2},{4,5},{5,4},{6,7},{7,6},{8,9},{9,8},{10,11... | collective-permute-start | bytes 2359304 | tf_op jit(solution)/shard_map/ppermute | solution.py:23
  79.4 25.1 %collective-permute-start.9 = (bf16[32,96,128]{2,1,0:T(8,128)(2,1)}, bf16[32,96,128]{2,1,0:T(8,128)(2,1)S(1)}, u32[]{:S(2)}, u32[]{:S(2)}) collective-permute-start(bf16[32,96,128]{2,1,0:T(8,128)(2,1)} %get-tuple-element.33), channel_id=1, source_target_pairs={{0,1},{1,0},{2,3},{3,2},{4,5},{5,4},{6,7},{7,6},{8,9},{9,8},{10,11... | collective-permute-start | bytes 2359304 | tf_op jit(solution)/shard_map/ppermute | solution.py:23
  107.4 18.1 %collective-permute-start.11 = (bf16[32,96,128]{2,1,0:T(8,128)(2,1)S(1)}, bf16[32,96,128]{2,1,0:T(8,128)(2,1)S(1)}, u32[]{:S(2)}, u32[]{:S(2)}) collective-permute-start(bf16[32,96,128]{2,1,0:T(8,128)(2,1)S(1)} %get-tuple-element.35.refs_0_), channel_id=1, source_target_pairs={{0,1},{1,0},{2,3},{3,2},{4,5},{5,4},{6,7},{7,6},{8,9},{9,8},{10,11... | collective-permute-start | bytes 2359304 | tf_op jit(solution)/shard_map/ppermute | solution.py:23
  135.4 9.0 %collective-permute-start.13 = (bf16[192,1024]{1,0:T(8,128)(2,1)}, bf16[192,1024]{1,0:T(8,128)(2,1)S(1)}, u32[]{:S(2)}, u32[]{:S(2)}) collective-permute-start(bf16[192,1024]{1,0:T(8,128)(2,1)} %get-tuple-element.38), channel_id=1, source_target_pairs={{0,6},{2,0},{4,2},{6,4},{1,7},{3,1},{5,3},{7,5},{8,14},{10,8},{12,... | collective-permute-start | bytes 1179656 | tf_op jit(solution)/shard_map/ppermute | solution.py:23
  135.5 35.5 %collective-permute-start.14 = (bf16[192,1024]{1,0:T(8,128)(2,1)}, bf16[192,1024]{1,0:T(8,128)(2,1)S(1)}, u32[]{:S(2)}, u32[]{:S(2)}) collective-permute-start(bf16[192,1024]{1,0:T(8,128)(2,1)} %get-tuple-element.39), channel_id=1, source_target_pairs={{0,4},{2,6},{4,0},{6,2},{1,5},{3,7},{5,1},{7,3},{8,12},{10,14},{12... | collective-permute-start | bytes 1179656 | tf_op jit(solution)/shard_map/ppermute | solution.py:23
  138.4 32.6 %collective-permute-start.15 = (bf16[192,1024]{1,0:T(8,128)(2,1)}, bf16[192,1024]{1,0:T(8,128)(2,1)S(1)}, u32[]{:S(2)}, u32[]{:S(2)}) collective-permute-start(bf16[192,1024]{1,0:T(8,128)(2,1)} %get-tuple-element.40), channel_id=1, source_target_pairs={{0,2},{2,4},{4,6},{6,0},{1,3},{3,5},{5,7},{7,1},{8,10},{10,12},{12... | collective-permute-start | bytes 1179656 | tf_op jit(solution)/shard_map/ppermute | solution.py:23
  172.4 7.8 %collective-permute-start.16 = (bf16[192,1024]{1,0:T(8,128)(2,1)S(1)}, bf16[192,1024]{1,0:T(8,128)(2,1)S(1)}, u32[]{:S(2)}, u32[]{:S(2)}) collective-permute-start(bf16[192,1024]{1,0:T(8,128)(2,1)S(1)} %pad_maximum_fusion.2), channel_id=1, source_target_pairs={{0,1},{1,0},{2,3},{3,2},{4,5},{5,4},{6,7},{7,6},{8,9},{9,8},{10,11... | collective-permute-start | bytes 1179656 | tf_op jit(solution)/shard_map/ppermute | solution.py:23
  180.3 9.1 %collective-permute-start.19 = (bf16[192,1024]{1,0:T(8,128)(2,1)S(1)}, bf16[192,1024]{1,0:T(8,128)(2,1)S(1)}, u32[]{:S(2)}, u32[]{:S(2)}) collective-permute-start(bf16[192,1024]{1,0:T(8,128)(2,1)S(1)} %fusion.refs_0_), channel_id=1, source_target_pairs={{0,6},{2,0},{4,2},{6,4},{1,7},{3,1},{5,3},{7,5},{8,14},{10,8},{12,... | collective-permute-start | bytes 1179656 | tf_op jit(solution)/shard_map/ppermute | solution.py:23
  180.4 37.8 %collective-permute-start.18 = (bf16[192,1024]{1,0:T(8,128)(2,1)S(1)}, bf16[192,1024]{1,0:T(8,128)(2,1)S(1)}, u32[]{:S(2)}, u32[]{:S(2)}) collective-permute-start(bf16[192,1024]{1,0:T(8,128)(2,1)S(1)} %fusion.refs_0_), channel_id=1, source_target_pairs={{0,4},{2,6},{4,0},{6,2},{1,5},{3,7},{5,1},{7,3},{8,12},{10,14},{12... | collective-permute-start | bytes 1179656 | tf_op jit(solution)/shard_map/ppermute | solution.py:23
  184.9 33.3 %collective-permute-start.17 = (bf16[192,1024]{1,0:T(8,128)(2,1)S(1)}, bf16[192,1024]{1,0:T(8,128)(2,1)S(1)}, u32[]{:S(2)}, u32[]{:S(2)}) collective-permute-start(bf16[192,1024]{1,0:T(8,128)(2,1)S(1)} %fusion.refs_0_), channel_id=1, source_target_pairs={{0,2},{2,4},{4,6},{6,0},{1,3},{3,5},{5,7},{7,1},{8,10},{10,12},{12... | collective-permute-start | bytes 1179656 | tf_op jit(solution)/shard_map/ppermute | solution.py:23
  229.8 17.3 %collective-permute-start.20 = (bf16[32,96,128]{2,1,0:T(8,128)(2,1)}, bf16[32,96,128]{2,1,0:T(8,128)(2,1)S(1)}, u32[]{:S(2)}, u32[]{:S(2)}) collective-permute-start(bf16[32,96,128]{2,1,0:T(8,128)(2,1)} %get-tuple-element.42), channel_id=1, source_target_pairs={{0,1},{1,0},{2,3},{3,2},{4,5},{5,4},{6,7},{7,6},{8,9},{9,8},{10,11... | collective-permute-start | bytes 2359304 | tf_op jit(solution)/shard_map/ppermute | solution.py:23
  241.4 22.6 %collective-permute-start.21 = (bf16[32,96,128]{2,1,0:T(8,128)(2,1)}, bf16[32,96,128]{2,1,0:T(8,128)(2,1)S(1)}, u32[]{:S(2)}, u32[]{:S(2)}) collective-permute-start(bf16[32,96,128]{2,1,0:T(8,128)(2,1)} %get-tuple-element.45), channel_id=1, source_target_pairs={{0,1},{1,0},{2,3},{3,2},{4,5},{5,4},{6,7},{7,6},{8,9},{9,8},{10,11... | collective-permute-start | bytes 2359304 | tf_op jit(solution)/shard_map/ppermute | solution.py:23
  267.9 16.2 %collective-permute-start.22 = (bf16[32,96,128]{2,1,0:T(8,128)(2,1)S(1)}, bf16[32,96,128]{2,1,0:T(8,128)(2,1)S(1)}, u32[]{:S(2)}, u32[]{:S(2)}) collective-permute-start(bf16[32,96,128]{2,1,0:T(8,128)(2,1)S(1)} %get-tuple-element.47.refs_0_), channel_id=1, source_target_pairs={{0,1},{1,0},{2,3},{3,2},{4,5},{5,4},{6,7},{7,6},{8,9},{9,8},{10,11... | collective-permute-start | bytes 2359304 | tf_op jit(solution)/shard_map/ppermute | solution.py:23
  294.6 39.8 %copy-start.11 = (bf16[192,1024]{1,0:T(8,128)(2,1)S(1)}, bf16[192,1024]{1,0:T(8,128)(2,1)}, u32[]{:S(2)}) copy-start(bf16[192,1024]{1,0:T(8,128)(2,1)} %copy-done.10) | copy-start | bytes 1179652
  294.6 6.9 %collective-permute-start.23 = (bf16[192,1024]{1,0:T(8,128)(2,1)}, bf16[192,1024]{1,0:T(8,128)(2,1)S(1)}, u32[]{:S(2)}, u32[]{:S(2)}) collective-permute-start(bf16[192,1024]{1,0:T(8,128)(2,1)} %get-tuple-element.50), channel_id=1, source_target_pairs={{0,6},{2,0},{4,2},{6,4},{1,7},{3,1},{5,3},{7,5},{8,14},{10,8},{12,... | collective-permute-start | bytes 1179656 | tf_op jit(solution)/shard_map/ppermute | solution.py:23
  294.7 33.9 %collective-permute-start.24 = (bf16[192,1024]{1,0:T(8,128)(2,1)}, bf16[192,1024]{1,0:T(8,128)(2,1)S(1)}, u32[]{:S(2)}, u32[]{:S(2)}) collective-permute-start(bf16[192,1024]{1,0:T(8,128)(2,1)} %get-tuple-element.51), channel_id=1, source_target_pairs={{0,4},{2,6},{4,0},{6,2},{1,5},{3,7},{5,1},{7,3},{8,12},{10,14},{12... | collective-permute-start | bytes 1179656 | tf_op jit(solution)/shard_map/ppermute | solution.py:23
  296.3 32.2 %collective-permute-start.25 = (bf16[192,1024]{1,0:T(8,128)(2,1)}, bf16[192,1024]{1,0:T(8,128)(2,1)S(1)}, u32[]{:S(2)}, u32[]{:S(2)}) collective-permute-start(bf16[192,1024]{1,0:T(8,128)(2,1)} %get-tuple-element.52), channel_id=1, source_target_pairs={{0,2},{2,4},{4,6},{6,0},{1,3},{3,5},{5,7},{7,1},{8,10},{10,12},{12... | collective-permute-start | bytes 1179656 | tf_op jit(solution)/shard_map/ppermute | solution.py:23
  329.8 4.6 %collective-permute-start.26 = (bf16[96,1024]{1,0:T(8,128)(2,1)S(1)}, bf16[96,1024]{1,0:T(8,128)(2,1)S(1)}, u32[]{:S(2)}, u32[]{:S(2)}) collective-permute-start(bf16[96,1024]{1,0:T(8,128)(2,1)S(1)} %slice.133), channel_id=1, source_target_pairs={{0,1},{1,0},{2,3},{3,2},{4,5},{5,4},{6,7},{7,6},{8,9},{9,8},{10,11... | collective-permute-start | bytes 589832 | tf_op jit(solution)/shard_map/ppermute | solution.py:23
  334.6 5.6 %collective-permute-start.27 = (bf16[96,1024]{1,0:T(8,128)(2,1)S(1)}, bf16[96,1024]{1,0:T(8,128)(2,1)S(1)}, u32[]{:S(2)}, u32[]{:S(2)}) collective-permute-start(bf16[96,1024]{1,0:T(8,128)(2,1)S(1)} %broadcast_select_fusion.5), channel_id=1, source_target_pairs={{0,8},{8,0},{1,9},{9,1},{2,10},{10,2},{3,11},{11,3},{4,12},{12,4},... | collective-permute-start | bytes 589832 | tf_op jit(solution)/shard_map/ppermute | solution.py:23
  (26 other events, 388.3 us)

commit v4 on v3

--- a/solution.py
+++ b/solution.py
@@ -11,7 +11,7 @@
 UNROLL = 16
 MIB = 1024 * 1024
 VMEM_LIMIT = 56 * MIB
-PIECES = 1
+PIECES = 2
 SLOW = 4
 
 perturb_scale = 0.5
@@ -40,7 +40,7 @@
     feature = cleared % block_rows
     per_owner = block_rows // owners
     feature = lax.rem(owner_index - feature // per_owner + owners, owners) * per_owner + feature % per_owner
-    is_down = jnp.arange(3)[:, None] == 2
+    is_down = jnp.arange(codes.shape[0])[:, None] % 3 == 2
     major = jnp.where(is_down, feature, column)
     minor = jnp.where(is_down, column, feature)
     major_count = max(block_rows, own_cols)
@@ -95,38 +95,17 @@
     return copies[0]
 
 
-def expand_into(words_ref, groups_ref, which, x_ref, tiles, total_ref, part_refs, copy):
-    length = words_ref.shape[0] // 3
-    rows = part_refs[0].shape[1]
-    total_ref[...] = jnp.zeros(total_ref.shape, jnp.float32)
-    copy.wait()
-
-    def read(block):
-        return x_ref[block]
-
-    def add(block, product):
-        total_ref[block] += product
-
-    multiply_tiles(words_ref, groups_ref, which, length, read, tiles, add)
-    for rep, part_ref in enumerate(part_refs):
-
-        def narrow(c, carry, rep=rep, part_ref=part_ref):
-            part_ref[c] = total_ref[c, pl.ds(rep * rows, rows), :].astype(jnp.bfloat16)
-            return carry
-
-        lax.fori_loop(0, total_ref.shape[0], narrow, 0, unroll=min(4, total_ref.shape[0]))
-
-
-def gate_kernel(owners, reps, words_ref, groups_ref, *refs):
+def expand_kernel(owners, reps, words_ref, groups_ref, *refs):
     blocks = refs[:owners]
-    gain_ref, left_ref, own_hbm, other_hbm, raw_ref, x_ref = refs[owners : owners + 6]
-    part_refs = refs[owners + 6 : owners + 6 + reps]
-    total_ref, tiles, sem = refs[owners + 6 + reps :]
+    gain_ref, left_ref, own_gate, other_gate, own_up, other_up, raw_ref = refs[owners : owners + 7]
+    part_refs = refs[owners + 7 : owners + 7 + reps]
+    total_ref, gate_tiles, gate_sem, up_tiles, up_sem, x_ref = refs[owners + 7 + reps :]
     all_rows, width = blocks[0].shape
     rows = all_rows // reps
     per_owner = width // BLOCK
     strip = 48 if all_rows % 48 == 0 else 16
-    copy = load_tiles(groups_ref[3], (own_hbm, other_hbm), tiles, sem)
+    gate_copy = load_tiles(groups_ref[3], (own_gate, other_gate), gate_tiles, gate_sem)
+    up_copy = load_tiles(groups_ref[3], (own_up, other_up), up_tiles, up_sem)
 
     def norm_rows(i, carry):
         at = pl.ds(pl.multiple_of(i * strip, strip), strip)
@@ -155,14 +134,24 @@
             preferred_element_type=jnp.float32,
         )
     raw_ref[...] = raw
-    expand_into(words_ref, groups_ref, 0, x_ref, tiles, total_ref, part_refs, copy)
-
-
-def up_kernel(reps, words_ref, groups_ref, x_ref, own_hbm, other_hbm, *refs):
-    part_refs = refs[:reps]
-    total_ref, tiles, sem = refs[reps:]
-    copy = load_tiles(groups_ref[3], (own_hbm, other_hbm), tiles, sem)
-    expand_into(words_ref, groups_ref, 1, x_ref, tiles, total_ref, part_refs, copy)
+
+    def read(block):
+        return x_ref[block]
+
+    def add(block, product):
+        total_ref[block] += product
+
+    for which, tiles, copy in ((0, gate_tiles, gate_copy), (1, up_tiles, up_copy)):
+        total_ref[...] = jnp.zeros(total_ref.shape, jnp.float32)
+        copy.wait()
+        multiply_tiles(words_ref, groups_ref, which, words_ref.shape[0] // 3, read, tiles, add)
+        for rep, part_ref in enumerate(part_refs):
+
+            def narrow(c, carry, which=which, rep=rep, part_ref=part_ref):
+                part_ref[which, c] = total_ref[c, pl.ds(rep * rows, rows), :].astype(jnp.bfloat16)
+                return carry
+
+            lax.fori_loop(0, total_ref.shape[0], narrow, 0, unroll=min(4, total_ref.shape[0]))
 
 
 SMEM = pl.BlockSpec(memory_space=pltpu.SMEM)
@@ -186,47 +175,31 @@
     ]
 
 
-def expand_gate(words, groups, blocks, gain, left, tiles, own_cols, reps):
+def expand(words, groups, blocks, gain, left, gate_tiles, up_tiles, own_cols, reps):
     owners = len(blocks)
     all_rows, width = blocks[0].shape
     rows = all_rows // reps
-    tile_count = tiles[0].shape[0]
+    tile_count = gate_tiles[0].shape[0]
+    scratch = tile_scratch(tile_count, own_cols, all_rows)
     out = pl.pallas_call(
-        functools.partial(gate_kernel, owners, reps),
-        out_shape=[
-            jax.ShapeDtypeStruct((rows, left.shape[0]), jnp.float32),
-            jax.ShapeDtypeStruct((owners * width // BLOCK, all_rows, BLOCK), jnp.bfloat16),
-        ]
-        + [jax.ShapeDtypeStruct((own_cols, rows, BLOCK), jnp.bfloat16)] * reps,
-        in_specs=[SMEM, SMEM] + [VMEM] * (owners + 2) + [HBM, HBM],
-        out_specs=[VMEM] * (2 + reps),
-        scratch_shapes=tile_scratch(tile_count, own_cols, all_rows),
+        functools.partial(expand_kernel, owners, reps),
+        out_shape=[jax.ShapeDtypeStruct((rows, left.shape[0]), jnp.float32)]
+        + [jax.ShapeDtypeStruct((2, own_cols, rows, BLOCK), jnp.bfloat16)] * reps,
+        in_specs=[SMEM, SMEM] + [VMEM] * (owners + 2) + [HBM] * 4,
+        out_specs=[VMEM] * (1 + reps),
+        scratch_shapes=scratch
+        + scratch[1:]
+        + [pltpu.VMEM((owners * width // BLOCK, all_rows, BLOCK), jnp.bfloat16)],
         compiler_params=pltpu.CompilerParams(vmem_limit_bytes=VMEM_LIMIT),
-        cost_estimate=tile_cost(tile_count, all_rows),
-        name="gate",
-    )(words, groups, *blocks, gain, left, *tiles)
-    return out[0], out[1], out[2:]
-
-
-def expand_up(words, groups, x, tiles, own_cols, reps):
-    all_rows = x.shape[1]
-    rows = all_rows // reps
-    tile_count = tiles[0].shape[0]
-    return pl.pallas_call(
-        functools.partial(up_kernel, reps),
-        out_shape=[jax.ShapeDtypeStruct((own_cols, rows, BLOCK), jnp.bfloat16)] * reps,
-        in_specs=[SMEM, SMEM, VMEM, HBM, HBM],
-        out_specs=[VMEM] * reps,
-        scratch_shapes=tile_scratch(tile_count, own_cols, all_rows),
-        compiler_params=pltpu.CompilerParams(vmem_limit_bytes=VMEM_LIMIT),
-        cost_estimate=tile_cost(tile_count, all_rows),
-        name="up",
-    )(words, groups, x, *tiles)
+        cost_estimate=tile_cost(2 * tile_count, all_rows),
+        name="expand",
+    )(words, groups, *blocks, gain, left, *gate_tiles, *up_tiles)
+    return out[0], out[1:]
 
 
 def activate_kernel(reps, *refs):
-    parts = (refs[:reps], refs[reps : 2 * reps])
-    raw_ref, picks_ref, wide_cols, down_cols, hidden_ref, coef_ref = refs[2 * reps :]
+    parts = refs[:reps]
+    raw_ref, picks_ref, wide_cols, down_cols, hidden_ref, coef_ref = refs[reps:]
     noise = picks_ref.shape[1]
     columns, rows = hidden_ref.shape[:2]
     picks = picks_ref[...]
@@ -240,8 +213,8 @@
             values = []
             for which in range(2):
                 value = low_rank[:, which * BLOCK : (which + 1) * BLOCK]
-                for part in parts[which]:
-                    value = value + part[c].astype(jnp.float32)
+                for part in parts:
+                    value = value + part[which, c].astype(jnp.float32)
                 values.append(value)
             gate, up = values
             hidden = (gate / (1.0 + jnp.exp(-gate)) * up).astype(jnp.bfloat16)
@@ -260,17 +233,17 @@
     coef_ref[...] = picks * down
 
 
-def activate(gates, ups, raw, picks, wide_cols, down_cols):
-    own_cols, rows = gates[0].shape[:2]
+def activate(parts, raw, picks, wide_cols, down_cols):
+    own_cols, rows = parts[0].shape[1:3]
     noise = picks.shape[1]
-    reps = len(gates)
+    reps = len(parts)
     return pl.pallas_call(
         functools.partial(activate_kernel, reps),
         out_shape=[
             jax.ShapeDtypeStruct((own_cols, rows, BLOCK), jnp.bfloat16),
             jax.ShapeDtypeStruct((rows, noise), jnp.float32),
         ],
-        in_specs=[VMEM] * (2 * reps + 4),
+        in_specs=[VMEM] * (reps + 4),
         out_specs=[VMEM] * 2,
         compiler_params=pltpu.CompilerParams(vmem_limit_bytes=16 * MIB),
         cost_estimate=pl.CostEstimate(
@@ -279,7 +252,7 @@
             transcendentals=own_cols * rows * BLOCK,
         ),
         name="activate",
-    )(*gates, *ups, raw, picks, wide_cols, down_cols)
+    )(*parts, raw, picks, wide_cols, down_cols)
 
 
 def contract_kernel(owners, reps, words_ref, groups_ref, *refs):
@@ -366,9 +339,16 @@
 
     codes = jnp.stack([gate_slot[0], up_slot[0], down_slot[0]])
     codes = lax.dynamic_slice_in_dim(codes, rep_index * tile_count, tile_count, axis=1)
-    words, groups = tile_plan(codes, block_rows, own_cols, owner_index, owners)
-    words = words.reshape(-1)
-
+    wide = jnp.concatenate([gate_left[0], up_left[0], down_right[0], norm_gain], axis=0)
+    other_codes, other_wide = hop(codes, "section", 1), hop(wide, "section", 1)
+    other_codes, other_wide, gate_tiles, up_tiles, down_tiles = lax.optimization_barrier(
+        (other_codes, other_wide, gate_tiles, up_tiles, down_tiles)
+    )
+    gate_pair = (gate_tiles[0], hop(gate_tiles[0], "section", 1))
+    up_pair = (up_tiles[0], hop(up_tiles[0], "section", 1))
+    down_pair = (down_tiles[0], hop(down_tiles[0], "section", 1))
+
+    plans = tile_plan(jnp.concatenate([codes, other_codes]), block_rows, own_cols, owner_index, owners)
     rotation = lax.rem(owner_index - jnp.arange(owners, dtype=jnp.int32) + owners, owners)
     noise = gate_left.shape[1]
 
@@ -381,35 +361,33 @@
     def owned(table):
         return jnp.take(table.reshape(table.shape[0], -1, BLOCK), columns, axis=1)
 
-    plan = jnp.concatenate([words, groups])
-    wide = rotated(jnp.concatenate([gate_left[0], up_left[0], down_right[0], norm_gain], axis=0))
     cols = owned(jnp.concatenate([gate_right[0], up_right[0], down_left[0]], axis=0))
-    mine = (plan, wide, cols)
-    theirs = tuple(hop(table, "section", 1) for table in mine)
-    gate_pair = (gate_tiles[0], hop(gate_tiles[0], "section", 1))
-    up_pair = (up_tiles[0], hop(up_tiles[0], "section", 1))
-    down_pair = (down_tiles[0], hop(down_tiles[0], "section", 1))
+    other_cols = hop(cols, "section", 1)
     picks = pick_matrix(row_member, member_seed, noise)
 
-    def layer(stream, picked, section):
+    def tables(section):
         own = section_index == section
-        plan, wide, cols = (jnp.where(own, a, b) for a, b in zip(mine, theirs))
-        words = plan[:-3]
-        groups = jnp.concatenate([plan[-3:], own.astype(jnp.int32)[None]])
-        left, right, gain = wide[: 2 * noise], wide[2 * noise : 3 * noise], wide[3 * noise :]
-        gate_cols, up_cols, down_cols = cols[:noise], cols[noise : 2 * noise], cols[2 * noise :]
+        words, groups = (jnp.where(own, table[:3], table[3:]) for table in plans)
+        groups = jnp.concatenate([groups, own.astype(jnp.int32)[None]])
+        chosen = rotated(jnp.where(own, wide, other_wide))
+        left, right, gain = chosen[: 2 * noise], chosen[2 * noise : 3 * noise], chosen[3 * noise :]
+        chosen = jnp.where(own, cols, other_cols)
+        gate_cols, up_cols, down_cols = chosen[:noise], chosen[noise : 2 * noise], chosen[2 * noise :]
         empty = jnp.zeros_like(gate_cols)
         wide_cols = jnp.concatenate(
             [jnp.concatenate([gate_cols, empty], axis=2), jnp.concatenate([empty, up_cols], axis=2)], axis=0
         ).transpose(1, 0, 2)
         down_cols = down_cols.reshape(noise, own_cols // 2, 2 * BLOCK).transpose(1, 0, 2)
-
+        return words.reshape(-1), groups, left, right, gain, wide_cols, down_cols
+
+    layers = [tables(section) for section in range(2)]
+
+    def layer(stream, picked, section):
+        words, groups, left, right, gain, wide_cols, down_cols = layers[section]
         blocks = [stream] + [hop(stream, "tensor", step) for step in range(1, owners)]
-        raw, x, gates = expand_gate(words, groups, blocks, gain, left, gate_pair, own_cols, reps)
-        gates = [gates[0]] + [hop(gates[g], "rep", -g) for g in range(1, reps)]
-        ups = expand_up(words, groups, x, up_pair, own_cols, reps)
-        ups = [ups[0]] + [hop(ups[g], "rep", -g) for g in range(1, reps)]
-        hidden, coef = activate(gates, ups, raw, picked, wide_cols, down_cols)
+        raw, parts = expand(words, groups, blocks, gain, left, gate_pair, up_pair, own_cols, reps)
+        parts = [parts[0]] + [hop(parts[g], "rep", -g) for g in range(1, reps)]
+        hidden, coef = activate(parts, raw, picked, wide_cols, down_cols)
         hiddens = [hidden] + [hop(hidden, "rep", g) for g in range(1, reps)]
         outs = contract(words, groups, hiddens, coef, right, down_pair, owners)
         summed = outs[0].astype(jnp.float32)

time: 345 us -> 279 us (0.81)
  waiting for transfers between devices: 216 us -> 87.7 us
  Pallas kernels: 66.7 us -> 97.6 us
  starting transfers between devices: 37.4 us -> 65.1 us
  local copies, waits for them, and re-layouts: 11.5 us -> 15.5 us
    ppermute x28 -> x44, waiting for transfers between devices: 216 us -> 87.7 us  [hop(): lax.ppermute(value, axis, [(i, (i + steps) % count) for i in range(count)])]
    ppermute x28 -> x44, starting transfers between devices: 37.4 us -> 65.1 us  [hop(): lax.ppermute(value, axis, [(i, (i + steps) % count) for i in range(count)])]
    pallas_call x2 -> x4, Pallas kernels: 18.6 us -> 36.1 us  [contract(): pl.pallas_call(functools.partial(contract_kernel, owners, reps), out_shap...]
    pallas_call x4, Pallas kernels: 42.4 us -> 51.8 us  [expand(): pl.pallas_call(functools.partial(expand_kernel, owners, reps), out_shape=...]
    pallas_call x2 -> x4, Pallas kernels: 5.68 us -> 9.69 us  [activate(): pl.pallas_call(functools.partial(activate_kernel, reps), out_shape=[jax.S...]
    unnamed x64 -> x93, local copies, waits for them, and re-layouts: 4.89 us -> 6.95 us
  transfers between devices with their start and end apart: 28 -> 44, of which waited for: 18 -> 18; matrix products, arithmetic and copies ran while one was open for 4% -> 7% of each run, Pallas kernels for 10% -> 35%
where the time goes in v4:
time: 279 us; the launch traced here: 278 us
  Pallas kernels  97.6 us (35%)
  waiting for transfers between devices  87.7 us (31%)
  starting transfers between devices  65.1 us (23%)
  local copies, waits for them, and re-layouts  15.5 us (6%)
  other arithmetic  11.6 us (4%)
    ppermute x44, waiting for transfers between devices, hop(): lax.ppermute(value, axis, [(i, (i + steps) % count) for i in range(count)])  87.7 us
    ppermute x44, starting transfers between devices, hop(): lax.ppermute(value, axis, [(i, (i + steps) % count) for i in range(count)])  65.1 us
    pallas_call x4, Pallas kernels, expand(): pl.pallas_call(functools.partial(expand_kernel, owners, reps), out_shape=...  51.8 us
    pallas_call x4, Pallas kernels, contract(): pl.pallas_call(functools.partial(contract_kernel, owners, reps), out_shap...  36.1 us
    pallas_call x4, Pallas kernels, activate(): pl.pallas_call(functools.partial(activate_kernel, reps), out_shape=[jax.S...  9.69 us
    unnamed x93, local copies, waits for them, and re-layouts  6.95 us
  transfers between devices with their start and end apart: 44, of which 18 were waited for; matrix products, arithmetic and copies ran while one was open for 7% of the time, Pallas kernels for 35%

profile of v4, /device:TPU:1, one launch (start us, length us, event | category | flops | bytes accessed | tf_op | source)
XLA Modules:
  0.0 278.4 jit_solution(1803183286641907318)
XLA Ops:
  4.7 2.6 collective-permute-start.2
  24.0 5.7 %collective-permute-done.4.refs_2_ = bf16[96,1024]{1,0:T(8,128)(2,1)S(1)} collective-permute-done((bf16[96,1024]{1,0:T(8,128)(2,1)S(1)}, bf16[96,1024]{1,0:T(8,128)(2,1)S(1)}, u32[]{:S(2)}, u32[]{:S(2)}) %collective-permute-start.4) | collective-permute-done | bytes 196640 | tf_op jit(solution)/shard_map/ppermute | solution.py:23
  30.2 2.7 collective-permute-start.16
  32.9 3.6 %collective-permute-start.17 = (bf16[96,1024]{1,0:T(8,128)(2,1)S(1)}, bf16[96,1024]{1,0:T(8,128)(2,1)S(1)}, u32[]{:S(2)}, u32[]{:S(2)}) collective-permute-start(bf16[96,1024]{1,0:T(8,128)(2,1)S(1)} %pad_maximum_fusion.4.refs_0_), channel_id=1, source_target_pairs={{0,4},{2,6},{4,0},{6,2},{1,5},{3,7},{5,1},{7,3},{8,12},{10,14},{12... | collective-permute-start | bytes 589832 | tf_op jit(solution)/shard_map/ppermute | solution.py:23
  37.1 13.1 %expand.4 = (f32[48,16]{1,0:T(8,128)}, bf16[2,32,48,128]{3,2,1,0:T(8,128)(2,1)}, bf16[2,32,48,128]{3,2,1,0:T(8,128)(2,1)}) custom-call(s32[864]{0:T(1024)} %reshape.556.words_ref, s32[4]{0:T(128)} %pad_add_fusion.1.groups_ref, bf16[96,1024]{1,0:T(8,128)(2,1)} %copy-done.21, bf16[96,1024]{1,0:T(8,128)(2,1)} %copy-done.29, bf16[96,1024]{1,0:T(8,128)(2,1)} %copy-done.30, ...), custom_call_target="tpu_custom_call" | custom-call | flops 6442450944 | bytes 16777216 | tf_op jit(solution)/shard_map/expand/pallas_call | solution.py:184
  52.9 13.1 %expand.5 = (f32[48,16]{1,0:T(8,128)}, bf16[2,32,48,128]{3,2,1,0:T(8,128)(2,1)}, bf16[2,32,48,128]{3,2,1,0:T(8,128)(2,1)}) custom-call(s32[864]{0:T(1024)} %reshape.556.words_ref, s32[4]{0:T(128)} %pad_add_fusion.1.groups_ref, bf16[96,1024]{1,0:T(8,128)(2,1)} %copy-done.20, bf16[96,1024]{1,0:T(8,128)(2,1)} %copy-done.35, bf16[96,1024]{1,0:T(8,128)(2,1)} %copy-done.38, ...), custom_call_target="tpu_custom_call" | custom-call | flops 6442450944 | bytes 16777216 | tf_op jit(solution)/shard_map/expand/pallas_call | solution.py:184
  67.2 2.4 activate.4
  73.4 10.1 %collective-permute-done.19.refs_1_ = bf16[2,32,48,128]{3,2,1,0:T(8,128)(2,1)S(1)} collective-permute-done((bf16[2,32,48,128]{3,2,1,0:T(8,128)(2,1)}, bf16[2,32,48,128]{3,2,1,0:T(8,128)(2,1)S(1)}, u32[]{:S(2)}, u32[]{:S(2)}) %collective-permute-start.19) | collective-permute-done | bytes 786464 | tf_op jit(solution)/shard_map/ppermute | solution.py:23
  83.5 2.4 activate.5
  88.8 3.2 %collective-permute-done.10.refs_1_ = bf16[32,48,128]{2,1,0:T(8,128)(2,1)} collective-permute-done((bf16[32,48,128]{2,1,0:T(8,128)(2,1)S(1)}, bf16[32,48,128]{2,1,0:T(8,128)(2,1)}, u32[]{:S(2)}, u32[]{:S(2)}) %collective-permute-start.10) | collective-permute-done | bytes 393248 | tf_op jit(solution)/shard_map/ppermute | solution.py:23
  92.0 9.0 %contract.4 = (bf16[96,1024]{1,0:T(8,128)(2,1)}, bf16[96,1024]{1,0:T(8,128)(2,1)}, bf16[96,1024]{1,0:T(8,128)(2,1)}, bf16[96,1024]{1,0:T(8,128)(2,1)}) custom-call(s32[864]{0:T(1024)} %reshape.556.words_ref, s32[4]{0:T(128)} %pad_add_fusion.1.groups_ref, bf16[32,48,128]{2,1,0:T(8,128)(2,1)} %copy-done.4, ...), custom_call_target="tpu_custom_call" | custom-call | flops 3221225472 | bytes 8388608 | tf_op jit(solution)/shard_map/contract/pallas_call | solution.py:300
  102.2 2.6 collective-permute-start.13
  105.6 9.1 %contract.5 = (bf16[96,1024]{1,0:T(8,128)(2,1)}, bf16[96,1024]{1,0:T(8,128)(2,1)}, bf16[96,1024]{1,0:T(8,128)(2,1)}, bf16[96,1024]{1,0:T(8,128)(2,1)}) custom-call(s32[864]{0:T(1024)} %reshape.556.words_ref, s32[4]{0:T(128)} %pad_add_fusion.1.groups_ref, bf16[32,48,128]{2,1,0:T(8,128)(2,1)} %copy-done.5, bf16[32,48,128]{2,1,0:T(8,128)(2,1)} %copy-done.23, ...), custom_call_target="tpu_custom_call" | custom-call | flops 3221225472 | bytes 8388608 | tf_op jit(solution)/shard_map/contract/pallas_call | solution.py:300
  114.6 2.9 %collective-permute-start.21 = (bf16[96,1024]{1,0:T(8,128)(2,1)}, bf16[96,1024]{1,0:T(8,128)(2,1)S(1)}, u32[]{:S(2)}, u32[]{:S(2)}) collective-permute-start(bf16[96,1024]{1,0:T(8,128)(2,1)} %get-tuple-element.67), channel_id=1, source_target_pairs={{0,6},{2,0},{4,2},{6,4},{1,7},{3,1},{5,3},{7,5},{8,14},{10,8},{12,... | collective-permute-start | bytes 589832 | tf_op jit(solution)/shard_map/ppermute | solution.py:23
  117.9 8.3 %collective-permute-done.13 = bf16[96,1024]{1,0:T(8,128)(2,1)S(1)} collective-permute-done((bf16[96,1024]{1,0:T(8,128)(2,1)}, bf16[96,1024]{1,0:T(8,128)(2,1)S(1)}, u32[]{:S(2)}, u32[]{:S(2)}) %collective-permute-start.13) | collective-permute-done | bytes 196640 | tf_op jit(solution)/shard_map/ppermute | solution.py:23
  126.9 12.0 %collective-permute-done.22 = bf16[96,1024]{1,0:T(8,128)(2,1)S(1)} collective-permute-done((bf16[96,1024]{1,0:T(8,128)(2,1)}, bf16[96,1024]{1,0:T(8,128)(2,1)S(1)}, u32[]{:S(2)}, u32[]{:S(2)}) %collective-permute-start.22) | collective-permute-done | bytes 196640 | tf_op jit(solution)/shard_map/ppermute | solution.py:23
  139.9 3.0 %collective-permute-start.27 = (bf16[96,1024]{1,0:T(8,128)(2,1)S(1)}, bf16[96,1024]{1,0:T(8,128)(2,1)S(1)}, u32[]{:S(2)}, u32[]{:S(2)}) collective-permute-start(bf16[96,1024]{1,0:T(8,128)(2,1)S(1)} %fusion.4.refs_0_), channel_id=1, source_target_pairs={{0,6},{2,0},{4,2},{6,4},{1,7},{3,1},{5,3},{7,5},{8,14},{10,8},{12,... | collective-permute-start | bytes 589832 | tf_op jit(solution)/shard_map/ppermute | solution.py:23
  147.4 8.5 %collective-permute-done.26.refs_2_ = bf16[96,1024]{1,0:T(8,128)(2,1)S(1)} collective-permute-done((bf16[96,1024]{1,0:T(8,128)(2,1)S(1)}, bf16[96,1024]{1,0:T(8,128)(2,1)S(1)}, u32[]{:S(2)}, u32[]{:S(2)}) %collective-permute-start.26) | collective-permute-done | bytes 196640 | tf_op jit(solution)/shard_map/ppermute | solution.py:23
  156.7 12.9 %expand.6 = (f32[48,16]{1,0:T(8,128)}, bf16[2,32,48,128]{3,2,1,0:T(8,128)(2,1)}, bf16[2,32,48,128]{3,2,1,0:T(8,128)(2,1)}) custom-call(s32[864]{0:T(1024)} %reshape.559.words_ref, s32[4]{0:T(128)} %pad_add_fusion.2.groups_ref, bf16[96,1024]{1,0:T(8,128)(2,1)} %copy-done.16, bf16[96,1024]{1,0:T(8,128)(2,1)} %copy-done.32, bf16[96,1024]{1,0:T(8,128)(2,1)} %copy-done.34, ...), custom_call_target="tpu_custom_call" | custom-call | flops 6442450944 | bytes 16777216 | tf_op jit(solution)/shard_map/expand/pallas_call | solution.py:184
  173.3 12.7 %expand.7 = (f32[48,16]{1,0:T(8,128)}, bf16[2,32,48,128]{3,2,1,0:T(8,128)(2,1)}, bf16[2,32,48,128]{3,2,1,0:T(8,128)(2,1)}) custom-call(s32[864]{0:T(1024)} %reshape.559.words_ref, s32[4]{0:T(128)} %pad_add_fusion.2.groups_ref, bf16[96,1024]{1,0:T(8,128)(2,1)} %copy-done.18, bf16[96,1024]{1,0:T(8,128)(2,1)} %copy-done.33, bf16[96,1024]{1,0:T(8,128)(2,1)} %copy-done.36, ...), custom_call_target="tpu_custom_call" | custom-call | flops 6442450944 | bytes 16777216 | tf_op jit(solution)/shard_map/expand/pallas_call | solution.py:184
  187.2 2.4 activate.6
  190.2 9.1 %collective-permute-done.37.refs_1_ = bf16[2,32,48,128]{3,2,1,0:T(8,128)(2,1)S(1)} collective-permute-done((bf16[2,32,48,128]{3,2,1,0:T(8,128)(2,1)}, bf16[2,32,48,128]{3,2,1,0:T(8,128)(2,1)S(1)}, u32[]{:S(2)}, u32[]{:S(2)}) %collective-permute-start.37) | collective-permute-done | bytes 786464 | tf_op jit(solution)/shard_map/ppermute | solution.py:23
  199.3 2.4 activate.7
  203.9 3.8 %collective-permute-done.29.refs_1_ = bf16[32,48,128]{2,1,0:T(8,128)(2,1)S(1)} collective-permute-done((bf16[32,48,128]{2,1,0:T(8,128)(2,1)S(1)}, bf16[32,48,128]{2,1,0:T(8,128)(2,1)S(1)}, u32[]{:S(2)}, u32[]{:S(2)}) %collective-permute-start.29) | collective-permute-done | bytes 393248 | tf_op jit(solution)/shard_map/ppermute | solution.py:23
  208.5 9.0 %contract.6 = (bf16[96,1024]{1,0:T(8,128)(2,1)}, bf16[96,1024]{1,0:T(8,128)(2,1)}, bf16[96,1024]{1,0:T(8,128)(2,1)}, bf16[96,1024]{1,0:T(8,128)(2,1)}) custom-call(s32[864]{0:T(1024)} %reshape.559.words_ref, s32[4]{0:T(128)} %pad_add_fusion.2.groups_ref, bf16[32,48,128]{2,1,0:T(8,128)(2,1)} %copy-done.7, bf16[32,48,128]{2,1,0:T(8,128)(2,1)} %copy-done.25, ...), custom_call_target="tpu_custom_call" | custom-call | flops 3221225472 | bytes 8388608 | tf_op jit(solution)/shard_map/contract/pallas_call | solution.py:300
  217.5 8.4 %collective-permute-start.30 = (bf16[96,1024]{1,0:T(8,128)(2,1)}, bf16[96,1024]{1,0:T(8,128)(2,1)S(1)}, u32[]{:S(2)}, u32[]{:S(2)}) collective-permute-start(bf16[96,1024]{1,0:T(8,128)(2,1)} %get-tuple-element.76), channel_id=1, source_target_pairs={{0,6},{2,0},{4,2},{6,4},{1,7},{3,1},{5,3},{7,5},{8,14},{10,8},{12,... | collective-permute-start | bytes 589832 | tf_op jit(solution)/shard_map/ppermute | solution.py:23
  225.9 9.1 %collective-permute-start.31 = (bf16[96,1024]{1,0:T(8,128)(2,1)}, bf16[96,1024]{1,0:T(8,128)(2,1)S(1)}, u32[]{:S(2)}, u32[]{:S(2)}) collective-permute-start(bf16[96,1024]{1,0:T(8,128)(2,1)} %get-tuple-element.77), channel_id=1, source_target_pairs={{0,4},{2,6},{4,0},{6,2},{1,5},{3,7},{5,1},{7,3},{8,12},{10,14},{12... | collective-permute-start | bytes 589832 | tf_op jit(solution)/shard_map/ppermute | solution.py:23
  235.7 9.1 %contract.7 = (bf16[96,1024]{1,0:T(8,128)(2,1)}, bf16[96,1024]{1,0:T(8,128)(2,1)}, bf16[96,1024]{1,0:T(8,128)(2,1)}, bf16[96,1024]{1,0:T(8,128)(2,1)}) custom-call(s32[864]{0:T(1024)} %reshape.559.words_ref, s32[4]{0:T(128)} %pad_add_fusion.2.groups_ref, bf16[32,48,128]{2,1,0:T(8,128)(2,1)} %copy-done.6, bf16[32,48,128]{2,1,0:T(8,128)(2,1)} %copy-done.24, ...), custom_call_target="tpu_custom_call" | custom-call | flops 3221225472 | bytes 8388608 | tf_op jit(solution)/shard_map/contract/pallas_call | solution.py:300
  244.8 2.5 collective-permute-start.39
  247.7 7.2 %collective-permute-done.31 = bf16[96,1024]{1,0:T(8,128)(2,1)S(1)} collective-permute-done((bf16[96,1024]{1,0:T(8,128)(2,1)}, bf16[96,1024]{1,0:T(8,128)(2,1)S(1)}, u32[]{:S(2)}, u32[]{:S(2)}) %collective-permute-start.31) | collective-permute-done | bytes 196640 | tf_op jit(solution)/shard_map/ppermute | solution.py:23
  257.1 11.1 %collective-permute-done.40 = bf16[96,1024]{1,0:T(8,128)(2,1)S(1)} collective-permute-done((bf16[96,1024]{1,0:T(8,128)(2,1)}, bf16[96,1024]{1,0:T(8,128)(2,1)S(1)}, u32[]{:S(2)}, u32[]{:S(2)}) %collective-permute-start.40) | collective-permute-done | bytes 196640 | tf_op jit(solution)/shard_map/ppermute | solution.py:23
  273.4 3.0 %collective-permute-start.43 = (bf16[96,1024]{1,0:T(8,128)(2,1)S(1)}, bf16[96,1024]{1,0:T(8,128)(2,1)S(1)}, u32[]{:S(2)}, u32[]{:S(2)}) collective-permute-start(bf16[96,1024]{1,0:T(8,128)(2,1)S(1)} %get-tuple-element.96), channel_id=1, source_target_pairs={{0,8},{8,0},{1,9},{9,1},{2,10},{10,2},{3,11},{11,3},{4,12},{12,4},... | collective-permute-start | bytes 589832 | tf_op jit(solution)/shard_map/ppermute | solution.py:23
  (241 shorter events, 60.4 us)
Async XLA Ops:
  3.2 29.7 %collective-permute-start.6 = (bf16[256,128,128]{2,1,0:T(8,128)(2,1)}, bf16[256,128,128]{2,1,0:T(8,128)(2,1)}, u32[]{:S(2)}, u32[]{:S(2)}) collective-permute-start(bf16[256,128,128]{2,1,0:T(8,128)(2,1)} %bitcast.52), channel_id=1, source_target_pairs={{0,8},{8,0},{1,9},{9,1},{2,10},{10,2},{3,11},{11,3},{4,12},{12,4},... | collective-permute-start | bytes 25165832 | tf_op jit(solution)/shard_map/ppermute | solution.py:23
  3.6 32.9 %collective-permute-start.7 = (bf16[256,128,128]{2,1,0:T(8,128)(2,1)}, bf16[256,128,128]{2,1,0:T(8,128)(2,1)}, u32[]{:S(2)}, u32[]{:S(2)}) collective-permute-start(bf16[256,128,128]{2,1,0:T(8,128)(2,1)} %bitcast.57), channel_id=1, source_target_pairs={{0,8},{8,0},{1,9},{9,1},{2,10},{10,2},{3,11},{11,3},{4,12},{12,4},... | collective-permute-start | bytes 25165832 | tf_op jit(solution)/shard_map/ppermute | solution.py:23
  8.1 80.7 %collective-permute-start.11 = (bf16[256,128,128]{2,1,0:T(8,128)(2,1)}, bf16[256,128,128]{2,1,0:T(8,128)(2,1)}, u32[]{:S(2)}, u32[]{:S(2)}) collective-permute-start(bf16[256,128,128]{2,1,0:T(8,128)(2,1)} %bitcast.62), channel_id=1, source_target_pairs={{0,8},{8,0},{1,9},{9,1},{2,10},{10,2},{3,11},{11,3},{4,12},{12,4},... | collective-permute-start | bytes 25165832 | tf_op jit(solution)/shard_map/ppermute | solution.py:23
  13.8 15.8 %collective-permute-start.4 = (bf16[96,1024]{1,0:T(8,128)(2,1)S(1)}, bf16[96,1024]{1,0:T(8,128)(2,1)S(1)}, u32[]{:S(2)}, u32[]{:S(2)}) collective-permute-start(bf16[96,1024]{1,0:T(8,128)(2,1)S(1)} %pad_maximum_fusion.2.refs_0_), channel_id=1, source_target_pairs={{0,4},{2,6},{4,0},{6,2},{1,5},{3,7},{5,1},{7,3},{8,12},{10,14},{12... | collective-permute-start | bytes 589832 | tf_op jit(solution)/shard_map/ppermute | solution.py:23
  29.6 36.7 %collective-permute-start.9 = (bf16[24,32,128]{2,0,1:T(8,128)(2,1)S(1)}, bf16[24,32,128]{2,0,1:T(8,128)(2,1)S(1)}, u32[]{:S(2)}, u32[]{:S(2)}) collective-permute-start(bf16[24,32,128]{2,0,1:T(8,128)(2,1)S(1)} %select_bitcast_fusion.2), channel_id=1, source_target_pairs={{0,8},{8,0},{1,9},{9,1},{2,10},{10,2},{3,11},{11,3},{4,12},{12,4},... | collective-permute-start | bytes 589832 | tf_op jit(solution)/shard_map/ppermute | solution.py:23
  30.2 20.1 %collective-permute-start.16 = (bf16[96,1024]{1,0:T(8,128)(2,1)S(1)}, bf16[96,1024]{1,0:T(8,128)(2,1)S(1)}, u32[]{:S(2)}, u32[]{:S(2)}) collective-permute-start(bf16[96,1024]{1,0:T(8,128)(2,1)S(1)} %pad_maximum_fusion.4.refs_0_), channel_id=1, source_target_pairs={{0,2},{2,4},{4,6},{6,0},{1,3},{3,5},{5,7},{7,1},{8,10},{10,12},{12... | collective-permute-start | bytes 589832 | tf_op jit(solution)/shard_map/ppermute | solution.py:23
  32.9 18.7 %collective-permute-start.17 = (bf16[96,1024]{1,0:T(8,128)(2,1)S(1)}, bf16[96,1024]{1,0:T(8,128)(2,1)S(1)}, u32[]{:S(2)}, u32[]{:S(2)}) collective-permute-start(bf16[96,1024]{1,0:T(8,128)(2,1)S(1)} %pad_maximum_fusion.4.refs_0_), channel_id=1, source_target_pairs={{0,4},{2,6},{4,0},{6,2},{1,5},{3,7},{5,1},{7,3},{8,12},{10,14},{12... | collective-permute-start | bytes 589832 | tf_op jit(solution)/shard_map/ppermute | solution.py:23
  36.5 15.1 %collective-permute-start.18 = (bf16[96,1024]{1,0:T(8,128)(2,1)S(1)}, bf16[96,1024]{1,0:T(8,128)(2,1)S(1)}, u32[]{:S(2)}, u32[]{:S(2)}) collective-permute-start(bf16[96,1024]{1,0:T(8,128)(2,1)S(1)} %pad_maximum_fusion.4.refs_0_), channel_id=1, source_target_pairs={{0,6},{2,0},{4,2},{6,4},{1,7},{3,1},{5,3},{7,5},{8,14},{10,8},{12,... | collective-permute-start | bytes 589832 | tf_op jit(solution)/shard_map/ppermute | solution.py:23
  50.3 16.3 %collective-permute-start.8 = (bf16[2,32,48,128]{3,2,1,0:T(8,128)(2,1)}, bf16[2,32,48,128]{3,2,1,0:T(8,128)(2,1)S(1)}, u32[]{:S(2)}, u32[]{:S(2)}) collective-permute-start(bf16[2,32,48,128]{3,2,1,0:T(8,128)(2,1)} %get-tuple-element.52), channel_id=1, source_target_pairs={{0,1},{1,0},{2,3},{3,2},{4,5},{5,4},{6,7},{7,6},{8,9},{9,8},{10,11... | collective-permute-start | bytes 2359304 | tf_op jit(solution)/shard_map/ppermute | solution.py:23
  66.0 17.5 %collective-permute-start.19 = (bf16[2,32,48,128]{3,2,1,0:T(8,128)(2,1)}, bf16[2,32,48,128]{3,2,1,0:T(8,128)(2,1)S(1)}, u32[]{:S(2)}, u32[]{:S(2)}) collective-permute-start(bf16[2,32,48,128]{3,2,1,0:T(8,128)(2,1)} %get-tuple-element.62), channel_id=1, source_target_pairs={{0,1},{1,0},{2,3},{3,2},{4,5},{5,4},{6,7},{7,6},{8,9},{9,8},{10,11... | collective-permute-start | bytes 2359304 | tf_op jit(solution)/shard_map/ppermute | solution.py:23
  70.2 21.8 %collective-permute-start.10 = (bf16[32,48,128]{2,1,0:T(8,128)(2,1)S(1)}, bf16[32,48,128]{2,1,0:T(8,128)(2,1)}, u32[]{:S(2)}, u32[]{:S(2)}) collective-permute-start(bf16[32,48,128]{2,1,0:T(8,128)(2,1)S(1)} %get-tuple-element.54.refs_0_), channel_id=1, source_target_pairs={{0,1},{1,0},{2,3},{3,2},{4,5},{5,4},{6,7},{7,6},{8,9},{9,8},{10,11... | collective-permute-start | bytes 1179656 | tf_op jit(solution)/shard_map/ppermute | solution.py:23
  86.0 18.8 %collective-permute-start.20 = (bf16[32,48,128]{2,1,0:T(8,128)(2,1)S(1)}, bf16[32,48,128]{2,1,0:T(8,128)(2,1)S(1)}, u32[]{:S(2)}, u32[]{:S(2)}) collective-permute-start(bf16[32,48,128]{2,1,0:T(8,128)(2,1)S(1)} %get-tuple-element.64.refs_0_), channel_id=1, source_target_pairs={{0,1},{1,0},{2,3},{3,2},{4,5},{5,4},{6,7},{7,6},{8,9},{9,8},{10,11... | collective-permute-start | bytes 1179656 | tf_op jit(solution)/shard_map/ppermute | solution.py:23
  101.1 16.5 %collective-permute-start.12 = (bf16[96,1024]{1,0:T(8,128)(2,1)}, bf16[96,1024]{1,0:T(8,128)(2,1)S(1)}, u32[]{:S(2)}, u32[]{:S(2)}) collective-permute-start(bf16[96,1024]{1,0:T(8,128)(2,1)} %get-tuple-element.58), channel_id=1, source_target_pairs={{0,6},{2,0},{4,2},{6,4},{1,7},{3,1},{5,3},{7,5},{8,14},{10,8},{12,... | collective-permute-start | bytes 589832 | tf_op jit(solution)/shard_map/ppermute | solution.py:23
  102.2 24.0 %collective-permute-start.13 = (bf16[96,1024]{1,0:T(8,128)(2,1)}, bf16[96,1024]{1,0:T(8,128)(2,1)S(1)}, u32[]{:S(2)}, u32[]{:S(2)}) collective-permute-start(bf16[96,1024]{1,0:T(8,128)(2,1)} %get-tuple-element.59), channel_id=1, source_target_pairs={{0,4},{2,6},{4,0},{6,2},{1,5},{3,7},{5,1},{7,3},{8,12},{10,14},{12... | collective-permute-start | bytes 589832 | tf_op jit(solution)/shard_map/ppermute | solution.py:23
  104.8 21.4 %collective-permute-start.14 = (bf16[96,1024]{1,0:T(8,128)(2,1)}, bf16[96,1024]{1,0:T(8,128)(2,1)S(1)}, u32[]{:S(2)}, u32[]{:S(2)}) collective-permute-start(bf16[96,1024]{1,0:T(8,128)(2,1)} %get-tuple-element.60), channel_id=1, source_target_pairs={{0,2},{2,4},{4,6},{6,0},{1,3},{3,5},{5,7},{7,1},{8,10},{10,12},{12... | collective-permute-start | bytes 589832 | tf_op jit(solution)/shard_map/ppermute | solution.py:23
  117.5 21.3 %collective-permute-start.22 = (bf16[96,1024]{1,0:T(8,128)(2,1)}, bf16[96,1024]{1,0:T(8,128)(2,1)S(1)}, u32[]{:S(2)}, u32[]{:S(2)}) collective-permute-start(bf16[96,1024]{1,0:T(8,128)(2,1)} %get-tuple-element.68), channel_id=1, source_target_pairs={{0,4},{2,6},{4,0},{6,2},{1,5},{3,7},{5,1},{7,3},{8,12},{10,14},{12... | collective-permute-start | bytes 589832 | tf_op jit(solution)/shard_map/ppermute | solution.py:23
  117.5 21.3 %collective-permute-start.23 = (bf16[96,1024]{1,0:T(8,128)(2,1)}, bf16[96,1024]{1,0:T(8,128)(2,1)S(1)}, u32[]{:S(2)}, u32[]{:S(2)}) collective-permute-start(bf16[96,1024]{1,0:T(8,128)(2,1)} %get-tuple-element.69), channel_id=1, source_target_pairs={{0,2},{2,4},{4,6},{6,0},{1,3},{3,5},{5,7},{7,1},{8,10},{10,12},{12... | collective-permute-start | bytes 589832 | tf_op jit(solution)/shard_map/ppermute | solution.py:23
  139.7 16.2 %collective-permute-start.26 = (bf16[96,1024]{1,0:T(8,128)(2,1)S(1)}, bf16[96,1024]{1,0:T(8,128)(2,1)S(1)}, u32[]{:S(2)}, u32[]{:S(2)}) collective-permute-start(bf16[96,1024]{1,0:T(8,128)(2,1)S(1)} %fusion.4.refs_0_), channel_id=1, source_target_pairs={{0,4},{2,6},{4,0},{6,2},{1,5},{3,7},{5,1},{7,3},{8,12},{10,14},{12... | collective-permute-start | bytes 589832 | tf_op jit(solution)/shard_map/ppermute | solution.py:23
  139.9 16.0 %collective-permute-start.27 = (bf16[96,1024]{1,0:T(8,128)(2,1)S(1)}, bf16[96,1024]{1,0:T(8,128)(2,1)S(1)}, u32[]{:S(2)}, u32[]{:S(2)}) collective-permute-start(bf16[96,1024]{1,0:T(8,128)(2,1)S(1)} %fusion.4.refs_0_), channel_id=1, source_target_pairs={{0,6},{2,0},{4,2},{6,4},{1,7},{3,1},{5,3},{7,5},{8,14},{10,8},{12,... | collective-permute-start | bytes 589832 | tf_op jit(solution)/shard_map/ppermute | solution.py:23
  144.1 26.2 %collective-permute-start.34 = (bf16[96,1024]{1,0:T(8,128)(2,1)S(1)}, bf16[96,1024]{1,0:T(8,128)(2,1)S(1)}, u32[]{:S(2)}, u32[]{:S(2)}) collective-permute-start(bf16[96,1024]{1,0:T(8,128)(2,1)S(1)} %fusion.5.refs_0_), channel_id=1, source_target_pairs={{0,2},{2,4},{4,6},{6,0},{1,3},{3,5},{5,7},{7,1},{8,10},{10,12},{12... | collective-permute-start | bytes 589832 | tf_op jit(solution)/shard_map/ppermute | solution.py:23
  144.1 27.8 %collective-permute-start.35 = (bf16[96,1024]{1,0:T(8,128)(2,1)S(1)}, bf16[96,1024]{1,0:T(8,128)(2,1)S(1)}, u32[]{:S(2)}, u32[]{:S(2)}) collective-permute-start(bf16[96,1024]{1,0:T(8,128)(2,1)S(1)} %fusion.5.refs_0_), channel_id=1, source_target_pairs={{0,4},{2,6},{4,0},{6,2},{1,5},{3,7},{5,1},{7,3},{8,12},{10,14},{12... | collective-permute-start | bytes 589832 | tf_op jit(solution)/shard_map/ppermute | solution.py:23
  146.2 25.8 %collective-permute-start.36 = (bf16[96,1024]{1,0:T(8,128)(2,1)S(1)}, bf16[96,1024]{1,0:T(8,128)(2,1)S(1)}, u32[]{:S(2)}, u32[]{:S(2)}) collective-permute-start(bf16[96,1024]{1,0:T(8,128)(2,1)S(1)} %fusion.5.refs_0_), channel_id=1, source_target_pairs={{0,6},{2,0},{4,2},{6,4},{1,7},{3,1},{5,3},{7,5},{8,14},{10,8},{12,... | collective-permute-start | bytes 589832 | tf_op jit(solution)/shard_map/ppermute | solution.py:23
  169.6 17.6 %collective-permute-start.28 = (bf16[2,32,48,128]{3,2,1,0:T(8,128)(2,1)}, bf16[2,32,48,128]{3,2,1,0:T(8,128)(2,1)S(1)}, u32[]{:S(2)}, u32[]{:S(2)}) collective-permute-start(bf16[2,32,48,128]{3,2,1,0:T(8,128)(2,1)} %get-tuple-element.71), channel_id=1, source_target_pairs={{0,1},{1,0},{2,3},{3,2},{4,5},{5,4},{6,7},{7,6},{8,9},{9,8},{10,11... | collective-permute-start | bytes 2359304 | tf_op jit(solution)/shard_map/ppermute | solution.py:23
  186.1 13.3 %collective-permute-start.37 = (bf16[2,32,48,128]{3,2,1,0:T(8,128)(2,1)}, bf16[2,32,48,128]{3,2,1,0:T(8,128)(2,1)S(1)}, u32[]{:S(2)}, u32[]{:S(2)}) collective-permute-start(bf16[2,32,48,128]{3,2,1,0:T(8,128)(2,1)} %get-tuple-element.80), channel_id=1, source_target_pairs={{0,1},{1,0},{2,3},{3,2},{4,5},{5,4},{6,7},{7,6},{8,9},{9,8},{10,11... | collective-permute-start | bytes 2359304 | tf_op jit(solution)/shard_map/ppermute | solution.py:23
  189.6 18.1 %collective-permute-start.29 = (bf16[32,48,128]{2,1,0:T(8,128)(2,1)S(1)}, bf16[32,48,128]{2,1,0:T(8,128)(2,1)S(1)}, u32[]{:S(2)}, u32[]{:S(2)}) collective-permute-start(bf16[32,48,128]{2,1,0:T(8,128)(2,1)S(1)} %get-tuple-element.73.refs_0_), channel_id=1, source_target_pairs={{0,1},{1,0},{2,3},{3,2},{4,5},{5,4},{6,7},{7,6},{8,9},{9,8},{10,11... | collective-permute-start | bytes 1179656 | tf_op jit(solution)/shard_map/ppermute | solution.py:23
  201.8 33.2 %collective-permute-start.38 = (bf16[32,48,128]{2,1,0:T(8,128)(2,1)S(1)}, bf16[32,48,128]{2,1,0:T(8,128)(2,1)S(1)}, u32[]{:S(2)}, u32[]{:S(2)}) collective-permute-start(bf16[32,48,128]{2,1,0:T(8,128)(2,1)S(1)} %get-tuple-element.82.refs_0_), channel_id=1, source_target_pairs={{0,1},{1,0},{2,3},{3,2},{4,5},{5,4},{6,7},{7,6},{8,9},{9,8},{10,11... | collective-permute-start | bytes 1179656 | tf_op jit(solution)/shard_map/ppermute | solution.py:23
  217.5 29.8 %collective-permute-start.30 = (bf16[96,1024]{1,0:T(8,128)(2,1)}, bf16[96,1024]{1,0:T(8,128)(2,1)S(1)}, u32[]{:S(2)}, u32[]{:S(2)}) collective-permute-start(bf16[96,1024]{1,0:T(8,128)(2,1)} %get-tuple-element.76), channel_id=1, source_target_pairs={{0,6},{2,0},{4,2},{6,4},{1,7},{3,1},{5,3},{7,5},{8,14},{10,8},{12,... | collective-permute-start | bytes 589832 | tf_op jit(solution)/shard_map/ppermute | solution.py:23
  225.9 29.0 %collective-permute-start.31 = (bf16[96,1024]{1,0:T(8,128)(2,1)}, bf16[96,1024]{1,0:T(8,128)(2,1)S(1)}, u32[]{:S(2)}, u32[]{:S(2)}) collective-permute-start(bf16[96,1024]{1,0:T(8,128)(2,1)} %get-tuple-element.77), channel_id=1, source_target_pairs={{0,4},{2,6},{4,0},{6,2},{1,5},{3,7},{5,1},{7,3},{8,12},{10,14},{12... | collective-permute-start | bytes 589832 | tf_op jit(solution)/shard_map/ppermute | solution.py:23
  235.0 20.0 %collective-permute-start.32 = (bf16[96,1024]{1,0:T(8,128)(2,1)}, bf16[96,1024]{1,0:T(8,128)(2,1)S(1)}, u32[]{:S(2)}, u32[]{:S(2)}) collective-permute-start(bf16[96,1024]{1,0:T(8,128)(2,1)} %get-tuple-element.78), channel_id=1, source_target_pairs={{0,2},{2,4},{4,6},{6,0},{1,3},{3,5},{5,7},{7,1},{8,10},{10,12},{12... | collective-permute-start | bytes 589832 | tf_op jit(solution)/shard_map/ppermute | solution.py:23
  247.3 20.8 %collective-permute-start.40 = (bf16[96,1024]{1,0:T(8,128)(2,1)}, bf16[96,1024]{1,0:T(8,128)(2,1)S(1)}, u32[]{:S(2)}, u32[]{:S(2)}) collective-permute-start(bf16[96,1024]{1,0:T(8,128)(2,1)} %get-tuple-element.86), channel_id=1, source_target_pairs={{0,4},{2,6},{4,0},{6,2},{1,5},{3,7},{5,1},{7,3},{8,12},{10,14},{12... | collective-permute-start | bytes 589832 | tf_op jit(solution)/shard_map/ppermute | solution.py:23
  247.3 20.8 %collective-permute-start.41 = (bf16[96,1024]{1,0:T(8,128)(2,1)}, bf16[96,1024]{1,0:T(8,128)(2,1)S(1)}, u32[]{:S(2)}, u32[]{:S(2)}) collective-permute-start(bf16[96,1024]{1,0:T(8,128)(2,1)} %get-tuple-element.87), channel_id=1, source_target_pairs={{0,2},{2,4},{4,6},{6,0},{1,3},{3,5},{5,7},{7,1},{8,10},{10,12},{12... | collective-permute-start | bytes 589832 | tf_op jit(solution)/shard_map/ppermute | solution.py:23
  255.1 16.2 %collective-permute-start.33 = (bf16[48,1024]{1,0:T(8,128)(2,1)S(1)}, bf16[48,1024]{1,0:T(8,128)(2,1)S(1)}, u32[]{:S(2)}, u32[]{:S(2)}) collective-permute-start(bf16[48,1024]{1,0:T(8,128)(2,1)S(1)} %slice.253), channel_id=1, source_target_pairs={{0,1},{1,0},{2,3},{3,2},{4,5},{5,4},{6,7},{7,6},{8,9},{9,8},{10,11... | collective-permute-start | bytes 294920 | tf_op jit(solution)/shard_map/ppermute | solution.py:23
  (58 other events, 553.6 us)

commit v5 on v4

--- a/solution.py
+++ b/solution.py
@@ -32,14 +32,12 @@
     return jnp.where(seed_of[:, None] == noise_ids[None, :], sign_values[:, None], jnp.float32(0.0))
 
 
-def tile_plan(codes, block_rows, own_cols, owner_index, owners):
+def tile_plan(codes, block_rows, own_cols):
     tile_count = codes.shape[1]
     active = codes >= 0
     cleared = jnp.where(active, codes, 0)
     column = cleared // block_rows
     feature = cleared % block_rows
-    per_owner = block_rows // owners
-    feature = lax.rem(owner_index - feature // per_owner + owners, owners) * per_owner + feature % per_owner
     is_down = jnp.arange(codes.shape[0])[:, None] % 3 == 2
     major = jnp.where(is_down, feature, column)
     minor = jnp.where(is_down, column, feature)
@@ -95,40 +93,54 @@
     return copies[0]
 
 
-def expand_kernel(owners, reps, words_ref, groups_ref, *refs):
-    blocks = refs[:owners]
-    gain_ref, left_ref, own_gate, other_gate, own_up, other_up, raw_ref = refs[owners : owners + 7]
-    part_refs = refs[owners + 7 : owners + 7 + reps]
-    total_ref, gate_tiles, gate_sem, up_tiles, up_sem, x_ref = refs[owners + 7 + reps :]
-    all_rows, width = blocks[0].shape
+def rows_of(place_ref, reps, rows, steps):
+    rep = lax.rem(place_ref[4] + (reps - steps), reps)
+    return pl.ds(pl.multiple_of(rep * rows, rows), rows)
+
+
+def expand_kernel(reps, words_ref, groups_ref, stream_ref, *refs):
+    gain_ref, left_ref, own_gate, other_gate, own_up, other_up, raw_ref = refs[:7]
+    part_refs = refs[7 : 7 + reps]
+    total_ref, gate_tiles, gate_sem, up_tiles, up_sem, x_ref = refs[7 + reps :]
+    features = gain_ref.shape[1]
+    all_rows = x_ref.shape[1]
     rows = all_rows // reps
-    per_owner = width // BLOCK
-    strip = 48 if all_rows % 48 == 0 else 16
+    strip = 48 if rows % 48 == 0 else 16
     gate_copy = load_tiles(groups_ref[3], (own_gate, other_gate), gate_tiles, gate_sem)
     up_copy = load_tiles(groups_ref[3], (own_up, other_up), up_tiles, up_sem)
 
-    def norm_rows(i, carry):
-        at = pl.ds(pl.multiple_of(i * strip, strip), strip)
-        squares = jnp.zeros((strip, BLOCK), jnp.float32)
-        for owner in range(owners):
-            for part in range(per_owner):
-                values = blocks[owner][at, pl.ds(part * BLOCK, BLOCK)].astype(jnp.float32)
+    for rep in range(reps):
+
+        def norm_rows(i, carry, rep=rep):
+            start = pl.multiple_of(i * strip, strip)
+            at = pl.ds(rep * rows + start, strip)
+
+            def load(d):
+                if len(stream_ref.shape) == 2:
+                    block = stream_ref[at, pl.ds(d * BLOCK, BLOCK)]
+                else:
+                    owner, lane = divmod(d * BLOCK, stream_ref.shape[2])
+                    owners = features // stream_ref.shape[2]
+                    block = stream_ref[rep * owners + owner, pl.ds(start, strip), pl.ds(lane, BLOCK)]
+                return block.astype(jnp.float32)
+
+            squares = jnp.zeros((strip, BLOCK), jnp.float32)
+            for d in range(features // BLOCK):
+                values = load(d)
                 squares = squares + values * values
-        total = jnp.sum(squares, axis=1, keepdims=True)
-        inverse = lax.rsqrt(total / (owners * width) + epsilon)
-        for owner in range(owners):
-            for part in range(per_owner):
-                values = blocks[owner][at, pl.ds(part * BLOCK, BLOCK)].astype(jnp.float32)
-                gain = gain_ref[:, pl.ds(owner * width + part * BLOCK, BLOCK)].astype(jnp.float32)
-                x_ref[owner * per_owner + part, at, :] = (values * inverse * gain).astype(jnp.bfloat16)
-        return carry
-
-    lax.fori_loop(0, all_rows // strip, norm_rows, 0)
+            inverse = lax.rsqrt(jnp.sum(squares, axis=1, keepdims=True) / features + epsilon)
+            for d in range(features // BLOCK):
+                gain = gain_ref[:, pl.ds(d * BLOCK, BLOCK)].astype(jnp.float32)
+                x_ref[d, at, :] = (load(d) * inverse * gain).astype(jnp.bfloat16)
+            return carry
+
+        lax.fori_loop(0, rows // strip, norm_rows, 0)
     raw = jnp.zeros(raw_ref.shape, jnp.float32)
     step = min(8, x_ref.shape[0])
+    own_rows = rows_of(groups_ref, reps, rows, 0)
     for d in range(0, x_ref.shape[0], step):
         raw = raw + lax.dot_general(
-            jnp.concatenate([x_ref[d + i, pl.ds(0, rows), :] for i in range(step)], axis=1),
+            jnp.concatenate([x_ref[d + i, own_rows, :] for i in range(step)], axis=1),
             left_ref[:, pl.ds(d * BLOCK, step * BLOCK)],
             (((1,), (1,)), ((), ())),
             preferred_element_type=jnp.float32,
@@ -148,7 +160,7 @@
         for rep, part_ref in enumerate(part_refs):
 
             def narrow(c, carry, which=which, rep=rep, part_ref=part_ref):
-                part_ref[which, c] = total_ref[c, pl.ds(rep * rows, rows), :].astype(jnp.bfloat16)
+                part_ref[which, c] = total_ref[c, rows_of(groups_ref, reps, rows, rep), :].astype(jnp.bfloat16)
                 return carry
 
             lax.fori_loop(0, total_ref.shape[0], narrow, 0, unroll=min(4, total_ref.shape[0]))
@@ -175,25 +187,23 @@
     ]
 
 
-def expand(words, groups, blocks, gain, left, gate_tiles, up_tiles, own_cols, reps):
-    owners = len(blocks)
-    all_rows, width = blocks[0].shape
+def expand(words, groups, stream, gain, left, gate_tiles, up_tiles, own_cols, reps):
+    features = gain.shape[1]
+    all_rows = stream.size // features
     rows = all_rows // reps
     tile_count = gate_tiles[0].shape[0]
     scratch = tile_scratch(tile_count, own_cols, all_rows)
     out = pl.pallas_call(
-        functools.partial(expand_kernel, owners, reps),
+        functools.partial(expand_kernel, reps),
         out_shape=[jax.ShapeDtypeStruct((rows, left.shape[0]), jnp.float32)]
         + [jax.ShapeDtypeStruct((2, own_cols, rows, BLOCK), jnp.bfloat16)] * reps,
-        in_specs=[SMEM, SMEM] + [VMEM] * (owners + 2) + [HBM] * 4,
+        in_specs=[SMEM, SMEM] + [VMEM] * 3 + [HBM] * 4,
         out_specs=[VMEM] * (1 + reps),
-        scratch_shapes=scratch
-        + scratch[1:]
-        + [pltpu.VMEM((owners * width // BLOCK, all_rows, BLOCK), jnp.bfloat16)],
+        scratch_shapes=scratch + scratch[1:] + [pltpu.VMEM((features // BLOCK, all_rows, BLOCK), jnp.bfloat16)],
         compiler_params=pltpu.CompilerParams(vmem_limit_bytes=VMEM_LIMIT),
         cost_estimate=tile_cost(2 * tile_count, all_rows),
         name="expand",
-    )(words, groups, *blocks, gain, left, *gate_tiles, *up_tiles)
+    )(words, groups, stream, gain, left, *gate_tiles, *up_tiles)
     return out[0], out[1:]
 
 
@@ -255,58 +265,67 @@
     )(*parts, raw, picks, wide_cols, down_cols)
 
 
-def contract_kernel(owners, reps, words_ref, groups_ref, *refs):
+def contract_kernel(reps, words_ref, groups_ref, *refs):
     hiddens = refs[:reps]
-    coef_ref, right_ref, own_hbm, other_hbm = refs[reps : reps + 4]
-    outs = refs[reps + 4 : reps + 4 + owners]
-    total_ref, tiles, sem = refs[reps + 4 + owners :]
-    rows = hiddens[0].shape[1]
-    per_owner = outs[0].shape[1] // BLOCK
+    coef_ref, right_ref, residual_ref, own_hbm, other_hbm, out_ref = refs[reps : reps + 6]
+    total_ref, tiles, sem, hidden_ref = refs[reps + 6 :]
+    columns, rows = hiddens[0].shape[:2]
     blocks = total_ref.shape[0]
     copy = load_tiles(groups_ref[3], (own_hbm, other_hbm), tiles, sem)
 
     def read(block):
-        return jnp.concatenate([hidden[block] for hidden in hiddens], axis=0)
+        return hidden_ref[block]
 
     def add(block, product):
         total_ref[block] += product
 
+    for rep, part_ref in enumerate(hiddens):
+
+        def gather(c, carry, rep=rep, part_ref=part_ref):
+            hidden_ref[c, rows_of(groups_ref, reps, rows, rep), :] = part_ref[c]
+            return carry
+
+        lax.fori_loop(0, columns, gather, 0, unroll=min(4, columns))
+
+    own_rows = rows_of(groups_ref, reps, rows, 0)
     coef = coef_ref[...]
     high = coef.astype(jnp.bfloat16)
     low = (coef - high.astype(jnp.float32)).astype(jnp.bfloat16)
     right = right_ref[...]
     both = jnp.concatenate([high, low], axis=1)
     twice = jnp.concatenate([right, right], axis=0)
+    total_ref[...] = jnp.zeros(total_ref.shape, jnp.float32)
     for d in range(0, blocks, 2):
         start = jnp.dot(both, twice[:, d * BLOCK : (d + 2) * BLOCK], preferred_element_type=jnp.float32)
         for i in range(2):
-            total_ref[d + i, pl.ds(0, rows), :] = start[:, i * BLOCK : (i + 1) * BLOCK]
-            if reps > 1:
-                total_ref[d + i, pl.ds(rows, (reps - 1) * rows), :] = jnp.zeros(
-                    ((reps - 1) * rows, BLOCK), jnp.float32
-                )
+            total_ref[d + i, own_rows, :] = start[:, i * BLOCK : (i + 1) * BLOCK]
+    own_blocks = residual_ref.shape[1] // BLOCK
+    for i in range(own_blocks):
+        total_ref[groups_ref[5] * own_blocks + i, own_rows, :] += residual_ref[
+            :, pl.ds(i * BLOCK, BLOCK)
+        ].astype(jnp.float32)
     copy.wait()
     multiply_tiles(words_ref, groups_ref, 2, words_ref.shape[0] // 3, read, tiles, add)
-    for owner in range(owners):
-        for part in range(per_owner):
-            outs[owner][:, pl.ds(part * BLOCK, BLOCK)] = total_ref[owner * per_owner + part].astype(jnp.bfloat16)
-
-
-def contract(words, groups, hiddens, coef, right, tiles, owners):
+    for d in range(blocks):
+        out_ref[:, pl.ds(d * BLOCK, BLOCK)] = total_ref[d].astype(jnp.bfloat16)
+
+
+def contract(words, groups, hiddens, coef, right, residual, tiles):
     own_cols, rows = hiddens[0].shape[:2]
     reps = len(hiddens)
     features = right.shape[1]
     tile_count = tiles[0].shape[0]
     return pl.pallas_call(
-        functools.partial(contract_kernel, owners, reps),
-        out_shape=[jax.ShapeDtypeStruct((reps * rows, features // owners), jnp.bfloat16)] * owners,
-        in_specs=[SMEM, SMEM] + [VMEM] * (reps + 2) + [HBM, HBM],
-        out_specs=[VMEM] * owners,
-        scratch_shapes=tile_scratch(tile_count, features // BLOCK, reps * rows),
+        functools.partial(contract_kernel, reps),
+        out_shape=jax.ShapeDtypeStruct((reps * rows, features), jnp.bfloat16),
+        in_specs=[SMEM, SMEM] + [VMEM] * (reps + 3) + [HBM, HBM],
+        out_specs=VMEM,
+        scratch_shapes=tile_scratch(tile_count, features // BLOCK, reps * rows)
+        + [pltpu.VMEM((own_cols, reps * rows, BLOCK), jnp.bfloat16)],
         compiler_params=pltpu.CompilerParams(vmem_limit_bytes=VMEM_LIMIT),
         cost_estimate=tile_cost(tile_count, reps * rows),
         name="contract",
-    )(words, groups, *hiddens, coef, right, *tiles)
+    )(words, groups, *hiddens, coef, right, residual, *tiles)
 
 
 def per_device(
@@ -348,13 +367,8 @@
     up_pair = (up_tiles[0], hop(up_tiles[0], "section", 1))
     down_pair = (down_tiles[0], hop(down_tiles[0], "section", 1))
 
-    plans = tile_plan(jnp.concatenate([codes, other_codes]), block_rows, own_cols, owner_index, owners)
-    rotation = lax.rem(owner_index - jnp.arange(owners, dtype=jnp.int32) + owners, owners)
+    plans = tile_plan(jnp.concatenate([codes, other_codes]), block_rows, own_cols)
     noise = gate_left.shape[1]
-
-    def rotated(table):
-        parts = table.reshape(table.shape[0], owners, width)
-        return jnp.take(parts, rotation, axis=1).reshape(table.shape)
 
     columns = lax.dynamic_slice_in_dim(owned_columns[0], owner_index * own_cols, own_cols)
 
@@ -368,8 +382,8 @@
     def tables(section):
         own = section_index == section
         words, groups = (jnp.where(own, table[:3], table[3:]) for table in plans)
-        groups = jnp.concatenate([groups, own.astype(jnp.int32)[None]])
-        chosen = rotated(jnp.where(own, wide, other_wide))
+        groups = jnp.concatenate([groups, jnp.stack([own.astype(jnp.int32), rep_index, owner_index])])
+        chosen = jnp.where(own, wide, other_wide)
         left, right, gain = chosen[: 2 * noise], chosen[2 * noise : 3 * noise], chosen[3 * noise :]
         chosen = jnp.where(own, cols, other_cols)
         gate_cols, up_cols, down_cols = chosen[:noise], chosen[noise : 2 * noise], chosen[2 * noise :]
@@ -382,41 +396,36 @@
 
     layers = [tables(section) for section in range(2)]
 
-    def layer(stream, picked, section):
+    def layer(stream, residual, picked, section):
         words, groups, left, right, gain, wide_cols, down_cols = layers[section]
-        blocks = [stream] + [hop(stream, "tensor", step) for step in range(1, owners)]
-        raw, parts = expand(words, groups, blocks, gain, left, gate_pair, up_pair, own_cols, reps)
+        raw, parts = expand(words, groups, stream, gain, left, gate_pair, up_pair, own_cols, reps)
         parts = [parts[0]] + [hop(parts[g], "rep", -g) for g in range(1, reps)]
         hidden, coef = activate(parts, raw, picked, wide_cols, down_cols)
         hiddens = [hidden] + [hop(hidden, "rep", g) for g in range(1, reps)]
-        outs = contract(words, groups, hiddens, coef, right, down_pair, owners)
-        summed = outs[0].astype(jnp.float32)
-        for step in range(1, owners):
-            summed = summed + hop(outs[step], "tensor", -step).astype(jnp.float32)
-        return summed
+        return contract(words, groups, hiddens, coef, right, residual, down_pair)
 
     half = rows // 2
     mine_rows = lax.dynamic_slice_in_dim(tokens, section_index * half, half)
     mine_picks = lax.dynamic_slice_in_dim(picks, section_index * half, half)
-    others = [hop(mine_rows, "rep", g) for g in range(1, reps)]
     piece = half // PIECES
     firsts, seconds = [], []
     for h in range(PIECES):
         cut = slice(h * piece, (h + 1) * piece)
-        stream = jnp.concatenate([value[cut] for value in [mine_rows] + others], axis=0)
-        summed = layer(stream, mine_picks[cut], 0)
-        own = stream[:piece].astype(jnp.float32) + summed[:piece]
-        summed = jnp.concatenate([own, summed[piece:]], axis=0).astype(jnp.bfloat16)
-        total = summed.astype(jnp.float32)
+        residual = mine_rows[cut]
+        stream = lax.all_gather(residual, ("rep", "tensor"))
+        partial = layer(stream, residual, mine_picks[cut], 0)
+        if h > 0:
+            partial, last = lax.optimization_barrier((partial, last))
+        stream = lax.psum(partial, ("tensor", "rep"))
+        last = stream
+        residual = lax.dynamic_slice(stream, (rep_index * piece, owner_index * width), (piece, width))
+        firsts.append(residual)
+        partial = layer(stream, residual, mine_picks[cut], 1)
+        summed = lax.psum_scatter(partial, "tensor", scatter_dimension=1, tiled=True)
+        value = lax.dynamic_slice_in_dim(summed, rep_index * piece, piece).astype(jnp.float32)
         for g in range(1, reps):
-            arrived = hop(summed, "rep", g).astype(jnp.float32)
-            total = total + jnp.roll(arrived, g * piece, axis=0)
-        stream = total.astype(jnp.bfloat16)
-        firsts.append(stream[:piece])
-        summed = layer(stream, mine_picks[cut], 1)
-        value = stream[:piece].astype(jnp.float32) + summed[:piece]
-        for g in range(1, reps):
-            sent = summed[g * piece : (g + 1) * piece].astype(jnp.bfloat16)
+            to = lax.rem(rep_index + (reps - g), reps)
+            sent = lax.dynamic_slice_in_dim(summed, to * piece, piece)
             value = value + hop(sent, "rep", -g).astype(jnp.float32)
         seconds.append(value.astype(jnp.bfloat16))
     first = jnp.concatenate(firsts, axis=0)

time: 279 us -> 414 us (1.48)
  waiting for transfers between devices: 87.7 us -> 200 us
  blocking collectives: 0 us -> 62.6 us
  starting transfers between devices: 65.1 us -> 16.9 us
  between operations: 0.92 us -> 13.6 us
  Pallas kernels: 97.6 us -> 91 us
    psum x0 -> x2, waiting for transfers between devices: none -> 130 us  [per_device(): stream = lax.psum(partial, ('tensor', 'rep'))]
    all_gather x0 -> x2, blocking collectives: none -> 62.6 us  [per_device(): stream = lax.all_gather(residual, ('rep', 'tensor'))]
    ppermute x44 -> x17, starting transfers between devices: 65.1 us -> 16.6 us  [hop(): lax.ppermute(value, axis, [(i, (i + steps) % count) for i in range(count)])]
    ppermute x44 -> x17, waiting for transfers between devices: 87.7 us -> 49.5 us  [hop(): lax.ppermute(value, axis, [(i, (i + steps) % count) for i in range(count)])]
    reduce_scatter x0 -> x2, waiting for transfers between devices: none -> 20.6 us  [per_device(): lax.psum_scatter(partial, 'tensor', scatter_dimension=1, tiled=True)]
    pallas_call x8, Pallas kernels: 87.9 us -> 81.3 us  [the longest x4 49.4 us: expand(): pl.pallas_call(functools.partial(expand_kernel, reps), out_shape=[jax.Sha...]
  transfers between devices with their start and end apart: 44 -> 21, of which waited for: 18 -> 12; matrix products, arithmetic and copies ran while one was open for 7% -> 4% of each run, Pallas kernels for 35% -> 22%
where the time goes in v5:
time: 414 us; the launch traced here: 411 us
  waiting for transfers between devices  200 us (48%)
  Pallas kernels  91 us (22%)
  blocking collectives  62.6 us (15%)
  starting transfers between devices  16.9 us (4%)
  local copies, waits for them, and re-layouts  16.4 us (4%)
  between operations  13.6 us (3%)
  other arithmetic  10.3 us (2%)
    psum x2, waiting for transfers between devices, per_device(): stream = lax.psum(partial, ('tensor', 'rep'))  130 us
    all_gather x2, blocking collectives, per_device(): stream = lax.all_gather(residual, ('rep', 'tensor'))  62.6 us
    ppermute x17, waiting for transfers between devices, hop(): lax.ppermute(value, axis, [(i, (i + steps) % count) for i in range(count)])  49.5 us
    pallas_call x4, Pallas kernels, expand(): pl.pallas_call(functools.partial(expand_kernel, reps), out_shape=[jax.Sha...  49.4 us
    pallas_call x4, Pallas kernels, contract(): pl.pallas_call(functools.partial(contract_kernel, reps), out_shape=jax.Sh...  31.9 us
    reduce_scatter x2, waiting for transfers between devices, per_device(): lax.psum_scatter(partial, 'tensor', scatter_dimension=1, tiled=True)  20.6 us
    ppermute x17, starting transfers between devices, hop(): lax.ppermute(value, axis, [(i, (i + steps) % count) for i in range(count)])  16.6 us
    pallas_call x4, Pallas kernels, activate(): pl.pallas_call(functools.partial(activate_kernel, reps), out_shape=[jax.S...  9.69 us
  transfers between devices with their start and end apart: 21, of which 12 were waited for; matrix products, arithmetic and copies ran while one was open for 4% of the time, Pallas kernels for 22%

profile of v5, /device:TPU:1, one launch (start us, length us, event | category | flops | bytes accessed | tf_op | source)
XLA Modules:
  0.0 410.7 jit_solution(7364098021908630615)
XLA Ops:
  11.4 1.2 pad_maximum_fusion
  14.2 32.3 %all-gather = bf16[384,1024]{1,0:T(8,128)(2,1)} all-gather(bf16[48,1024]{1,0:T(8,128)(2,1)S(1)} %get-tuple-element.69.refs_4_), channel_id=2, replica_groups=mesh['pop'=2,'section'=2,'tensor'=4,'rep'=2] {'rep','tensor'}, dimensions={0}, use_global_device_ids=true | all-gather | bytes 884736 | tf_op jit(solution)/shard_map/all_gather | solution.py:415
  46.5 30.3 %all-gather.1 = bf16[384,1024]{1,0:T(8,128)(2,1)} all-gather(bf16[48,1024]{1,0:T(8,128)(2,1)S(1)} %get-tuple-element.70.refs_4_), channel_id=3, replica_groups=mesh['pop'=2,'section'=2,'tensor'=4,'rep'=2] {'rep','tensor'}, dimensions={0}, use_global_device_ids=true | all-gather | bytes 884736 | tf_op jit(solution)/shard_map/all_gather | solution.py:415
  81.4 11.1 %expand.4 = (f32[48,16]{1,0:T(8,128)}, bf16[2,32,48,128]{3,2,1,0:T(8,128)(2,1)}, bf16[2,32,48,128]{3,2,1,0:T(8,128)(2,1)}) custom-call(s32[864]{0:T(1024)} %reshape.465.words_ref, s32[6]{0:T(128)} %add_add_fusion.groups_ref, bf16[8,48,1024]{2,1,0:T(8,128)(2,1)} %bitcast.58, bf16[1,4096]{1,0:T(2,128)(2,1)} %slice.90.refs_0_, bf16[16,4096]{1,0:T(8,128)(2,1)} %slice.91.refs_1_, ...), custom_call_target="tpu_custom_call" | custom-call | flops 6442450944 | bytes 16777216 | tf_op jit(solution)/shard_map/expand/pallas_call | solution.py:196
  94.4 9.2 %collective-permute-done.4.refs_1_ = bf16[2,32,48,128]{3,2,1,0:T(8,128)(2,1)S(1)} collective-permute-done((bf16[2,32,48,128]{3,2,1,0:T(8,128)(2,1)}, bf16[2,32,48,128]{3,2,1,0:T(8,128)(2,1)S(1)}, u32[]{:S(2)}, u32[]{:S(2)}) %collective-permute-start.4) | collective-permute-done | bytes 786464 | tf_op jit(solution)/shard_map/ppermute | solution.py:23
  103.7 2.4 activate.4
  107.2 11.1 %expand.5 = (f32[48,16]{1,0:T(8,128)}, bf16[2,32,48,128]{3,2,1,0:T(8,128)(2,1)}, bf16[2,32,48,128]{3,2,1,0:T(8,128)(2,1)}) custom-call(s32[864]{0:T(1024)} %reshape.465.words_ref, s32[6]{0:T(128)} %add_add_fusion.groups_ref, bf16[8,48,1024]{2,1,0:T(8,128)(2,1)} %bitcast.57, bf16[1,4096]{1,0:T(2,128)(2,1)} %slice.90.refs_0_, bf16[16,4096]{1,0:T(8,128)(2,1)} %slice.91.refs_1_, ...), custom_call_target="tpu_custom_call" | custom-call | flops 6442450944 | bytes 16777216 | tf_op jit(solution)/shard_map/expand/pallas_call | solution.py:196
  120.1 8.0 %contract.4 = bf16[96,4096]{1,0:T(8,128)(2,1)} custom-call(s32[864]{0:T(1024)} %reshape.465.words_ref, s32[6]{0:T(128)} %add_add_fusion.groups_ref, bf16[32,48,128]{2,1,0:T(8,128)(2,1)} %copy-done.6, bf16[32,48,128]{2,1,0:T(8,128)(2,1)} %copy-done.22, f32[48,8]{1,0:T(8,128)} %copy-done.13, bf16[8,4096]{1,0:T(8,128)(2,1)} %slice.96.refs_3_, ...), custom_call_target="tpu_custom_call" | custom-call | flops 3221225472 | bytes 8388608 | tf_op jit(solution)/shard_map/contract/pallas_call | solution.py:318
  130.7 3.0 collective-permute-done.8.refs_1_
  133.6 2.4 activate.5
  136.7 1.2 collective-permute-start.9
  137.8 83.0 %all-reduce.7.cloned.1.call-done.stream_ref = bf16[96,4096]{1,0:T(8,128)(2,1)} async-done(((bf16[96,4096]{1,0:T(8,128)(2,1)}), bf16[96,4096]{1,0:T(8,128)(2,1)}) %all-reduce.7.cloned.1.call-update) | async-done | bytes 786448 | tf_op jit(solution)/shard_map/psum | solution.py:419
  220.8 13.6 %expand.6 = (f32[48,16]{1,0:T(8,128)}, bf16[2,32,48,128]{3,2,1,0:T(8,128)(2,1)}, bf16[2,32,48,128]{3,2,1,0:T(8,128)(2,1)}) custom-call(s32[864]{0:T(1024)} %reshape.467.words_ref, s32[6]{0:T(128)} %add_add_fusion.1.groups_ref, bf16[96,4096]{1,0:T(8,128)(2,1)} %all-reduce.7.cloned.1.call-done.stream_ref, bf16[1,4096]{1,0:T(2,128)(2,1)} %slice.98.refs_0_, ...), custom_call_target="tpu_custom_call" | custom-call | flops 6442450944 | bytes 16777216 | tf_op jit(solution)/shard_map/expand/pallas_call | solution.py:196
  236.0 8.0 %contract.5 = bf16[96,4096]{1,0:T(8,128)(2,1)} custom-call(s32[864]{0:T(1024)} %reshape.465.words_ref, s32[6]{0:T(128)} %add_add_fusion.groups_ref, bf16[32,48,128]{2,1,0:T(8,128)(2,1)} %copy-done.5, bf16[32,48,128]{2,1,0:T(8,128)(2,1)} %copy-done.21, f32[48,8]{1,0:T(8,128)} %copy-done.12, bf16[8,4096]{1,0:T(8,128)(2,1)} %slice.96.refs_3_, ...), custom_call_target="tpu_custom_call" | custom-call | flops 3221225472 | bytes 8388608 | tf_op jit(solution)/shard_map/contract/pallas_call | solution.py:318
  244.1 8.5 %collective-permute-done.10.refs_1_ = bf16[2,32,48,128]{3,2,1,0:T(8,128)(2,1)S(1)} collective-permute-done((bf16[2,32,48,128]{3,2,1,0:T(8,128)(2,1)}, bf16[2,32,48,128]{3,2,1,0:T(8,128)(2,1)S(1)}, u32[]{:S(2)}, u32[]{:S(2)}) %collective-permute-start.10) | collective-permute-done | bytes 786464 | tf_op jit(solution)/shard_map/ppermute | solution.py:23
  252.6 2.4 activate.6
  255.0 2.2 collective-permute-start.11
  257.8 1.5 dynamic_slice.40.refs_4_
  259.4 3.4 collective-permute-done.11.refs_1_
  263.5 8.0 %contract.6 = bf16[96,4096]{1,0:T(8,128)(2,1)} custom-call(s32[864]{0:T(1024)} %reshape.467.words_ref, s32[6]{0:T(128)} %add_add_fusion.1.groups_ref, bf16[32,48,128]{2,1,0:T(8,128)(2,1)} %copy-done.4, bf16[32,48,128]{2,1,0:T(8,128)(2,1)} %copy-done.20, f32[48,8]{1,0:T(8,128)} %copy-done.11, bf16[8,4096]{1,0:T(8,128)(2,1)} %slice.103.refs_3_, ...), custom_call_target="tpu_custom_call" | custom-call | flops 3221225472 | bytes 8388608 | tf_op jit(solution)/shard_map/contract/pallas_call | solution.py:318
  271.8 46.5 %all-reduce.9.cloned.1.call-done.stream_ref = bf16[96,4096]{1,0:T(8,128)(2,1)} async-done(((bf16[96,4096]{1,0:T(8,128)(2,1)}), bf16[96,4096]{1,0:T(8,128)(2,1)}) %all-reduce.9.cloned.1.call-update) | async-done | bytes 786448 | tf_op jit(solution)/shard_map/psum | solution.py:419
  318.3 13.6 %expand.7 = (f32[48,16]{1,0:T(8,128)}, bf16[2,32,48,128]{3,2,1,0:T(8,128)(2,1)}, bf16[2,32,48,128]{3,2,1,0:T(8,128)(2,1)}) custom-call(s32[864]{0:T(1024)} %reshape.467.words_ref, s32[6]{0:T(128)} %add_add_fusion.1.groups_ref, bf16[96,4096]{1,0:T(8,128)(2,1)} %all-reduce.9.cloned.1.call-done.stream_ref, bf16[1,4096]{1,0:T(2,128)(2,1)} %slice.98.refs_0_, ...), custom_call_target="tpu_custom_call" | custom-call | flops 6442450944 | bytes 16777216 | tf_op jit(solution)/shard_map/expand/pallas_call | solution.py:196
  332.6 16.9 %collective-permute-done.13.refs_1_ = bf16[2,32,48,128]{3,2,1,0:T(8,128)(2,1)S(1)} collective-permute-done((bf16[2,32,48,128]{3,2,1,0:T(8,128)(2,1)}, bf16[2,32,48,128]{3,2,1,0:T(8,128)(2,1)S(1)}, u32[]{:S(2)}, u32[]{:S(2)}) %collective-permute-start.13) | collective-permute-done | bytes 786464 | tf_op jit(solution)/shard_map/ppermute | solution.py:23
  351.4 2.4 activate.7
  355.0 1.5 dynamic_slice.41.refs_4_
  356.5 5.4 %collective-permute-done.14.refs_1_ = bf16[32,48,128]{2,1,0:T(8,128)(2,1)S(1)} collective-permute-done((bf16[32,48,128]{2,1,0:T(8,128)(2,1)S(1)}, bf16[32,48,128]{2,1,0:T(8,128)(2,1)S(1)}, u32[]{:S(2)}, u32[]{:S(2)}) %collective-permute-start.14) | collective-permute-done | bytes 393248 | tf_op jit(solution)/shard_map/ppermute | solution.py:23
  362.6 8.0 %contract.7 = bf16[96,4096]{1,0:T(8,128)(2,1)} custom-call(s32[864]{0:T(1024)} %reshape.467.words_ref, s32[6]{0:T(128)} %add_add_fusion.1.groups_ref, bf16[32,48,128]{2,1,0:T(8,128)(2,1)} %copy-done.7, bf16[32,48,128]{2,1,0:T(8,128)(2,1)} %copy-done.23, f32[48,8]{1,0:T(8,128)} %copy-done.14, bf16[8,4096]{1,0:T(8,128)(2,1)} %slice.103.refs_3_, ...), custom_call_target="tpu_custom_call" | custom-call | flops 3221225472 | bytes 8388608 | tf_op jit(solution)/shard_map/contract/pallas_call | solution.py:318
  371.7 1.4 collective-permute-start.12
  373.1 20.6 %reduce-scatter.5.cloned.1.call-done = bf16[96,1024]{1,0:T(8,128)(2,1)} async-done(((bf16[96,4096]{1,0:T(8,128)(2,1)}), bf16[96,1024]{1,0:T(8,128)(2,1)}) %reduce-scatter.5.cloned.1.call-update) | async-done | bytes 196624 | tf_op jit(solution)/shard_map/reduce_scatter | solution.py:424
  394.6 1.2 collective-permute-start.15
  396.7 1.3 collective-permute-done.15
  399.1 3.2 collective-permute-start.16
  (143 shorter events, 32.2 us)
Async XLA Ops:
  6.5 214.3 %all-reduce.7.cloned.1.call-start = ((), (), s32[]{:S(2)}) async-start(), calls=%async_computation.2 | async-start | bytes 1572864 | tf_op jit(solution)/shard_map/psum | solution.py:419
  7.6 2.2 collective-permute-start.1
  8.5 1.3 collective-permute-start
  9.8 71.6 %collective-permute-start.2 = (bf16[256,128,128]{2,1,0:T(8,128)(2,1)}, bf16[256,128,128]{2,1,0:T(8,128)(2,1)}, u32[]{:S(2)}, u32[]{:S(2)}) collective-permute-start(bf16[256,128,128]{2,1,0:T(8,128)(2,1)} %bitcast.42), channel_id=1, source_target_pairs={{0,8},{8,0},{1,9},{9,1},{2,10},{10,2},{3,11},{11,3},{4,12},{12,4},... | collective-permute-start | bytes 25165832 | tf_op jit(solution)/shard_map/ppermute | solution.py:23
  10.1 71.3 %collective-permute-start.3 = (bf16[256,128,128]{2,1,0:T(8,128)(2,1)}, bf16[256,128,128]{2,1,0:T(8,128)(2,1)}, u32[]{:S(2)}, u32[]{:S(2)}) collective-permute-start(bf16[256,128,128]{2,1,0:T(8,128)(2,1)} %bitcast.47), channel_id=1, source_target_pairs={{0,8},{8,0},{1,9},{9,1},{2,10},{10,2},{3,11},{11,3},{4,12},{12,4},... | collective-permute-start | bytes 25165832 | tf_op jit(solution)/shard_map/ppermute | solution.py:23
  10.3 109.0 %collective-permute-start.7 = (bf16[256,128,128]{2,1,0:T(8,128)(2,1)}, bf16[256,128,128]{2,1,0:T(8,128)(2,1)}, u32[]{:S(2)}, u32[]{:S(2)}) collective-permute-start(bf16[256,128,128]{2,1,0:T(8,128)(2,1)} %bitcast.52), channel_id=1, source_target_pairs={{0,8},{8,0},{1,9},{9,1},{2,10},{10,2},{3,11},{11,3},{4,12},{12,4},... | collective-permute-start | bytes 25165832 | tf_op jit(solution)/shard_map/ppermute | solution.py:23
  12.6 64.2 %copy-start.24 = (bf16[1,8,4096]{2,1,0:T(8,128)(2,1)S(1)}, bf16[1,8,4096]{2,1,0:T(8,128)(2,1)}, u32[]{:S(2)}) copy-start(bf16[1,8,4096]{2,1,0:T(8,128)(2,1)} %param.31) | copy-start | bytes 196612
  12.6 64.1 %copy-start.25 = (bf16[1,8,4096]{2,1,0:T(8,128)(2,1)S(1)}, bf16[1,8,4096]{2,1,0:T(8,128)(2,1)}, u32[]{:S(2)}) copy-start(bf16[1,8,4096]{2,1,0:T(8,128)(2,1)} %param.28) | copy-start | bytes 196612
  12.7 64.1 %copy-start.26 = (bf16[1,8,4096]{2,1,0:T(8,128)(2,1)S(1)}, bf16[1,8,4096]{2,1,0:T(8,128)(2,1)}, u32[]{:S(2)}) copy-start(bf16[1,8,4096]{2,1,0:T(8,128)(2,1)} %param.26) | copy-start | bytes 196612
  12.7 64.1 %copy-start.28 = (bf16[1,4096]{1,0:T(2,128)(2,1)S(1)}, bf16[1,4096]{1,0:T(2,128)(2,1)}, u32[]{:S(2)}) copy-start(bf16[1,4096]{1,0:T(2,128)(2,1)} %param.18) | copy-start | bytes 24580
  13.5 80.1 %collective-permute-start.5 = (bf16[24,32,128]{2,0,1:T(8,128)(2,1)S(1)}, bf16[24,32,128]{2,0,1:T(8,128)(2,1)S(1)}, u32[]{:S(2)}, u32[]{:S(2)}) collective-permute-start(bf16[24,32,128]{2,0,1:T(8,128)(2,1)S(1)} %select_bitcast_fusion), channel_id=1, source_target_pairs={{0,8},{8,0},{1,9},{9,1},{2,10},{10,2},{3,11},{11,3},{4,12},{12,4},... | collective-permute-start | bytes 589832 | tf_op jit(solution)/shard_map/ppermute | solution.py:23
  14.1 64.2 %copy-start.16 = (bf16[48,1024]{1,0:T(8,128)(2,1)}, bf16[48,1024]{1,0:T(8,128)(2,1)S(1)}, u32[]{:S(2)}) copy-start(bf16[48,1024]{1,0:T(8,128)(2,1)S(1)} %get-tuple-element.70.refs_4_) | copy-start | bytes 294916
  14.1 64.2 %copy-start.17 = (bf16[48,1024]{1,0:T(8,128)(2,1)}, bf16[48,1024]{1,0:T(8,128)(2,1)S(1)}, u32[]{:S(2)}) copy-start(bf16[48,1024]{1,0:T(8,128)(2,1)S(1)} %get-tuple-element.69.refs_4_) | copy-start | bytes 294916
  92.5 11.1 %collective-permute-start.4 = (bf16[2,32,48,128]{3,2,1,0:T(8,128)(2,1)}, bf16[2,32,48,128]{3,2,1,0:T(8,128)(2,1)S(1)}, u32[]{:S(2)}, u32[]{:S(2)}) collective-permute-start(bf16[2,32,48,128]{3,2,1,0:T(8,128)(2,1)} %get-tuple-element.36), channel_id=1, source_target_pairs={{0,1},{1,0},{2,3},{3,2},{4,5},{5,4},{6,7},{7,6},{8,9},{9,8},{10,11... | collective-permute-start | bytes 2359304 | tf_op jit(solution)/shard_map/ppermute | solution.py:23
  106.1 13.2 %collective-permute-start.6 = (bf16[32,48,128]{2,1,0:T(8,128)(2,1)S(1)}, bf16[32,48,128]{2,1,0:T(8,128)(2,1)S(1)}, u32[]{:S(2)}, u32[]{:S(2)}) collective-permute-start(bf16[32,48,128]{2,1,0:T(8,128)(2,1)S(1)} %get-tuple-element.38.refs_0_), channel_id=1, source_target_pairs={{0,1},{1,0},{2,3},{3,2},{4,5},{5,4},{6,7},{7,6},{8,9},{9,8},{10,11... | collective-permute-start | bytes 1179656 | tf_op jit(solution)/shard_map/ppermute | solution.py:23
  118.3 15.3 %collective-permute-start.8 = (bf16[2,32,48,128]{3,2,1,0:T(8,128)(2,1)}, bf16[2,32,48,128]{3,2,1,0:T(8,128)(2,1)S(1)}, u32[]{:S(2)}, u32[]{:S(2)}) collective-permute-start(bf16[2,32,48,128]{3,2,1,0:T(8,128)(2,1)} %get-tuple-element.42), channel_id=1, source_target_pairs={{0,1},{1,0},{2,3},{3,2},{4,5},{5,4},{6,7},{7,6},{8,9},{9,8},{10,11... | collective-permute-start | bytes 2359304 | tf_op jit(solution)/shard_map/ppermute | solution.py:23
  120.1 13.6 %copy-start.8 = (f32[48,16]{1,0:T(8,128)S(1)}, f32[48,16]{1,0:T(8,128)}, u32[]{:S(2)}) copy-start(f32[48,16]{1,0:T(8,128)} %get-tuple-element.43.refs_2_) | copy-start | bytes 9220
  128.1 190.2 %all-reduce.9.cloned.1.call-start = ((), (), s32[]{:S(2)}) async-start(), calls=%async_computation.3 | async-start | bytes 1572864 | tf_op jit(solution)/shard_map/psum | solution.py:419
  136.7 97.8 %copy-start.5 = (bf16[32,48,128]{2,1,0:T(8,128)(2,1)}, bf16[32,48,128]{2,1,0:T(8,128)(2,1)S(1)}, u32[]{:S(2)}) copy-start(bf16[32,48,128]{2,1,0:T(8,128)(2,1)S(1)} %get-tuple-element.44.refs_0_) | copy-start | bytes 1179652
  136.7 98.6 %collective-permute-start.9 = (bf16[32,48,128]{2,1,0:T(8,128)(2,1)S(1)}, bf16[32,48,128]{2,1,0:T(8,128)(2,1)S(1)}, u32[]{:S(2)}, u32[]{:S(2)}) collective-permute-start(bf16[32,48,128]{2,1,0:T(8,128)(2,1)S(1)} %get-tuple-element.44.refs_0_), channel_id=1, source_target_pairs={{0,1},{1,0},{2,3},{3,2},{4,5},{5,4},{6,7},{7,6},{8,9},{9,8},{10,11... | collective-permute-start | bytes 1179656 | tf_op jit(solution)/shard_map/ppermute | solution.py:23
  234.5 18.1 %collective-permute-start.10 = (bf16[2,32,48,128]{3,2,1,0:T(8,128)(2,1)}, bf16[2,32,48,128]{3,2,1,0:T(8,128)(2,1)S(1)}, u32[]{:S(2)}, u32[]{:S(2)}) collective-permute-start(bf16[2,32,48,128]{3,2,1,0:T(8,128)(2,1)} %get-tuple-element.48), channel_id=1, source_target_pairs={{0,1},{1,0},{2,3},{3,2},{4,5},{5,4},{6,7},{7,6},{8,9},{9,8},{10,11... | collective-permute-start | bytes 2359304 | tf_op jit(solution)/shard_map/ppermute | solution.py:23
  236.0 16.6 %copy-start.10 = (f32[48,16]{1,0:T(8,128)S(1)}, f32[48,16]{1,0:T(8,128)}, u32[]{:S(2)}) copy-start(f32[48,16]{1,0:T(8,128)} %get-tuple-element.49.refs_2_) | copy-start | bytes 9220
  244.0 126.7 %reduce-scatter.3.cloned.1.call-start = ((), (), s32[]{:S(2)}) async-start(), calls=%async_computation.4 | async-start | bytes 983040 | tf_op jit(solution)/shard_map/reduce_scatter | solution.py:424
  255.0 7.8 %collective-permute-start.11 = (bf16[32,48,128]{2,1,0:T(8,128)(2,1)S(1)}, bf16[32,48,128]{2,1,0:T(8,128)(2,1)S(1)}, u32[]{:S(2)}, u32[]{:S(2)}) collective-permute-start(bf16[32,48,128]{2,1,0:T(8,128)(2,1)S(1)} %get-tuple-element.50.refs_0_), channel_id=1, source_target_pairs={{0,1},{1,0},{2,3},{3,2},{4,5},{5,4},{6,7},{7,6},{8,9},{9,8},{10,11... | collective-permute-start | bytes 1179656 | tf_op jit(solution)/shard_map/ppermute | solution.py:23
  271.5 122.2 %reduce-scatter.5.cloned.1.call-start = ((), (), s32[]{:S(2)}) async-start(), calls=%async_computation.5 | async-start | bytes 983040 | tf_op jit(solution)/shard_map/reduce_scatter | solution.py:424
  331.9 17.6 %collective-permute-start.13 = (bf16[2,32,48,128]{3,2,1,0:T(8,128)(2,1)}, bf16[2,32,48,128]{3,2,1,0:T(8,128)(2,1)S(1)}, u32[]{:S(2)}, u32[]{:S(2)}) collective-permute-start(bf16[2,32,48,128]{3,2,1,0:T(8,128)(2,1)} %get-tuple-element.53), channel_id=1, source_target_pairs={{0,1},{1,0},{2,3},{3,2},{4,5},{5,4},{6,7},{7,6},{8,9},{9,8},{10,11... | collective-permute-start | bytes 2359304 | tf_op jit(solution)/shard_map/ppermute | solution.py:23
  353.8 8.1 %collective-permute-start.14 = (bf16[32,48,128]{2,1,0:T(8,128)(2,1)S(1)}, bf16[32,48,128]{2,1,0:T(8,128)(2,1)S(1)}, u32[]{:S(2)}, u32[]{:S(2)}) collective-permute-start(bf16[32,48,128]{2,1,0:T(8,128)(2,1)S(1)} %get-tuple-element.55.refs_0_), channel_id=1, source_target_pairs={{0,1},{1,0},{2,3},{3,2},{4,5},{5,4},{6,7},{7,6},{8,9},{9,8},{10,11... | collective-permute-start | bytes 1179656 | tf_op jit(solution)/shard_map/ppermute | solution.py:23
  370.6 28.4 %copy-start.18 = (bf16[48,1024]{1,0:T(8,128)(2,1)S(1)}, bf16[48,1024]{1,0:T(8,128)(2,1)}, u32[]{:S(2)}) copy-start(bf16[48,1024]{1,0:T(8,128)(2,1)} %dynamic_slice.40.refs_4_) | copy-start | bytes 294916
  370.6 28.4 %copy-start.19 = (bf16[48,1024]{1,0:T(8,128)(2,1)S(1)}, bf16[48,1024]{1,0:T(8,128)(2,1)}, u32[]{:S(2)}) copy-start(bf16[48,1024]{1,0:T(8,128)(2,1)} %dynamic_slice.41.refs_4_) | copy-start | bytes 294916
  371.7 24.2 %collective-permute-start.12 = (bf16[48,1024]{1,0:T(8,128)(2,1)S(1)}, bf16[48,1024]{1,0:T(8,128)(2,1)S(1)}, u32[]{:S(2)}, u32[]{:S(2)}) collective-permute-start(bf16[48,1024]{1,0:T(8,128)(2,1)S(1)} %constant_dynamic-slice_fusion.1), channel_id=1, source_target_pairs={{0,1},{1,0},{2,3},{3,2},{4,5},{5,4},{6,7},{7,6},{8,9},{9,8},{10,11... | collective-permute-start | bytes 294920 | tf_op jit(solution)/shard_map/ppermute | solution.py:23
  394.6 3.5 collective-permute-start.15
  399.1 4.2 %collective-permute-start.16 = (bf16[96,1024]{1,0:T(8,128)(2,1)S(1)}, bf16[96,1024]{1,0:T(8,128)(2,1)S(1)}, u32[]{:S(2)}, u32[]{:S(2)}) collective-permute-start(bf16[96,1024]{1,0:T(8,128)(2,1)S(1)} %get-tuple-element.66), channel_id=1, source_target_pairs={{0,8},{8,0},{1,9},{9,1},{2,10},{10,2},{3,11},{11,3},{4,12},{12,4},... | collective-permute-start | bytes 589832 | tf_op jit(solution)/shard_map/ppermute | solution.py:23
  (21 other events, 126.7 us)
Sparse Core Ops, SparseCore 0:
  128.2 92.5 all-reduce.6
  244.2 74.0 all-reduce.8
  320.6 22.1 reduce-scatter.2
  370.8 22.8 reduce-scatter.4

commit v6 on v4

--- a/solution.py
+++ b/solution.py
@@ -11,7 +11,6 @@
 UNROLL = 16
 MIB = 1024 * 1024
 VMEM_LIMIT = 56 * MIB
-PIECES = 2
 SLOW = 4
 
 perturb_scale = 0.5
@@ -21,6 +20,12 @@
 def hop(value, axis, steps):
     count = lax.axis_size(axis)
     return lax.ppermute(value, axis, [(i, (i + steps) % count) for i in range(count)])
+
+
+def hop_within(section, value, axis, steps):
+    count = lax.axis_size(axis)
+    base = section * count
+    return lax.ppermute(value, ("section", axis), [(base + i, base + (i + steps) % count) for i in range(count)])
 
 
 def pick_matrix(row_member, member_seed, noise_count):
@@ -337,9 +342,15 @@
     block_rows = gate_left.shape[2] // BLOCK
     tile_count = gate_tiles.shape[1]
 
+    half = rows // 2
+    mine_rows = lax.dynamic_slice_in_dim(tokens, section_index * half, half)
+    others = [hop(mine_rows, "rep", g) for g in range(1, reps)]
+    stream = jnp.concatenate([mine_rows] + others, axis=0)
+
     codes = jnp.stack([gate_slot[0], up_slot[0], down_slot[0]])
     codes = lax.dynamic_slice_in_dim(codes, rep_index * tile_count, tile_count, axis=1)
     wide = jnp.concatenate([gate_left[0], up_left[0], down_right[0], norm_gain], axis=0)
+    codes, wide, stream = lax.optimization_barrier((codes, wide, stream))
     other_codes, other_wide = hop(codes, "section", 1), hop(wide, "section", 1)
     other_codes, other_wide, gate_tiles, up_tiles, down_tiles = lax.optimization_barrier(
         (other_codes, other_wide, gate_tiles, up_tiles, down_tiles)
@@ -382,9 +393,8 @@
 
     layers = [tables(section) for section in range(2)]
 
-    def layer(stream, picked, section):
+    def layer(blocks, picked, section):
         words, groups, left, right, gain, wide_cols, down_cols = layers[section]
-        blocks = [stream] + [hop(stream, "tensor", step) for step in range(1, owners)]
         raw, parts = expand(words, groups, blocks, gain, left, gate_pair, up_pair, own_cols, reps)
         parts = [parts[0]] + [hop(parts[g], "rep", -g) for g in range(1, reps)]
         hidden, coef = activate(parts, raw, picked, wide_cols, down_cols)
@@ -395,32 +405,29 @@
             summed = summed + hop(outs[step], "tensor", -step).astype(jnp.float32)
         return summed
 
-    half = rows // 2
-    mine_rows = lax.dynamic_slice_in_dim(tokens, section_index * half, half)
     mine_picks = lax.dynamic_slice_in_dim(picks, section_index * half, half)
-    others = [hop(mine_rows, "rep", g) for g in range(1, reps)]
-    piece = half // PIECES
-    firsts, seconds = [], []
-    for h in range(PIECES):
-        cut = slice(h * piece, (h + 1) * piece)
-        stream = jnp.concatenate([value[cut] for value in [mine_rows] + others], axis=0)
-        summed = layer(stream, mine_picks[cut], 0)
-        own = stream[:piece].astype(jnp.float32) + summed[:piece]
-        summed = jnp.concatenate([own, summed[piece:]], axis=0).astype(jnp.bfloat16)
-        total = summed.astype(jnp.float32)
-        for g in range(1, reps):
-            arrived = hop(summed, "rep", g).astype(jnp.float32)
-            total = total + jnp.roll(arrived, g * piece, axis=0)
-        stream = total.astype(jnp.bfloat16)
-        firsts.append(stream[:piece])
-        summed = layer(stream, mine_picks[cut], 1)
-        value = stream[:piece].astype(jnp.float32) + summed[:piece]
-        for g in range(1, reps):
-            sent = summed[g * piece : (g + 1) * piece].astype(jnp.bfloat16)
-            value = value + hop(sent, "rep", -g).astype(jnp.float32)
-        seconds.append(value.astype(jnp.bfloat16))
-    first = jnp.concatenate(firsts, axis=0)
-    second = jnp.concatenate(seconds, axis=0)
+    early = [hop_within(0, stream, "tensor", step) for step in range(1, owners)]
+    seen = early[-1][:16, :BLOCK] if owners > 1 else stream[:16, :BLOCK]
+    seen = lax.ppermute(seen, "section", [(0, 1)])
+    waiting = jnp.where(seen[0, 0] == seen[0, 0], stream, jnp.zeros_like(stream))
+    late = [hop_within(1, waiting, "tensor", step) for step in range(1, owners)]
+    blocks = [stream] + [jnp.where(section_index == 0, a, b) for a, b in zip(early, late)]
+    summed = layer(blocks, mine_picks, 0)
+    own = stream[:half].astype(jnp.float32) + summed[:half]
+    summed = jnp.concatenate([own, summed[half:]], axis=0).astype(jnp.bfloat16)
+    total = summed.astype(jnp.float32)
+    for g in range(1, reps):
+        arrived = hop(summed, "rep", g).astype(jnp.float32)
+        total = total + jnp.roll(arrived, g * half, axis=0)
+    stream = total.astype(jnp.bfloat16)
+    first = stream[:half]
+    blocks = [stream] + [hop(stream, "tensor", step) for step in range(1, owners)]
+    summed = layer(blocks, mine_picks, 1)
+    value = first.astype(jnp.float32) + summed[:half]
+    for g in range(1, reps):
+        sent = summed[g * half : (g + 1) * half].astype(jnp.bfloat16)
+        value = value + hop(sent, "rep", -g).astype(jnp.float32)
+    second = value.astype(jnp.bfloat16)
     kept = jnp.where(section_index == 0, first, second)
     received = hop(jnp.where(section_index == 0, second, first), "section", 1)
     out = jnp.where(

time: 279 us -> 355 us (1.27)
  waiting for transfers between devices: 87.7 us -> 216 us
  Pallas kernels: 97.6 us -> 57 us
  starting transfers between devices: 65.1 us -> 47.9 us
  local copies, waits for them, and re-layouts: 15.5 us -> 19.1 us
    ppermute x44 -> x23, waiting for transfers between devices: 87.7 us -> 188 us  [hop(): lax.ppermute(value, axis, [(i, (i + steps) % count) for i in range(count)])]
    ppermute x44 -> x23, starting transfers between devices: 65.1 us -> 34.7 us  [hop(): lax.ppermute(value, axis, [(i, (i + steps) % count) for i in range(count)])]
    ppermute x0 -> x7, waiting for transfers between devices: none -> 28.3 us  [the longest x6 18.9 us: hop_within(): lax.ppermute(value, ('section', axis), [(base + i, base + (i + steps) % c...]
    pallas_call x4 -> x2, Pallas kernels: 51.8 us -> 31 us  [expand(): pl.pallas_call(functools.partial(expand_kernel, owners, reps), out_shape=...]
    pallas_call x4 -> x2, Pallas kernels: 36.1 us -> 20.3 us  [contract(): pl.pallas_call(functools.partial(contract_kernel, owners, reps), out_shap...]
    ppermute x0 -> x7, starting transfers between devices: none -> 13.2 us  [the longest x6 11.9 us: hop_within(): lax.ppermute(value, ('section', axis), [(base + i, base + (i + steps) % c...]
    pallas_call x4 -> x2, Pallas kernels: 9.69 us -> 5.68 us  [activate(): pl.pallas_call(functools.partial(activate_kernel, reps), out_shape=[jax.S...]
  transfers between devices with their start and end apart: 44 -> 30, of which waited for: 18 -> 20; matrix products, arithmetic and copies ran while one was open for 7% -> 6% of each run, Pallas kernels for 35% -> 5%
where the time goes in v6:
time: 355 us
  waiting for transfers between devices  216 us (61%)
  Pallas kernels  57 us (16%)
  starting transfers between devices  47.9 us (13%)
  local copies, waits for them, and re-layouts  19.1 us (5%)
  other arithmetic  12.7 us (4%)
    ppermute x23, waiting for transfers between devices, hop(): lax.ppermute(value, axis, [(i, (i + steps) % count) for i in range(count)])  188 us
    ppermute x23, starting transfers between devices, hop(): lax.ppermute(value, axis, [(i, (i + steps) % count) for i in range(count)])  34.7 us
    pallas_call x2, Pallas kernels, expand(): pl.pallas_call(functools.partial(expand_kernel, owners, reps), out_shape=...  31 us
    pallas_call x2, Pallas kernels, contract(): pl.pallas_call(functools.partial(contract_kernel, owners, reps), out_shap...  20.3 us
    ppermute x6, waiting for transfers between devices, hop_within(): lax.ppermute(value, ('section', axis), [(base + i, base + (i + steps) % c...  18.9 us
    ppermute x6, starting transfers between devices, hop_within(): lax.ppermute(value, ('section', axis), [(base + i, base + (i + steps) % c...  11.9 us
    ppermute x1, waiting for transfers between devices, per_device(): seen = lax.ppermute(seen, 'section', [(0, 1)])  9.43 us
  transfers between devices with their start and end apart: 30, of which 20 were waited for; matrix products, arithmetic and copies ran while one was open for 6% of the time, Pallas kernels for 5%

profile of v6, /device:TPU:1, one launch (start us, length us, event | category | flops | bytes accessed | tf_op | source)
XLA Modules:
  0.0 354.8 jit_solution(6694435749679225122)
XLA Ops:
  1.0 2.1 collective-permute-start
  4.9 2.9 collective-permute-done
  13.4 7.1 %collective-permute-start.15 = (bf16[256,128,128]{2,1,0:T(8,128)(2,1)}, bf16[256,128,128]{2,1,0:T(8,128)(2,1)}, u32[]{:S(2)}, u32[]{:S(2)}) collective-permute-start(bf16[256,128,128]{2,1,0:T(8,128)(2,1)} %bitcast.70), channel_id=1, source_target_pairs={{0,8},{8,0},{1,9},{9,1},{2,10},{10,2},{3,11},{11,3},{4,12},{12,4},... | collective-permute-start | bytes 25165832 | tf_op jit(solution)/shard_map/ppermute | solution.py:22
  26.0 9.4 %collective-permute-done.5 = bf16[16,128]{1,0:T(8,128)(2,1)S(1)} collective-permute-done((bf16[16,128]{1,0:T(8,128)(2,1)S(1)}, bf16[16,128]{1,0:T(8,128)(2,1)S(1)}, u32[]{:S(2)}, u32[]{:S(2)}) %collective-permute-start.5) | collective-permute-done | bytes 4128 | tf_op jit(solution)/shard_map/ppermute | solution.py:411
  37.2 5.5 %collective-permute-start.9 = (bf16[192,1024]{1,0:T(8,128)(2,1)S(1)}, bf16[192,1024]{1,0:T(8,128)(2,1)S(1)}, u32[]{:S(2)}, u32[]{:S(2)}) collective-permute-start(bf16[192,1024]{1,0:T(8,128)(2,1)S(1)} %broadcast_select_fusion), channel_id=1, source_target_pairs={{8,14},{10,8},{12,10},{14,12},{9,15},{11,9},{13,11},{15,13},{24,30... | collective-permute-start | bytes 1179656 | tf_op jit(solution)/shard_map/ppermute | solution.py:28
  42.7 1.9 collective-permute-start.8
  47.3 1.7 collective-permute-done.9
  49.7 10.9 %collective-permute-done.8 = bf16[192,1024]{1,0:T(8,128)(2,1)S(1)} collective-permute-done((bf16[192,1024]{1,0:T(8,128)(2,1)S(1)}, bf16[192,1024]{1,0:T(8,128)(2,1)S(1)}, u32[]{:S(2)}, u32[]{:S(2)}) %collective-permute-start.8) | collective-permute-done | bytes 393248 | tf_op jit(solution)/shard_map/ppermute | solution.py:28
  60.6 2.5 collective-permute-start.6
  64.6 6.3 %collective-permute-done.6 = bf16[192,1024]{1,0:T(8,128)(2,1)S(1)} collective-permute-done((bf16[192,1024]{1,0:T(8,128)(2,1)S(1)}, bf16[192,1024]{1,0:T(8,128)(2,1)S(1)}, u32[]{:S(2)}, u32[]{:S(2)}) %collective-permute-start.6) | collective-permute-done | bytes 393248 | tf_op jit(solution)/shard_map/ppermute | solution.py:28
  71.7 15.1 %expand.2 = (f32[96,16]{1,0:T(8,128)}, bf16[2,32,96,128]{3,2,1,0:T(8,128)(2,1)}, bf16[2,32,96,128]{3,2,1,0:T(8,128)(2,1)}) custom-call(s32[864]{0:T(1024)} %reshape.509.words_ref, s32[4]{0:T(128)} %pad_add_fusion.1.groups_ref, bf16[192,1024]{1,0:T(8,128)(2,1)} %copy-done.10, bf16[192,1024]{1,0:T(8,128)(2,1)} %broadcast_select_fusion.3.refs_1_, ...), custom_call_target="tpu_custom_call" | custom-call | flops 12884901888 | bytes 16777216 | tf_op jit(solution)/shard_map/expand/pallas_call | solution.py:189
  87.6 1.7 gather_fusion
  91.9 25.2 %collective-permute-done.12.refs_1_ = bf16[2,32,96,128]{3,2,1,0:T(8,128)(2,1)S(1)} collective-permute-done((bf16[2,32,96,128]{3,2,1,0:T(8,128)(2,1)}, bf16[2,32,96,128]{3,2,1,0:T(8,128)(2,1)S(1)}, u32[]{:S(2)}, u32[]{:S(2)}) %collective-permute-start.12) | collective-permute-done | bytes 1572896 | tf_op jit(solution)/shard_map/ppermute | solution.py:22
  117.0 2.8 activate.2
  122.1 8.7 %collective-permute-done.14.refs_1_ = bf16[32,96,128]{2,1,0:T(8,128)(2,1)S(1)} collective-permute-done((bf16[32,96,128]{2,1,0:T(8,128)(2,1)S(1)}, bf16[32,96,128]{2,1,0:T(8,128)(2,1)S(1)}, u32[]{:S(2)}, u32[]{:S(2)}) %collective-permute-start.14) | collective-permute-done | bytes 786464 | tf_op jit(solution)/shard_map/ppermute | solution.py:22
  131.7 10.2 %contract.2 = (bf16[192,1024]{1,0:T(8,128)(2,1)}, bf16[192,1024]{1,0:T(8,128)(2,1)}, bf16[192,1024]{1,0:T(8,128)(2,1)}, bf16[192,1024]{1,0:T(8,128)(2,1)}) custom-call(s32[864]{0:T(1024)} %reshape.509.words_ref, s32[4]{0:T(128)} %pad_add_fusion.1.groups_ref, bf16[32,96,128]{2,1,0:T(8,128)(2,1)} %copy-done.6, bf16[32,96,128]{2,1,0:T(8,128)(2,1)} %copy-done.24, ...), custom_call_target="tpu_custom_call" | custom-call | flops 6442450944 | bytes 8388608 | tf_op jit(solution)/shard_map/contract/pallas_call | solution.py:305
  142.0 5.9 %collective-permute-start.17 = (bf16[192,1024]{1,0:T(8,128)(2,1)}, bf16[192,1024]{1,0:T(8,128)(2,1)S(1)}, u32[]{:S(2)}, u32[]{:S(2)}) collective-permute-start(bf16[192,1024]{1,0:T(8,128)(2,1)} %get-tuple-element.47), channel_id=1, source_target_pairs={{0,4},{2,6},{4,0},{6,2},{1,5},{3,7},{5,1},{7,3},{8,12},{10,14},{12... | collective-permute-start | bytes 1179656 | tf_op jit(solution)/shard_map/ppermute | solution.py:22
  150.4 27.4 %collective-permute-done.17 = bf16[192,1024]{1,0:T(8,128)(2,1)S(1)} collective-permute-done((bf16[192,1024]{1,0:T(8,128)(2,1)}, bf16[192,1024]{1,0:T(8,128)(2,1)S(1)}, u32[]{:S(2)}, u32[]{:S(2)}) %collective-permute-start.17) | collective-permute-done | bytes 393248 | tf_op jit(solution)/shard_map/ppermute | solution.py:22
  180.5 5.9 %collective-permute-done.19 = bf16[192,1024]{1,0:T(8,128)(2,1)S(1)} collective-permute-done((bf16[192,1024]{1,0:T(8,128)(2,1)S(1)}, bf16[192,1024]{1,0:T(8,128)(2,1)S(1)}, u32[]{:S(2)}, u32[]{:S(2)}) %collective-permute-start.19) | collective-permute-done | bytes 393248 | tf_op jit(solution)/shard_map/ppermute | solution.py:22
  186.6 2.1 collective-permute-start.21
  193.4 3.3 collective-permute-done.22.refs_3_
  196.7 26.6 %collective-permute-done.21.refs_2_ = bf16[192,1024]{1,0:T(8,128)(2,1)S(1)} collective-permute-done((bf16[192,1024]{1,0:T(8,128)(2,1)S(1)}, bf16[192,1024]{1,0:T(8,128)(2,1)S(1)}, u32[]{:S(2)}, u32[]{:S(2)}) %collective-permute-start.21) | collective-permute-done | bytes 393248 | tf_op jit(solution)/shard_map/ppermute | solution.py:22
  224.3 15.9 %expand.3 = (f32[96,16]{1,0:T(8,128)}, bf16[2,32,96,128]{3,2,1,0:T(8,128)(2,1)}, bf16[2,32,96,128]{3,2,1,0:T(8,128)(2,1)}) custom-call(s32[864]{0:T(1024)} %reshape.512.words_ref, s32[4]{0:T(128)} %pad_add_fusion.2.groups_ref, bf16[192,1024]{1,0:T(8,128)(2,1)} %copy-done.12, bf16[192,1024]{1,0:T(8,128)(2,1)} %copy-done.28, bf16[192,1024]{1,0:T(8,128)(2,1)} %copy-done.27, ...), custom_call_target="tpu_custom_call" | custom-call | flops 12884901888 | bytes 16777216 | tf_op jit(solution)/shard_map/expand/pallas_call | solution.py:189
  241.4 34.3 %collective-permute-done.23.refs_1_ = bf16[2,32,96,128]{3,2,1,0:T(8,128)(2,1)S(1)} collective-permute-done((bf16[2,32,96,128]{3,2,1,0:T(8,128)(2,1)}, bf16[2,32,96,128]{3,2,1,0:T(8,128)(2,1)S(1)}, u32[]{:S(2)}, u32[]{:S(2)}) %collective-permute-start.23) | collective-permute-done | bytes 1572896 | tf_op jit(solution)/shard_map/ppermute | solution.py:22
  278.0 2.8 activate.3
  282.1 1.5 slice.163
  283.6 14.9 %collective-permute-done.24.refs_1_ = bf16[32,96,128]{2,1,0:T(8,128)(2,1)S(1)} collective-permute-done((bf16[32,96,128]{2,1,0:T(8,128)(2,1)S(1)}, bf16[32,96,128]{2,1,0:T(8,128)(2,1)S(1)}, u32[]{:S(2)}, u32[]{:S(2)}) %collective-permute-start.24) | collective-permute-done | bytes 786464 | tf_op jit(solution)/shard_map/ppermute | solution.py:22
  299.4 10.2 %contract.3 = (bf16[192,1024]{1,0:T(8,128)(2,1)}, bf16[192,1024]{1,0:T(8,128)(2,1)}, bf16[192,1024]{1,0:T(8,128)(2,1)}, bf16[192,1024]{1,0:T(8,128)(2,1)}) custom-call(s32[864]{0:T(1024)} %reshape.512.words_ref, s32[4]{0:T(128)} %pad_add_fusion.2.groups_ref, bf16[32,96,128]{2,1,0:T(8,128)(2,1)} %copy-done.7, bf16[32,96,128]{2,1,0:T(8,128)(2,1)} %copy-done.25, ...), custom_call_target="tpu_custom_call" | custom-call | flops 6442450944 | bytes 8388608 | tf_op jit(solution)/shard_map/contract/pallas_call | solution.py:305
  311.5 7.0 %collective-permute-done.25 = bf16[192,1024]{1,0:T(8,128)(2,1)S(1)} collective-permute-done((bf16[192,1024]{1,0:T(8,128)(2,1)}, bf16[192,1024]{1,0:T(8,128)(2,1)S(1)}, u32[]{:S(2)}, u32[]{:S(2)}) %collective-permute-start.25) | collective-permute-done | bytes 393248 | tf_op jit(solution)/shard_map/ppermute | solution.py:22
  318.6 24.0 %collective-permute-done.26 = bf16[192,1024]{1,0:T(8,128)(2,1)S(1)} collective-permute-done((bf16[192,1024]{1,0:T(8,128)(2,1)}, bf16[192,1024]{1,0:T(8,128)(2,1)S(1)}, u32[]{:S(2)}, u32[]{:S(2)}) %collective-permute-start.26) | collective-permute-done | bytes 393248 | tf_op jit(solution)/shard_map/ppermute | solution.py:22
  345.2 3.3 collective-permute-done.28
  348.7 4.2 %collective-permute-start.29 = (bf16[96,1024]{1,0:T(8,128)(2,1)S(1)}, bf16[96,1024]{1,0:T(8,128)(2,1)S(1)}, u32[]{:S(2)}, u32[]{:S(2)}) collective-permute-start(bf16[96,1024]{1,0:T(8,128)(2,1)S(1)} %broadcast_select_fusion.8), channel_id=1, source_target_pairs={{0,8},{8,0},{1,9},{9,1},{2,10},{10,2},{3,11},{11,3},{4,12},{12,4},... | collective-permute-start | bytes 589832 | tf_op jit(solution)/shard_map/ppermute | solution.py:22
  (166 shorter events, 49.6 us)
Async XLA Ops:
  1.0 6.7 %collective-permute-start = (bf16[96,1024]{1,0:T(8,128)(2,1)S(1)}, bf16[96,1024]{1,0:T(8,128)(2,1)S(1)}, u32[]{:S(2)}, u32[]{:S(2)}) collective-permute-start(bf16[96,1024]{1,0:T(8,128)(2,1)S(1)} %constant_dynamic-slice_fusion.1), channel_id=1, source_target_pairs={{0,1},{1,0},{2,3},{3,2},{4,5},{5,4},{6,7},{7,6},{8,9},{9,8},{10,11... | collective-permute-start | bytes 589832 | tf_op jit(solution)/shard_map/ppermute | solution.py:22
  7.8 41.2 %copy-start.10 = (bf16[192,1024]{1,0:T(8,128)(2,1)}, bf16[192,1024]{1,0:T(8,128)(2,1)S(1)}, u32[]{:S(2)}) copy-start(bf16[192,1024]{1,0:T(8,128)(2,1)S(1)} %pad_maximum_fusion.1.refs_0_) | copy-start | bytes 1179652
  7.8 2.5 collective-permute-start.2
  9.1 1.2 collective-permute-start.1
  10.3 61.4 %collective-permute-start.10 = (bf16[256,128,128]{2,1,0:T(8,128)(2,1)}, bf16[256,128,128]{2,1,0:T(8,128)(2,1)}, u32[]{:S(2)}, u32[]{:S(2)}) collective-permute-start(bf16[256,128,128]{2,1,0:T(8,128)(2,1)} %bitcast.64), channel_id=1, source_target_pairs={{0,8},{8,0},{1,9},{9,1},{2,10},{10,2},{3,11},{11,3},{4,12},{12,4},... | collective-permute-start | bytes 25165832 | tf_op jit(solution)/shard_map/ppermute | solution.py:22
  10.6 61.1 %collective-permute-start.11 = (bf16[256,128,128]{2,1,0:T(8,128)(2,1)}, bf16[256,128,128]{2,1,0:T(8,128)(2,1)}, u32[]{:S(2)}, u32[]{:S(2)}) collective-permute-start(bf16[256,128,128]{2,1,0:T(8,128)(2,1)} %bitcast.67), channel_id=1, source_target_pairs={{0,8},{8,0},{1,9},{9,1},{2,10},{10,2},{3,11},{11,3},{4,12},{12,4},... | collective-permute-start | bytes 25165832 | tf_op jit(solution)/shard_map/ppermute | solution.py:22
  12.0 30.7 %collective-permute-start.7 = (bf16[192,1024]{1,0:T(8,128)(2,1)S(1)}, bf16[192,1024]{1,0:T(8,128)(2,1)S(1)}, u32[]{:S(2)}, u32[]{:S(2)}) collective-permute-start(bf16[192,1024]{1,0:T(8,128)(2,1)S(1)} %pad_maximum_fusion.1.refs_0_), channel_id=1, source_target_pairs={{0,4},{2,6},{4,0},{6,2},{1,5},{3,7},{5,1},{7,3},{16,20},{18,22},{2... | collective-permute-start | bytes 1179656 | tf_op jit(solution)/shard_map/ppermute | solution.py:28
  12.7 12.0 %collective-permute-start.4 = (bf16[192,1024]{1,0:T(8,128)(2,1)S(1)}, bf16[192,1024]{1,0:T(8,128)(2,1)S(1)}, u32[]{:S(2)}, u32[]{:S(2)}) collective-permute-start(bf16[192,1024]{1,0:T(8,128)(2,1)S(1)} %pad_maximum_fusion.1.refs_0_), channel_id=1, source_target_pairs={{0,6},{2,0},{4,2},{6,4},{1,7},{3,1},{5,3},{7,5},{16,22},{18,16},{2... | collective-permute-start | bytes 1179656 | tf_op jit(solution)/shard_map/ppermute | solution.py:28
  13.4 108.7 %collective-permute-start.15 = (bf16[256,128,128]{2,1,0:T(8,128)(2,1)}, bf16[256,128,128]{2,1,0:T(8,128)(2,1)}, u32[]{:S(2)}, u32[]{:S(2)}) collective-permute-start(bf16[256,128,128]{2,1,0:T(8,128)(2,1)} %bitcast.70), channel_id=1, source_target_pairs={{0,8},{8,0},{1,9},{9,1},{2,10},{10,2},{3,11},{11,3},{4,12},{12,4},... | collective-permute-start | bytes 25165832 | tf_op jit(solution)/shard_map/ppermute | solution.py:22
  24.7 10.7 %collective-permute-start.5 = (bf16[16,128]{1,0:T(8,128)(2,1)S(1)}, bf16[16,128]{1,0:T(8,128)(2,1)S(1)}, u32[]{:S(2)}, u32[]{:S(2)}) collective-permute-start(bf16[16,128]{1,0:T(8,128)(2,1)S(1)} %slice.145), channel_id=1, source_target_pairs={{0,8},{1,9},{2,10},{3,11},{4,12},{5,13},{6,14},{7,15},{16,24},{17,... | collective-permute-start | bytes 12296 | tf_op jit(solution)/shard_map/ppermute | solution.py:411
  37.2 11.7 %collective-permute-start.9 = (bf16[192,1024]{1,0:T(8,128)(2,1)S(1)}, bf16[192,1024]{1,0:T(8,128)(2,1)S(1)}, u32[]{:S(2)}, u32[]{:S(2)}) collective-permute-start(bf16[192,1024]{1,0:T(8,128)(2,1)S(1)} %broadcast_select_fusion), channel_id=1, source_target_pairs={{8,14},{10,8},{12,10},{14,12},{9,15},{11,9},{13,11},{15,13},{24,30... | collective-permute-start | bytes 1179656 | tf_op jit(solution)/shard_map/ppermute | solution.py:28
  42.7 17.8 %collective-permute-start.8 = (bf16[192,1024]{1,0:T(8,128)(2,1)S(1)}, bf16[192,1024]{1,0:T(8,128)(2,1)S(1)}, u32[]{:S(2)}, u32[]{:S(2)}) collective-permute-start(bf16[192,1024]{1,0:T(8,128)(2,1)S(1)} %broadcast_select_fusion), channel_id=1, source_target_pairs={{8,12},{10,14},{12,8},{14,10},{9,13},{11,15},{13,9},{15,11},{24,28... | collective-permute-start | bytes 1179656 | tf_op jit(solution)/shard_map/ppermute | solution.py:28
  49.0 15.7 %collective-permute-start.3 = (bf16[192,1024]{1,0:T(8,128)(2,1)S(1)}, bf16[192,1024]{1,0:T(8,128)(2,1)S(1)}, u32[]{:S(2)}, u32[]{:S(2)}) collective-permute-start(bf16[192,1024]{1,0:T(8,128)(2,1)S(1)} %pad_maximum_fusion.1.refs_0_), channel_id=1, source_target_pairs={{0,2},{2,4},{4,6},{6,0},{1,3},{3,5},{5,7},{7,1},{16,18},{18,20},{2... | collective-permute-start | bytes 1179656 | tf_op jit(solution)/shard_map/ppermute | solution.py:28
  60.6 10.3 %collective-permute-start.6 = (bf16[192,1024]{1,0:T(8,128)(2,1)S(1)}, bf16[192,1024]{1,0:T(8,128)(2,1)S(1)}, u32[]{:S(2)}, u32[]{:S(2)}) collective-permute-start(bf16[192,1024]{1,0:T(8,128)(2,1)S(1)} %broadcast_select_fusion), channel_id=1, source_target_pairs={{8,10},{10,12},{12,14},{14,8},{9,11},{11,13},{13,15},{15,9},{24,26... | collective-permute-start | bytes 1179656 | tf_op jit(solution)/shard_map/ppermute | solution.py:28
  86.9 30.2 %collective-permute-start.12 = (bf16[2,32,96,128]{3,2,1,0:T(8,128)(2,1)}, bf16[2,32,96,128]{3,2,1,0:T(8,128)(2,1)S(1)}, u32[]{:S(2)}, u32[]{:S(2)}) collective-permute-start(bf16[2,32,96,128]{3,2,1,0:T(8,128)(2,1)} %get-tuple-element.40), channel_id=1, source_target_pairs={{0,1},{1,0},{2,3},{3,2},{4,5},{5,4},{6,7},{7,6},{8,9},{9,8},{10,11... | collective-permute-start | bytes 4718600 | tf_op jit(solution)/shard_map/ppermute | solution.py:22
  89.5 1.5 collective-permute-start.13
  119.9 10.9 %collective-permute-start.14 = (bf16[32,96,128]{2,1,0:T(8,128)(2,1)S(1)}, bf16[32,96,128]{2,1,0:T(8,128)(2,1)S(1)}, u32[]{:S(2)}, u32[]{:S(2)}) collective-permute-start(bf16[32,96,128]{2,1,0:T(8,128)(2,1)S(1)} %get-tuple-element.42.refs_0_), channel_id=1, source_target_pairs={{0,1},{1,0},{2,3},{3,2},{4,5},{5,4},{6,7},{7,6},{8,9},{9,8},{10,11... | collective-permute-start | bytes 2359304 | tf_op jit(solution)/shard_map/ppermute | solution.py:22
  141.9 8.5 %collective-permute-start.16 = (bf16[192,1024]{1,0:T(8,128)(2,1)}, bf16[192,1024]{1,0:T(8,128)(2,1)S(1)}, u32[]{:S(2)}, u32[]{:S(2)}) collective-permute-start(bf16[192,1024]{1,0:T(8,128)(2,1)} %get-tuple-element.46), channel_id=1, source_target_pairs={{0,6},{2,0},{4,2},{6,4},{1,7},{3,1},{5,3},{7,5},{8,14},{10,8},{12,... | collective-permute-start | bytes 1179656 | tf_op jit(solution)/shard_map/ppermute | solution.py:22
  142.0 35.9 %collective-permute-start.17 = (bf16[192,1024]{1,0:T(8,128)(2,1)}, bf16[192,1024]{1,0:T(8,128)(2,1)S(1)}, u32[]{:S(2)}, u32[]{:S(2)}) collective-permute-start(bf16[192,1024]{1,0:T(8,128)(2,1)} %get-tuple-element.47), channel_id=1, source_target_pairs={{0,4},{2,6},{4,0},{6,2},{1,5},{3,7},{5,1},{7,3},{8,12},{10,14},{12... | collective-permute-start | bytes 1179656 | tf_op jit(solution)/shard_map/ppermute | solution.py:22
  147.9 29.9 %collective-permute-start.18 = (bf16[192,1024]{1,0:T(8,128)(2,1)}, bf16[192,1024]{1,0:T(8,128)(2,1)S(1)}, u32[]{:S(2)}, u32[]{:S(2)}) collective-permute-start(bf16[192,1024]{1,0:T(8,128)(2,1)} %get-tuple-element.48), channel_id=1, source_target_pairs={{0,2},{2,4},{4,6},{6,0},{1,3},{3,5},{5,7},{7,1},{8,10},{10,12},{12... | collective-permute-start | bytes 1179656 | tf_op jit(solution)/shard_map/ppermute | solution.py:22
  179.2 7.1 %collective-permute-start.19 = (bf16[192,1024]{1,0:T(8,128)(2,1)S(1)}, bf16[192,1024]{1,0:T(8,128)(2,1)S(1)}, u32[]{:S(2)}, u32[]{:S(2)}) collective-permute-start(bf16[192,1024]{1,0:T(8,128)(2,1)S(1)} %pad_maximum_fusion.2), channel_id=1, source_target_pairs={{0,1},{1,0},{2,3},{3,2},{4,5},{5,4},{6,7},{7,6},{8,9},{9,8},{10,11... | collective-permute-start | bytes 1179656 | tf_op jit(solution)/shard_map/ppermute | solution.py:22
  186.5 10.2 %collective-permute-start.22 = (bf16[192,1024]{1,0:T(8,128)(2,1)S(1)}, bf16[192,1024]{1,0:T(8,128)(2,1)S(1)}, u32[]{:S(2)}, u32[]{:S(2)}) collective-permute-start(bf16[192,1024]{1,0:T(8,128)(2,1)S(1)} %fusion.refs_0_), channel_id=1, source_target_pairs={{0,6},{2,0},{4,2},{6,4},{1,7},{3,1},{5,3},{7,5},{8,14},{10,8},{12,... | collective-permute-start | bytes 1179656 | tf_op jit(solution)/shard_map/ppermute | solution.py:22
  186.6 36.7 %collective-permute-start.21 = (bf16[192,1024]{1,0:T(8,128)(2,1)S(1)}, bf16[192,1024]{1,0:T(8,128)(2,1)S(1)}, u32[]{:S(2)}, u32[]{:S(2)}) collective-permute-start(bf16[192,1024]{1,0:T(8,128)(2,1)S(1)} %fusion.refs_0_), channel_id=1, source_target_pairs={{0,4},{2,6},{4,0},{6,2},{1,5},{3,7},{5,1},{7,3},{8,12},{10,14},{12... | collective-permute-start | bytes 1179656 | tf_op jit(solution)/shard_map/ppermute | solution.py:22
  188.7 34.7 %collective-permute-start.20 = (bf16[192,1024]{1,0:T(8,128)(2,1)S(1)}, bf16[192,1024]{1,0:T(8,128)(2,1)S(1)}, u32[]{:S(2)}, u32[]{:S(2)}) collective-permute-start(bf16[192,1024]{1,0:T(8,128)(2,1)S(1)} %fusion.refs_0_), channel_id=1, source_target_pairs={{0,2},{2,4},{4,6},{6,0},{1,3},{3,5},{5,7},{7,1},{8,10},{10,12},{12... | collective-permute-start | bytes 1179656 | tf_op jit(solution)/shard_map/ppermute | solution.py:22
  240.1 35.6 %collective-permute-start.23 = (bf16[2,32,96,128]{3,2,1,0:T(8,128)(2,1)}, bf16[2,32,96,128]{3,2,1,0:T(8,128)(2,1)S(1)}, u32[]{:S(2)}, u32[]{:S(2)}) collective-permute-start(bf16[2,32,96,128]{3,2,1,0:T(8,128)(2,1)} %get-tuple-element.50), channel_id=1, source_target_pairs={{0,1},{1,0},{2,3},{3,2},{4,5},{5,4},{6,7},{7,6},{8,9},{9,8},{10,11... | collective-permute-start | bytes 4718600 | tf_op jit(solution)/shard_map/ppermute | solution.py:22
  280.8 17.6 %collective-permute-start.24 = (bf16[32,96,128]{2,1,0:T(8,128)(2,1)S(1)}, bf16[32,96,128]{2,1,0:T(8,128)(2,1)S(1)}, u32[]{:S(2)}, u32[]{:S(2)}) collective-permute-start(bf16[32,96,128]{2,1,0:T(8,128)(2,1)S(1)} %get-tuple-element.52.refs_0_), channel_id=1, source_target_pairs={{0,1},{1,0},{2,3},{3,2},{4,5},{5,4},{6,7},{7,6},{8,9},{9,8},{10,11... | collective-permute-start | bytes 2359304 | tf_op jit(solution)/shard_map/ppermute | solution.py:22
  309.5 39.0 %copy-start.13 = (bf16[192,1024]{1,0:T(8,128)(2,1)S(1)}, bf16[192,1024]{1,0:T(8,128)(2,1)}, u32[]{:S(2)}) copy-start(bf16[192,1024]{1,0:T(8,128)(2,1)} %copy-done.12) | copy-start | bytes 1179652
  309.6 9.0 %collective-permute-start.25 = (bf16[192,1024]{1,0:T(8,128)(2,1)}, bf16[192,1024]{1,0:T(8,128)(2,1)S(1)}, u32[]{:S(2)}, u32[]{:S(2)}) collective-permute-start(bf16[192,1024]{1,0:T(8,128)(2,1)} %get-tuple-element.55), channel_id=1, source_target_pairs={{0,6},{2,0},{4,2},{6,4},{1,7},{3,1},{5,3},{7,5},{8,14},{10,8},{12,... | collective-permute-start | bytes 1179656 | tf_op jit(solution)/shard_map/ppermute | solution.py:22
  309.6 33.0 %collective-permute-start.26 = (bf16[192,1024]{1,0:T(8,128)(2,1)}, bf16[192,1024]{1,0:T(8,128)(2,1)S(1)}, u32[]{:S(2)}, u32[]{:S(2)}) collective-permute-start(bf16[192,1024]{1,0:T(8,128)(2,1)} %get-tuple-element.56), channel_id=1, source_target_pairs={{0,4},{2,6},{4,0},{6,2},{1,5},{3,7},{5,1},{7,3},{8,12},{10,14},{12... | collective-permute-start | bytes 1179656 | tf_op jit(solution)/shard_map/ppermute | solution.py:22
  310.1 32.5 %collective-permute-start.27 = (bf16[192,1024]{1,0:T(8,128)(2,1)}, bf16[192,1024]{1,0:T(8,128)(2,1)S(1)}, u32[]{:S(2)}, u32[]{:S(2)}) collective-permute-start(bf16[192,1024]{1,0:T(8,128)(2,1)} %get-tuple-element.57), channel_id=1, source_target_pairs={{0,2},{2,4},{4,6},{6,0},{1,3},{3,5},{5,7},{7,1},{8,10},{10,12},{12... | collective-permute-start | bytes 1179656 | tf_op jit(solution)/shard_map/ppermute | solution.py:22
  343.9 4.6 %collective-permute-start.28 = (bf16[96,1024]{1,0:T(8,128)(2,1)S(1)}, bf16[96,1024]{1,0:T(8,128)(2,1)S(1)}, u32[]{:S(2)}, u32[]{:S(2)}) collective-permute-start(bf16[96,1024]{1,0:T(8,128)(2,1)S(1)} %slice.190), channel_id=1, source_target_pairs={{0,1},{1,0},{2,3},{3,2},{4,5},{5,4},{6,7},{7,6},{8,9},{9,8},{10,11... | collective-permute-start | bytes 589832 | tf_op jit(solution)/shard_map/ppermute | solution.py:22
  348.7 5.3 %collective-permute-start.29 = (bf16[96,1024]{1,0:T(8,128)(2,1)S(1)}, bf16[96,1024]{1,0:T(8,128)(2,1)S(1)}, u32[]{:S(2)}, u32[]{:S(2)}) collective-permute-start(bf16[96,1024]{1,0:T(8,128)(2,1)S(1)} %broadcast_select_fusion.8), channel_id=1, source_target_pairs={{0,8},{8,0},{1,9},{9,1},{2,10},{10,2},{3,11},{11,3},{4,12},{12,4},... | collective-permute-start | bytes 589832 | tf_op jit(solution)/shard_map/ppermute | solution.py:22
  (28 other events, 403.3 us)

commit v7 on v4

--- a/solution.py
+++ b/solution.py
@@ -11,7 +11,6 @@
 UNROLL = 16
 MIB = 1024 * 1024
 VMEM_LIMIT = 56 * MIB
-PIECES = 2
 SLOW = 4
 
 perturb_scale = 0.5
@@ -96,34 +95,40 @@
 
 
 def expand_kernel(owners, reps, words_ref, groups_ref, *refs):
-    blocks = refs[:owners]
-    gain_ref, left_ref, own_gate, other_gate, own_up, other_up, raw_ref = refs[owners : owners + 7]
-    part_refs = refs[owners + 7 : owners + 7 + reps]
-    total_ref, gate_tiles, gate_sem, up_tiles, up_sem, x_ref = refs[owners + 7 + reps :]
-    all_rows, width = blocks[0].shape
-    rows = all_rows // reps
+    spans = len(refs) - 13 - reps
+    blocks = refs[:spans]
+    gain_ref, left_ref, own_gate, other_gate, own_up, other_up, raw_ref = refs[spans : spans + 7]
+    part_refs = refs[spans + 7 : spans + 7 + reps]
+    total_ref, gate_tiles, gate_sem, up_tiles, up_sem, x_ref = refs[spans + 7 + reps :]
+    span_rows, width = blocks[0].shape
+    split = spans // owners
+    rows = part_refs[0].shape[2]
     per_owner = width // BLOCK
-    strip = 48 if all_rows % 48 == 0 else 16
+    strip = 48 if rows % 48 == 0 else 16
     gate_copy = load_tiles(groups_ref[3], (own_gate, other_gate), gate_tiles, gate_sem)
     up_copy = load_tiles(groups_ref[3], (own_up, other_up), up_tiles, up_sem)
 
-    def norm_rows(i, carry):
-        at = pl.ds(pl.multiple_of(i * strip, strip), strip)
-        squares = jnp.zeros((strip, BLOCK), jnp.float32)
-        for owner in range(owners):
-            for part in range(per_owner):
-                values = blocks[owner][at, pl.ds(part * BLOCK, BLOCK)].astype(jnp.float32)
-                squares = squares + values * values
-        total = jnp.sum(squares, axis=1, keepdims=True)
-        inverse = lax.rsqrt(total / (owners * width) + epsilon)
-        for owner in range(owners):
-            for part in range(per_owner):
-                values = blocks[owner][at, pl.ds(part * BLOCK, BLOCK)].astype(jnp.float32)
-                gain = gain_ref[:, pl.ds(owner * width + part * BLOCK, BLOCK)].astype(jnp.float32)
-                x_ref[owner * per_owner + part, at, :] = (values * inverse * gain).astype(jnp.bfloat16)
-        return carry
-
-    lax.fori_loop(0, all_rows // strip, norm_rows, 0)
+    for span in range(split):
+
+        def norm_rows(i, carry, span=span):
+            start = pl.multiple_of(i * strip, strip)
+            at = pl.ds(start, strip)
+            squares = jnp.zeros((strip, BLOCK), jnp.float32)
+            for owner in range(owners):
+                for part in range(per_owner):
+                    values = blocks[owner * split + span][at, pl.ds(part * BLOCK, BLOCK)].astype(jnp.float32)
+                    squares = squares + values * values
+            total = jnp.sum(squares, axis=1, keepdims=True)
+            inverse = lax.rsqrt(total / (owners * width) + epsilon)
+            for owner in range(owners):
+                for part in range(per_owner):
+                    values = blocks[owner * split + span][at, pl.ds(part * BLOCK, BLOCK)].astype(jnp.float32)
+                    gain = gain_ref[:, pl.ds(owner * width + part * BLOCK, BLOCK)].astype(jnp.float32)
+                    normed = (values * inverse * gain).astype(jnp.bfloat16)
+                    x_ref[owner * per_owner + part, pl.ds(span * span_rows + start, strip), :] = normed
+            return carry
+
+        lax.fori_loop(0, span_rows // strip, norm_rows, 0)
     raw = jnp.zeros(raw_ref.shape, jnp.float32)
     step = min(8, x_ref.shape[0])
     for d in range(0, x_ref.shape[0], step):
@@ -176,8 +181,9 @@
 
 
 def expand(words, groups, blocks, gain, left, gate_tiles, up_tiles, own_cols, reps):
-    owners = len(blocks)
-    all_rows, width = blocks[0].shape
+    features = gain.shape[1]
+    owners = features // blocks[0].shape[1]
+    all_rows = sum(block.size for block in blocks) // features
     rows = all_rows // reps
     tile_count = gate_tiles[0].shape[0]
     scratch = tile_scratch(tile_count, own_cols, all_rows)
@@ -185,11 +191,11 @@
         functools.partial(expand_kernel, owners, reps),
         out_shape=[jax.ShapeDtypeStruct((rows, left.shape[0]), jnp.float32)]
         + [jax.ShapeDtypeStruct((2, own_cols, rows, BLOCK), jnp.bfloat16)] * reps,
-        in_specs=[SMEM, SMEM] + [VMEM] * (owners + 2) + [HBM] * 4,
+        in_specs=[SMEM, SMEM] + [VMEM] * (len(blocks) + 2) + [HBM] * 4,
         out_specs=[VMEM] * (1 + reps),
         scratch_shapes=scratch
         + scratch[1:]
-        + [pltpu.VMEM((owners * width // BLOCK, all_rows, BLOCK), jnp.bfloat16)],
+        + [pltpu.VMEM((features // BLOCK, all_rows, BLOCK), jnp.bfloat16)],
         compiler_params=pltpu.CompilerParams(vmem_limit_bytes=VMEM_LIMIT),
         cost_estimate=tile_cost(2 * tile_count, all_rows),
         name="expand",
@@ -199,7 +205,8 @@
 
 def activate_kernel(reps, *refs):
     parts = refs[:reps]
-    raw_ref, picks_ref, wide_cols, down_cols, hidden_ref, coef_ref = refs[reps:]
+    raw_ref, picks_ref, wide_cols, down_cols = refs[reps : reps + 4]
+    hidden_ref, coef_ref = refs[-2:]
     noise = picks_ref.shape[1]
     columns, rows = hidden_ref.shape[:2]
     picks = picks_ref[...]
@@ -233,7 +240,7 @@
     coef_ref[...] = picks * down
 
 
-def activate(parts, raw, picks, wide_cols, down_cols):
+def activate(parts, raw, picks, wide_cols, down_cols, after):
     own_cols, rows = parts[0].shape[1:3]
     noise = picks.shape[1]
     reps = len(parts)
@@ -243,7 +250,7 @@
             jax.ShapeDtypeStruct((own_cols, rows, BLOCK), jnp.bfloat16),
             jax.ShapeDtypeStruct((rows, noise), jnp.float32),
         ],
-        in_specs=[VMEM] * (reps + 4),
+        in_specs=[VMEM] * (reps + 4) + [HBM] * len(after),
         out_specs=[VMEM] * 2,
         compiler_params=pltpu.CompilerParams(vmem_limit_bytes=16 * MIB),
         cost_estimate=pl.CostEstimate(
@@ -252,7 +259,7 @@
             transcendentals=own_cols * rows * BLOCK,
         ),
         name="activate",
-    )(*parts, raw, picks, wide_cols, down_cols)
+    )(*parts, raw, picks, wide_cols, down_cols, *after)
 
 
 def contract_kernel(owners, reps, words_ref, groups_ref, *refs):
@@ -337,6 +344,18 @@
     block_rows = gate_left.shape[2] // BLOCK
     tile_count = gate_tiles.shape[1]
 
+    half = rows // 2
+    piece = half // 2
+    mine_rows = lax.dynamic_slice_in_dim(tokens, section_index * half, half)
+    others = [hop(mine_rows, "rep", g) for g in range(1, reps)]
+
+    def gather(value):
+        return [hop(value, "tensor", step) for step in range(1, owners)]
+
+    first_spans = [value[:piece] for value in [mine_rows] + others]
+    first_blocks = [[span] + gather(span) for span in first_spans]
+    first_blocks = [first_blocks[g][step] for step in range(owners) for g in range(reps)]
+
     codes = jnp.stack([gate_slot[0], up_slot[0], down_slot[0]])
     codes = lax.dynamic_slice_in_dim(codes, rep_index * tile_count, tile_count, axis=1)
     wide = jnp.concatenate([gate_left[0], up_left[0], down_right[0], norm_gain], axis=0)
@@ -382,45 +401,67 @@
 
     layers = [tables(section) for section in range(2)]
 
-    def layer(stream, picked, section):
-        words, groups, left, right, gain, wide_cols, down_cols = layers[section]
-        blocks = [stream] + [hop(stream, "tensor", step) for step in range(1, owners)]
-        raw, parts = expand(words, groups, blocks, gain, left, gate_pair, up_pair, own_cols, reps)
-        parts = [parts[0]] + [hop(parts[g], "rep", -g) for g in range(1, reps)]
-        hidden, coef = activate(parts, raw, picked, wide_cols, down_cols)
-        hiddens = [hidden] + [hop(hidden, "rep", g) for g in range(1, reps)]
-        outs = contract(words, groups, hiddens, coef, right, down_pair, owners)
+    def expanded(blocks, section):
+        words, groups, left, _, gain, _, _ = layers[section]
+        return expand(words, groups, blocks, gain, left, gate_pair, up_pair, own_cols, reps)
+
+    def activated(parts, raw, picked, section, after=()):
+        wide_cols, down_cols = layers[section][5:]
+        received = [hop(part, "rep", -(g + 1)) for g, part in enumerate(parts[1:])]
+        hidden, coef = activate([parts[0]] + received, raw, picked, wide_cols, down_cols, after)
+        return coef, hidden, [hop(hidden, "rep", g) for g in range(1, reps)]
+
+    def contracted(coef, hidden, received, section):
+        words, groups, _, right, _, _, _ = layers[section]
+        return contract(words, groups, [hidden] + received, coef, right, down_pair, owners)
+
+    def scattered(outs):
         summed = outs[0].astype(jnp.float32)
         for step in range(1, owners):
             summed = summed + hop(outs[step], "tensor", -step).astype(jnp.float32)
         return summed
 
-    half = rows // 2
-    mine_rows = lax.dynamic_slice_in_dim(tokens, section_index * half, half)
-    mine_picks = lax.dynamic_slice_in_dim(picks, section_index * half, half)
-    others = [hop(mine_rows, "rep", g) for g in range(1, reps)]
-    piece = half // PIECES
-    firsts, seconds = [], []
-    for h in range(PIECES):
-        cut = slice(h * piece, (h + 1) * piece)
-        stream = jnp.concatenate([value[cut] for value in [mine_rows] + others], axis=0)
-        summed = layer(stream, mine_picks[cut], 0)
-        own = stream[:piece].astype(jnp.float32) + summed[:piece]
+    def streamed(own_rows, summed):
+        own = own_rows.astype(jnp.float32) + summed[:piece]
         summed = jnp.concatenate([own, summed[piece:]], axis=0).astype(jnp.bfloat16)
         total = summed.astype(jnp.float32)
         for g in range(1, reps):
             arrived = hop(summed, "rep", g).astype(jnp.float32)
             total = total + jnp.roll(arrived, g * piece, axis=0)
-        stream = total.astype(jnp.bfloat16)
-        firsts.append(stream[:piece])
-        summed = layer(stream, mine_picks[cut], 1)
-        value = stream[:piece].astype(jnp.float32) + summed[:piece]
+        return total.astype(jnp.bfloat16)
+
+    def finished(own_rows, summed):
+        value = own_rows.astype(jnp.float32) + summed[:piece]
         for g in range(1, reps):
             sent = summed[g * piece : (g + 1) * piece].astype(jnp.bfloat16)
             value = value + hop(sent, "rep", -g).astype(jnp.float32)
-        seconds.append(value.astype(jnp.bfloat16))
-    first = jnp.concatenate(firsts, axis=0)
-    second = jnp.concatenate(seconds, axis=0)
+        return value.astype(jnp.bfloat16)
+
+    mine_picks = lax.dynamic_slice_in_dim(picks, section_index * half, half)
+    cuts = (slice(0, piece), slice(piece, half))
+    picked = [mine_picks[cut] for cut in cuts]
+    streams = [mine_rows[cut] for cut in cuts]
+    stream = jnp.concatenate([value[cuts[1]] for value in [mine_rows] + others], axis=0)
+    blocks = [first_blocks, [stream] + gather(stream)]
+    results = []
+    for section in range(2):
+        raw, parts = expanded(blocks[0], section)
+        next_raw, next_parts = expanded(blocks[1], section)
+        coef, hidden, received = activated(parts, raw, picked[0], section)
+        outs = contracted(coef, hidden, received, section)
+        coef, hidden, received = activated(next_parts, next_raw, picked[1], section, outs[:1])
+        next_outs = contracted(coef, hidden, received, section)
+        if section == 0:
+            first = streamed(streams[0], scattered(outs))
+            first_blocks = [first] + gather(first)
+            later = jnp.where(first[0, 0] == first[0, 0], streams[1], jnp.zeros_like(streams[1]))
+            second = streamed(later, scattered(next_outs))
+            blocks = [first_blocks, [second] + gather(second)]
+            streams = [first[:piece], second[:piece]]
+        else:
+            streams = [finished(streams[0], scattered(outs)), finished(streams[1], scattered(next_outs))]
+        results.append(jnp.concatenate(streams, axis=0))
+    first, second = results
     kept = jnp.where(section_index == 0, first, second)
     received = hop(jnp.where(section_index == 0, second, first), "section", 1)
     out = jnp.where(

time: 279 us -> 292 us (1.047)
  Pallas kernels: 97.6 us -> 88.1 us
  waiting for transfers between devices: 87.7 us -> 95.3 us
  starting transfers between devices: 65.1 us -> 71.2 us
  local copies, waits for them, and re-layouts: 15.5 us -> 20.2 us
    ppermute x44 -> x47, waiting for transfers between devices: 87.7 us -> 95.3 us  [hop(): lax.ppermute(value, axis, [(i, (i + steps) % count) for i in range(count)])]
    pallas_call x4, Pallas kernels: 36.1 us -> 30 us  [contract(): pl.pallas_call(functools.partial(contract_kernel, owners, reps), out_shap...]
    ppermute x44 -> x47, starting transfers between devices: 65.1 us -> 71.2 us  [hop(): lax.ppermute(value, axis, [(i, (i + steps) % count) for i in range(count)])]
    pallas_call x4, Pallas kernels: 51.8 us -> 48.5 us  [expand(): pl.pallas_call(functools.partial(expand_kernel, owners, reps), out_shape=...]
    unnamed x93 -> x111, local copies, waits for them, and re-layouts: 6.95 us -> 10.2 us
  transfers between devices with their start and end apart: 44 -> 47, of which waited for: 18 -> 16; matrix products, arithmetic and copies ran while one was open for 7% -> 7% of each run, Pallas kernels for 35% -> 30%
where the time goes in v7:
time: 292 us; the launch traced here: 289 us
  waiting for transfers between devices  95.3 us (33%)
  Pallas kernels  88.1 us (30%)
  starting transfers between devices  71.2 us (24%)
  local copies, waits for them, and re-layouts  20.2 us (7%)
  other arithmetic  11.5 us (4%)
    ppermute x47, waiting for transfers between devices, hop(): lax.ppermute(value, axis, [(i, (i + steps) % count) for i in range(count)])  95.3 us
    ppermute x47, starting transfers between devices, hop(): lax.ppermute(value, axis, [(i, (i + steps) % count) for i in range(count)])  71.2 us
    pallas_call x4, Pallas kernels, expand(): pl.pallas_call(functools.partial(expand_kernel, owners, reps), out_shape=...  48.5 us
    pallas_call x4, Pallas kernels, contract(): pl.pallas_call(functools.partial(contract_kernel, owners, reps), out_shap...  30 us
    unnamed x111, local copies, waits for them, and re-layouts  10.2 us
    pallas_call x4, Pallas kernels, activate(): pl.pallas_call(functools.partial(activate_kernel, reps), out_shape=[jax.S...  9.69 us
  transfers between devices with their start and end apart: 47, of which 16 were waited for; matrix products, arithmetic and copies ran while one was open for 7% of the time, Pallas kernels for 30%

profile of v7, /device:TPU:1, one launch (start us, length us, event | category | flops | bytes accessed | tf_op | source)
XLA Modules:
  0.0 288.6 jit_solution(14917228448574785250)
XLA Ops:
  4.6 2.7 collective-permute-start.3
  24.9 2.8 collective-permute-done.4.refs_3_
  28.5 3.4 %collective-permute-done.6.refs_5_ = bf16[48,1024]{1,0:T(8,128)(2,1)S(1)} collective-permute-done((bf16[48,1024]{1,0:T(8,128)(2,1)S(1)}, bf16[48,1024]{1,0:T(8,128)(2,1)S(1)}, u32[]{:S(2)}, u32[]{:S(2)}) %collective-permute-start.6) | collective-permute-done | bytes 98336 | tf_op jit(solution)/shard_map/ppermute | solution.py:22
  32.0 2.9 collective-permute-start.12
  35.5 11.8 %expand.4 = (f32[48,16]{1,0:T(8,128)}, bf16[2,32,48,128]{3,2,1,0:T(8,128)(2,1)}, bf16[2,32,48,128]{3,2,1,0:T(8,128)(2,1)}) custom-call(s32[864]{0:T(1024)} %reshape.557.words_ref, s32[4]{0:T(128)} %pad_add_fusion.1.groups_ref, bf16[48,1024]{1,0:T(8,128)(2,1)} %copy-done.23, bf16[48,1024]{1,0:T(8,128)(2,1)} %copy-done.26, bf16[48,1024]{1,0:T(8,128)(2,1)} %copy-done.44, ...), custom_call_target="tpu_custom_call" | custom-call | flops 6442450944 | bytes 16777216 | tf_op jit(solution)/shard_map/expand/pallas_call | solution.py:190
  53.0 13.0 %collective-permute-done.11.refs_1_ = bf16[2,32,48,128]{3,2,1,0:T(8,128)(2,1)S(1)} collective-permute-done((bf16[2,32,48,128]{3,2,1,0:T(8,128)(2,1)}, bf16[2,32,48,128]{3,2,1,0:T(8,128)(2,1)S(1)}, u32[]{:S(2)}, u32[]{:S(2)}) %collective-permute-start.11) | collective-permute-done | bytes 786464 | tf_op jit(solution)/shard_map/ppermute | solution.py:22
  66.0 2.4 activate.4
  71.8 11.9 %expand.5 = (f32[48,16]{1,0:T(8,128)}, bf16[2,32,48,128]{3,2,1,0:T(8,128)(2,1)}, bf16[2,32,48,128]{3,2,1,0:T(8,128)(2,1)}) custom-call(s32[864]{0:T(1024)} %reshape.557.words_ref, s32[4]{0:T(128)} %pad_add_fusion.1.groups_ref, bf16[96,1024]{1,0:T(8,128)(2,1)} %copy-done.25, bf16[96,1024]{1,0:T(8,128)(2,1)} %copy-done.34, bf16[96,1024]{1,0:T(8,128)(2,1)} %copy-done.35, ...), custom_call_target="tpu_custom_call" | custom-call | flops 6442450944 | bytes 16777216 | tf_op jit(solution)/shard_map/expand/pallas_call | solution.py:190
  85.6 7.5 %contract.4 = (bf16[96,1024]{1,0:T(8,128)(2,1)}, bf16[96,1024]{1,0:T(8,128)(2,1)}, bf16[96,1024]{1,0:T(8,128)(2,1)}, bf16[96,1024]{1,0:T(8,128)(2,1)}) custom-call(s32[864]{0:T(1024)} %reshape.557.words_ref, s32[4]{0:T(128)} %pad_add_fusion.1.groups_ref, bf16[32,48,128]{2,1,0:T(8,128)(2,1)} %copy-done.8, bf16[32,48,128]{2,1,0:T(8,128)(2,1)} %copy-done.28, ...), custom_call_target="tpu_custom_call" | custom-call | flops 3221225472 | bytes 8388608 | tf_op jit(solution)/shard_map/contract/pallas_call | solution.py:307
  93.1 4.0 %collective-permute-start.15 = (bf16[96,1024]{1,0:T(8,128)(2,1)}, bf16[96,1024]{1,0:T(8,128)(2,1)S(1)}, u32[]{:S(2)}, u32[]{:S(2)}) collective-permute-start(bf16[96,1024]{1,0:T(8,128)(2,1)} %get-tuple-element.58), channel_id=1, source_target_pairs={{0,6},{2,0},{4,2},{6,4},{1,7},{3,1},{5,3},{7,5},{8,14},{10,8},{12,... | collective-permute-start | bytes 589832 | tf_op jit(solution)/shard_map/ppermute | solution.py:22
  97.5 3.3 %collective-permute-done.22.refs_1_ = bf16[2,32,48,128]{3,2,1,0:T(8,128)(2,1)S(1)} collective-permute-done((bf16[2,32,48,128]{3,2,1,0:T(8,128)(2,1)}, bf16[2,32,48,128]{3,2,1,0:T(8,128)(2,1)S(1)}, u32[]{:S(2)}, u32[]{:S(2)}) %collective-permute-start.22) | collective-permute-done | bytes 786464 | tf_op jit(solution)/shard_map/ppermute | solution.py:22
  101.7 2.4 activate.5
  104.9 8.4 %collective-permute-done.16 = bf16[96,1024]{1,0:T(8,128)(2,1)S(1)} collective-permute-done((bf16[96,1024]{1,0:T(8,128)(2,1)}, bf16[96,1024]{1,0:T(8,128)(2,1)S(1)}, u32[]{:S(2)}, u32[]{:S(2)}) %collective-permute-start.16) | collective-permute-done | bytes 196640 | tf_op jit(solution)/shard_map/ppermute | solution.py:22
  115.5 7.5 %contract.5 = (bf16[96,1024]{1,0:T(8,128)(2,1)}, bf16[96,1024]{1,0:T(8,128)(2,1)}, bf16[96,1024]{1,0:T(8,128)(2,1)}, bf16[96,1024]{1,0:T(8,128)(2,1)}) custom-call(s32[864]{0:T(1024)} %reshape.557.words_ref, s32[4]{0:T(128)} %pad_add_fusion.1.groups_ref, bf16[32,48,128]{2,1,0:T(8,128)(2,1)} %copy-done.7, bf16[32,48,128]{2,1,0:T(8,128)(2,1)} %copy-done.27, ...), custom_call_target="tpu_custom_call" | custom-call | flops 3221225472 | bytes 8388608 | tf_op jit(solution)/shard_map/contract/pallas_call | solution.py:307
  124.1 3.4 %collective-permute-start.25 = (bf16[96,1024]{1,0:T(8,128)(2,1)}, bf16[96,1024]{1,0:T(8,128)(2,1)S(1)}, u32[]{:S(2)}, u32[]{:S(2)}) collective-permute-start(bf16[96,1024]{1,0:T(8,128)(2,1)} %get-tuple-element.68), channel_id=1, source_target_pairs={{0,4},{2,6},{4,0},{6,2},{1,5},{3,7},{5,1},{7,3},{8,12},{10,14},{12... | collective-permute-start | bytes 589832 | tf_op jit(solution)/shard_map/ppermute | solution.py:22
  130.8 13.0 %collective-permute-done.25 = bf16[96,1024]{1,0:T(8,128)(2,1)S(1)} collective-permute-done((bf16[96,1024]{1,0:T(8,128)(2,1)}, bf16[96,1024]{1,0:T(8,128)(2,1)S(1)}, u32[]{:S(2)}, u32[]{:S(2)}) %collective-permute-start.25) | collective-permute-done | bytes 196640 | tf_op jit(solution)/shard_map/ppermute | solution.py:22
  148.6 2.4 collective-permute-start.30
  154.5 8.8 %collective-permute-done.29.refs_2_ = bf16[96,1024]{1,0:T(8,128)(2,1)S(1)} collective-permute-done((bf16[96,1024]{1,0:T(8,128)(2,1)S(1)}, bf16[96,1024]{1,0:T(8,128)(2,1)S(1)}, u32[]{:S(2)}, u32[]{:S(2)}) %collective-permute-start.29) | collective-permute-done | bytes 196640 | tf_op jit(solution)/shard_map/ppermute | solution.py:22
  164.0 12.5 %expand.6 = (f32[48,16]{1,0:T(8,128)}, bf16[2,32,48,128]{3,2,1,0:T(8,128)(2,1)}, bf16[2,32,48,128]{3,2,1,0:T(8,128)(2,1)}) custom-call(s32[864]{0:T(1024)} %reshape.560.words_ref, s32[4]{0:T(128)} %pad_add_fusion.2.groups_ref, bf16[96,1024]{1,0:T(8,128)(2,1)} %copy-done.19, bf16[96,1024]{1,0:T(8,128)(2,1)} %copy-done.37, bf16[96,1024]{1,0:T(8,128)(2,1)} %copy-done.39, ...), custom_call_target="tpu_custom_call" | custom-call | flops 6442450944 | bytes 16777216 | tf_op jit(solution)/shard_map/expand/pallas_call | solution.py:190
  180.3 12.3 %expand.7 = (f32[48,16]{1,0:T(8,128)}, bf16[2,32,48,128]{3,2,1,0:T(8,128)(2,1)}, bf16[2,32,48,128]{3,2,1,0:T(8,128)(2,1)}) custom-call(s32[864]{0:T(1024)} %reshape.560.words_ref, s32[4]{0:T(128)} %pad_add_fusion.2.groups_ref, bf16[96,1024]{1,0:T(8,128)(2,1)} %copy-done.21, bf16[96,1024]{1,0:T(8,128)(2,1)} %copy-done.38, bf16[96,1024]{1,0:T(8,128)(2,1)} %copy-done.40, ...), custom_call_target="tpu_custom_call" | custom-call | flops 6442450944 | bytes 16777216 | tf_op jit(solution)/shard_map/expand/pallas_call | solution.py:190
  193.5 2.4 activate.6
  197.3 18.9 %collective-permute-done.32.refs_1_ = bf16[32,48,128]{2,1,0:T(8,128)(2,1)S(1)} collective-permute-done((bf16[32,48,128]{2,1,0:T(8,128)(2,1)S(1)}, bf16[32,48,128]{2,1,0:T(8,128)(2,1)S(1)}, u32[]{:S(2)}, u32[]{:S(2)}) %collective-permute-start.32) | collective-permute-done | bytes 393248 | tf_op jit(solution)/shard_map/ppermute | solution.py:22
  217.0 7.5 %contract.6 = (bf16[96,1024]{1,0:T(8,128)(2,1)}, bf16[96,1024]{1,0:T(8,128)(2,1)}, bf16[96,1024]{1,0:T(8,128)(2,1)}, bf16[96,1024]{1,0:T(8,128)(2,1)}) custom-call(s32[864]{0:T(1024)} %reshape.560.words_ref, s32[4]{0:T(128)} %pad_add_fusion.2.groups_ref, bf16[32,48,128]{2,1,0:T(8,128)(2,1)} %copy-done.10, bf16[32,48,128]{2,1,0:T(8,128)(2,1)} %copy-done.30, ...), custom_call_target="tpu_custom_call" | custom-call | flops 3221225472 | bytes 8388608 | tf_op jit(solution)/shard_map/contract/pallas_call | solution.py:307
  225.4 2.4 activate.7
  230.2 8.0 %collective-permute-start.33 = (bf16[96,1024]{1,0:T(8,128)(2,1)S(1)}, bf16[96,1024]{1,0:T(8,128)(2,1)S(1)}, u32[]{:S(2)}, u32[]{:S(2)}) collective-permute-start(bf16[96,1024]{1,0:T(8,128)(2,1)S(1)} %copy-done.53), channel_id=1, source_target_pairs={{0,6},{2,0},{4,2},{6,4},{1,7},{3,1},{5,3},{7,5},{8,14},{10,8},{12,... | collective-permute-start | bytes 589832 | tf_op jit(solution)/shard_map/ppermute | solution.py:22
  238.2 6.9 %collective-permute-start.34 = (bf16[96,1024]{1,0:T(8,128)(2,1)S(1)}, bf16[96,1024]{1,0:T(8,128)(2,1)S(1)}, u32[]{:S(2)}, u32[]{:S(2)}) collective-permute-start(bf16[96,1024]{1,0:T(8,128)(2,1)S(1)} %copy-done.52), channel_id=1, source_target_pairs={{0,4},{2,6},{4,0},{6,2},{1,5},{3,7},{5,1},{7,3},{8,12},{10,14},{12... | collective-permute-start | bytes 589832 | tf_op jit(solution)/shard_map/ppermute | solution.py:22
  246.4 7.5 %contract.7 = (bf16[96,1024]{1,0:T(8,128)(2,1)}, bf16[96,1024]{1,0:T(8,128)(2,1)}, bf16[96,1024]{1,0:T(8,128)(2,1)}, bf16[96,1024]{1,0:T(8,128)(2,1)}) custom-call(s32[864]{0:T(1024)} %reshape.560.words_ref, s32[4]{0:T(128)} %pad_add_fusion.2.groups_ref, bf16[32,48,128]{2,1,0:T(8,128)(2,1)} %copy-done.9, bf16[32,48,128]{2,1,0:T(8,128)(2,1)} %copy-done.29, ...), custom_call_target="tpu_custom_call" | custom-call | flops 3221225472 | bytes 8388608 | tf_op jit(solution)/shard_map/contract/pallas_call | solution.py:307
  253.9 3.6 %collective-permute-start.42 = (bf16[96,1024]{1,0:T(8,128)(2,1)}, bf16[96,1024]{1,0:T(8,128)(2,1)S(1)}, u32[]{:S(2)}, u32[]{:S(2)}) collective-permute-start(bf16[96,1024]{1,0:T(8,128)(2,1)} %get-tuple-element.85), channel_id=1, source_target_pairs={{0,6},{2,0},{4,2},{6,4},{1,7},{3,1},{5,3},{7,5},{8,14},{10,8},{12,... | collective-permute-start | bytes 589832 | tf_op jit(solution)/shard_map/ppermute | solution.py:22
  257.5 4.6 %collective-permute-start.43 = (bf16[96,1024]{1,0:T(8,128)(2,1)}, bf16[96,1024]{1,0:T(8,128)(2,1)S(1)}, u32[]{:S(2)}, u32[]{:S(2)}) collective-permute-start(bf16[96,1024]{1,0:T(8,128)(2,1)} %get-tuple-element.86), channel_id=1, source_target_pairs={{0,4},{2,6},{4,0},{6,2},{1,5},{3,7},{5,1},{7,3},{8,12},{10,14},{12... | collective-permute-start | bytes 589832 | tf_op jit(solution)/shard_map/ppermute | solution.py:22
  265.0 13.8 %collective-permute-done.43 = bf16[96,1024]{1,0:T(8,128)(2,1)S(1)} collective-permute-done((bf16[96,1024]{1,0:T(8,128)(2,1)}, bf16[96,1024]{1,0:T(8,128)(2,1)S(1)}, u32[]{:S(2)}, u32[]{:S(2)}) %collective-permute-start.43) | collective-permute-done | bytes 196640 | tf_op jit(solution)/shard_map/ppermute | solution.py:22
  280.8 2.7 collective-permute-done.45
  283.6 3.1 %collective-permute-start.46 = (bf16[96,1024]{1,0:T(8,128)(2,1)S(1)}, bf16[96,1024]{1,0:T(8,128)(2,1)S(1)}, u32[]{:S(2)}, u32[]{:S(2)}) collective-permute-start(bf16[96,1024]{1,0:T(8,128)(2,1)S(1)} %get-tuple-element.96), channel_id=1, source_target_pairs={{0,8},{8,0},{1,9},{9,1},{2,10},{10,2},{3,11},{11,3},{4,12},{12,4},... | collective-permute-start | bytes 589832 | tf_op jit(solution)/shard_map/ppermute | solution.py:22
  (265 shorter events, 68.8 us)
Async XLA Ops:
  3.2 31.7 %collective-permute-start.10 = (bf16[256,128,128]{2,1,0:T(8,128)(2,1)}, bf16[256,128,128]{2,1,0:T(8,128)(2,1)}, u32[]{:S(2)}, u32[]{:S(2)}) collective-permute-start(bf16[256,128,128]{2,1,0:T(8,128)(2,1)} %bitcast.58), channel_id=1, source_target_pairs={{0,8},{8,0},{1,9},{9,1},{2,10},{10,2},{3,11},{11,3},{4,12},{12,4},... | collective-permute-start | bytes 25165832 | tf_op jit(solution)/shard_map/ppermute | solution.py:22
  3.5 31.4 %collective-permute-start.9 = (bf16[256,128,128]{2,1,0:T(8,128)(2,1)}, bf16[256,128,128]{2,1,0:T(8,128)(2,1)}, u32[]{:S(2)}, u32[]{:S(2)}) collective-permute-start(bf16[256,128,128]{2,1,0:T(8,128)(2,1)} %bitcast.53), channel_id=1, source_target_pairs={{0,8},{8,0},{1,9},{9,1},{2,10},{10,2},{3,11},{11,3},{4,12},{12,4},... | collective-permute-start | bytes 25165832 | tf_op jit(solution)/shard_map/ppermute | solution.py:22
  4.6 16.7 %collective-permute-start.3 = (bf16[48,1024]{1,0:T(8,128)(2,1)S(1)}, bf16[48,1024]{1,0:T(8,128)(2,1)S(1)}, u32[]{:S(2)}, u32[]{:S(2)}) collective-permute-start(bf16[48,1024]{1,0:T(8,128)(2,1)S(1)} %get-tuple-element.99.refs_0_), channel_id=1, source_target_pairs={{0,2},{2,4},{4,6},{6,0},{1,3},{3,5},{5,7},{7,1},{8,10},{10,12},{12... | collective-permute-start | bytes 294920 | tf_op jit(solution)/shard_map/ppermute | solution.py:22
  7.3 77.5 %collective-permute-start.14 = (bf16[256,128,128]{2,1,0:T(8,128)(2,1)}, bf16[256,128,128]{2,1,0:T(8,128)(2,1)}, u32[]{:S(2)}, u32[]{:S(2)}) collective-permute-start(bf16[256,128,128]{2,1,0:T(8,128)(2,1)} %bitcast.63), channel_id=1, source_target_pairs={{0,8},{8,0},{1,9},{9,1},{2,10},{10,2},{3,11},{11,3},{4,12},{12,4},... | collective-permute-start | bytes 25165832 | tf_op jit(solution)/shard_map/ppermute | solution.py:22
  32.0 19.2 %collective-permute-start.12 = (bf16[24,32,128]{2,0,1:T(8,128)(2,1)S(1)}, bf16[24,32,128]{2,0,1:T(8,128)(2,1)S(1)}, u32[]{:S(2)}, u32[]{:S(2)}) collective-permute-start(bf16[24,32,128]{2,0,1:T(8,128)(2,1)S(1)} %select_bitcast_fusion.2), channel_id=1, source_target_pairs={{0,8},{8,0},{1,9},{9,1},{2,10},{10,2},{3,11},{11,3},{4,12},{12,4},... | collective-permute-start | bytes 589832 | tf_op jit(solution)/shard_map/ppermute | solution.py:22
  47.3 18.6 %collective-permute-start.11 = (bf16[2,32,48,128]{3,2,1,0:T(8,128)(2,1)}, bf16[2,32,48,128]{3,2,1,0:T(8,128)(2,1)S(1)}, u32[]{:S(2)}, u32[]{:S(2)}) collective-permute-start(bf16[2,32,48,128]{3,2,1,0:T(8,128)(2,1)} %get-tuple-element.52), channel_id=1, source_target_pairs={{0,1},{1,0},{2,3},{3,2},{4,5},{5,4},{6,7},{7,6},{8,9},{9,8},{10,11... | collective-permute-start | bytes 2359304 | tf_op jit(solution)/shard_map/ppermute | solution.py:22
  49.0 21.3 %collective-permute-start.19 = (bf16[96,1024]{1,0:T(8,128)(2,1)S(1)}, bf16[96,1024]{1,0:T(8,128)(2,1)S(1)}, u32[]{:S(2)}, u32[]{:S(2)}) collective-permute-start(bf16[96,1024]{1,0:T(8,128)(2,1)S(1)} %pad_maximum_fusion.3.refs_0_), channel_id=1, source_target_pairs={{0,2},{2,4},{4,6},{6,0},{1,3},{3,5},{5,7},{7,1},{8,10},{10,12},{12... | collective-permute-start | bytes 589832 | tf_op jit(solution)/shard_map/ppermute | solution.py:22
  50.6 19.8 %collective-permute-start.20 = (bf16[96,1024]{1,0:T(8,128)(2,1)S(1)}, bf16[96,1024]{1,0:T(8,128)(2,1)S(1)}, u32[]{:S(2)}, u32[]{:S(2)}) collective-permute-start(bf16[96,1024]{1,0:T(8,128)(2,1)S(1)} %pad_maximum_fusion.3.refs_0_), channel_id=1, source_target_pairs={{0,4},{2,6},{4,0},{6,2},{1,5},{3,7},{5,1},{7,3},{8,12},{10,14},{12... | collective-permute-start | bytes 589832 | tf_op jit(solution)/shard_map/ppermute | solution.py:22
  51.2 19.1 %collective-permute-start.21 = (bf16[96,1024]{1,0:T(8,128)(2,1)S(1)}, bf16[96,1024]{1,0:T(8,128)(2,1)S(1)}, u32[]{:S(2)}, u32[]{:S(2)}) collective-permute-start(bf16[96,1024]{1,0:T(8,128)(2,1)S(1)} %pad_maximum_fusion.3.refs_0_), channel_id=1, source_target_pairs={{0,6},{2,0},{4,2},{6,4},{1,7},{3,1},{5,3},{7,5},{8,14},{10,8},{12,... | collective-permute-start | bytes 589832 | tf_op jit(solution)/shard_map/ppermute | solution.py:22
  69.0 15.9 %collective-permute-start.13 = (bf16[32,48,128]{2,1,0:T(8,128)(2,1)S(1)}, bf16[32,48,128]{2,1,0:T(8,128)(2,1)S(1)}, u32[]{:S(2)}, u32[]{:S(2)}) collective-permute-start(bf16[32,48,128]{2,1,0:T(8,128)(2,1)S(1)} %get-tuple-element.54.refs_0_), channel_id=1, source_target_pairs={{0,1},{1,0},{2,3},{3,2},{4,5},{5,4},{6,7},{7,6},{8,9},{9,8},{10,11... | collective-permute-start | bytes 1179656 | tf_op jit(solution)/shard_map/ppermute | solution.py:22
  83.7 17.1 %collective-permute-start.22 = (bf16[2,32,48,128]{3,2,1,0:T(8,128)(2,1)}, bf16[2,32,48,128]{3,2,1,0:T(8,128)(2,1)S(1)}, u32[]{:S(2)}, u32[]{:S(2)}) collective-permute-start(bf16[2,32,48,128]{3,2,1,0:T(8,128)(2,1)} %get-tuple-element.62), channel_id=1, source_target_pairs={{0,1},{1,0},{2,3},{3,2},{4,5},{5,4},{6,7},{7,6},{8,9},{9,8},{10,11... | collective-permute-start | bytes 2359304 | tf_op jit(solution)/shard_map/ppermute | solution.py:22
  93.1 11.8 %collective-permute-start.15 = (bf16[96,1024]{1,0:T(8,128)(2,1)}, bf16[96,1024]{1,0:T(8,128)(2,1)S(1)}, u32[]{:S(2)}, u32[]{:S(2)}) collective-permute-start(bf16[96,1024]{1,0:T(8,128)(2,1)} %get-tuple-element.58), channel_id=1, source_target_pairs={{0,6},{2,0},{4,2},{6,4},{1,7},{3,1},{5,3},{7,5},{8,14},{10,8},{12,... | collective-permute-start | bytes 589832 | tf_op jit(solution)/shard_map/ppermute | solution.py:22
  97.1 16.2 %collective-permute-start.16 = (bf16[96,1024]{1,0:T(8,128)(2,1)}, bf16[96,1024]{1,0:T(8,128)(2,1)S(1)}, u32[]{:S(2)}, u32[]{:S(2)}) collective-permute-start(bf16[96,1024]{1,0:T(8,128)(2,1)} %get-tuple-element.59), channel_id=1, source_target_pairs={{0,4},{2,6},{4,0},{6,2},{1,5},{3,7},{5,1},{7,3},{8,12},{10,14},{12... | collective-permute-start | bytes 589832 | tf_op jit(solution)/shard_map/ppermute | solution.py:22
  97.5 15.8 %collective-permute-start.17 = (bf16[96,1024]{1,0:T(8,128)(2,1)}, bf16[96,1024]{1,0:T(8,128)(2,1)S(1)}, u32[]{:S(2)}, u32[]{:S(2)}) collective-permute-start(bf16[96,1024]{1,0:T(8,128)(2,1)} %get-tuple-element.60), channel_id=1, source_target_pairs={{0,2},{2,4},{4,6},{6,0},{1,3},{3,5},{5,7},{7,1},{8,10},{10,12},{12... | collective-permute-start | bytes 589832 | tf_op jit(solution)/shard_map/ppermute | solution.py:22
  113.5 15.4 %collective-permute-start.18 = (bf16[96,1024]{1,0:T(8,128)(2,1)S(1)}, bf16[96,1024]{1,0:T(8,128)(2,1)S(1)}, u32[]{:S(2)}, u32[]{:S(2)}) collective-permute-start(bf16[96,1024]{1,0:T(8,128)(2,1)S(1)} %pad_maximum_fusion.2), channel_id=1, source_target_pairs={{0,1},{1,0},{2,3},{3,2},{4,5},{5,4},{6,7},{7,6},{8,9},{9,8},{10,11... | collective-permute-start | bytes 589832 | tf_op jit(solution)/shard_map/ppermute | solution.py:22
  124.1 19.7 %collective-permute-start.25 = (bf16[96,1024]{1,0:T(8,128)(2,1)}, bf16[96,1024]{1,0:T(8,128)(2,1)S(1)}, u32[]{:S(2)}, u32[]{:S(2)}) collective-permute-start(bf16[96,1024]{1,0:T(8,128)(2,1)} %get-tuple-element.68), channel_id=1, source_target_pairs={{0,4},{2,6},{4,0},{6,2},{1,5},{3,7},{5,1},{7,3},{8,12},{10,14},{12... | collective-permute-start | bytes 589832 | tf_op jit(solution)/shard_map/ppermute | solution.py:22
  127.5 16.3 %collective-permute-start.26 = (bf16[96,1024]{1,0:T(8,128)(2,1)}, bf16[96,1024]{1,0:T(8,128)(2,1)S(1)}, u32[]{:S(2)}, u32[]{:S(2)}) collective-permute-start(bf16[96,1024]{1,0:T(8,128)(2,1)} %get-tuple-element.69), channel_id=1, source_target_pairs={{0,2},{2,4},{4,6},{6,0},{1,3},{3,5},{5,7},{7,1},{8,10},{10,12},{12... | collective-permute-start | bytes 589832 | tf_op jit(solution)/shard_map/ppermute | solution.py:22
  146.8 16.4 %collective-permute-start.29 = (bf16[96,1024]{1,0:T(8,128)(2,1)S(1)}, bf16[96,1024]{1,0:T(8,128)(2,1)S(1)}, u32[]{:S(2)}, u32[]{:S(2)}) collective-permute-start(bf16[96,1024]{1,0:T(8,128)(2,1)S(1)} %fusion.4.refs_0_), channel_id=1, source_target_pairs={{0,4},{2,6},{4,0},{6,2},{1,5},{3,7},{5,1},{7,3},{8,12},{10,14},{12... | collective-permute-start | bytes 589832 | tf_op jit(solution)/shard_map/ppermute | solution.py:22
  148.6 14.6 %collective-permute-start.30 = (bf16[96,1024]{1,0:T(8,128)(2,1)S(1)}, bf16[96,1024]{1,0:T(8,128)(2,1)S(1)}, u32[]{:S(2)}, u32[]{:S(2)}) collective-permute-start(bf16[96,1024]{1,0:T(8,128)(2,1)S(1)} %fusion.4.refs_0_), channel_id=1, source_target_pairs={{0,6},{2,0},{4,2},{6,4},{1,7},{3,1},{5,3},{7,5},{8,14},{10,8},{12,... | collective-permute-start | bytes 589832 | tf_op jit(solution)/shard_map/ppermute | solution.py:22
  151.1 26.3 %collective-permute-start.37 = (bf16[96,1024]{1,0:T(8,128)(2,1)S(1)}, bf16[96,1024]{1,0:T(8,128)(2,1)S(1)}, u32[]{:S(2)}, u32[]{:S(2)}) collective-permute-start(bf16[96,1024]{1,0:T(8,128)(2,1)S(1)} %fusion.5.refs_0_), channel_id=1, source_target_pairs={{0,2},{2,4},{4,6},{6,0},{1,3},{3,5},{5,7},{7,1},{8,10},{10,12},{12... | collective-permute-start | bytes 589832 | tf_op jit(solution)/shard_map/ppermute | solution.py:22
  151.2 27.8 %collective-permute-start.38 = (bf16[96,1024]{1,0:T(8,128)(2,1)S(1)}, bf16[96,1024]{1,0:T(8,128)(2,1)S(1)}, u32[]{:S(2)}, u32[]{:S(2)}) collective-permute-start(bf16[96,1024]{1,0:T(8,128)(2,1)S(1)} %fusion.5.refs_0_), channel_id=1, source_target_pairs={{0,4},{2,6},{4,0},{6,2},{1,5},{3,7},{5,1},{7,3},{8,12},{10,14},{12... | collective-permute-start | bytes 589832 | tf_op jit(solution)/shard_map/ppermute | solution.py:22
  153.3 25.6 %collective-permute-start.39 = (bf16[96,1024]{1,0:T(8,128)(2,1)S(1)}, bf16[96,1024]{1,0:T(8,128)(2,1)S(1)}, u32[]{:S(2)}, u32[]{:S(2)}) collective-permute-start(bf16[96,1024]{1,0:T(8,128)(2,1)S(1)} %fusion.5.refs_0_), channel_id=1, source_target_pairs={{0,6},{2,0},{4,2},{6,4},{1,7},{3,1},{5,3},{7,5},{8,14},{10,8},{12,... | collective-permute-start | bytes 589832 | tf_op jit(solution)/shard_map/ppermute | solution.py:22
  176.5 17.0 %collective-permute-start.31 = (bf16[2,32,48,128]{3,2,1,0:T(8,128)(2,1)}, bf16[2,32,48,128]{3,2,1,0:T(8,128)(2,1)S(1)}, u32[]{:S(2)}, u32[]{:S(2)}) collective-permute-start(bf16[2,32,48,128]{3,2,1,0:T(8,128)(2,1)} %get-tuple-element.71), channel_id=1, source_target_pairs={{0,1},{1,0},{2,3},{3,2},{4,5},{5,4},{6,7},{7,6},{8,9},{9,8},{10,11... | collective-permute-start | bytes 2359304 | tf_op jit(solution)/shard_map/ppermute | solution.py:22
  192.6 31.9 %collective-permute-start.40 = (bf16[2,32,48,128]{3,2,1,0:T(8,128)(2,1)}, bf16[2,32,48,128]{3,2,1,0:T(8,128)(2,1)S(1)}, u32[]{:S(2)}, u32[]{:S(2)}) collective-permute-start(bf16[2,32,48,128]{3,2,1,0:T(8,128)(2,1)} %get-tuple-element.80), channel_id=1, source_target_pairs={{0,1},{1,0},{2,3},{3,2},{4,5},{5,4},{6,7},{7,6},{8,9},{9,8},{10,11... | collective-permute-start | bytes 2359304 | tf_op jit(solution)/shard_map/ppermute | solution.py:22
  196.0 20.2 %collective-permute-start.32 = (bf16[32,48,128]{2,1,0:T(8,128)(2,1)S(1)}, bf16[32,48,128]{2,1,0:T(8,128)(2,1)S(1)}, u32[]{:S(2)}, u32[]{:S(2)}) collective-permute-start(bf16[32,48,128]{2,1,0:T(8,128)(2,1)S(1)} %get-tuple-element.73.refs_0_), channel_id=1, source_target_pairs={{0,1},{1,0},{2,3},{3,2},{4,5},{5,4},{6,7},{7,6},{8,9},{9,8},{10,11... | collective-permute-start | bytes 1179656 | tf_op jit(solution)/shard_map/ppermute | solution.py:22
  228.5 17.2 %collective-permute-start.41 = (bf16[32,48,128]{2,1,0:T(8,128)(2,1)S(1)}, bf16[32,48,128]{2,1,0:T(8,128)(2,1)S(1)}, u32[]{:S(2)}, u32[]{:S(2)}) collective-permute-start(bf16[32,48,128]{2,1,0:T(8,128)(2,1)S(1)} %get-tuple-element.82.refs_0_), channel_id=1, source_target_pairs={{0,1},{1,0},{2,3},{3,2},{4,5},{5,4},{6,7},{7,6},{8,9},{9,8},{10,11... | collective-permute-start | bytes 1179656 | tf_op jit(solution)/shard_map/ppermute | solution.py:22
  230.2 31.9 %collective-permute-start.33 = (bf16[96,1024]{1,0:T(8,128)(2,1)S(1)}, bf16[96,1024]{1,0:T(8,128)(2,1)S(1)}, u32[]{:S(2)}, u32[]{:S(2)}) collective-permute-start(bf16[96,1024]{1,0:T(8,128)(2,1)S(1)} %copy-done.53), channel_id=1, source_target_pairs={{0,6},{2,0},{4,2},{6,4},{1,7},{3,1},{5,3},{7,5},{8,14},{10,8},{12,... | collective-permute-start | bytes 589832 | tf_op jit(solution)/shard_map/ppermute | solution.py:22
  238.2 23.9 %collective-permute-start.34 = (bf16[96,1024]{1,0:T(8,128)(2,1)S(1)}, bf16[96,1024]{1,0:T(8,128)(2,1)S(1)}, u32[]{:S(2)}, u32[]{:S(2)}) collective-permute-start(bf16[96,1024]{1,0:T(8,128)(2,1)S(1)} %copy-done.52), channel_id=1, source_target_pairs={{0,4},{2,6},{4,0},{6,2},{1,5},{3,7},{5,1},{7,3},{8,12},{10,14},{12... | collective-permute-start | bytes 589832 | tf_op jit(solution)/shard_map/ppermute | solution.py:22
  245.1 16.9 %collective-permute-start.35 = (bf16[96,1024]{1,0:T(8,128)(2,1)S(1)}, bf16[96,1024]{1,0:T(8,128)(2,1)S(1)}, u32[]{:S(2)}, u32[]{:S(2)}) collective-permute-start(bf16[96,1024]{1,0:T(8,128)(2,1)S(1)} %copy-done.51), channel_id=1, source_target_pairs={{0,2},{2,4},{4,6},{6,0},{1,3},{3,5},{5,7},{7,1},{8,10},{10,12},{12... | collective-permute-start | bytes 589832 | tf_op jit(solution)/shard_map/ppermute | solution.py:22
  257.5 21.4 %collective-permute-start.43 = (bf16[96,1024]{1,0:T(8,128)(2,1)}, bf16[96,1024]{1,0:T(8,128)(2,1)S(1)}, u32[]{:S(2)}, u32[]{:S(2)}) collective-permute-start(bf16[96,1024]{1,0:T(8,128)(2,1)} %get-tuple-element.86), channel_id=1, source_target_pairs={{0,4},{2,6},{4,0},{6,2},{1,5},{3,7},{5,1},{7,3},{8,12},{10,14},{12... | collective-permute-start | bytes 589832 | tf_op jit(solution)/shard_map/ppermute | solution.py:22
  262.1 16.8 %collective-permute-start.44 = (bf16[96,1024]{1,0:T(8,128)(2,1)}, bf16[96,1024]{1,0:T(8,128)(2,1)S(1)}, u32[]{:S(2)}, u32[]{:S(2)}) collective-permute-start(bf16[96,1024]{1,0:T(8,128)(2,1)} %get-tuple-element.87), channel_id=1, source_target_pairs={{0,2},{2,4},{4,6},{6,0},{1,3},{3,5},{5,7},{7,1},{8,10},{10,12},{12... | collective-permute-start | bytes 589832 | tf_op jit(solution)/shard_map/ppermute | solution.py:22
  262.2 18.5 %collective-permute-start.36 = (bf16[48,1024]{1,0:T(8,128)(2,1)S(1)}, bf16[48,1024]{1,0:T(8,128)(2,1)S(1)}, u32[]{:S(2)}, u32[]{:S(2)}) collective-permute-start(bf16[48,1024]{1,0:T(8,128)(2,1)S(1)} %slice.257), channel_id=1, source_target_pairs={{0,1},{1,0},{2,3},{3,2},{4,5},{5,4},{6,7},{7,6},{8,9},{9,8},{10,11... | collective-permute-start | bytes 294920 | tf_op jit(solution)/shard_map/ppermute | solution.py:22
  (70 other events, 631.7 us)

commit v8 on v7

--- a/solution.py
+++ b/solution.py
@@ -11,6 +11,7 @@
 UNROLL = 16
 MIB = 1024 * 1024
 VMEM_LIMIT = 56 * MIB
+COPIES = 8
 SLOW = 4
 
 perturb_scale = 0.5
@@ -87,19 +88,26 @@
 
 
 def load_tiles(own, choices, tiles, sem):
-    copies = [pltpu.make_async_copy(tiles_hbm, tiles.at[pl.ds(0, tiles_hbm.shape[0])], sem) for tiles_hbm in choices]
-    pl.when(own == 1)(copies[0].start)
-    pl.when(own != 1)(copies[1].start)
-    tiles[tiles.shape[0] - 1] = jnp.zeros((BLOCK, BLOCK), tiles.dtype)
-    return copies[0]
-
-
-def expand_kernel(owners, reps, words_ref, groups_ref, *refs):
-    spans = len(refs) - 13 - reps
+    count = tiles.shape[0] - 1
+    step = -(-count // COPIES)
+
+    def copies(tiles_hbm):
+        for first in range(0, count, step):
+            part = pl.ds(first, min(step, count - first))
+            pltpu.make_async_copy(tiles_hbm.at[part], tiles.at[part], sem).start()
+
+    pl.when(own == 1)(functools.partial(copies, choices[0]))
+    pl.when(own != 1)(functools.partial(copies, choices[1]))
+    tiles[count] = jnp.zeros((BLOCK, BLOCK), tiles.dtype)
+    return pltpu.make_async_copy(choices[0], tiles.at[pl.ds(0, count)], sem)
+
+
+def expand_kernel(owners, reps, unread, words_ref, groups_ref, *refs):
+    spans = len(refs) - 13 - reps - unread
     blocks = refs[:spans]
-    gain_ref, left_ref, own_gate, other_gate, own_up, other_up, raw_ref = refs[spans : spans + 7]
-    part_refs = refs[spans + 7 : spans + 7 + reps]
-    total_ref, gate_tiles, gate_sem, up_tiles, up_sem, x_ref = refs[spans + 7 + reps :]
+    gain_ref, left_ref, own_gate, other_gate, own_up, other_up = refs[spans : spans + 6]
+    raw_ref, *part_refs = refs[spans + 6 + unread : spans + 7 + unread + reps]
+    total_ref, gate_tiles, gate_sem, up_tiles, up_sem, x_ref = refs[-6:]
     span_rows, width = blocks[0].shape
     split = spans // owners
     rows = part_refs[0].shape[2]
@@ -180,7 +188,7 @@
     ]
 
 
-def expand(words, groups, blocks, gain, left, gate_tiles, up_tiles, own_cols, reps):
+def expand(words, groups, blocks, gain, left, gate_tiles, up_tiles, own_cols, reps, after):
     features = gain.shape[1]
     owners = features // blocks[0].shape[1]
     all_rows = sum(block.size for block in blocks) // features
@@ -188,10 +196,10 @@
     tile_count = gate_tiles[0].shape[0]
     scratch = tile_scratch(tile_count, own_cols, all_rows)
     out = pl.pallas_call(
-        functools.partial(expand_kernel, owners, reps),
+        functools.partial(expand_kernel, owners, reps, len(after)),
         out_shape=[jax.ShapeDtypeStruct((rows, left.shape[0]), jnp.float32)]
         + [jax.ShapeDtypeStruct((2, own_cols, rows, BLOCK), jnp.bfloat16)] * reps,
-        in_specs=[SMEM, SMEM] + [VMEM] * (len(blocks) + 2) + [HBM] * 4,
+        in_specs=[SMEM, SMEM] + [VMEM] * (len(blocks) + 2) + [HBM] * (4 + len(after)),
         out_specs=[VMEM] * (1 + reps),
         scratch_shapes=scratch
         + scratch[1:]
@@ -199,7 +207,7 @@
         compiler_params=pltpu.CompilerParams(vmem_limit_bytes=VMEM_LIMIT),
         cost_estimate=tile_cost(2 * tile_count, all_rows),
         name="expand",
-    )(words, groups, *blocks, gain, left, *gate_tiles, *up_tiles)
+    )(words, groups, *blocks, gain, left, *gate_tiles, *up_tiles, *after)
     return out[0], out[1:]
 
 
@@ -265,8 +273,8 @@
 def contract_kernel(owners, reps, words_ref, groups_ref, *refs):
     hiddens = refs[:reps]
     coef_ref, right_ref, own_hbm, other_hbm = refs[reps : reps + 4]
-    outs = refs[reps + 4 : reps + 4 + owners]
-    total_ref, tiles, sem = refs[reps + 4 + owners :]
+    outs = refs[-3 - owners : -3]
+    total_ref, tiles, sem = refs[-3:]
     rows = hiddens[0].shape[1]
     per_owner = outs[0].shape[1] // BLOCK
     blocks = total_ref.shape[0]
@@ -299,7 +307,7 @@
             outs[owner][:, pl.ds(part * BLOCK, BLOCK)] = total_ref[owner * per_owner + part].astype(jnp.bfloat16)
 
 
-def contract(words, groups, hiddens, coef, right, tiles, owners):
+def contract(words, groups, hiddens, coef, right, tiles, owners, after):
     own_cols, rows = hiddens[0].shape[:2]
     reps = len(hiddens)
     features = right.shape[1]
@@ -307,13 +315,13 @@
     return pl.pallas_call(
         functools.partial(contract_kernel, owners, reps),
         out_shape=[jax.ShapeDtypeStruct((reps * rows, features // owners), jnp.bfloat16)] * owners,
-        in_specs=[SMEM, SMEM] + [VMEM] * (reps + 2) + [HBM, HBM],
+        in_specs=[SMEM, SMEM] + [VMEM] * (reps + 2) + [HBM] * (2 + len(after)),
         out_specs=[VMEM] * owners,
         scratch_shapes=tile_scratch(tile_count, features // BLOCK, reps * rows),
         compiler_params=pltpu.CompilerParams(vmem_limit_bytes=VMEM_LIMIT),
         cost_estimate=tile_cost(tile_count, reps * rows),
         name="contract",
-    )(words, groups, *hiddens, coef, right, *tiles)
+    )(words, groups, *hiddens, coef, right, *tiles, *after)
 
 
 def per_device(
@@ -401,9 +409,9 @@
 
     layers = [tables(section) for section in range(2)]
 
-    def expanded(blocks, section):
+    def expanded(blocks, section, after=()):
         words, groups, left, _, gain, _, _ = layers[section]
-        return expand(words, groups, blocks, gain, left, gate_pair, up_pair, own_cols, reps)
+        return expand(words, groups, blocks, gain, left, gate_pair, up_pair, own_cols, reps, after)
 
     def activated(parts, raw, picked, section, after=()):
         wide_cols, down_cols = layers[section][5:]
@@ -411,9 +419,9 @@
         hidden, coef = activate([parts[0]] + received, raw, picked, wide_cols, down_cols, after)
         return coef, hidden, [hop(hidden, "rep", g) for g in range(1, reps)]
 
-    def contracted(coef, hidden, received, section):
+    def contracted(coef, hidden, received, section, after=()):
         words, groups, _, right, _, _, _ = layers[section]
-        return contract(words, groups, [hidden] + received, coef, right, down_pair, owners)
+        return contract(words, groups, [hidden] + received, coef, right, down_pair, owners, after)
 
     def scattered(outs):
         summed = outs[0].astype(jnp.float32)
@@ -444,19 +452,20 @@
     stream = jnp.concatenate([value[cuts[1]] for value in [mine_rows] + others], axis=0)
     blocks = [first_blocks, [stream] + gather(stream)]
     results = []
+    raw, parts = expanded(blocks[0], 0)
     for section in range(2):
-        raw, parts = expanded(blocks[0], section)
-        next_raw, next_parts = expanded(blocks[1], section)
         coef, hidden, received = activated(parts, raw, picked[0], section)
-        outs = contracted(coef, hidden, received, section)
-        coef, hidden, received = activated(next_parts, next_raw, picked[1], section, outs[:1])
+        next_raw, parts = expanded(blocks[1], section, after=(received if section else [coef])[:1])
+        outs = contracted(coef, hidden, received, section, after=(next_raw,))
+        coef, hidden, received = activated(parts, next_raw, picked[1], section, after=(outs[0],))
+        streams[0] = jnp.where(coef[0, 0] == coef[0, 0], streams[0], jnp.zeros_like(streams[0]))
         next_outs = contracted(coef, hidden, received, section)
         if section == 0:
             first = streamed(streams[0], scattered(outs))
-            first_blocks = [first] + gather(first)
-            later = jnp.where(first[0, 0] == first[0, 0], streams[1], jnp.zeros_like(streams[1]))
+            raw, parts = expanded([first] + gather(first), 1)
+            later = jnp.where(raw[0, 0] == raw[0, 0], streams[1], jnp.zeros_like(streams[1]))
             second = streamed(later, scattered(next_outs))
-            blocks = [first_blocks, [second] + gather(second)]
+            blocks = [None, [second] + gather(second)]
             streams = [first[:piece], second[:piece]]
         else:
             streams = [finished(streams[0], scattered(outs)), finished(streams[1], scattered(next_outs))]

time: 292 us -> 293 us (level); the launches traced: 289 us -> 298 us
  waiting for transfers between devices: 95.3 us -> 82.9 us
  Pallas kernels: 88.1 us -> 99 us
  starting transfers between devices: 71.2 us -> 76.3 us
    ppermute x47, waiting for transfers between devices: 95.3 us -> 82.9 us  [hop(): lax.ppermute(value, axis, [(i, (i + steps) % count) for i in range(count)])]
    pallas_call x4, Pallas kernels: 48.5 us -> 56.8 us  [expand(): pl.pallas_call(functools.partial(expand_kernel, owners, reps, len(after))...]
    ppermute x47, starting transfers between devices: 71.2 us -> 76.3 us  [hop(): lax.ppermute(value, axis, [(i, (i + steps) % count) for i in range(count)])]
  transfers between devices with their start and end apart: 47 -> 47, of which waited for: 16 -> 17; matrix products, arithmetic and copies ran while one was open for 7% -> 8% of each run, Pallas kernels for 30% -> 27%
where the time goes in v8:
time: 293 us; the launch traced here: 298 us
  Pallas kernels  99 us (34%)
  waiting for transfers between devices  82.9 us (28%)
  starting transfers between devices  76.3 us (26%)
  local copies, waits for them, and re-layouts  22.1 us (8%)
  other arithmetic  12.4 us (4%)
  between operations  4.98 us (2%)
    ppermute x47, waiting for transfers between devices, hop(): lax.ppermute(value, axis, [(i, (i + steps) % count) for i in range(count)])  82.9 us
    ppermute x47, starting transfers between devices, hop(): lax.ppermute(value, axis, [(i, (i + steps) % count) for i in range(count)])  76.3 us
    pallas_call x4, Pallas kernels, expand(): pl.pallas_call(functools.partial(expand_kernel, owners, reps, len(after))...  56.8 us
    pallas_call x4, Pallas kernels, contract(): pl.pallas_call(functools.partial(contract_kernel, owners, reps), out_shap...  32.4 us
    pallas_call x4, Pallas kernels, activate(): pl.pallas_call(functools.partial(activate_kernel, reps), out_shape=[jax.S...  9.69 us
    unnamed x111, local copies, waits for them, and re-layouts  9.56 us
  transfers between devices with their start and end apart: 47, of which 17 were waited for; matrix products, arithmetic and copies ran while one was open for 8% of the time, Pallas kernels for 27%

profile of v8, /device:TPU:1, one launch (start us, length us, event | category | flops | bytes accessed | tf_op | source)
XLA Modules:
  0.0 297.6 jit_solution(11451648745660090671)
XLA Ops:
  5.0 4.5 %collective-permute-start.12 = (bf16[48,1024]{1,0:T(8,128)(2,1)S(1)}, bf16[48,1024]{1,0:T(8,128)(2,1)S(1)}, u32[]{:S(2)}, u32[]{:S(2)}) collective-permute-start(bf16[48,1024]{1,0:T(8,128)(2,1)S(1)} %get-tuple-element.99.refs_0_), channel_id=1, source_target_pairs={{0,6},{2,0},{4,2},{6,4},{1,7},{3,1},{5,3},{7,5},{8,14},{10,8},{12,... | collective-permute-start | bytes 294920 | tf_op jit(solution)/shard_map/ppermute | solution.py:23
  27.6 4.2 %collective-permute-done.11.refs_5_ = bf16[48,1024]{1,0:T(8,128)(2,1)S(1)} collective-permute-done((bf16[48,1024]{1,0:T(8,128)(2,1)S(1)}, bf16[48,1024]{1,0:T(8,128)(2,1)S(1)}, u32[]{:S(2)}, u32[]{:S(2)}) %collective-permute-start.11) | collective-permute-done | bytes 98336 | tf_op jit(solution)/shard_map/ppermute | solution.py:23
  31.8 4.7 %collective-permute-start.15 = (bf16[24,32,128]{2,0,1:T(8,128)(2,1)S(1)}, bf16[24,32,128]{2,0,1:T(8,128)(2,1)S(1)}, u32[]{:S(2)}, u32[]{:S(2)}) collective-permute-start(bf16[24,32,128]{2,0,1:T(8,128)(2,1)S(1)} %select_bitcast_fusion.2), channel_id=1, source_target_pairs={{0,8},{8,0},{1,9},{9,1},{2,10},{10,2},{3,11},{11,3},{4,12},{12,4},... | collective-permute-start | bytes 589832 | tf_op jit(solution)/shard_map/ppermute | solution.py:23
  37.1 15.5 %expand.4 = (f32[48,16]{1,0:T(8,128)}, bf16[2,32,48,128]{3,2,1,0:T(8,128)(2,1)}, bf16[2,32,48,128]{3,2,1,0:T(8,128)(2,1)}) custom-call(s32[864]{0:T(1024)} %reshape.559.words_ref, s32[4]{0:T(128)} %pad_add_fusion.1.groups_ref, bf16[48,1024]{1,0:T(8,128)(2,1)} %copy-done.24, bf16[48,1024]{1,0:T(8,128)(2,1)} %copy-done.27, bf16[48,1024]{1,0:T(8,128)(2,1)} %copy-done.46, ...), custom_call_target="tpu_custom_call" | custom-call | flops 6442450944 | bytes 16777216 | tf_op jit(solution)/shard_map/expand/pallas_call | solution.py:198
  55.8 13.4 %collective-permute-done.14.refs_1_ = bf16[2,32,48,128]{3,2,1,0:T(8,128)(2,1)S(1)} collective-permute-done((bf16[2,32,48,128]{3,2,1,0:T(8,128)(2,1)}, bf16[2,32,48,128]{3,2,1,0:T(8,128)(2,1)S(1)}, u32[]{:S(2)}, u32[]{:S(2)}) %collective-permute-start.14) | collective-permute-done | bytes 786464 | tf_op jit(solution)/shard_map/ppermute | solution.py:23
  69.2 2.4 activate.4
  74.2 15.6 %expand.5 = (f32[48,16]{1,0:T(8,128)}, bf16[2,32,48,128]{3,2,1,0:T(8,128)(2,1)}, bf16[2,32,48,128]{3,2,1,0:T(8,128)(2,1)}) custom-call(s32[864]{0:T(1024)} %reshape.559.words_ref, s32[4]{0:T(128)} %pad_add_fusion.1.groups_ref, bf16[96,1024]{1,0:T(8,128)(2,1)} %copy-done.26, bf16[96,1024]{1,0:T(8,128)(2,1)} %copy-done.36, bf16[96,1024]{1,0:T(8,128)(2,1)} %copy-done.35, ...), custom_call_target="tpu_custom_call" | custom-call | flops 6442450944 | bytes 16777216 | tf_op jit(solution)/shard_map/expand/pallas_call | solution.py:198
  91.6 8.3 %contract.4 = (bf16[96,1024]{1,0:T(8,128)(2,1)}, bf16[96,1024]{1,0:T(8,128)(2,1)}, bf16[96,1024]{1,0:T(8,128)(2,1)}, bf16[96,1024]{1,0:T(8,128)(2,1)}) custom-call(s32[864]{0:T(1024)} %reshape.559.words_ref, s32[4]{0:T(128)} %pad_add_fusion.1.groups_ref, bf16[32,48,128]{2,1,0:T(8,128)(2,1)} %copy-done.9, bf16[32,48,128]{2,1,0:T(8,128)(2,1)} %copy-done.29, ...), custom_call_target="tpu_custom_call" | custom-call | flops 3221225472 | bytes 8388608 | tf_op jit(solution)/shard_map/contract/pallas_call | solution.py:315
  104.9 13.5 %collective-permute-done.20 = bf16[96,1024]{1,0:T(8,128)(2,1)S(1)} collective-permute-done((bf16[96,1024]{1,0:T(8,128)(2,1)}, bf16[96,1024]{1,0:T(8,128)(2,1)S(1)}, u32[]{:S(2)}, u32[]{:S(2)}) %collective-permute-start.20) | collective-permute-done | bytes 196640 | tf_op jit(solution)/shard_map/ppermute | solution.py:23
  120.5 2.4 activate.5
  129.8 2.8 collective-permute-start.24
  134.0 3.7 %collective-permute-done.26.refs_1_ = bf16[32,48,128]{2,1,0:T(8,128)(2,1)S(1)} collective-permute-done((bf16[32,48,128]{2,1,0:T(8,128)(2,1)S(1)}, bf16[32,48,128]{2,1,0:T(8,128)(2,1)S(1)}, u32[]{:S(2)}, u32[]{:S(2)}) %collective-permute-start.26) | collective-permute-done | bytes 393248 | tf_op jit(solution)/shard_map/ppermute | solution.py:23
  138.4 8.3 %contract.5 = (bf16[96,1024]{1,0:T(8,128)(2,1)}, bf16[96,1024]{1,0:T(8,128)(2,1)}, bf16[96,1024]{1,0:T(8,128)(2,1)}, bf16[96,1024]{1,0:T(8,128)(2,1)}) custom-call(s32[864]{0:T(1024)} %reshape.559.words_ref, s32[4]{0:T(128)} %pad_add_fusion.1.groups_ref, bf16[32,48,128]{2,1,0:T(8,128)(2,1)} %copy-done.7, bf16[32,48,128]{2,1,0:T(8,128)(2,1)} %copy-done.28, ...), custom_call_target="tpu_custom_call" | custom-call | flops 3221225472 | bytes 8388608 | tf_op jit(solution)/shard_map/contract/pallas_call | solution.py:315
  146.8 3.5 %collective-permute-start.28 = (bf16[96,1024]{1,0:T(8,128)(2,1)}, bf16[96,1024]{1,0:T(8,128)(2,1)S(1)}, u32[]{:S(2)}, u32[]{:S(2)}) collective-permute-start(bf16[96,1024]{1,0:T(8,128)(2,1)} %get-tuple-element.69), channel_id=1, source_target_pairs={{0,4},{2,6},{4,0},{6,2},{1,5},{3,7},{5,1},{7,3},{8,12},{10,14},{12... | collective-permute-start | bytes 589832 | tf_op jit(solution)/shard_map/ppermute | solution.py:23
  152.4 13.0 %expand.6 = (f32[48,16]{1,0:T(8,128)}, bf16[2,32,48,128]{3,2,1,0:T(8,128)(2,1)}, bf16[2,32,48,128]{3,2,1,0:T(8,128)(2,1)}) custom-call(s32[864]{0:T(1024)} %reshape.562.words_ref, s32[4]{0:T(128)} %pad_add_fusion.2.groups_ref, bf16[96,1024]{1,0:T(8,128)(2,1)} %copy-done.19, bf16[96,1024]{1,0:T(8,128)(2,1)} %copy-done.39, bf16[96,1024]{1,0:T(8,128)(2,1)} %copy-done.38, ...), custom_call_target="tpu_custom_call" | custom-call | flops 6442450944 | bytes 16777216 | tf_op jit(solution)/shard_map/expand/pallas_call | solution.py:198
  168.0 2.3 collective-permute-start.34
  170.6 15.5 %collective-permute-done.34.refs_1_ = bf16[2,32,48,128]{3,2,1,0:T(8,128)(2,1)S(1)} collective-permute-done((bf16[2,32,48,128]{3,2,1,0:T(8,128)(2,1)}, bf16[2,32,48,128]{3,2,1,0:T(8,128)(2,1)S(1)}, u32[]{:S(2)}, u32[]{:S(2)}) %collective-permute-start.34) | collective-permute-done | bytes 786464 | tf_op jit(solution)/shard_map/ppermute | solution.py:23
  186.1 2.4 activate.6
  190.4 3.0 %collective-permute-start.33 = (bf16[96,1024]{1,0:T(8,128)(2,1)S(1)}, bf16[96,1024]{1,0:T(8,128)(2,1)S(1)}, u32[]{:S(2)}, u32[]{:S(2)}) collective-permute-start(bf16[96,1024]{1,0:T(8,128)(2,1)S(1)} %fusion.5.refs_0_), channel_id=1, source_target_pairs={{0,6},{2,0},{4,2},{6,4},{1,7},{3,1},{5,3},{7,5},{8,14},{10,8},{12,... | collective-permute-start | bytes 589832 | tf_op jit(solution)/shard_map/ppermute | solution.py:23
  196.1 12.4 %collective-permute-done.32.refs_2_ = bf16[96,1024]{1,0:T(8,128)(2,1)S(1)} collective-permute-done((bf16[96,1024]{1,0:T(8,128)(2,1)S(1)}, bf16[96,1024]{1,0:T(8,128)(2,1)S(1)}, u32[]{:S(2)}, u32[]{:S(2)}) %collective-permute-start.32) | collective-permute-done | bytes 196640 | tf_op jit(solution)/shard_map/ppermute | solution.py:23
  210.0 12.7 %expand.7 = (f32[48,16]{1,0:T(8,128)}, bf16[2,32,48,128]{3,2,1,0:T(8,128)(2,1)}, bf16[2,32,48,128]{3,2,1,0:T(8,128)(2,1)}) custom-call(s32[864]{0:T(1024)} %reshape.562.words_ref, s32[4]{0:T(128)} %pad_add_fusion.2.groups_ref, bf16[96,1024]{1,0:T(8,128)(2,1)} %copy-done.21, bf16[96,1024]{1,0:T(8,128)(2,1)} %copy-done.42, bf16[96,1024]{1,0:T(8,128)(2,1)} %copy-done.41, ...), custom_call_target="tpu_custom_call" | custom-call | flops 6442450944 | bytes 16777216 | tf_op jit(solution)/shard_map/expand/pallas_call | solution.py:198
  225.0 8.0 %contract.6 = (bf16[96,1024]{1,0:T(8,128)(2,1)}, bf16[96,1024]{1,0:T(8,128)(2,1)}, bf16[96,1024]{1,0:T(8,128)(2,1)}, bf16[96,1024]{1,0:T(8,128)(2,1)}) custom-call(s32[864]{0:T(1024)} %reshape.562.words_ref, s32[4]{0:T(128)} %pad_add_fusion.2.groups_ref, bf16[32,48,128]{2,1,0:T(8,128)(2,1)} %copy-done.8, bf16[32,48,128]{2,1,0:T(8,128)(2,1)} %copy-done.23, ...), custom_call_target="tpu_custom_call" | custom-call | flops 3221225472 | bytes 8388608 | tf_op jit(solution)/shard_map/contract/pallas_call | solution.py:315
  233.0 5.5 %collective-permute-done.36.refs_1_ = bf16[2,32,48,128]{3,2,1,0:T(8,128)(2,1)S(1)} collective-permute-done((bf16[2,32,48,128]{3,2,1,0:T(8,128)(2,1)}, bf16[2,32,48,128]{3,2,1,0:T(8,128)(2,1)S(1)}, u32[]{:S(2)}, u32[]{:S(2)}) %collective-permute-start.36) | collective-permute-done | bytes 786464 | tf_op jit(solution)/shard_map/ppermute | solution.py:23
  239.4 2.4 activate.7
  243.9 4.6 %collective-permute-start.37 = (bf16[96,1024]{1,0:T(8,128)(2,1)S(1)}, bf16[96,1024]{1,0:T(8,128)(2,1)S(1)}, u32[]{:S(2)}, u32[]{:S(2)}) collective-permute-start(bf16[96,1024]{1,0:T(8,128)(2,1)S(1)} %copy-done.53), channel_id=1, source_target_pairs={{0,6},{2,0},{4,2},{6,4},{1,7},{3,1},{5,3},{7,5},{8,14},{10,8},{12,... | collective-permute-start | bytes 589832 | tf_op jit(solution)/shard_map/ppermute | solution.py:23
  248.5 5.5 %collective-permute-start.38 = (bf16[96,1024]{1,0:T(8,128)(2,1)S(1)}, bf16[96,1024]{1,0:T(8,128)(2,1)S(1)}, u32[]{:S(2)}, u32[]{:S(2)}) collective-permute-start(bf16[96,1024]{1,0:T(8,128)(2,1)S(1)} %copy-done.52), channel_id=1, source_target_pairs={{0,4},{2,6},{4,0},{6,2},{1,5},{3,7},{5,1},{7,3},{8,12},{10,14},{12... | collective-permute-start | bytes 589832 | tf_op jit(solution)/shard_map/ppermute | solution.py:23
  256.2 7.9 %contract.7 = (bf16[96,1024]{1,0:T(8,128)(2,1)}, bf16[96,1024]{1,0:T(8,128)(2,1)}, bf16[96,1024]{1,0:T(8,128)(2,1)}, bf16[96,1024]{1,0:T(8,128)(2,1)}) custom-call(s32[864]{0:T(1024)} %reshape.562.words_ref, s32[4]{0:T(128)} %pad_add_fusion.2.groups_ref, bf16[32,48,128]{2,1,0:T(8,128)(2,1)} %copy-done.10, bf16[32,48,128]{2,1,0:T(8,128)(2,1)} %copy-done.30, ...), custom_call_target="tpu_custom_call" | custom-call | flops 3221225472 | bytes 8388608 | tf_op jit(solution)/shard_map/contract/pallas_call | solution.py:315
  264.1 3.1 %collective-permute-start.42 = (bf16[96,1024]{1,0:T(8,128)(2,1)}, bf16[96,1024]{1,0:T(8,128)(2,1)S(1)}, u32[]{:S(2)}, u32[]{:S(2)}) collective-permute-start(bf16[96,1024]{1,0:T(8,128)(2,1)} %get-tuple-element.85), channel_id=1, source_target_pairs={{0,6},{2,0},{4,2},{6,4},{1,7},{3,1},{5,3},{7,5},{8,14},{10,8},{12,... | collective-permute-start | bytes 589832 | tf_op jit(solution)/shard_map/ppermute | solution.py:23
  267.2 3.8 %collective-permute-start.43 = (bf16[96,1024]{1,0:T(8,128)(2,1)}, bf16[96,1024]{1,0:T(8,128)(2,1)S(1)}, u32[]{:S(2)}, u32[]{:S(2)}) collective-permute-start(bf16[96,1024]{1,0:T(8,128)(2,1)} %get-tuple-element.86), channel_id=1, source_target_pairs={{0,4},{2,6},{4,0},{6,2},{1,5},{3,7},{5,1},{7,3},{8,12},{10,14},{12... | collective-permute-start | bytes 589832 | tf_op jit(solution)/shard_map/ppermute | solution.py:23
  276.6 4.2 %collective-permute-done.43 = bf16[96,1024]{1,0:T(8,128)(2,1)S(1)} collective-permute-done((bf16[96,1024]{1,0:T(8,128)(2,1)}, bf16[96,1024]{1,0:T(8,128)(2,1)S(1)}, u32[]{:S(2)}, u32[]{:S(2)}) %collective-permute-start.43) | collective-permute-done | bytes 196640 | tf_op jit(solution)/shard_map/ppermute | solution.py:23
  285.4 2.3 collective-permute-done.45
  287.8 7.9 %collective-permute-start.46 = (bf16[96,1024]{1,0:T(8,128)(2,1)S(1)}, bf16[96,1024]{1,0:T(8,128)(2,1)S(1)}, u32[]{:S(2)}, u32[]{:S(2)}) collective-permute-start(bf16[96,1024]{1,0:T(8,128)(2,1)S(1)} %get-tuple-element.96), channel_id=1, source_target_pairs={{0,8},{8,0},{1,9},{9,1},{2,10},{10,2},{3,11},{11,3},{4,12},{12,4},... | collective-permute-start | bytes 589832 | tf_op jit(solution)/shard_map/ppermute | solution.py:23
  (267 shorter events, 73.2 us)
Async XLA Ops:
  3.2 33.3 %collective-permute-start.6 = (bf16[256,128,128]{2,1,0:T(8,128)(2,1)}, bf16[256,128,128]{2,1,0:T(8,128)(2,1)}, u32[]{:S(2)}, u32[]{:S(2)}) collective-permute-start(bf16[256,128,128]{2,1,0:T(8,128)(2,1)} %bitcast.55), channel_id=1, source_target_pairs={{0,8},{8,0},{1,9},{9,1},{2,10},{10,2},{3,11},{11,3},{4,12},{12,4},... | collective-permute-start | bytes 25165832 | tf_op jit(solution)/shard_map/ppermute | solution.py:23
  3.5 33.0 %collective-permute-start.7 = (bf16[256,128,128]{2,1,0:T(8,128)(2,1)}, bf16[256,128,128]{2,1,0:T(8,128)(2,1)}, u32[]{:S(2)}, u32[]{:S(2)}) collective-permute-start(bf16[256,128,128]{2,1,0:T(8,128)(2,1)} %bitcast.60), channel_id=1, source_target_pairs={{0,8},{8,0},{1,9},{9,1},{2,10},{10,2},{3,11},{11,3},{4,12},{12,4},... | collective-permute-start | bytes 25165832 | tf_op jit(solution)/shard_map/ppermute | solution.py:23
  3.7 87.1 %collective-permute-start.18 = (bf16[256,128,128]{2,1,0:T(8,128)(2,1)}, bf16[256,128,128]{2,1,0:T(8,128)(2,1)}, u32[]{:S(2)}, u32[]{:S(2)}) collective-permute-start(bf16[256,128,128]{2,1,0:T(8,128)(2,1)} %bitcast.65), channel_id=1, source_target_pairs={{0,8},{8,0},{1,9},{9,1},{2,10},{10,2},{3,11},{11,3},{4,12},{12,4},... | collective-permute-start | bytes 25165832 | tf_op jit(solution)/shard_map/ppermute | solution.py:23
  5.0 15.1 %collective-permute-start.12 = (bf16[48,1024]{1,0:T(8,128)(2,1)S(1)}, bf16[48,1024]{1,0:T(8,128)(2,1)S(1)}, u32[]{:S(2)}, u32[]{:S(2)}) collective-permute-start(bf16[48,1024]{1,0:T(8,128)(2,1)S(1)} %get-tuple-element.99.refs_0_), channel_id=1, source_target_pairs={{0,6},{2,0},{4,2},{6,4},{1,7},{3,1},{5,3},{7,5},{8,14},{10,8},{12,... | collective-permute-start | bytes 294920 | tf_op jit(solution)/shard_map/ppermute | solution.py:23
  31.8 22.6 %collective-permute-start.15 = (bf16[24,32,128]{2,0,1:T(8,128)(2,1)S(1)}, bf16[24,32,128]{2,0,1:T(8,128)(2,1)S(1)}, u32[]{:S(2)}, u32[]{:S(2)}) collective-permute-start(bf16[24,32,128]{2,0,1:T(8,128)(2,1)S(1)} %select_bitcast_fusion.2), channel_id=1, source_target_pairs={{0,8},{8,0},{1,9},{9,1},{2,10},{10,2},{3,11},{11,3},{4,12},{12,4},... | collective-permute-start | bytes 589832 | tf_op jit(solution)/shard_map/ppermute | solution.py:23
  52.7 16.5 %collective-permute-start.14 = (bf16[2,32,48,128]{3,2,1,0:T(8,128)(2,1)}, bf16[2,32,48,128]{3,2,1,0:T(8,128)(2,1)S(1)}, u32[]{:S(2)}, u32[]{:S(2)}) collective-permute-start(bf16[2,32,48,128]{3,2,1,0:T(8,128)(2,1)} %get-tuple-element.52), channel_id=1, source_target_pairs={{0,1},{1,0},{2,3},{3,2},{4,5},{5,4},{6,7},{7,6},{8,9},{9,8},{10,11... | collective-permute-start | bytes 2359304 | tf_op jit(solution)/shard_map/ppermute | solution.py:23
  53.9 19.5 %collective-permute-start.5 = (bf16[96,1024]{1,0:T(8,128)(2,1)S(1)}, bf16[96,1024]{1,0:T(8,128)(2,1)S(1)}, u32[]{:S(2)}, u32[]{:S(2)}) collective-permute-start(bf16[96,1024]{1,0:T(8,128)(2,1)S(1)} %pad_maximum_fusion.2.refs_0_), channel_id=1, source_target_pairs={{0,6},{2,0},{4,2},{6,4},{1,7},{3,1},{5,3},{7,5},{8,14},{10,8},{12,... | collective-permute-start | bytes 589832 | tf_op jit(solution)/shard_map/ppermute | solution.py:23
  54.0 19.4 %collective-permute-start.4 = (bf16[96,1024]{1,0:T(8,128)(2,1)S(1)}, bf16[96,1024]{1,0:T(8,128)(2,1)S(1)}, u32[]{:S(2)}, u32[]{:S(2)}) collective-permute-start(bf16[96,1024]{1,0:T(8,128)(2,1)S(1)} %pad_maximum_fusion.2.refs_0_), channel_id=1, source_target_pairs={{0,4},{2,6},{4,0},{6,2},{1,5},{3,7},{5,1},{7,3},{8,12},{10,14},{12... | collective-permute-start | bytes 589832 | tf_op jit(solution)/shard_map/ppermute | solution.py:23
  54.4 19.0 %collective-permute-start.3 = (bf16[96,1024]{1,0:T(8,128)(2,1)S(1)}, bf16[96,1024]{1,0:T(8,128)(2,1)S(1)}, u32[]{:S(2)}, u32[]{:S(2)}) collective-permute-start(bf16[96,1024]{1,0:T(8,128)(2,1)S(1)} %pad_maximum_fusion.2.refs_0_), channel_id=1, source_target_pairs={{0,2},{2,4},{4,6},{6,0},{1,3},{3,5},{5,7},{7,1},{8,10},{10,12},{12... | collective-permute-start | bytes 589832 | tf_op jit(solution)/shard_map/ppermute | solution.py:23
  72.2 18.6 %collective-permute-start.17 = (bf16[32,48,128]{2,1,0:T(8,128)(2,1)S(1)}, bf16[32,48,128]{2,1,0:T(8,128)(2,1)S(1)}, u32[]{:S(2)}, u32[]{:S(2)}) collective-permute-start(bf16[32,48,128]{2,1,0:T(8,128)(2,1)S(1)} %get-tuple-element.58.refs_0_), channel_id=1, source_target_pairs={{0,1},{1,0},{2,3},{3,2},{4,5},{5,4},{6,7},{7,6},{8,9},{9,8},{10,11... | collective-permute-start | bytes 1179656 | tf_op jit(solution)/shard_map/ppermute | solution.py:23
  89.8 29.7 %collective-permute-start.16 = (bf16[2,32,48,128]{3,2,1,0:T(8,128)(2,1)}, bf16[2,32,48,128]{3,2,1,0:T(8,128)(2,1)S(1)}, u32[]{:S(2)}, u32[]{:S(2)}) collective-permute-start(bf16[2,32,48,128]{3,2,1,0:T(8,128)(2,1)} %get-tuple-element.56), channel_id=1, source_target_pairs={{0,1},{1,0},{2,3},{3,2},{4,5},{5,4},{6,7},{7,6},{8,9},{9,8},{10,11... | collective-permute-start | bytes 2359304 | tf_op jit(solution)/shard_map/ppermute | solution.py:23
  99.9 18.5 %collective-permute-start.20 = (bf16[96,1024]{1,0:T(8,128)(2,1)}, bf16[96,1024]{1,0:T(8,128)(2,1)S(1)}, u32[]{:S(2)}, u32[]{:S(2)}) collective-permute-start(bf16[96,1024]{1,0:T(8,128)(2,1)} %get-tuple-element.63), channel_id=1, source_target_pairs={{0,4},{2,6},{4,0},{6,2},{1,5},{3,7},{5,1},{7,3},{8,12},{10,14},{12... | collective-permute-start | bytes 589832 | tf_op jit(solution)/shard_map/ppermute | solution.py:23
  102.1 16.4 %collective-permute-start.21 = (bf16[96,1024]{1,0:T(8,128)(2,1)}, bf16[96,1024]{1,0:T(8,128)(2,1)S(1)}, u32[]{:S(2)}, u32[]{:S(2)}) collective-permute-start(bf16[96,1024]{1,0:T(8,128)(2,1)} %get-tuple-element.64), channel_id=1, source_target_pairs={{0,2},{2,4},{4,6},{6,0},{1,3},{3,5},{5,7},{7,1},{8,10},{10,12},{12... | collective-permute-start | bytes 589832 | tf_op jit(solution)/shard_map/ppermute | solution.py:23
  129.7 20.6 %collective-permute-start.25 = (bf16[96,1024]{1,0:T(8,128)(2,1)S(1)}, bf16[96,1024]{1,0:T(8,128)(2,1)S(1)}, u32[]{:S(2)}, u32[]{:S(2)}) collective-permute-start(bf16[96,1024]{1,0:T(8,128)(2,1)S(1)} %fusion.4.refs_0_), channel_id=1, source_target_pairs={{0,6},{2,0},{4,2},{6,4},{1,7},{3,1},{5,3},{7,5},{8,14},{10,8},{12,... | collective-permute-start | bytes 589832 | tf_op jit(solution)/shard_map/ppermute | solution.py:23
  129.8 21.9 %collective-permute-start.24 = (bf16[96,1024]{1,0:T(8,128)(2,1)S(1)}, bf16[96,1024]{1,0:T(8,128)(2,1)S(1)}, u32[]{:S(2)}, u32[]{:S(2)}) collective-permute-start(bf16[96,1024]{1,0:T(8,128)(2,1)S(1)} %fusion.4.refs_0_), channel_id=1, source_target_pairs={{0,4},{2,6},{4,0},{6,2},{1,5},{3,7},{5,1},{7,3},{8,12},{10,14},{12... | collective-permute-start | bytes 589832 | tf_op jit(solution)/shard_map/ppermute | solution.py:23
  132.6 19.1 %collective-permute-start.23 = (bf16[96,1024]{1,0:T(8,128)(2,1)S(1)}, bf16[96,1024]{1,0:T(8,128)(2,1)S(1)}, u32[]{:S(2)}, u32[]{:S(2)}) collective-permute-start(bf16[96,1024]{1,0:T(8,128)(2,1)S(1)} %fusion.4.refs_0_), channel_id=1, source_target_pairs={{0,2},{2,4},{4,6},{6,0},{1,3},{3,5},{5,7},{7,1},{8,10},{10,12},{12... | collective-permute-start | bytes 589832 | tf_op jit(solution)/shard_map/ppermute | solution.py:23
  146.7 23.5 %collective-permute-start.27 = (bf16[96,1024]{1,0:T(8,128)(2,1)}, bf16[96,1024]{1,0:T(8,128)(2,1)S(1)}, u32[]{:S(2)}, u32[]{:S(2)}) collective-permute-start(bf16[96,1024]{1,0:T(8,128)(2,1)} %get-tuple-element.68), channel_id=1, source_target_pairs={{0,6},{2,0},{4,2},{6,4},{1,7},{3,1},{5,3},{7,5},{8,14},{10,8},{12,... | collective-permute-start | bytes 589832 | tf_op jit(solution)/shard_map/ppermute | solution.py:23
  146.8 23.5 %collective-permute-start.28 = (bf16[96,1024]{1,0:T(8,128)(2,1)}, bf16[96,1024]{1,0:T(8,128)(2,1)S(1)}, u32[]{:S(2)}, u32[]{:S(2)}) collective-permute-start(bf16[96,1024]{1,0:T(8,128)(2,1)} %get-tuple-element.69), channel_id=1, source_target_pairs={{0,4},{2,6},{4,0},{6,2},{1,5},{3,7},{5,1},{7,3},{8,12},{10,14},{12... | collective-permute-start | bytes 589832 | tf_op jit(solution)/shard_map/ppermute | solution.py:23
  150.3 20.0 %collective-permute-start.29 = (bf16[96,1024]{1,0:T(8,128)(2,1)}, bf16[96,1024]{1,0:T(8,128)(2,1)S(1)}, u32[]{:S(2)}, u32[]{:S(2)}) collective-permute-start(bf16[96,1024]{1,0:T(8,128)(2,1)} %get-tuple-element.70), channel_id=1, source_target_pairs={{0,2},{2,4},{4,6},{6,0},{1,3},{3,5},{5,7},{7,1},{8,10},{10,12},{12... | collective-permute-start | bytes 589832 | tf_op jit(solution)/shard_map/ppermute | solution.py:23
  168.0 18.1 %collective-permute-start.34 = (bf16[2,32,48,128]{3,2,1,0:T(8,128)(2,1)}, bf16[2,32,48,128]{3,2,1,0:T(8,128)(2,1)S(1)}, u32[]{:S(2)}, u32[]{:S(2)}) collective-permute-start(bf16[2,32,48,128]{3,2,1,0:T(8,128)(2,1)} %get-tuple-element.72), channel_id=1, source_target_pairs={{0,1},{1,0},{2,3},{3,2},{4,5},{5,4},{6,7},{7,6},{8,9},{9,8},{10,11... | collective-permute-start | bytes 2359304 | tf_op jit(solution)/shard_map/ppermute | solution.py:23
  170.5 19.8 %collective-permute-start.30 = (bf16[96,1024]{1,0:T(8,128)(2,1)S(1)}, bf16[96,1024]{1,0:T(8,128)(2,1)S(1)}, u32[]{:S(2)}, u32[]{:S(2)}) collective-permute-start(bf16[96,1024]{1,0:T(8,128)(2,1)S(1)} %pad_maximum_fusion.4), channel_id=1, source_target_pairs={{0,1},{1,0},{2,3},{3,2},{4,5},{5,4},{6,7},{7,6},{8,9},{9,8},{10,11... | collective-permute-start | bytes 589832 | tf_op jit(solution)/shard_map/ppermute | solution.py:23
  189.1 19.4 %collective-permute-start.35 = (bf16[32,48,128]{2,1,0:T(8,128)(2,1)S(1)}, bf16[32,48,128]{2,1,0:T(8,128)(2,1)S(1)}, u32[]{:S(2)}, u32[]{:S(2)}) collective-permute-start(bf16[32,48,128]{2,1,0:T(8,128)(2,1)S(1)} %get-tuple-element.73.refs_0_), channel_id=1, source_target_pairs={{0,1},{1,0},{2,3},{3,2},{4,5},{5,4},{6,7},{7,6},{8,9},{9,8},{10,11... | collective-permute-start | bytes 1179656 | tf_op jit(solution)/shard_map/ppermute | solution.py:23
  193.4 15.1 %collective-permute-start.32 = (bf16[96,1024]{1,0:T(8,128)(2,1)S(1)}, bf16[96,1024]{1,0:T(8,128)(2,1)S(1)}, u32[]{:S(2)}, u32[]{:S(2)}) collective-permute-start(bf16[96,1024]{1,0:T(8,128)(2,1)S(1)} %fusion.5.refs_0_), channel_id=1, source_target_pairs={{0,4},{2,6},{4,0},{6,2},{1,5},{3,7},{5,1},{7,3},{8,12},{10,14},{12... | collective-permute-start | bytes 589832 | tf_op jit(solution)/shard_map/ppermute | solution.py:23
  193.4 15.1 %collective-permute-start.31 = (bf16[96,1024]{1,0:T(8,128)(2,1)S(1)}, bf16[96,1024]{1,0:T(8,128)(2,1)S(1)}, u32[]{:S(2)}, u32[]{:S(2)}) collective-permute-start(bf16[96,1024]{1,0:T(8,128)(2,1)S(1)} %fusion.5.refs_0_), channel_id=1, source_target_pairs={{0,2},{2,4},{4,6},{6,0},{1,3},{3,5},{5,7},{7,1},{8,10},{10,12},{12... | collective-permute-start | bytes 589832 | tf_op jit(solution)/shard_map/ppermute | solution.py:23
  222.8 15.7 %collective-permute-start.36 = (bf16[2,32,48,128]{3,2,1,0:T(8,128)(2,1)}, bf16[2,32,48,128]{3,2,1,0:T(8,128)(2,1)S(1)}, u32[]{:S(2)}, u32[]{:S(2)}) collective-permute-start(bf16[2,32,48,128]{3,2,1,0:T(8,128)(2,1)} %get-tuple-element.75), channel_id=1, source_target_pairs={{0,1},{1,0},{2,3},{3,2},{4,5},{5,4},{6,7},{7,6},{8,9},{9,8},{10,11... | collective-permute-start | bytes 2359304 | tf_op jit(solution)/shard_map/ppermute | solution.py:23
  242.5 13.0 %collective-permute-start.41 = (bf16[32,48,128]{2,1,0:T(8,128)(2,1)S(1)}, bf16[32,48,128]{2,1,0:T(8,128)(2,1)S(1)}, u32[]{:S(2)}, u32[]{:S(2)}) collective-permute-start(bf16[32,48,128]{2,1,0:T(8,128)(2,1)S(1)} %get-tuple-element.83.refs_0_), channel_id=1, source_target_pairs={{0,1},{1,0},{2,3},{3,2},{4,5},{5,4},{6,7},{7,6},{8,9},{9,8},{10,11... | collective-permute-start | bytes 1179656 | tf_op jit(solution)/shard_map/ppermute | solution.py:23
  243.9 27.2 %collective-permute-start.37 = (bf16[96,1024]{1,0:T(8,128)(2,1)S(1)}, bf16[96,1024]{1,0:T(8,128)(2,1)S(1)}, u32[]{:S(2)}, u32[]{:S(2)}) collective-permute-start(bf16[96,1024]{1,0:T(8,128)(2,1)S(1)} %copy-done.53), channel_id=1, source_target_pairs={{0,6},{2,0},{4,2},{6,4},{1,7},{3,1},{5,3},{7,5},{8,14},{10,8},{12,... | collective-permute-start | bytes 589832 | tf_op jit(solution)/shard_map/ppermute | solution.py:23
  248.5 23.9 %collective-permute-start.38 = (bf16[96,1024]{1,0:T(8,128)(2,1)S(1)}, bf16[96,1024]{1,0:T(8,128)(2,1)S(1)}, u32[]{:S(2)}, u32[]{:S(2)}) collective-permute-start(bf16[96,1024]{1,0:T(8,128)(2,1)S(1)} %copy-done.52), channel_id=1, source_target_pairs={{0,4},{2,6},{4,0},{6,2},{1,5},{3,7},{5,1},{7,3},{8,12},{10,14},{12... | collective-permute-start | bytes 589832 | tf_op jit(solution)/shard_map/ppermute | solution.py:23
  254.1 18.4 %collective-permute-start.39 = (bf16[96,1024]{1,0:T(8,128)(2,1)S(1)}, bf16[96,1024]{1,0:T(8,128)(2,1)S(1)}, u32[]{:S(2)}, u32[]{:S(2)}) collective-permute-start(bf16[96,1024]{1,0:T(8,128)(2,1)S(1)} %copy-done.51), channel_id=1, source_target_pairs={{0,2},{2,4},{4,6},{6,0},{1,3},{3,5},{5,7},{7,1},{8,10},{10,12},{12... | collective-permute-start | bytes 589832 | tf_op jit(solution)/shard_map/ppermute | solution.py:23
  264.1 12.5 %collective-permute-start.42 = (bf16[96,1024]{1,0:T(8,128)(2,1)}, bf16[96,1024]{1,0:T(8,128)(2,1)S(1)}, u32[]{:S(2)}, u32[]{:S(2)}) collective-permute-start(bf16[96,1024]{1,0:T(8,128)(2,1)} %get-tuple-element.85), channel_id=1, source_target_pairs={{0,6},{2,0},{4,2},{6,4},{1,7},{3,1},{5,3},{7,5},{8,14},{10,8},{12,... | collective-permute-start | bytes 589832 | tf_op jit(solution)/shard_map/ppermute | solution.py:23
  267.2 13.6 %collective-permute-start.43 = (bf16[96,1024]{1,0:T(8,128)(2,1)}, bf16[96,1024]{1,0:T(8,128)(2,1)S(1)}, u32[]{:S(2)}, u32[]{:S(2)}) collective-permute-start(bf16[96,1024]{1,0:T(8,128)(2,1)} %get-tuple-element.86), channel_id=1, source_target_pairs={{0,4},{2,6},{4,0},{6,2},{1,5},{3,7},{5,1},{7,3},{8,12},{10,14},{12... | collective-permute-start | bytes 589832 | tf_op jit(solution)/shard_map/ppermute | solution.py:23
  272.6 12.7 %collective-permute-start.40 = (bf16[48,1024]{1,0:T(8,128)(2,1)S(1)}, bf16[48,1024]{1,0:T(8,128)(2,1)S(1)}, u32[]{:S(2)}, u32[]{:S(2)}) collective-permute-start(bf16[48,1024]{1,0:T(8,128)(2,1)S(1)} %slice.266), channel_id=1, source_target_pairs={{0,1},{1,0},{2,3},{3,2},{4,5},{5,4},{6,7},{7,6},{8,9},{9,8},{10,11... | collective-permute-start | bytes 294920 | tf_op jit(solution)/shard_map/ppermute | solution.py:23
  (70 other events, 665.3 us)

commit v9 on v8

--- a/solution.py
+++ b/solution.py
@@ -102,41 +102,40 @@
     return pltpu.make_async_copy(choices[0], tiles.at[pl.ds(0, count)], sem)
 
 
-def expand_kernel(owners, reps, unread, words_ref, groups_ref, *refs):
-    spans = len(refs) - 13 - reps - unread
-    blocks = refs[:spans]
-    gain_ref, left_ref, own_gate, other_gate, own_up, other_up = refs[spans : spans + 6]
-    raw_ref, *part_refs = refs[spans + 6 + unread : spans + 7 + unread + reps]
+def expand_kernel(reps, words_ref, groups_ref, *refs):
+    stacks = refs[:reps]
+    gain_ref, left_ref, own_gate, other_gate, own_up, other_up = refs[reps : reps + 6]
+    raw_ref, *part_refs = refs[reps + 6 : 2 * reps + 7]
     total_ref, gate_tiles, gate_sem, up_tiles, up_sem, x_ref = refs[-6:]
-    span_rows, width = blocks[0].shape
-    split = spans // owners
-    rows = part_refs[0].shape[2]
+    owners, rows, width = stacks[0].shape
     per_owner = width // BLOCK
     strip = 48 if rows % 48 == 0 else 16
     gate_copy = load_tiles(groups_ref[3], (own_gate, other_gate), gate_tiles, gate_sem)
-    up_copy = load_tiles(groups_ref[3], (own_up, other_up), up_tiles, up_sem)
-
-    for span in range(split):
-
-        def norm_rows(i, carry, span=span):
+
+    for rep in range(reps):
+
+        def norm_rows(i, carry, rep=rep):
             start = pl.multiple_of(i * strip, strip)
             at = pl.ds(start, strip)
+
+            def load(owner, part):
+                return stacks[rep][owner, at, pl.ds(part * BLOCK, BLOCK)].astype(jnp.float32)
+
             squares = jnp.zeros((strip, BLOCK), jnp.float32)
             for owner in range(owners):
                 for part in range(per_owner):
-                    values = blocks[owner * split + span][at, pl.ds(part * BLOCK, BLOCK)].astype(jnp.float32)
+                    values = load(owner, part)
                     squares = squares + values * values
             total = jnp.sum(squares, axis=1, keepdims=True)
             inverse = lax.rsqrt(total / (owners * width) + epsilon)
             for owner in range(owners):
                 for part in range(per_owner):
-                    values = blocks[owner * split + span][at, pl.ds(part * BLOCK, BLOCK)].astype(jnp.float32)
                     gain = gain_ref[:, pl.ds(owner * width + part * BLOCK, BLOCK)].astype(jnp.float32)
-                    normed = (values * inverse * gain).astype(jnp.bfloat16)
-                    x_ref[owner * per_owner + part, pl.ds(span * span_rows + start, strip), :] = normed
+                    normed = (load(owner, part) * inverse * gain).astype(jnp.bfloat16)
+                    x_ref[owner * per_owner + part, pl.ds(rep * rows + start, strip), :] = normed
             return carry
 
-        lax.fori_loop(0, span_rows // strip, norm_rows, 0)
+        lax.fori_loop(0, rows // strip, norm_rows, 0)
     raw = jnp.zeros(raw_ref.shape, jnp.float32)
     step = min(8, x_ref.shape[0])
     for d in range(0, x_ref.shape[0], step):
@@ -154,9 +153,13 @@
     def add(block, product):
         total_ref[block] += product
 
-    for which, tiles, copy in ((0, gate_tiles, gate_copy), (1, up_tiles, up_copy)):
+    for which, tiles in ((0, gate_tiles), (1, up_tiles)):
         total_ref[...] = jnp.zeros(total_ref.shape, jnp.float32)
-        copy.wait()
+        if which == 0:
+            gate_copy.wait()
+            up_copy = load_tiles(groups_ref[3], (own_up, other_up), up_tiles, up_sem)
+        else:
+            up_copy.wait()
         multiply_tiles(words_ref, groups_ref, which, words_ref.shape[0] // 3, read, tiles, add)
         for rep, part_ref in enumerate(part_refs):
 
@@ -188,26 +191,25 @@
     ]
 
 
-def expand(words, groups, blocks, gain, left, gate_tiles, up_tiles, own_cols, reps, after):
+def expand(words, groups, stacks, gain, left, gate_tiles, up_tiles, own_cols):
+    reps = len(stacks)
     features = gain.shape[1]
-    owners = features // blocks[0].shape[1]
-    all_rows = sum(block.size for block in blocks) // features
-    rows = all_rows // reps
+    rows = stacks[0].shape[1]
     tile_count = gate_tiles[0].shape[0]
-    scratch = tile_scratch(tile_count, own_cols, all_rows)
+    scratch = tile_scratch(tile_count, own_cols, reps * rows)
     out = pl.pallas_call(
-        functools.partial(expand_kernel, owners, reps, len(after)),
+        functools.partial(expand_kernel, reps),
         out_shape=[jax.ShapeDtypeStruct((rows, left.shape[0]), jnp.float32)]
         + [jax.ShapeDtypeStruct((2, own_cols, rows, BLOCK), jnp.bfloat16)] * reps,
-        in_specs=[SMEM, SMEM] + [VMEM] * (len(blocks) + 2) + [HBM] * (4 + len(after)),
+        in_specs=[SMEM, SMEM] + [VMEM] * (reps + 2) + [HBM] * 4,
         out_specs=[VMEM] * (1 + reps),
         scratch_shapes=scratch
         + scratch[1:]
-        + [pltpu.VMEM((features // BLOCK, all_rows, BLOCK), jnp.bfloat16)],
+        + [pltpu.VMEM((features // BLOCK, reps * rows, BLOCK), jnp.bfloat16)],
         compiler_params=pltpu.CompilerParams(vmem_limit_bytes=VMEM_LIMIT),
-        cost_estimate=tile_cost(2 * tile_count, all_rows),
+        cost_estimate=tile_cost(2 * tile_count, reps * rows),
         name="expand",
-    )(words, groups, *blocks, gain, left, *gate_tiles, *up_tiles, *after)
+    )(words, groups, *stacks, gain, left, *gate_tiles, *up_tiles)
     return out[0], out[1:]
 
 
@@ -248,7 +250,7 @@
     coef_ref[...] = picks * down
 
 
-def activate(parts, raw, picks, wide_cols, down_cols, after):
+def activate(parts, raw, picks, wide_cols, down_cols):
     own_cols, rows = parts[0].shape[1:3]
     noise = picks.shape[1]
     reps = len(parts)
@@ -258,7 +260,7 @@
             jax.ShapeDtypeStruct((own_cols, rows, BLOCK), jnp.bfloat16),
             jax.ShapeDtypeStruct((rows, noise), jnp.float32),
         ],
-        in_specs=[VMEM] * (reps + 4) + [HBM] * len(after),
+        in_specs=[VMEM] * (reps + 4),
         out_specs=[VMEM] * 2,
         compiler_params=pltpu.CompilerParams(vmem_limit_bytes=16 * MIB),
         cost_estimate=pl.CostEstimate(
@@ -267,16 +269,15 @@
             transcendentals=own_cols * rows * BLOCK,
         ),
         name="activate",
-    )(*parts, raw, picks, wide_cols, down_cols, *after)
-
-
-def contract_kernel(owners, reps, words_ref, groups_ref, *refs):
+    )(*parts, raw, picks, wide_cols, down_cols)
+
+
+def contract_kernel(reps, words_ref, groups_ref, *refs):
     hiddens = refs[:reps]
     coef_ref, right_ref, own_hbm, other_hbm = refs[reps : reps + 4]
-    outs = refs[-3 - owners : -3]
+    outs = refs[-3 - reps : -3]
     total_ref, tiles, sem = refs[-3:]
     rows = hiddens[0].shape[1]
-    per_owner = outs[0].shape[1] // BLOCK
     blocks = total_ref.shape[0]
     copy = load_tiles(groups_ref[3], (own_hbm, other_hbm), tiles, sem)
 
@@ -302,26 +303,26 @@
                 )
     copy.wait()
     multiply_tiles(words_ref, groups_ref, 2, words_ref.shape[0] // 3, read, tiles, add)
-    for owner in range(owners):
-        for part in range(per_owner):
-            outs[owner][:, pl.ds(part * BLOCK, BLOCK)] = total_ref[owner * per_owner + part].astype(jnp.bfloat16)
-
-
-def contract(words, groups, hiddens, coef, right, tiles, owners, after):
+    for rep in range(reps):
+        for d in range(blocks):
+            outs[rep][:, pl.ds(d * BLOCK, BLOCK)] = total_ref[d, pl.ds(rep * rows, rows), :].astype(jnp.bfloat16)
+
+
+def contract(words, groups, hiddens, coef, right, tiles):
     own_cols, rows = hiddens[0].shape[:2]
     reps = len(hiddens)
     features = right.shape[1]
     tile_count = tiles[0].shape[0]
     return pl.pallas_call(
-        functools.partial(contract_kernel, owners, reps),
-        out_shape=[jax.ShapeDtypeStruct((reps * rows, features // owners), jnp.bfloat16)] * owners,
-        in_specs=[SMEM, SMEM] + [VMEM] * (reps + 2) + [HBM] * (2 + len(after)),
-        out_specs=[VMEM] * owners,
+        functools.partial(contract_kernel, reps),
+        out_shape=[jax.ShapeDtypeStruct((rows, features), jnp.bfloat16)] * reps,
+        in_specs=[SMEM, SMEM] + [VMEM] * (reps + 2) + [HBM] * 2,
+        out_specs=[VMEM] * reps,
         scratch_shapes=tile_scratch(tile_count, features // BLOCK, reps * rows),
         compiler_params=pltpu.CompilerParams(vmem_limit_bytes=VMEM_LIMIT),
         cost_estimate=tile_cost(tile_count, reps * rows),
         name="contract",
-    )(words, groups, *hiddens, coef, right, *tiles, *after)
+    )(words, groups, *hiddens, coef, right, *tiles)
 
 
 def per_device(
@@ -355,14 +356,13 @@
     half = rows // 2
     piece = half // 2
     mine_rows = lax.dynamic_slice_in_dim(tokens, section_index * half, half)
-    others = [hop(mine_rows, "rep", g) for g in range(1, reps)]
-
-    def gather(value):
-        return [hop(value, "tensor", step) for step in range(1, owners)]
-
-    first_spans = [value[:piece] for value in [mine_rows] + others]
-    first_blocks = [[span] + gather(span) for span in first_spans]
-    first_blocks = [first_blocks[g][step] for step in range(owners) for g in range(reps)]
+    streams = [mine_rows[:piece], mine_rows[piece:]]
+
+    def gathered(own):
+        stack = jnp.stack([own] + [hop(own, "tensor", step) for step in range(1, owners)])
+        return [stack] + [hop(stack, "rep", g) for g in range(1, reps)]
+
+    stacks = [gathered(stream) for stream in streams]
 
     codes = jnp.stack([gate_slot[0], up_slot[0], down_slot[0]])
     codes = lax.dynamic_slice_in_dim(codes, rep_index * tile_count, tile_count, axis=1)
@@ -409,67 +409,33 @@
 
     layers = [tables(section) for section in range(2)]
 
-    def expanded(blocks, section, after=()):
-        words, groups, left, _, gain, _, _ = layers[section]
-        return expand(words, groups, blocks, gain, left, gate_pair, up_pair, own_cols, reps, after)
-
-    def activated(parts, raw, picked, section, after=()):
-        wide_cols, down_cols = layers[section][5:]
-        received = [hop(part, "rep", -(g + 1)) for g, part in enumerate(parts[1:])]
-        hidden, coef = activate([parts[0]] + received, raw, picked, wide_cols, down_cols, after)
-        return coef, hidden, [hop(hidden, "rep", g) for g in range(1, reps)]
-
-    def contracted(coef, hidden, received, section, after=()):
-        words, groups, _, right, _, _, _ = layers[section]
-        return contract(words, groups, [hidden] + received, coef, right, down_pair, owners, after)
-
-    def scattered(outs):
-        summed = outs[0].astype(jnp.float32)
+    mine_picks = lax.dynamic_slice_in_dim(picks, section_index * half, half)
+    picked = [mine_picks[:piece], mine_picks[piece:]]
+
+    def layer(stacks, picked, section):
+        words, groups, left, right, gain, wide_cols, down_cols = layers[section]
+        raw, parts = expand(words, groups, stacks, gain, left, gate_pair, up_pair, own_cols)
+        parts = [parts[0]] + [hop(parts[g], "rep", -g) for g in range(1, reps)]
+        hidden, coef = activate(parts, raw, picked, wide_cols, down_cols)
+        hiddens = [hidden] + [hop(hidden, "rep", g) for g in range(1, reps)]
+        return contract(words, groups, hiddens, coef, right, down_pair)
+
+    def scattered(own, outs):
+        total = outs[0].astype(jnp.float32)
+        for g in range(1, reps):
+            total = total + hop(outs[g], "rep", -g).astype(jnp.float32)
+        value = own.astype(jnp.float32) + total[:, :width]
         for step in range(1, owners):
-            summed = summed + hop(outs[step], "tensor", -step).astype(jnp.float32)
-        return summed
-
-    def streamed(own_rows, summed):
-        own = own_rows.astype(jnp.float32) + summed[:piece]
-        summed = jnp.concatenate([own, summed[piece:]], axis=0).astype(jnp.bfloat16)
-        total = summed.astype(jnp.float32)
-        for g in range(1, reps):
-            arrived = hop(summed, "rep", g).astype(jnp.float32)
-            total = total + jnp.roll(arrived, g * piece, axis=0)
-        return total.astype(jnp.bfloat16)
-
-    def finished(own_rows, summed):
-        value = own_rows.astype(jnp.float32) + summed[:piece]
-        for g in range(1, reps):
-            sent = summed[g * piece : (g + 1) * piece].astype(jnp.bfloat16)
-            value = value + hop(sent, "rep", -g).astype(jnp.float32)
+            sent = total[:, step * width : (step + 1) * width].astype(jnp.bfloat16)
+            value = value + hop(sent, "tensor", -step).astype(jnp.float32)
         return value.astype(jnp.bfloat16)
 
-    mine_picks = lax.dynamic_slice_in_dim(picks, section_index * half, half)
-    cuts = (slice(0, piece), slice(piece, half))
-    picked = [mine_picks[cut] for cut in cuts]
-    streams = [mine_rows[cut] for cut in cuts]
-    stream = jnp.concatenate([value[cuts[1]] for value in [mine_rows] + others], axis=0)
-    blocks = [first_blocks, [stream] + gather(stream)]
     results = []
-    raw, parts = expanded(blocks[0], 0)
     for section in range(2):
-        coef, hidden, received = activated(parts, raw, picked[0], section)
-        next_raw, parts = expanded(blocks[1], section, after=(received if section else [coef])[:1])
-        outs = contracted(coef, hidden, received, section, after=(next_raw,))
-        coef, hidden, received = activated(parts, next_raw, picked[1], section, after=(outs[0],))
-        streams[0] = jnp.where(coef[0, 0] == coef[0, 0], streams[0], jnp.zeros_like(streams[0]))
-        next_outs = contracted(coef, hidden, received, section)
+        streams = [scattered(own, layer(stack, p, section)) for own, stack, p in zip(streams, stacks, picked)]
+        results.append(jnp.concatenate(streams, axis=0))
         if section == 0:
-            first = streamed(streams[0], scattered(outs))
-            raw, parts = expanded([first] + gather(first), 1)
-            later = jnp.where(raw[0, 0] == raw[0, 0], streams[1], jnp.zeros_like(streams[1]))
-            second = streamed(later, scattered(next_outs))
-            blocks = [None, [second] + gather(second)]
-            streams = [first[:piece], second[:piece]]
-        else:
-            streams = [finished(streams[0], scattered(outs)), finished(streams[1], scattered(next_outs))]
-        results.append(jnp.concatenate(streams, axis=0))
+            stacks = [gathered(stream) for stream in streams]
     first, second = results
     kept = jnp.where(section_index == 0, first, second)
     received = hop(jnp.where(section_index == 0, second, first), "section", 1)

time: 293 us -> 259 us (0.88); the launches traced: 298 us -> 259 us
  starting transfers between devices: 76.3 us -> 54.9 us
  local copies, waits for them, and re-layouts: 22.1 us -> 14.6 us
  Pallas kernels: 99 us -> 93.1 us
  between operations: 4.98 us -> 0.8 us
    ppermute x47, starting transfers between devices: 76.3 us -> 54.9 us  [hop(): lax.ppermute(value, axis, [(i, (i + steps) % count) for i in range(count)])]
    pallas_call x8, Pallas kernels: 89.3 us -> 83.4 us  [the longest x4 47.9 us: expand(): pl.pallas_call(functools.partial(expand_kernel, reps), out_shape=[jax.Sha...]
    unnamed x111 -> x75, local copies, waits for them, and re-layouts: 9.56 us -> 6.11 us
    slice x14 -> x6, local copies, waits for them, and re-layouts: 4.18 us -> 1.04 us  [the longest x1 0.95 us: per_device(): streams = [mine_rows[:piece], mine_rows[piece:]]]
  transfers between devices with their start and end apart: 47 -> 47, of which waited for: 17 -> 24; matrix products, arithmetic and copies ran while one was open for 8% -> 7% of each run, Pallas kernels for 27% -> 36%
where the time goes in v9:
time: 259 us
  Pallas kernels  93.1 us (36%)
  waiting for transfers between devices  84.4 us (33%)
  starting transfers between devices  54.9 us (21%)
  local copies, waits for them, and re-layouts  14.6 us (6%)
  other arithmetic  10.7 us (4%)
    ppermute x47, waiting for transfers between devices, hop(): lax.ppermute(value, axis, [(i, (i + steps) % count) for i in range(count)])  84.4 us
    ppermute x47, starting transfers between devices, hop(): lax.ppermute(value, axis, [(i, (i + steps) % count) for i in range(count)])  54.9 us
    pallas_call x4, Pallas kernels, expand(): pl.pallas_call(functools.partial(expand_kernel, reps), out_shape=[jax.Sha...  47.9 us
    pallas_call x4, Pallas kernels, contract(): pl.pallas_call(functools.partial(contract_kernel, reps), out_shape=[jax.S...  35.6 us
    pallas_call x4, Pallas kernels, activate(): pl.pallas_call(functools.partial(activate_kernel, reps), out_shape=[jax.S...  9.69 us
    unnamed x75, local copies, waits for them, and re-layouts  6.11 us
  transfers between devices with their start and end apart: 47, of which 24 were waited for; matrix products, arithmetic and copies ran while one was open for 7% of the time, Pallas kernels for 36%

profile of v9, /device:TPU:1, one launch (start us, length us, event | category | flops | bytes accessed | tf_op | source)
XLA Modules:
  0.0 258.5 jit_solution(8199951542213654738)
XLA Ops:
  5.0 2.5 collective-permute-start.2
  7.5 2.3 collective-permute-start.3
  18.0 4.6 %collective-permute-done.16 = bf16[48,1024]{1,0:T(8,128)(2,1)S(1)} collective-permute-done((bf16[48,1024]{1,0:T(8,128)(2,1)S(1)}, bf16[48,1024]{1,0:T(8,128)(2,1)S(1)}, u32[]{:S(2)}, u32[]{:S(2)}) %collective-permute-start.16) | collective-permute-done | bytes 98336 | tf_op jit(solution)/shard_map/ppermute | solution.py:23
  23.9 3.8 %collective-permute-done.17 = bf16[48,1024]{1,0:T(8,128)(2,1)S(1)} collective-permute-done((bf16[48,1024]{1,0:T(8,128)(2,1)S(1)}, bf16[48,1024]{1,0:T(8,128)(2,1)S(1)}, u32[]{:S(2)}, u32[]{:S(2)}) %collective-permute-start.17) | collective-permute-done | bytes 98336 | tf_op jit(solution)/shard_map/ppermute | solution.py:23
  38.8 11.8 %expand.4 = (f32[48,16]{1,0:T(8,128)}, bf16[2,32,48,128]{3,2,1,0:T(8,128)(2,1)}, bf16[2,32,48,128]{3,2,1,0:T(8,128)(2,1)}) custom-call(s32[864]{0:T(1024)} %reshape.556.words_ref, s32[4]{0:T(128)} %pad_add_fusion.1.groups_ref, bf16[4,48,1024]{2,1,0:T(8,128)(2,1)} %copy-done.16, bf16[4,48,1024]{2,1,0:T(8,128)(2,1)} %copy-done.20, bf16[1,4096]{1,0:T(2,128)(2,1)} %bitcast.107, ...), custom_call_target="tpu_custom_call" | custom-call | flops 6442450944 | bytes 16777216 | tf_op jit(solution)/shard_map/expand/pallas_call | solution.py:200
  52.2 11.8 %expand.5 = (f32[48,16]{1,0:T(8,128)}, bf16[2,32,48,128]{3,2,1,0:T(8,128)(2,1)}, bf16[2,32,48,128]{3,2,1,0:T(8,128)(2,1)}) custom-call(s32[864]{0:T(1024)} %reshape.556.words_ref, s32[4]{0:T(128)} %pad_add_fusion.1.groups_ref, bf16[4,48,1024]{2,1,0:T(8,128)(2,1)} %copy-done.17, bf16[4,48,1024]{2,1,0:T(8,128)(2,1)} %copy-done.22, bf16[1,4096]{1,0:T(2,128)(2,1)} %bitcast.108, ...), custom_call_target="tpu_custom_call" | custom-call | flops 6442450944 | bytes 16777216 | tf_op jit(solution)/shard_map/expand/pallas_call | solution.py:200
  65.0 2.3 collective-permute-done.8.refs_1_
  67.3 2.4 activate.4
  71.5 12.7 %collective-permute-done.20.refs_1_ = bf16[2,32,48,128]{3,2,1,0:T(8,128)(2,1)S(1)} collective-permute-done((bf16[2,32,48,128]{3,2,1,0:T(8,128)(2,1)}, bf16[2,32,48,128]{3,2,1,0:T(8,128)(2,1)S(1)}, u32[]{:S(2)}, u32[]{:S(2)}) %collective-permute-start.20) | collective-permute-done | bytes 786464 | tf_op jit(solution)/shard_map/ppermute | solution.py:23
  84.1 2.4 activate.5
  88.2 4.3 %collective-permute-done.10.refs_1_ = bf16[32,48,128]{2,1,0:T(8,128)(2,1)S(1)} collective-permute-done((bf16[32,48,128]{2,1,0:T(8,128)(2,1)S(1)}, bf16[32,48,128]{2,1,0:T(8,128)(2,1)S(1)}, u32[]{:S(2)}, u32[]{:S(2)}) %collective-permute-start.10) | collective-permute-done | bytes 393248 | tf_op jit(solution)/shard_map/ppermute | solution.py:23
  93.3 8.7 %contract.4 = (bf16[48,4096]{1,0:T(8,128)(2,1)}, bf16[48,4096]{1,0:T(8,128)(2,1)}) custom-call(s32[864]{0:T(1024)} %reshape.556.words_ref, s32[4]{0:T(128)} %pad_add_fusion.1.groups_ref, bf16[32,48,128]{2,1,0:T(8,128)(2,1)} %copy-done.5, bf16[32,48,128]{2,1,0:T(8,128)(2,1)} %copy-done.29, f32[48,8]{1,0:T(8,128)} %copy-done.12, bf16[8,4096]{1,0:T(8,128)(2,1)} %bitcast.91, ...), custom_call_target="tpu_custom_call" | custom-call | flops 3221225472 | bytes 8388608 | tf_op jit(solution)/shard_map/contract/pallas_call | solution.py:316
  105.8 8.7 %contract.5 = (bf16[48,4096]{1,0:T(8,128)(2,1)}, bf16[48,4096]{1,0:T(8,128)(2,1)}) custom-call(s32[864]{0:T(1024)} %reshape.556.words_ref, s32[4]{0:T(128)} %pad_add_fusion.1.groups_ref, bf16[32,48,128]{2,1,0:T(8,128)(2,1)} %copy-done.4, bf16[32,48,128]{2,1,0:T(8,128)(2,1)} %copy-done.28, f32[48,8]{1,0:T(8,128)} %copy-done.10, bf16[8,4096]{1,0:T(8,128)(2,1)} %bitcast.92, ...), custom_call_target="tpu_custom_call" | custom-call | flops 3221225472 | bytes 8388608 | tf_op jit(solution)/shard_map/contract/pallas_call | solution.py:316
  115.2 4.3 %collective-permute-start.13 = (bf16[48,1024]{1,0:T(8,128)(2,1)S(1)}, bf16[48,1024]{1,0:T(8,128)(2,1)S(1)}, u32[]{:S(2)}, u32[]{:S(2)}) collective-permute-start(bf16[48,1024]{1,0:T(8,128)(2,1)S(1)} %get-tuple-element.92), channel_id=1, source_target_pairs={{0,6},{2,0},{4,2},{6,4},{1,7},{3,1},{5,3},{7,5},{8,14},{10,8},{12,... | collective-permute-start | bytes 294920 | tf_op jit(solution)/shard_map/ppermute | solution.py:23
  121.7 3.3 %collective-permute-done.14 = bf16[48,1024]{1,0:T(8,128)(2,1)S(1)} collective-permute-done((bf16[48,1024]{1,0:T(8,128)(2,1)S(1)}, bf16[48,1024]{1,0:T(8,128)(2,1)S(1)}, u32[]{:S(2)}, u32[]{:S(2)}) %collective-permute-start.14) | collective-permute-done | bytes 98336 | tf_op jit(solution)/shard_map/ppermute | solution.py:23
  132.5 2.4 collective-permute-done.27
  136.0 4.5 %collective-permute-done.24 = bf16[48,1024]{1,0:T(8,128)(2,1)S(1)} collective-permute-done((bf16[48,1024]{1,0:T(8,128)(2,1)S(1)}, bf16[48,1024]{1,0:T(8,128)(2,1)S(1)}, u32[]{:S(2)}, u32[]{:S(2)}) %collective-permute-start.24) | collective-permute-done | bytes 98336 | tf_op jit(solution)/shard_map/ppermute | solution.py:23
  144.4 2.5 collective-permute-done.36
  146.9 2.3 collective-permute-done.37
  149.3 4.0 %collective-permute-start.39 = (bf16[4,48,1024]{2,1,0:T(8,128)(2,1)S(1)}, bf16[4,48,1024]{2,1,0:T(8,128)(2,1)S(1)}, u32[]{:S(2)}, u32[]{:S(2)}) collective-permute-start(bf16[4,48,1024]{2,1,0:T(8,128)(2,1)S(1)} %pad_maximum_fusion.4.refs_0_), channel_id=1, source_target_pairs={{0,1},{1,0},{2,3},{3,2},{4,5},{5,4},{6,7},{7,6},{8,9},{9,8},{10,11... | collective-permute-start | bytes 1179656 | tf_op jit(solution)/shard_map/ppermute | solution.py:23
  154.1 12.2 %expand.6 = (f32[48,16]{1,0:T(8,128)}, bf16[2,32,48,128]{3,2,1,0:T(8,128)(2,1)}, bf16[2,32,48,128]{3,2,1,0:T(8,128)(2,1)}) custom-call(s32[864]{0:T(1024)} %reshape.559.words_ref, s32[4]{0:T(128)} %pad_add_fusion.2.groups_ref, bf16[4,48,1024]{2,1,0:T(8,128)(2,1)} %copy-done.18, bf16[4,48,1024]{2,1,0:T(8,128)(2,1)} %copy-done.21, bf16[1,4096]{1,0:T(2,128)(2,1)} %bitcast.105, ...), custom_call_target="tpu_custom_call" | custom-call | flops 6442450944 | bytes 16777216 | tf_op jit(solution)/shard_map/expand/pallas_call | solution.py:200
  167.2 12.2 %expand.7 = (f32[48,16]{1,0:T(8,128)}, bf16[2,32,48,128]{3,2,1,0:T(8,128)(2,1)}, bf16[2,32,48,128]{3,2,1,0:T(8,128)(2,1)}) custom-call(s32[864]{0:T(1024)} %reshape.559.words_ref, s32[4]{0:T(128)} %pad_add_fusion.2.groups_ref, bf16[4,48,1024]{2,1,0:T(8,128)(2,1)} %copy-done.19, bf16[4,48,1024]{2,1,0:T(8,128)(2,1)} %copy-done.23, bf16[1,4096]{1,0:T(2,128)(2,1)} %bitcast.106, ...), custom_call_target="tpu_custom_call" | custom-call | flops 6442450944 | bytes 16777216 | tf_op jit(solution)/shard_map/expand/pallas_call | solution.py:200
  180.9 2.4 activate.6
  184.1 14.3 %collective-permute-done.40.refs_1_ = bf16[2,32,48,128]{3,2,1,0:T(8,128)(2,1)S(1)} collective-permute-done((bf16[2,32,48,128]{3,2,1,0:T(8,128)(2,1)}, bf16[2,32,48,128]{3,2,1,0:T(8,128)(2,1)S(1)}, u32[]{:S(2)}, u32[]{:S(2)}) %collective-permute-start.40) | collective-permute-done | bytes 786464 | tf_op jit(solution)/shard_map/ppermute | solution.py:23
  198.5 2.4 activate.7
  203.1 3.7 %collective-permute-done.31.refs_1_ = bf16[32,48,128]{2,1,0:T(8,128)(2,1)S(1)} collective-permute-done((bf16[32,48,128]{2,1,0:T(8,128)(2,1)S(1)}, bf16[32,48,128]{2,1,0:T(8,128)(2,1)S(1)}, u32[]{:S(2)}, u32[]{:S(2)}) %collective-permute-start.31) | collective-permute-done | bytes 393248 | tf_op jit(solution)/shard_map/ppermute | solution.py:23
  207.5 9.1 %contract.6 = (bf16[48,4096]{1,0:T(8,128)(2,1)}, bf16[48,4096]{1,0:T(8,128)(2,1)}) custom-call(s32[864]{0:T(1024)} %reshape.559.words_ref, s32[4]{0:T(128)} %pad_add_fusion.2.groups_ref, bf16[32,48,128]{2,1,0:T(8,128)(2,1)} %copy-done.6, bf16[32,48,128]{2,1,0:T(8,128)(2,1)} %copy-done.30, f32[48,8]{1,0:T(8,128)} %copy-done.14, bf16[8,4096]{1,0:T(8,128)(2,1)} %bitcast.93, ...), custom_call_target="tpu_custom_call" | custom-call | flops 3221225472 | bytes 8388608 | tf_op jit(solution)/shard_map/contract/pallas_call | solution.py:316
  219.6 9.1 %contract.7 = (bf16[48,4096]{1,0:T(8,128)(2,1)}, bf16[48,4096]{1,0:T(8,128)(2,1)}) custom-call(s32[864]{0:T(1024)} %reshape.559.words_ref, s32[4]{0:T(128)} %pad_add_fusion.2.groups_ref, bf16[32,48,128]{2,1,0:T(8,128)(2,1)} %copy-done.7, bf16[32,48,128]{2,1,0:T(8,128)(2,1)} %copy-done.31, f32[48,8]{1,0:T(8,128)} %copy-done.15, bf16[8,4096]{1,0:T(8,128)(2,1)} %bitcast.94, ...), custom_call_target="tpu_custom_call" | custom-call | flops 3221225472 | bytes 8388608 | tf_op jit(solution)/shard_map/contract/pallas_call | solution.py:316
  231.6 6.5 %collective-permute-done.42 = bf16[48,4096]{1,0:T(8,128)(2,1)S(1)} collective-permute-done((bf16[48,4096]{1,0:T(8,128)(2,1)}, bf16[48,4096]{1,0:T(8,128)(2,1)S(1)}, u32[]{:S(2)}, u32[]{:S(2)}) %collective-permute-start.42) | collective-permute-done | bytes 393248 | tf_op jit(solution)/shard_map/ppermute | solution.py:23
  238.2 3.9 %collective-permute-start.43 = (bf16[48,1024]{1,0:T(8,128)(2,1)S(1)}, bf16[48,1024]{1,0:T(8,128)(2,1)S(1)}, u32[]{:S(2)}, u32[]{:S(2)}) collective-permute-start(bf16[48,1024]{1,0:T(8,128)(2,1)S(1)} %get-tuple-element.97), channel_id=1, source_target_pairs={{0,6},{2,0},{4,2},{6,4},{1,7},{3,1},{5,3},{7,5},{8,14},{10,8},{12,... | collective-permute-start | bytes 294920 | tf_op jit(solution)/shard_map/ppermute | solution.py:23
  243.7 7.7 %collective-permute-done.44 = bf16[48,1024]{1,0:T(8,128)(2,1)S(1)} collective-permute-done((bf16[48,1024]{1,0:T(8,128)(2,1)S(1)}, bf16[48,1024]{1,0:T(8,128)(2,1)S(1)}, u32[]{:S(2)}, u32[]{:S(2)}) %collective-permute-start.44) | collective-permute-done | bytes 98336 | tf_op jit(solution)/shard_map/ppermute | solution.py:23
  251.5 5.1 %collective-permute-start.46 = (bf16[96,1024]{1,0:T(8,128)(2,1)S(1)}, bf16[96,1024]{1,0:T(8,128)(2,1)S(1)}, u32[]{:S(2)}, u32[]{:S(2)}) collective-permute-start(bf16[96,1024]{1,0:T(8,128)(2,1)S(1)} %get-tuple-element.88), channel_id=1, source_target_pairs={{0,8},{8,0},{1,9},{9,1},{2,10},{10,2},{3,11},{11,3},{4,12},{12,4},... | collective-permute-start | bytes 589832 | tf_op jit(solution)/shard_map/ppermute | solution.py:23
  (221 shorter events, 67.7 us)
Async XLA Ops:
  3.2 35.6 %collective-permute-start.6 = (bf16[256,128,128]{2,1,0:T(8,128)(2,1)}, bf16[256,128,128]{2,1,0:T(8,128)(2,1)}, u32[]{:S(2)}, u32[]{:S(2)}) collective-permute-start(bf16[256,128,128]{2,1,0:T(8,128)(2,1)} %bitcast.68), channel_id=1, source_target_pairs={{0,8},{8,0},{1,9},{9,1},{2,10},{10,2},{3,11},{11,3},{4,12},{12,4},... | collective-permute-start | bytes 25165832 | tf_op jit(solution)/shard_map/ppermute | solution.py:23
  3.5 35.2 %collective-permute-start.7 = (bf16[256,128,128]{2,1,0:T(8,128)(2,1)}, bf16[256,128,128]{2,1,0:T(8,128)(2,1)}, u32[]{:S(2)}, u32[]{:S(2)}) collective-permute-start(bf16[256,128,128]{2,1,0:T(8,128)(2,1)} %bitcast.73), channel_id=1, source_target_pairs={{0,8},{8,0},{1,9},{9,1},{2,10},{10,2},{3,11},{11,3},{4,12},{12,4},... | collective-permute-start | bytes 25165832 | tf_op jit(solution)/shard_map/ppermute | solution.py:23
  3.7 84.6 %collective-permute-start.11 = (bf16[256,128,128]{2,1,0:T(8,128)(2,1)}, bf16[256,128,128]{2,1,0:T(8,128)(2,1)}, u32[]{:S(2)}, u32[]{:S(2)}) collective-permute-start(bf16[256,128,128]{2,1,0:T(8,128)(2,1)} %bitcast.78), channel_id=1, source_target_pairs={{0,8},{8,0},{1,9},{9,1},{2,10},{10,2},{3,11},{11,3},{4,12},{12,4},... | collective-permute-start | bytes 25165832 | tf_op jit(solution)/shard_map/ppermute | solution.py:23
  5.0 9.4 %collective-permute-start.2 = (bf16[48,1024]{1,0:T(8,128)(2,1)S(1)}, bf16[48,1024]{1,0:T(8,128)(2,1)S(1)}, u32[]{:S(2)}, u32[]{:S(2)}) collective-permute-start(bf16[48,1024]{1,0:T(8,128)(2,1)S(1)} %get-tuple-element.95), channel_id=1, source_target_pairs={{0,2},{2,4},{4,6},{6,0},{1,3},{3,5},{5,7},{7,1},{8,10},{10,12},{12... | collective-permute-start | bytes 294920 | tf_op jit(solution)/shard_map/ppermute | solution.py:23
  7.5 9.5 %collective-permute-start.3 = (bf16[48,1024]{1,0:T(8,128)(2,1)S(1)}, bf16[48,1024]{1,0:T(8,128)(2,1)S(1)}, u32[]{:S(2)}, u32[]{:S(2)}) collective-permute-start(bf16[48,1024]{1,0:T(8,128)(2,1)S(1)} %get-tuple-element.95), channel_id=1, source_target_pairs={{0,4},{2,6},{4,0},{6,2},{1,5},{3,7},{5,1},{7,3},{8,12},{10,14},{12... | collective-permute-start | bytes 294920 | tf_op jit(solution)/shard_map/ppermute | solution.py:23
  17.9 9.8 %collective-permute-start.17 = (bf16[48,1024]{1,0:T(8,128)(2,1)S(1)}, bf16[48,1024]{1,0:T(8,128)(2,1)S(1)}, u32[]{:S(2)}, u32[]{:S(2)}) collective-permute-start(bf16[48,1024]{1,0:T(8,128)(2,1)S(1)} %get-tuple-element.96), channel_id=1, source_target_pairs={{0,4},{2,6},{4,0},{6,2},{1,5},{3,7},{5,1},{7,3},{8,12},{10,14},{12... | collective-permute-start | bytes 294920 | tf_op jit(solution)/shard_map/ppermute | solution.py:23
  27.7 37.0 %collective-permute-start.9 = (bf16[24,32,128]{2,0,1:T(8,128)(2,1)S(1)}, bf16[24,32,128]{2,0,1:T(8,128)(2,1)S(1)}, u32[]{:S(2)}, u32[]{:S(2)}) collective-permute-start(bf16[24,32,128]{2,0,1:T(8,128)(2,1)S(1)} %select_bitcast_fusion.2), channel_id=1, source_target_pairs={{0,8},{8,0},{1,9},{9,1},{2,10},{10,2},{3,11},{11,3},{4,12},{12,4},... | collective-permute-start | bytes 589832 | tf_op jit(solution)/shard_map/ppermute | solution.py:23
  28.3 9.2 %collective-permute-start.5 = (bf16[4,48,1024]{2,1,0:T(8,128)(2,1)S(1)}, bf16[4,48,1024]{2,1,0:T(8,128)(2,1)S(1)}, u32[]{:S(2)}, u32[]{:S(2)}) collective-permute-start(bf16[4,48,1024]{2,1,0:T(8,128)(2,1)S(1)} %pad_maximum_fusion.1.refs_0_), channel_id=1, source_target_pairs={{0,1},{1,0},{2,3},{3,2},{4,5},{5,4},{6,7},{7,6},{8,9},{9,8},{10,11... | collective-permute-start | bytes 1179656 | tf_op jit(solution)/shard_map/ppermute | solution.py:23
  37.5 13.8 %collective-permute-start.19 = (bf16[4,48,1024]{2,1,0:T(8,128)(2,1)S(1)}, bf16[4,48,1024]{2,1,0:T(8,128)(2,1)S(1)}, u32[]{:S(2)}, u32[]{:S(2)}) collective-permute-start(bf16[4,48,1024]{2,1,0:T(8,128)(2,1)S(1)} %pad_maximum_fusion.2.refs_0_), channel_id=1, source_target_pairs={{0,1},{1,0},{2,3},{3,2},{4,5},{5,4},{6,7},{7,6},{8,9},{9,8},{10,11... | collective-permute-start | bytes 1179656 | tf_op jit(solution)/shard_map/ppermute | solution.py:23
  50.5 16.7 %collective-permute-start.8 = (bf16[2,32,48,128]{3,2,1,0:T(8,128)(2,1)}, bf16[2,32,48,128]{3,2,1,0:T(8,128)(2,1)S(1)}, u32[]{:S(2)}, u32[]{:S(2)}) collective-permute-start(bf16[2,32,48,128]{3,2,1,0:T(8,128)(2,1)} %get-tuple-element.44), channel_id=1, source_target_pairs={{0,1},{1,0},{2,3},{3,2},{4,5},{5,4},{6,7},{7,6},{8,9},{9,8},{10,11... | collective-permute-start | bytes 2359304 | tf_op jit(solution)/shard_map/ppermute | solution.py:23
  64.0 20.2 %collective-permute-start.20 = (bf16[2,32,48,128]{3,2,1,0:T(8,128)(2,1)}, bf16[2,32,48,128]{3,2,1,0:T(8,128)(2,1)S(1)}, u32[]{:S(2)}, u32[]{:S(2)}) collective-permute-start(bf16[2,32,48,128]{3,2,1,0:T(8,128)(2,1)} %get-tuple-element.52), channel_id=1, source_target_pairs={{0,1},{1,0},{2,3},{3,2},{4,5},{5,4},{6,7},{7,6},{8,9},{9,8},{10,11... | collective-permute-start | bytes 2359304 | tf_op jit(solution)/shard_map/ppermute | solution.py:23
  69.7 22.8 %collective-permute-start.10 = (bf16[32,48,128]{2,1,0:T(8,128)(2,1)S(1)}, bf16[32,48,128]{2,1,0:T(8,128)(2,1)S(1)}, u32[]{:S(2)}, u32[]{:S(2)}) collective-permute-start(bf16[32,48,128]{2,1,0:T(8,128)(2,1)S(1)} %get-tuple-element.46.refs_0_), channel_id=1, source_target_pairs={{0,1},{1,0},{2,3},{3,2},{4,5},{5,4},{6,7},{7,6},{8,9},{9,8},{10,11... | collective-permute-start | bytes 1179656 | tf_op jit(solution)/shard_map/ppermute | solution.py:23
  87.2 17.9 %collective-permute-start.21 = (bf16[32,48,128]{2,1,0:T(8,128)(2,1)S(1)}, bf16[32,48,128]{2,1,0:T(8,128)(2,1)S(1)}, u32[]{:S(2)}, u32[]{:S(2)}) collective-permute-start(bf16[32,48,128]{2,1,0:T(8,128)(2,1)S(1)} %get-tuple-element.54.refs_0_), channel_id=1, source_target_pairs={{0,1},{1,0},{2,3},{3,2},{4,5},{5,4},{6,7},{7,6},{8,9},{9,8},{10,11... | collective-permute-start | bytes 1179656 | tf_op jit(solution)/shard_map/ppermute | solution.py:23
  102.0 13.0 %collective-permute-start.12 = (bf16[48,4096]{1,0:T(8,128)(2,1)}, bf16[48,4096]{1,0:T(8,128)(2,1)S(1)}, u32[]{:S(2)}, u32[]{:S(2)}) collective-permute-start(bf16[48,4096]{1,0:T(8,128)(2,1)} %get-tuple-element.50), channel_id=1, source_target_pairs={{0,1},{1,0},{2,3},{3,2},{4,5},{5,4},{6,7},{7,6},{8,9},{9,8},{10,11... | collective-permute-start | bytes 1179656 | tf_op jit(solution)/shard_map/ppermute | solution.py:23
  126.5 8.4 %collective-permute-start.27 = (bf16[48,1024]{1,0:T(8,128)(2,1)S(1)}, bf16[48,1024]{1,0:T(8,128)(2,1)S(1)}, u32[]{:S(2)}, u32[]{:S(2)}) collective-permute-start(bf16[48,1024]{1,0:T(8,128)(2,1)S(1)} %fusion.23), channel_id=1, source_target_pairs={{0,4},{2,6},{4,0},{6,2},{1,5},{3,7},{5,1},{7,3},{8,12},{10,14},{12... | collective-permute-start | bytes 294920 | tf_op jit(solution)/shard_map/ppermute | solution.py:23
  130.2 10.3 %collective-permute-start.24 = (bf16[48,1024]{1,0:T(8,128)(2,1)S(1)}, bf16[48,1024]{1,0:T(8,128)(2,1)S(1)}, u32[]{:S(2)}, u32[]{:S(2)}) collective-permute-start(bf16[48,1024]{1,0:T(8,128)(2,1)S(1)} %get-tuple-element.104), channel_id=1, source_target_pairs={{0,4},{2,6},{4,0},{6,2},{1,5},{3,7},{5,1},{7,3},{8,12},{10,14},{12... | collective-permute-start | bytes 294920 | tf_op jit(solution)/shard_map/ppermute | solution.py:23
  132.1 8.3 %collective-permute-start.25 = (bf16[48,1024]{1,0:T(8,128)(2,1)S(1)}, bf16[48,1024]{1,0:T(8,128)(2,1)S(1)}, u32[]{:S(2)}, u32[]{:S(2)}) collective-permute-start(bf16[48,1024]{1,0:T(8,128)(2,1)S(1)} %get-tuple-element.103), channel_id=1, source_target_pairs={{0,2},{2,4},{4,6},{6,0},{1,3},{3,5},{5,7},{7,1},{8,10},{10,12},{12... | collective-permute-start | bytes 294920 | tf_op jit(solution)/shard_map/ppermute | solution.py:23
  135.0 18.3 %collective-permute-start.29 = (bf16[4,48,1024]{2,1,0:T(8,128)(2,1)S(1)}, bf16[4,48,1024]{2,1,0:T(8,128)(2,1)S(1)}, u32[]{:S(2)}, u32[]{:S(2)}) collective-permute-start(bf16[4,48,1024]{2,1,0:T(8,128)(2,1)S(1)} %pad_maximum_fusion.3.refs_0_), channel_id=1, source_target_pairs={{0,1},{1,0},{2,3},{3,2},{4,5},{5,4},{6,7},{7,6},{8,9},{9,8},{10,11... | collective-permute-start | bytes 1179656 | tf_op jit(solution)/shard_map/ppermute | solution.py:23
  140.6 8.7 %collective-permute-start.37 = (bf16[48,1024]{1,0:T(8,128)(2,1)S(1)}, bf16[48,1024]{1,0:T(8,128)(2,1)S(1)}, u32[]{:S(2)}, u32[]{:S(2)}) collective-permute-start(bf16[48,1024]{1,0:T(8,128)(2,1)S(1)} %fusion.19), channel_id=1, source_target_pairs={{0,4},{2,6},{4,0},{6,2},{1,5},{3,7},{5,1},{7,3},{8,12},{10,14},{12... | collective-permute-start | bytes 294920 | tf_op jit(solution)/shard_map/ppermute | solution.py:23
  141.7 7.6 %collective-permute-start.38 = (bf16[48,1024]{1,0:T(8,128)(2,1)S(1)}, bf16[48,1024]{1,0:T(8,128)(2,1)S(1)}, u32[]{:S(2)}, u32[]{:S(2)}) collective-permute-start(bf16[48,1024]{1,0:T(8,128)(2,1)S(1)} %fusion.19), channel_id=1, source_target_pairs={{0,6},{2,0},{4,2},{6,4},{1,7},{3,1},{5,3},{7,5},{8,14},{10,8},{12,... | collective-permute-start | bytes 294920 | tf_op jit(solution)/shard_map/ppermute | solution.py:23
  149.3 17.1 %collective-permute-start.39 = (bf16[4,48,1024]{2,1,0:T(8,128)(2,1)S(1)}, bf16[4,48,1024]{2,1,0:T(8,128)(2,1)S(1)}, u32[]{:S(2)}, u32[]{:S(2)}) collective-permute-start(bf16[4,48,1024]{2,1,0:T(8,128)(2,1)S(1)} %pad_maximum_fusion.4.refs_0_), channel_id=1, source_target_pairs={{0,1},{1,0},{2,3},{3,2},{4,5},{5,4},{6,7},{7,6},{8,9},{9,8},{10,11... | collective-permute-start | bytes 1179656 | tf_op jit(solution)/shard_map/ppermute | solution.py:23
  166.3 14.6 %collective-permute-start.30 = (bf16[2,32,48,128]{3,2,1,0:T(8,128)(2,1)}, bf16[2,32,48,128]{3,2,1,0:T(8,128)(2,1)S(1)}, u32[]{:S(2)}, u32[]{:S(2)}) collective-permute-start(bf16[2,32,48,128]{3,2,1,0:T(8,128)(2,1)} %get-tuple-element.59), channel_id=1, source_target_pairs={{0,1},{1,0},{2,3},{3,2},{4,5},{5,4},{6,7},{7,6},{8,9},{9,8},{10,11... | collective-permute-start | bytes 2359304 | tf_op jit(solution)/shard_map/ppermute | solution.py:23
  179.4 19.1 %collective-permute-start.40 = (bf16[2,32,48,128]{3,2,1,0:T(8,128)(2,1)}, bf16[2,32,48,128]{3,2,1,0:T(8,128)(2,1)S(1)}, u32[]{:S(2)}, u32[]{:S(2)}) collective-permute-start(bf16[2,32,48,128]{3,2,1,0:T(8,128)(2,1)} %get-tuple-element.66), channel_id=1, source_target_pairs={{0,1},{1,0},{2,3},{3,2},{4,5},{5,4},{6,7},{7,6},{8,9},{9,8},{10,11... | collective-permute-start | bytes 2359304 | tf_op jit(solution)/shard_map/ppermute | solution.py:23
  183.4 23.4 %collective-permute-start.31 = (bf16[32,48,128]{2,1,0:T(8,128)(2,1)S(1)}, bf16[32,48,128]{2,1,0:T(8,128)(2,1)S(1)}, u32[]{:S(2)}, u32[]{:S(2)}) collective-permute-start(bf16[32,48,128]{2,1,0:T(8,128)(2,1)S(1)} %get-tuple-element.61.refs_0_), channel_id=1, source_target_pairs={{0,1},{1,0},{2,3},{3,2},{4,5},{5,4},{6,7},{7,6},{8,9},{9,8},{10,11... | collective-permute-start | bytes 1179656 | tf_op jit(solution)/shard_map/ppermute | solution.py:23
  200.9 18.0 %collective-permute-start.41 = (bf16[32,48,128]{2,1,0:T(8,128)(2,1)S(1)}, bf16[32,48,128]{2,1,0:T(8,128)(2,1)S(1)}, u32[]{:S(2)}, u32[]{:S(2)}) collective-permute-start(bf16[32,48,128]{2,1,0:T(8,128)(2,1)S(1)} %get-tuple-element.68.refs_0_), channel_id=1, source_target_pairs={{0,1},{1,0},{2,3},{3,2},{4,5},{5,4},{6,7},{7,6},{8,9},{9,8},{10,11... | collective-permute-start | bytes 1179656 | tf_op jit(solution)/shard_map/ppermute | solution.py:23
  216.6 12.2 %collective-permute-start.32 = (bf16[48,4096]{1,0:T(8,128)(2,1)}, bf16[48,4096]{1,0:T(8,128)(2,1)S(1)}, u32[]{:S(2)}, u32[]{:S(2)}) collective-permute-start(bf16[48,4096]{1,0:T(8,128)(2,1)} %get-tuple-element.64), channel_id=1, source_target_pairs={{0,1},{1,0},{2,3},{3,2},{4,5},{5,4},{6,7},{7,6},{8,9},{9,8},{10,11... | collective-permute-start | bytes 1179656 | tf_op jit(solution)/shard_map/ppermute | solution.py:23
  228.8 9.2 %collective-permute-start.42 = (bf16[48,4096]{1,0:T(8,128)(2,1)}, bf16[48,4096]{1,0:T(8,128)(2,1)S(1)}, u32[]{:S(2)}, u32[]{:S(2)}) collective-permute-start(bf16[48,4096]{1,0:T(8,128)(2,1)} %get-tuple-element.71), channel_id=1, source_target_pairs={{0,1},{1,0},{2,3},{3,2},{4,5},{5,4},{6,7},{7,6},{8,9},{9,8},{10,11... | collective-permute-start | bytes 1179656 | tf_op jit(solution)/shard_map/ppermute | solution.py:23
  229.0 13.0 %collective-permute-start.33 = (bf16[48,1024]{1,0:T(8,128)(2,1)S(1)}, bf16[48,1024]{1,0:T(8,128)(2,1)S(1)}, u32[]{:S(2)}, u32[]{:S(2)}) collective-permute-start(bf16[48,1024]{1,0:T(8,128)(2,1)S(1)} %get-tuple-element.89), channel_id=1, source_target_pairs={{0,6},{2,0},{4,2},{6,4},{1,7},{3,1},{5,3},{7,5},{8,14},{10,8},{12,... | collective-permute-start | bytes 294920 | tf_op jit(solution)/shard_map/ppermute | solution.py:23
  231.2 11.2 %collective-permute-start.34 = (bf16[48,1024]{1,0:T(8,128)(2,1)S(1)}, bf16[48,1024]{1,0:T(8,128)(2,1)S(1)}, u32[]{:S(2)}, u32[]{:S(2)}) collective-permute-start(bf16[48,1024]{1,0:T(8,128)(2,1)S(1)} %get-tuple-element.91), channel_id=1, source_target_pairs={{0,4},{2,6},{4,0},{6,2},{1,5},{3,7},{5,1},{7,3},{8,12},{10,14},{12... | collective-permute-start | bytes 294920 | tf_op jit(solution)/shard_map/ppermute | solution.py:23
  231.2 11.2 %collective-permute-start.35 = (bf16[48,1024]{1,0:T(8,128)(2,1)S(1)}, bf16[48,1024]{1,0:T(8,128)(2,1)S(1)}, u32[]{:S(2)}, u32[]{:S(2)}) collective-permute-start(bf16[48,1024]{1,0:T(8,128)(2,1)S(1)} %get-tuple-element.90), channel_id=1, source_target_pairs={{0,2},{2,4},{4,6},{6,0},{1,3},{3,5},{5,7},{7,1},{8,10},{10,12},{12... | collective-permute-start | bytes 294920 | tf_op jit(solution)/shard_map/ppermute | solution.py:23
  242.1 9.3 %collective-permute-start.44 = (bf16[48,1024]{1,0:T(8,128)(2,1)S(1)}, bf16[48,1024]{1,0:T(8,128)(2,1)S(1)}, u32[]{:S(2)}, u32[]{:S(2)}) collective-permute-start(bf16[48,1024]{1,0:T(8,128)(2,1)S(1)} %get-tuple-element.99), channel_id=1, source_target_pairs={{0,4},{2,6},{4,0},{6,2},{1,5},{3,7},{5,1},{7,3},{8,12},{10,14},{12... | collective-permute-start | bytes 294920 | tf_op jit(solution)/shard_map/ppermute | solution.py:23
  242.1 9.3 %collective-permute-start.45 = (bf16[48,1024]{1,0:T(8,128)(2,1)S(1)}, bf16[48,1024]{1,0:T(8,128)(2,1)S(1)}, u32[]{:S(2)}, u32[]{:S(2)}) collective-permute-start(bf16[48,1024]{1,0:T(8,128)(2,1)S(1)} %get-tuple-element.98), channel_id=1, source_target_pairs={{0,2},{2,4},{4,6},{6,0},{1,3},{3,5},{5,7},{7,1},{8,10},{10,12},{12... | collective-permute-start | bytes 294920 | tf_op jit(solution)/shard_map/ppermute | solution.py:23
  (52 other events, 501.6 us)

commit v10 on v9

--- a/solution.py
+++ b/solution.py
@@ -87,9 +87,9 @@
     lax.fori_loop(0, groups_ref[which], group, 0)
 
 
-def load_tiles(own, choices, tiles, sem):
+def load_tiles(own, choices, tiles, sem, parts):
     count = tiles.shape[0] - 1
-    step = -(-count // COPIES)
+    step = -(-count // parts)
 
     def copies(tiles_hbm):
         for first in range(0, count, step):
@@ -110,7 +110,8 @@
     owners, rows, width = stacks[0].shape
     per_owner = width // BLOCK
     strip = 48 if rows % 48 == 0 else 16
-    gate_copy = load_tiles(groups_ref[3], (own_gate, other_gate), gate_tiles, gate_sem)
+    gate_copy = load_tiles(groups_ref[3], (own_gate, other_gate), gate_tiles, gate_sem, 1)
+    up_copy = load_tiles(groups_ref[3], (own_up, other_up), up_tiles, up_sem, 1)
 
     for rep in range(reps):
 
@@ -155,11 +156,7 @@
 
     for which, tiles in ((0, gate_tiles), (1, up_tiles)):
         total_ref[...] = jnp.zeros(total_ref.shape, jnp.float32)
-        if which == 0:
-            gate_copy.wait()
-            up_copy = load_tiles(groups_ref[3], (own_up, other_up), up_tiles, up_sem)
-        else:
-            up_copy.wait()
+        (gate_copy, up_copy)[which].wait()
         multiply_tiles(words_ref, groups_ref, which, words_ref.shape[0] // 3, read, tiles, add)
         for rep, part_ref in enumerate(part_refs):
 
@@ -279,7 +276,7 @@
     total_ref, tiles, sem = refs[-3:]
     rows = hiddens[0].shape[1]
     blocks = total_ref.shape[0]
-    copy = load_tiles(groups_ref[3], (own_hbm, other_hbm), tiles, sem)
+    copy = load_tiles(groups_ref[3], (own_hbm, other_hbm), tiles, sem, COPIES)
 
     def read(block):
         return jnp.concatenate([hidden[block] for hidden in hiddens], axis=0)
@@ -368,11 +365,12 @@
     codes = lax.dynamic_slice_in_dim(codes, rep_index * tile_count, tile_count, axis=1)
     wide = jnp.concatenate([gate_left[0], up_left[0], down_right[0], norm_gain], axis=0)
     other_codes, other_wide = hop(codes, "section", 1), hop(wide, "section", 1)
-    other_codes, other_wide, gate_tiles, up_tiles, down_tiles = lax.optimization_barrier(
-        (other_codes, other_wide, gate_tiles, up_tiles, down_tiles)
+    other_codes, other_wide, gate_tiles, up_tiles = lax.optimization_barrier(
+        (other_codes, other_wide, gate_tiles, up_tiles)
     )
     gate_pair = (gate_tiles[0], hop(gate_tiles[0], "section", 1))
     up_pair = (up_tiles[0], hop(up_tiles[0], "section", 1))
+    stacks, down_tiles = lax.optimization_barrier((stacks, down_tiles))
     down_pair = (down_tiles[0], hop(down_tiles[0], "section", 1))
 
     plans = tile_plan(jnp.concatenate([codes, other_codes]), block_rows, own_cols, owner_index, owners)

time: 259 us -> 275 us (1.062)
  waiting for transfers between devices: 84.4 us -> 94.8 us
  starting transfers between devices: 54.9 us -> 60.9 us
    ppermute x47, waiting for transfers between devices: 84.4 us -> 94.8 us  [hop(): lax.ppermute(value, axis, [(i, (i + steps) % count) for i in range(count)])]
    ppermute x47, starting transfers between devices: 54.9 us -> 60.9 us  [hop(): lax.ppermute(value, axis, [(i, (i + steps) % count) for i in range(count)])]
    unnamed x75 -> x81, local copies, waits for them, and re-layouts: 6.11 us -> 5.28 us
  transfers between devices with their start and end apart: 47 -> 47, of which waited for: 24 -> 23; matrix products, arithmetic and copies ran while one was open for 7% -> 6% of each run, Pallas kernels for 36% -> 35%
where the time goes in v10:
time: 275 us
  Pallas kernels  95.4 us (35%)
  waiting for transfers between devices  94.8 us (34%)
  starting transfers between devices  60.9 us (22%)
  local copies, waits for them, and re-layouts  13.7 us (5%)
  other arithmetic  9.45 us (3%)
    ppermute x47, waiting for transfers between devices, hop(): lax.ppermute(value, axis, [(i, (i + steps) % count) for i in range(count)])  94.8 us
    ppermute x47, starting transfers between devices, hop(): lax.ppermute(value, axis, [(i, (i + steps) % count) for i in range(count)])  60.9 us
    pallas_call x4, Pallas kernels, expand(): pl.pallas_call(functools.partial(expand_kernel, reps), out_shape=[jax.Sha...  50.2 us
    pallas_call x4, Pallas kernels, contract(): pl.pallas_call(functools.partial(contract_kernel, reps), out_shape=[jax.S...  35.5 us
    pallas_call x4, Pallas kernels, activate(): pl.pallas_call(functools.partial(activate_kernel, reps), out_shape=[jax.S...  9.69 us
  transfers between devices with their start and end apart: 47, of which 23 were waited for; matrix products, arithmetic and copies ran while one was open for 6% of the time, Pallas kernels for 35%

profile of v10, /device:TPU:1, one launch (start us, length us, event | category | flops | bytes accessed | tf_op | source)
XLA Modules:
  0.0 275.1 jit_solution(17758363191528633378)
XLA Ops:
  4.7 2.7 collective-permute-start.2
  12.6 4.4 %collective-permute-done.3 = bf16[48,1024]{1,0:T(8,128)(2,1)S(1)} collective-permute-done((bf16[48,1024]{1,0:T(8,128)(2,1)S(1)}, bf16[48,1024]{1,0:T(8,128)(2,1)S(1)}, u32[]{:S(2)}, u32[]{:S(2)}) %collective-permute-start.3) | collective-permute-done | bytes 98336 | tf_op jit(solution)/shard_map/ppermute | solution.py:23
  17.0 3.9 %collective-permute-start.8 = (bf16[48,1024]{1,0:T(8,128)(2,1)S(1)}, bf16[48,1024]{1,0:T(8,128)(2,1)S(1)}, u32[]{:S(2)}, u32[]{:S(2)}) collective-permute-start(bf16[48,1024]{1,0:T(8,128)(2,1)S(1)} %get-tuple-element.111), channel_id=1, source_target_pairs={{0,6},{2,0},{4,2},{6,4},{1,7},{3,1},{5,3},{7,5},{8,14},{10,8},{12,... | collective-permute-start | bytes 294920 | tf_op jit(solution)/shard_map/ppermute | solution.py:23
  23.7 2.5 collective-permute-done.6
  27.5 3.6 %collective-permute-done.5.refs_1_ = bf16[4,48,1024]{2,1,0:T(8,128)(2,1)S(1)} collective-permute-done((bf16[4,48,1024]{2,1,0:T(8,128)(2,1)S(1)}, bf16[4,48,1024]{2,1,0:T(8,128)(2,1)S(1)}, u32[]{:S(2)}, u32[]{:S(2)}) %collective-permute-start.5) | collective-permute-done | bytes 393248 | tf_op jit(solution)/shard_map/ppermute | solution.py:23
  31.1 8.4 %collective-permute-done.9.refs_1_ = bf16[4,48,1024]{2,1,0:T(8,128)(2,1)S(1)} collective-permute-done((bf16[4,48,1024]{2,1,0:T(8,128)(2,1)S(1)}, bf16[4,48,1024]{2,1,0:T(8,128)(2,1)S(1)}, u32[]{:S(2)}, u32[]{:S(2)}) %collective-permute-start.9) | collective-permute-done | bytes 393248 | tf_op jit(solution)/shard_map/ppermute | solution.py:23
  39.5 2.9 %collective-permute-start.15 = (bf16[256,128,128]{2,1,0:T(8,128)(2,1)}, bf16[256,128,128]{2,1,0:T(8,128)(2,1)}, u32[]{:S(2)}, u32[]{:S(2)}) collective-permute-start(bf16[256,128,128]{2,1,0:T(8,128)(2,1)} %bitcast.78), channel_id=1, source_target_pairs={{0,8},{8,0},{1,9},{9,1},{2,10},{10,2},{3,11},{11,3},{4,12},{12,4},... | collective-permute-start | bytes 25165832 | tf_op jit(solution)/shard_map/ppermute | solution.py:23
  52.1 13.0 %expand.4 = (f32[48,16]{1,0:T(8,128)}, bf16[2,32,48,128]{3,2,1,0:T(8,128)(2,1)}, bf16[2,32,48,128]{3,2,1,0:T(8,128)(2,1)}) custom-call(s32[864]{0:T(1024)} %reshape.556.words_ref, s32[4]{0:T(128)} %pad_add_fusion.1.groups_ref, bf16[4,48,1024]{2,1,0:T(8,128)(2,1)} %copy-done.16, bf16[4,48,1024]{2,1,0:T(8,128)(2,1)} %copy-done.20, bf16[1,4096]{1,0:T(2,128)(2,1)} %bitcast.107, ...), custom_call_target="tpu_custom_call" | custom-call | flops 6442450944 | bytes 16777216 | tf_op jit(solution)/shard_map/expand/pallas_call | solution.py:197
  66.7 12.9 %expand.5 = (f32[48,16]{1,0:T(8,128)}, bf16[2,32,48,128]{3,2,1,0:T(8,128)(2,1)}, bf16[2,32,48,128]{3,2,1,0:T(8,128)(2,1)}) custom-call(s32[864]{0:T(1024)} %reshape.556.words_ref, s32[4]{0:T(128)} %pad_add_fusion.1.groups_ref, bf16[4,48,1024]{2,1,0:T(8,128)(2,1)} %copy-done.17, bf16[4,48,1024]{2,1,0:T(8,128)(2,1)} %copy-done.21, bf16[1,4096]{1,0:T(2,128)(2,1)} %bitcast.108, ...), custom_call_target="tpu_custom_call" | custom-call | flops 6442450944 | bytes 16777216 | tf_op jit(solution)/shard_map/expand/pallas_call | solution.py:197
  80.4 3.9 %collective-permute-done.12.refs_1_ = bf16[2,32,48,128]{3,2,1,0:T(8,128)(2,1)S(1)} collective-permute-done((bf16[2,32,48,128]{3,2,1,0:T(8,128)(2,1)}, bf16[2,32,48,128]{3,2,1,0:T(8,128)(2,1)S(1)}, u32[]{:S(2)}, u32[]{:S(2)}) %collective-permute-start.12) | collective-permute-done | bytes 786464 | tf_op jit(solution)/shard_map/ppermute | solution.py:23
  84.3 2.4 activate.4
  88.7 12.4 %collective-permute-done.20.refs_1_ = bf16[2,32,48,128]{3,2,1,0:T(8,128)(2,1)S(1)} collective-permute-done((bf16[2,32,48,128]{3,2,1,0:T(8,128)(2,1)}, bf16[2,32,48,128]{3,2,1,0:T(8,128)(2,1)S(1)}, u32[]{:S(2)}, u32[]{:S(2)}) %collective-permute-start.20) | collective-permute-done | bytes 786464 | tf_op jit(solution)/shard_map/ppermute | solution.py:23
  101.1 2.4 activate.5
  105.5 4.1 %collective-permute-done.14.refs_1_ = bf16[32,48,128]{2,1,0:T(8,128)(2,1)S(1)} collective-permute-done((bf16[32,48,128]{2,1,0:T(8,128)(2,1)S(1)}, bf16[32,48,128]{2,1,0:T(8,128)(2,1)S(1)}, u32[]{:S(2)}, u32[]{:S(2)}) %collective-permute-start.14) | collective-permute-done | bytes 393248 | tf_op jit(solution)/shard_map/ppermute | solution.py:23
  110.3 8.7 %contract.4 = (bf16[48,4096]{1,0:T(8,128)(2,1)}, bf16[48,4096]{1,0:T(8,128)(2,1)}) custom-call(s32[864]{0:T(1024)} %reshape.556.words_ref, s32[4]{0:T(128)} %pad_add_fusion.1.groups_ref, bf16[32,48,128]{2,1,0:T(8,128)(2,1)} %copy-done.5, bf16[32,48,128]{2,1,0:T(8,128)(2,1)} %copy-done.29, f32[48,8]{1,0:T(8,128)} %copy-done.12, bf16[8,4096]{1,0:T(8,128)(2,1)} %bitcast.91, ...), custom_call_target="tpu_custom_call" | custom-call | flops 3221225472 | bytes 8388608 | tf_op jit(solution)/shard_map/contract/pallas_call | solution.py:313
  123.1 8.7 %contract.5 = (bf16[48,4096]{1,0:T(8,128)(2,1)}, bf16[48,4096]{1,0:T(8,128)(2,1)}) custom-call(s32[864]{0:T(1024)} %reshape.556.words_ref, s32[4]{0:T(128)} %pad_add_fusion.1.groups_ref, bf16[32,48,128]{2,1,0:T(8,128)(2,1)} %copy-done.4, bf16[32,48,128]{2,1,0:T(8,128)(2,1)} %copy-done.28, f32[48,8]{1,0:T(8,128)} %copy-done.10, bf16[8,4096]{1,0:T(8,128)(2,1)} %bitcast.92, ...), custom_call_target="tpu_custom_call" | custom-call | flops 3221225472 | bytes 8388608 | tf_op jit(solution)/shard_map/contract/pallas_call | solution.py:313
  133.7 6.6 %collective-permute-done.22 = bf16[48,4096]{1,0:T(8,128)(2,1)S(1)} collective-permute-done((bf16[48,4096]{1,0:T(8,128)(2,1)}, bf16[48,4096]{1,0:T(8,128)(2,1)S(1)}, u32[]{:S(2)}, u32[]{:S(2)}) %collective-permute-start.22) | collective-permute-done | bytes 393248 | tf_op jit(solution)/shard_map/ppermute | solution.py:23
  148.7 3.0 %collective-permute-start.29 = (bf16[4,48,1024]{2,1,0:T(8,128)(2,1)S(1)}, bf16[4,48,1024]{2,1,0:T(8,128)(2,1)S(1)}, u32[]{:S(2)}, u32[]{:S(2)}) collective-permute-start(bf16[4,48,1024]{2,1,0:T(8,128)(2,1)S(1)} %pad_maximum_fusion.3.refs_0_), channel_id=1, source_target_pairs={{0,1},{1,0},{2,3},{3,2},{4,5},{5,4},{6,7},{7,6},{8,9},{9,8},{10,11... | collective-permute-start | bytes 1179656 | tf_op jit(solution)/shard_map/ppermute | solution.py:23
  152.7 7.5 %collective-permute-done.24 = bf16[48,1024]{1,0:T(8,128)(2,1)S(1)} collective-permute-done((bf16[48,1024]{1,0:T(8,128)(2,1)S(1)}, bf16[48,1024]{1,0:T(8,128)(2,1)S(1)}, u32[]{:S(2)}, u32[]{:S(2)}) %collective-permute-start.24) | collective-permute-done | bytes 98336 | tf_op jit(solution)/shard_map/ppermute | solution.py:23
  167.3 4.1 %collective-permute-start.39 = (bf16[4,48,1024]{2,1,0:T(8,128)(2,1)S(1)}, bf16[4,48,1024]{2,1,0:T(8,128)(2,1)S(1)}, u32[]{:S(2)}, u32[]{:S(2)}) collective-permute-start(bf16[4,48,1024]{2,1,0:T(8,128)(2,1)S(1)} %pad_maximum_fusion.4.refs_0_), channel_id=1, source_target_pairs={{0,1},{1,0},{2,3},{3,2},{4,5},{5,4},{6,7},{7,6},{8,9},{9,8},{10,11... | collective-permute-start | bytes 1179656 | tf_op jit(solution)/shard_map/ppermute | solution.py:23
  172.2 12.2 %expand.6 = (f32[48,16]{1,0:T(8,128)}, bf16[2,32,48,128]{3,2,1,0:T(8,128)(2,1)}, bf16[2,32,48,128]{3,2,1,0:T(8,128)(2,1)}) custom-call(s32[864]{0:T(1024)} %reshape.559.words_ref, s32[4]{0:T(128)} %pad_add_fusion.2.groups_ref, bf16[4,48,1024]{2,1,0:T(8,128)(2,1)} %copy-done.18, bf16[4,48,1024]{2,1,0:T(8,128)(2,1)} %copy-done.22, bf16[1,4096]{1,0:T(2,128)(2,1)} %bitcast.105, ...), custom_call_target="tpu_custom_call" | custom-call | flops 6442450944 | bytes 16777216 | tf_op jit(solution)/shard_map/expand/pallas_call | solution.py:197
  185.2 12.1 %expand.7 = (f32[48,16]{1,0:T(8,128)}, bf16[2,32,48,128]{3,2,1,0:T(8,128)(2,1)}, bf16[2,32,48,128]{3,2,1,0:T(8,128)(2,1)}) custom-call(s32[864]{0:T(1024)} %reshape.559.words_ref, s32[4]{0:T(128)} %pad_add_fusion.2.groups_ref, bf16[4,48,1024]{2,1,0:T(8,128)(2,1)} %copy-done.19, bf16[4,48,1024]{2,1,0:T(8,128)(2,1)} %copy-done.23, bf16[1,4096]{1,0:T(2,128)(2,1)} %bitcast.106, ...), custom_call_target="tpu_custom_call" | custom-call | flops 6442450944 | bytes 16777216 | tf_op jit(solution)/shard_map/expand/pallas_call | solution.py:197
  199.4 2.4 activate.6
  202.9 14.4 %collective-permute-done.40.refs_1_ = bf16[2,32,48,128]{3,2,1,0:T(8,128)(2,1)S(1)} collective-permute-done((bf16[2,32,48,128]{3,2,1,0:T(8,128)(2,1)}, bf16[2,32,48,128]{3,2,1,0:T(8,128)(2,1)S(1)}, u32[]{:S(2)}, u32[]{:S(2)}) %collective-permute-start.40) | collective-permute-done | bytes 786464 | tf_op jit(solution)/shard_map/ppermute | solution.py:23
  217.3 2.4 activate.7
  221.0 4.7 %collective-permute-done.31.refs_1_ = bf16[32,48,128]{2,1,0:T(8,128)(2,1)S(1)} collective-permute-done((bf16[32,48,128]{2,1,0:T(8,128)(2,1)S(1)}, bf16[32,48,128]{2,1,0:T(8,128)(2,1)S(1)}, u32[]{:S(2)}, u32[]{:S(2)}) %collective-permute-start.31) | collective-permute-done | bytes 393248 | tf_op jit(solution)/shard_map/ppermute | solution.py:23
  226.5 9.0 %contract.6 = (bf16[48,4096]{1,0:T(8,128)(2,1)}, bf16[48,4096]{1,0:T(8,128)(2,1)}) custom-call(s32[864]{0:T(1024)} %reshape.559.words_ref, s32[4]{0:T(128)} %pad_add_fusion.2.groups_ref, bf16[32,48,128]{2,1,0:T(8,128)(2,1)} %copy-done.6, bf16[32,48,128]{2,1,0:T(8,128)(2,1)} %copy-done.30, f32[48,8]{1,0:T(8,128)} %copy-done.14, bf16[8,4096]{1,0:T(8,128)(2,1)} %bitcast.93, ...), custom_call_target="tpu_custom_call" | custom-call | flops 3221225472 | bytes 8388608 | tf_op jit(solution)/shard_map/contract/pallas_call | solution.py:313
  237.6 9.1 %contract.7 = (bf16[48,4096]{1,0:T(8,128)(2,1)}, bf16[48,4096]{1,0:T(8,128)(2,1)}) custom-call(s32[864]{0:T(1024)} %reshape.559.words_ref, s32[4]{0:T(128)} %pad_add_fusion.2.groups_ref, bf16[32,48,128]{2,1,0:T(8,128)(2,1)} %copy-done.7, bf16[32,48,128]{2,1,0:T(8,128)(2,1)} %copy-done.31, f32[48,8]{1,0:T(8,128)} %copy-done.15, bf16[8,4096]{1,0:T(8,128)(2,1)} %bitcast.94, ...), custom_call_target="tpu_custom_call" | custom-call | flops 3221225472 | bytes 8388608 | tf_op jit(solution)/shard_map/contract/pallas_call | solution.py:313
  247.2 6.1 %collective-permute-start.33 = (bf16[48,1024]{1,0:T(8,128)(2,1)S(1)}, bf16[48,1024]{1,0:T(8,128)(2,1)S(1)}, u32[]{:S(2)}, u32[]{:S(2)}) collective-permute-start(bf16[48,1024]{1,0:T(8,128)(2,1)S(1)} %get-tuple-element.97), channel_id=1, source_target_pairs={{0,6},{2,0},{4,2},{6,4},{1,7},{3,1},{5,3},{7,5},{8,14},{10,8},{12,... | collective-permute-start | bytes 294920 | tf_op jit(solution)/shard_map/ppermute | solution.py:23
  255.2 3.9 %collective-permute-start.43 = (bf16[48,1024]{1,0:T(8,128)(2,1)S(1)}, bf16[48,1024]{1,0:T(8,128)(2,1)S(1)}, u32[]{:S(2)}, u32[]{:S(2)}) collective-permute-start(bf16[48,1024]{1,0:T(8,128)(2,1)S(1)} %get-tuple-element.103), channel_id=1, source_target_pairs={{0,6},{2,0},{4,2},{6,4},{1,7},{3,1},{5,3},{7,5},{8,14},{10,8},{12,... | collective-permute-start | bytes 294920 | tf_op jit(solution)/shard_map/ppermute | solution.py:23
  261.6 8.7 %collective-permute-done.44 = bf16[48,1024]{1,0:T(8,128)(2,1)S(1)} collective-permute-done((bf16[48,1024]{1,0:T(8,128)(2,1)S(1)}, bf16[48,1024]{1,0:T(8,128)(2,1)S(1)}, u32[]{:S(2)}, u32[]{:S(2)}) %collective-permute-start.44) | collective-permute-done | bytes 98336 | tf_op jit(solution)/shard_map/ppermute | solution.py:23
  270.5 2.7 collective-permute-start.46
  (227 shorter events, 68.6 us)
Async XLA Ops:
  3.2 48.9 %collective-permute-start.10 = (bf16[256,128,128]{2,1,0:T(8,128)(2,1)}, bf16[256,128,128]{2,1,0:T(8,128)(2,1)}, u32[]{:S(2)}, u32[]{:S(2)}) collective-permute-start(bf16[256,128,128]{2,1,0:T(8,128)(2,1)} %bitcast.68), channel_id=1, source_target_pairs={{0,8},{8,0},{1,9},{9,1},{2,10},{10,2},{3,11},{11,3},{4,12},{12,4},... | collective-permute-start | bytes 25165832 | tf_op jit(solution)/shard_map/ppermute | solution.py:23
  3.6 48.5 %collective-permute-start.11 = (bf16[256,128,128]{2,1,0:T(8,128)(2,1)}, bf16[256,128,128]{2,1,0:T(8,128)(2,1)}, u32[]{:S(2)}, u32[]{:S(2)}) collective-permute-start(bf16[256,128,128]{2,1,0:T(8,128)(2,1)} %bitcast.73), channel_id=1, source_target_pairs={{0,8},{8,0},{1,9},{9,1},{2,10},{10,2},{3,11},{11,3},{4,12},{12,4},... | collective-permute-start | bytes 25165832 | tf_op jit(solution)/shard_map/ppermute | solution.py:23
  4.7 7.8 %collective-permute-start.2 = (bf16[48,1024]{1,0:T(8,128)(2,1)S(1)}, bf16[48,1024]{1,0:T(8,128)(2,1)S(1)}, u32[]{:S(2)}, u32[]{:S(2)}) collective-permute-start(bf16[48,1024]{1,0:T(8,128)(2,1)S(1)} %get-tuple-element.112), channel_id=1, source_target_pairs={{0,2},{2,4},{4,6},{6,0},{1,3},{3,5},{5,7},{7,1},{8,10},{10,12},{12... | collective-permute-start | bytes 294920 | tf_op jit(solution)/shard_map/ppermute | solution.py:23
  7.4 9.6 %collective-permute-start.3 = (bf16[48,1024]{1,0:T(8,128)(2,1)S(1)}, bf16[48,1024]{1,0:T(8,128)(2,1)S(1)}, u32[]{:S(2)}, u32[]{:S(2)}) collective-permute-start(bf16[48,1024]{1,0:T(8,128)(2,1)S(1)} %get-tuple-element.112), channel_id=1, source_target_pairs={{0,4},{2,6},{4,0},{6,2},{1,5},{3,7},{5,1},{7,3},{8,12},{10,14},{12... | collective-permute-start | bytes 294920 | tf_op jit(solution)/shard_map/ppermute | solution.py:23
  9.7 11.2 %collective-permute-start.4 = (bf16[48,1024]{1,0:T(8,128)(2,1)S(1)}, bf16[48,1024]{1,0:T(8,128)(2,1)S(1)}, u32[]{:S(2)}, u32[]{:S(2)}) collective-permute-start(bf16[48,1024]{1,0:T(8,128)(2,1)S(1)} %get-tuple-element.112), channel_id=1, source_target_pairs={{0,6},{2,0},{4,2},{6,4},{1,7},{3,1},{5,3},{7,5},{8,14},{10,8},{12,... | collective-permute-start | bytes 294920 | tf_op jit(solution)/shard_map/ppermute | solution.py:23
  12.5 10.0 %collective-permute-start.7 = (bf16[48,1024]{1,0:T(8,128)(2,1)S(1)}, bf16[48,1024]{1,0:T(8,128)(2,1)S(1)}, u32[]{:S(2)}, u32[]{:S(2)}) collective-permute-start(bf16[48,1024]{1,0:T(8,128)(2,1)S(1)} %get-tuple-element.111), channel_id=1, source_target_pairs={{0,4},{2,6},{4,0},{6,2},{1,5},{3,7},{5,1},{7,3},{8,12},{10,14},{12... | collective-permute-start | bytes 294920 | tf_op jit(solution)/shard_map/ppermute | solution.py:23
  22.5 8.6 %collective-permute-start.5 = (bf16[4,48,1024]{2,1,0:T(8,128)(2,1)S(1)}, bf16[4,48,1024]{2,1,0:T(8,128)(2,1)S(1)}, u32[]{:S(2)}, u32[]{:S(2)}) collective-permute-start(bf16[4,48,1024]{2,1,0:T(8,128)(2,1)S(1)} %pad_maximum_fusion.1.refs_0_), channel_id=1, source_target_pairs={{0,1},{1,0},{2,3},{3,2},{4,5},{5,4},{6,7},{7,6},{8,9},{9,8},{10,11... | collective-permute-start | bytes 1179656 | tf_op jit(solution)/shard_map/ppermute | solution.py:23
  26.3 13.3 %collective-permute-start.9 = (bf16[4,48,1024]{2,1,0:T(8,128)(2,1)S(1)}, bf16[4,48,1024]{2,1,0:T(8,128)(2,1)S(1)}, u32[]{:S(2)}, u32[]{:S(2)}) collective-permute-start(bf16[4,48,1024]{2,1,0:T(8,128)(2,1)S(1)} %pad_maximum_fusion.2.refs_0_), channel_id=1, source_target_pairs={{0,1},{1,0},{2,3},{3,2},{4,5},{5,4},{6,7},{7,6},{8,9},{9,8},{10,11... | collective-permute-start | bytes 1179656 | tf_op jit(solution)/shard_map/ppermute | solution.py:23
  39.5 66.0 %collective-permute-start.15 = (bf16[256,128,128]{2,1,0:T(8,128)(2,1)}, bf16[256,128,128]{2,1,0:T(8,128)(2,1)}, u32[]{:S(2)}, u32[]{:S(2)}) collective-permute-start(bf16[256,128,128]{2,1,0:T(8,128)(2,1)} %bitcast.78), channel_id=1, source_target_pairs={{0,8},{8,0},{1,9},{9,1},{2,10},{10,2},{3,11},{11,3},{4,12},{12,4},... | collective-permute-start | bytes 25165832 | tf_op jit(solution)/shard_map/ppermute | solution.py:23
  44.4 35.7 %collective-permute-start.13 = (bf16[24,32,128]{2,0,1:T(8,128)(2,1)S(1)}, bf16[24,32,128]{2,0,1:T(8,128)(2,1)S(1)}, u32[]{:S(2)}, u32[]{:S(2)}) collective-permute-start(bf16[24,32,128]{2,0,1:T(8,128)(2,1)S(1)} %select_bitcast_fusion.2), channel_id=1, source_target_pairs={{0,8},{8,0},{1,9},{9,1},{2,10},{10,2},{3,11},{11,3},{4,12},{12,4},... | collective-permute-start | bytes 589832 | tf_op jit(solution)/shard_map/ppermute | solution.py:23
  65.1 19.2 %collective-permute-start.12 = (bf16[2,32,48,128]{3,2,1,0:T(8,128)(2,1)}, bf16[2,32,48,128]{3,2,1,0:T(8,128)(2,1)S(1)}, u32[]{:S(2)}, u32[]{:S(2)}) collective-permute-start(bf16[2,32,48,128]{3,2,1,0:T(8,128)(2,1)} %get-tuple-element.50), channel_id=1, source_target_pairs={{0,1},{1,0},{2,3},{3,2},{4,5},{5,4},{6,7},{7,6},{8,9},{9,8},{10,11... | collective-permute-start | bytes 2359304 | tf_op jit(solution)/shard_map/ppermute | solution.py:23
  79.7 21.4 %collective-permute-start.20 = (bf16[2,32,48,128]{3,2,1,0:T(8,128)(2,1)}, bf16[2,32,48,128]{3,2,1,0:T(8,128)(2,1)S(1)}, u32[]{:S(2)}, u32[]{:S(2)}) collective-permute-start(bf16[2,32,48,128]{3,2,1,0:T(8,128)(2,1)} %get-tuple-element.60), channel_id=1, source_target_pairs={{0,1},{1,0},{2,3},{3,2},{4,5},{5,4},{6,7},{7,6},{8,9},{9,8},{10,11... | collective-permute-start | bytes 2359304 | tf_op jit(solution)/shard_map/ppermute | solution.py:23
  86.7 22.8 %collective-permute-start.14 = (bf16[32,48,128]{2,1,0:T(8,128)(2,1)S(1)}, bf16[32,48,128]{2,1,0:T(8,128)(2,1)S(1)}, u32[]{:S(2)}, u32[]{:S(2)}) collective-permute-start(bf16[32,48,128]{2,1,0:T(8,128)(2,1)S(1)} %get-tuple-element.52.refs_0_), channel_id=1, source_target_pairs={{0,1},{1,0},{2,3},{3,2},{4,5},{5,4},{6,7},{7,6},{8,9},{9,8},{10,11... | collective-permute-start | bytes 1179656 | tf_op jit(solution)/shard_map/ppermute | solution.py:23
  104.2 18.2 %collective-permute-start.21 = (bf16[32,48,128]{2,1,0:T(8,128)(2,1)S(1)}, bf16[32,48,128]{2,1,0:T(8,128)(2,1)S(1)}, u32[]{:S(2)}, u32[]{:S(2)}) collective-permute-start(bf16[32,48,128]{2,1,0:T(8,128)(2,1)S(1)} %get-tuple-element.62.refs_0_), channel_id=1, source_target_pairs={{0,1},{1,0},{2,3},{3,2},{4,5},{5,4},{6,7},{7,6},{8,9},{9,8},{10,11... | collective-permute-start | bytes 1179656 | tf_op jit(solution)/shard_map/ppermute | solution.py:23
  119.0 13.0 %collective-permute-start.16 = (bf16[48,4096]{1,0:T(8,128)(2,1)}, bf16[48,4096]{1,0:T(8,128)(2,1)S(1)}, u32[]{:S(2)}, u32[]{:S(2)}) collective-permute-start(bf16[48,4096]{1,0:T(8,128)(2,1)} %get-tuple-element.56), channel_id=1, source_target_pairs={{0,1},{1,0},{2,3},{3,2},{4,5},{5,4},{6,7},{7,6},{8,9},{9,8},{10,11... | collective-permute-start | bytes 1179656 | tf_op jit(solution)/shard_map/ppermute | solution.py:23
  131.8 8.4 %collective-permute-start.22 = (bf16[48,4096]{1,0:T(8,128)(2,1)}, bf16[48,4096]{1,0:T(8,128)(2,1)S(1)}, u32[]{:S(2)}, u32[]{:S(2)}) collective-permute-start(bf16[48,4096]{1,0:T(8,128)(2,1)} %get-tuple-element.65), channel_id=1, source_target_pairs={{0,1},{1,0},{2,3},{3,2},{4,5},{5,4},{6,7},{7,6},{8,9},{9,8},{10,11... | collective-permute-start | bytes 1179656 | tf_op jit(solution)/shard_map/ppermute | solution.py:23
  132.2 8.2 %collective-permute-start.17 = (bf16[48,1024]{1,0:T(8,128)(2,1)S(1)}, bf16[48,1024]{1,0:T(8,128)(2,1)S(1)}, u32[]{:S(2)}, u32[]{:S(2)}) collective-permute-start(bf16[48,1024]{1,0:T(8,128)(2,1)S(1)} %get-tuple-element.100), channel_id=1, source_target_pairs={{0,6},{2,0},{4,2},{6,4},{1,7},{3,1},{5,3},{7,5},{8,14},{10,8},{12,... | collective-permute-start | bytes 294920 | tf_op jit(solution)/shard_map/ppermute | solution.py:23
  133.3 7.0 %collective-permute-start.18 = (bf16[48,1024]{1,0:T(8,128)(2,1)S(1)}, bf16[48,1024]{1,0:T(8,128)(2,1)S(1)}, u32[]{:S(2)}, u32[]{:S(2)}) collective-permute-start(bf16[48,1024]{1,0:T(8,128)(2,1)S(1)} %get-tuple-element.102), channel_id=1, source_target_pairs={{0,4},{2,6},{4,0},{6,2},{1,5},{3,7},{5,1},{7,3},{8,12},{10,14},{12... | collective-permute-start | bytes 294920 | tf_op jit(solution)/shard_map/ppermute | solution.py:23
  133.3 7.1 %collective-permute-start.19 = (bf16[48,1024]{1,0:T(8,128)(2,1)S(1)}, bf16[48,1024]{1,0:T(8,128)(2,1)S(1)}, u32[]{:S(2)}, u32[]{:S(2)}) collective-permute-start(bf16[48,1024]{1,0:T(8,128)(2,1)S(1)} %get-tuple-element.101), channel_id=1, source_target_pairs={{0,2},{2,4},{4,6},{6,0},{1,3},{3,5},{5,7},{7,1},{8,10},{10,12},{12... | collective-permute-start | bytes 294920 | tf_op jit(solution)/shard_map/ppermute | solution.py:23
  146.1 14.1 %collective-permute-start.24 = (bf16[48,1024]{1,0:T(8,128)(2,1)S(1)}, bf16[48,1024]{1,0:T(8,128)(2,1)S(1)}, u32[]{:S(2)}, u32[]{:S(2)}) collective-permute-start(bf16[48,1024]{1,0:T(8,128)(2,1)S(1)} %get-tuple-element.110), channel_id=1, source_target_pairs={{0,4},{2,6},{4,0},{6,2},{1,5},{3,7},{5,1},{7,3},{8,12},{10,14},{12... | collective-permute-start | bytes 294920 | tf_op jit(solution)/shard_map/ppermute | solution.py:23
  146.5 13.7 %collective-permute-start.25 = (bf16[48,1024]{1,0:T(8,128)(2,1)S(1)}, bf16[48,1024]{1,0:T(8,128)(2,1)S(1)}, u32[]{:S(2)}, u32[]{:S(2)}) collective-permute-start(bf16[48,1024]{1,0:T(8,128)(2,1)S(1)} %get-tuple-element.109), channel_id=1, source_target_pairs={{0,2},{2,4},{4,6},{6,0},{1,3},{3,5},{5,7},{7,1},{8,10},{10,12},{12... | collective-permute-start | bytes 294920 | tf_op jit(solution)/shard_map/ppermute | solution.py:23
  148.7 22.7 %collective-permute-start.29 = (bf16[4,48,1024]{2,1,0:T(8,128)(2,1)S(1)}, bf16[4,48,1024]{2,1,0:T(8,128)(2,1)S(1)}, u32[]{:S(2)}, u32[]{:S(2)}) collective-permute-start(bf16[4,48,1024]{2,1,0:T(8,128)(2,1)S(1)} %pad_maximum_fusion.3.refs_0_), channel_id=1, source_target_pairs={{0,1},{1,0},{2,3},{3,2},{4,5},{5,4},{6,7},{7,6},{8,9},{9,8},{10,11... | collective-permute-start | bytes 1179656 | tf_op jit(solution)/shard_map/ppermute | solution.py:23
  167.3 17.2 %collective-permute-start.39 = (bf16[4,48,1024]{2,1,0:T(8,128)(2,1)S(1)}, bf16[4,48,1024]{2,1,0:T(8,128)(2,1)S(1)}, u32[]{:S(2)}, u32[]{:S(2)}) collective-permute-start(bf16[4,48,1024]{2,1,0:T(8,128)(2,1)S(1)} %pad_maximum_fusion.4.refs_0_), channel_id=1, source_target_pairs={{0,1},{1,0},{2,3},{3,2},{4,5},{5,4},{6,7},{7,6},{8,9},{9,8},{10,11... | collective-permute-start | bytes 1179656 | tf_op jit(solution)/shard_map/ppermute | solution.py:23
  184.3 15.0 %collective-permute-start.30 = (bf16[2,32,48,128]{3,2,1,0:T(8,128)(2,1)}, bf16[2,32,48,128]{3,2,1,0:T(8,128)(2,1)S(1)}, u32[]{:S(2)}, u32[]{:S(2)}) collective-permute-start(bf16[2,32,48,128]{3,2,1,0:T(8,128)(2,1)} %get-tuple-element.67), channel_id=1, source_target_pairs={{0,1},{1,0},{2,3},{3,2},{4,5},{5,4},{6,7},{7,6},{8,9},{9,8},{10,11... | collective-permute-start | bytes 2359304 | tf_op jit(solution)/shard_map/ppermute | solution.py:23
  197.4 19.9 %collective-permute-start.40 = (bf16[2,32,48,128]{3,2,1,0:T(8,128)(2,1)}, bf16[2,32,48,128]{3,2,1,0:T(8,128)(2,1)S(1)}, u32[]{:S(2)}, u32[]{:S(2)}) collective-permute-start(bf16[2,32,48,128]{3,2,1,0:T(8,128)(2,1)} %get-tuple-element.74), channel_id=1, source_target_pairs={{0,1},{1,0},{2,3},{3,2},{4,5},{5,4},{6,7},{7,6},{8,9},{9,8},{10,11... | collective-permute-start | bytes 2359304 | tf_op jit(solution)/shard_map/ppermute | solution.py:23
  201.8 23.9 %collective-permute-start.31 = (bf16[32,48,128]{2,1,0:T(8,128)(2,1)S(1)}, bf16[32,48,128]{2,1,0:T(8,128)(2,1)S(1)}, u32[]{:S(2)}, u32[]{:S(2)}) collective-permute-start(bf16[32,48,128]{2,1,0:T(8,128)(2,1)S(1)} %get-tuple-element.69.refs_0_), channel_id=1, source_target_pairs={{0,1},{1,0},{2,3},{3,2},{4,5},{5,4},{6,7},{7,6},{8,9},{9,8},{10,11... | collective-permute-start | bytes 1179656 | tf_op jit(solution)/shard_map/ppermute | solution.py:23
  219.7 17.1 %collective-permute-start.41 = (bf16[32,48,128]{2,1,0:T(8,128)(2,1)S(1)}, bf16[32,48,128]{2,1,0:T(8,128)(2,1)S(1)}, u32[]{:S(2)}, u32[]{:S(2)}) collective-permute-start(bf16[32,48,128]{2,1,0:T(8,128)(2,1)S(1)} %get-tuple-element.76.refs_0_), channel_id=1, source_target_pairs={{0,1},{1,0},{2,3},{3,2},{4,5},{5,4},{6,7},{7,6},{8,9},{9,8},{10,11... | collective-permute-start | bytes 1179656 | tf_op jit(solution)/shard_map/ppermute | solution.py:23
  235.5 11.5 %collective-permute-start.32 = (bf16[48,4096]{1,0:T(8,128)(2,1)}, bf16[48,4096]{1,0:T(8,128)(2,1)S(1)}, u32[]{:S(2)}, u32[]{:S(2)}) collective-permute-start(bf16[48,4096]{1,0:T(8,128)(2,1)} %get-tuple-element.72), channel_id=1, source_target_pairs={{0,1},{1,0},{2,3},{3,2},{4,5},{5,4},{6,7},{7,6},{8,9},{9,8},{10,11... | collective-permute-start | bytes 1179656 | tf_op jit(solution)/shard_map/ppermute | solution.py:23
  246.7 8.3 %collective-permute-start.42 = (bf16[48,4096]{1,0:T(8,128)(2,1)}, bf16[48,4096]{1,0:T(8,128)(2,1)S(1)}, u32[]{:S(2)}, u32[]{:S(2)}) collective-permute-start(bf16[48,4096]{1,0:T(8,128)(2,1)} %get-tuple-element.79), channel_id=1, source_target_pairs={{0,1},{1,0},{2,3},{3,2},{4,5},{5,4},{6,7},{7,6},{8,9},{9,8},{10,11... | collective-permute-start | bytes 1179656 | tf_op jit(solution)/shard_map/ppermute | solution.py:23
  247.2 11.9 %collective-permute-start.33 = (bf16[48,1024]{1,0:T(8,128)(2,1)S(1)}, bf16[48,1024]{1,0:T(8,128)(2,1)S(1)}, u32[]{:S(2)}, u32[]{:S(2)}) collective-permute-start(bf16[48,1024]{1,0:T(8,128)(2,1)S(1)} %get-tuple-element.97), channel_id=1, source_target_pairs={{0,6},{2,0},{4,2},{6,4},{1,7},{3,1},{5,3},{7,5},{8,14},{10,8},{12,... | collective-permute-start | bytes 294920 | tf_op jit(solution)/shard_map/ppermute | solution.py:23
  259.0 11.3 %collective-permute-start.44 = (bf16[48,1024]{1,0:T(8,128)(2,1)S(1)}, bf16[48,1024]{1,0:T(8,128)(2,1)S(1)}, u32[]{:S(2)}, u32[]{:S(2)}) collective-permute-start(bf16[48,1024]{1,0:T(8,128)(2,1)S(1)} %get-tuple-element.105), channel_id=1, source_target_pairs={{0,4},{2,6},{4,0},{6,2},{1,5},{3,7},{5,1},{7,3},{8,12},{10,14},{12... | collective-permute-start | bytes 294920 | tf_op jit(solution)/shard_map/ppermute | solution.py:23
  259.0 11.3 %collective-permute-start.45 = (bf16[48,1024]{1,0:T(8,128)(2,1)S(1)}, bf16[48,1024]{1,0:T(8,128)(2,1)S(1)}, u32[]{:S(2)}, u32[]{:S(2)}) collective-permute-start(bf16[48,1024]{1,0:T(8,128)(2,1)S(1)} %get-tuple-element.104), channel_id=1, source_target_pairs={{0,2},{2,4},{4,6},{6,0},{1,3},{3,5},{5,7},{7,1},{8,10},{10,12},{12... | collective-permute-start | bytes 294920 | tf_op jit(solution)/shard_map/ppermute | solution.py:23
  (55 other events, 719.8 us)

commit v11 on v9

--- a/solution.py
+++ b/solution.py
@@ -362,12 +362,12 @@
         stack = jnp.stack([own] + [hop(own, "tensor", step) for step in range(1, owners)])
         return [stack] + [hop(stack, "rep", g) for g in range(1, reps)]
 
-    stacks = [gathered(stream) for stream in streams]
-
     codes = jnp.stack([gate_slot[0], up_slot[0], down_slot[0]])
     codes = lax.dynamic_slice_in_dim(codes, rep_index * tile_count, tile_count, axis=1)
     wide = jnp.concatenate([gate_left[0], up_left[0], down_right[0], norm_gain], axis=0)
+    codes, wide, streams[0] = lax.optimization_barrier((codes, wide, streams[0]))
     other_codes, other_wide = hop(codes, "section", 1), hop(wide, "section", 1)
+    stacks = [gathered(stream) for stream in streams]
     other_codes, other_wide, gate_tiles, up_tiles, down_tiles = lax.optimization_barrier(
         (other_codes, other_wide, gate_tiles, up_tiles, down_tiles)
     )

time: 259 us -> 258 us (level)
  starting transfers between devices: 54.9 us -> 49.1 us
  Pallas kernels: 93.1 us -> 95.9 us
    ppermute x47, starting transfers between devices: 54.9 us -> 49.1 us  [hop(): lax.ppermute(value, axis, [(i, (i + steps) % count) for i in range(count)])]
    pallas_call x4, Pallas kernels: 47.9 us -> 51.5 us  [expand(): pl.pallas_call(functools.partial(expand_kernel, reps), out_shape=[jax.Sha...]
    unnamed x75 -> x67, local copies, waits for them, and re-layouts: 6.11 us -> 6.16 us
  transfers between devices with their start and end apart: 47 -> 47, of which waited for: 24 -> 21; matrix products, arithmetic and copies ran while one was open for 7% -> 6% of each run, Pallas kernels for 36% -> 37%
where the time goes in v11:
time: 258 us; the launch traced here: 256 us
  Pallas kernels  95.9 us (37%)
  waiting for transfers between devices  85.5 us (33%)
  starting transfers between devices  49.1 us (19%)
  local copies, waits for them, and re-layouts  14.7 us (6%)
  other arithmetic  10.6 us (4%)
    ppermute x47, waiting for transfers between devices, hop(): lax.ppermute(value, axis, [(i, (i + steps) % count) for i in range(count)])  85.5 us
    pallas_call x4, Pallas kernels, expand(): pl.pallas_call(functools.partial(expand_kernel, reps), out_shape=[jax.Sha...  51.5 us
    ppermute x47, starting transfers between devices, hop(): lax.ppermute(value, axis, [(i, (i + steps) % count) for i in range(count)])  49.1 us
    pallas_call x4, Pallas kernels, contract(): pl.pallas_call(functools.partial(contract_kernel, reps), out_shape=[jax.S...  34.8 us
    pallas_call x4, Pallas kernels, activate(): pl.pallas_call(functools.partial(activate_kernel, reps), out_shape=[jax.S...  9.69 us
    unnamed x67, local copies, waits for them, and re-layouts  6.16 us
  transfers between devices with their start and end apart: 47, of which 21 were waited for; matrix products, arithmetic and copies ran while one was open for 6% of the time, Pallas kernels for 37%

profile of v11, /device:TPU:1, one launch (start us, length us, event | category | flops | bytes accessed | tf_op | source)
XLA Modules:
  0.0 256.5 jit_solution(6855935998780352221)
XLA Ops:
  5.0 2.7 %collective-permute-start.2 = (bf16[48,1024]{1,0:T(8,128)(2,1)S(1)}, bf16[48,1024]{1,0:T(8,128)(2,1)S(1)}, u32[]{:S(2)}, u32[]{:S(2)}) collective-permute-start(bf16[48,1024]{1,0:T(8,128)(2,1)S(1)} %get-tuple-element.42), channel_id=1, source_target_pairs={{0,2},{2,4},{4,6},{6,0},{1,3},{3,5},{5,7},{7,1},{8,10},{10,12},{12... | collective-permute-start | bytes 294920 | tf_op jit(solution)/shard_map/ppermute | solution.py:23
  7.6 2.3 collective-permute-start.3
  18.4 4.3 %collective-permute-done.16 = bf16[48,1024]{1,0:T(8,128)(2,1)S(1)} collective-permute-done((bf16[48,1024]{1,0:T(8,128)(2,1)S(1)}, bf16[48,1024]{1,0:T(8,128)(2,1)S(1)}, u32[]{:S(2)}, u32[]{:S(2)}) %collective-permute-start.16) | collective-permute-done | bytes 98336 | tf_op jit(solution)/shard_map/ppermute | solution.py:23
  24.3 3.6 %collective-permute-done.17 = bf16[48,1024]{1,0:T(8,128)(2,1)S(1)} collective-permute-done((bf16[48,1024]{1,0:T(8,128)(2,1)S(1)}, bf16[48,1024]{1,0:T(8,128)(2,1)S(1)}, u32[]{:S(2)}, u32[]{:S(2)}) %collective-permute-start.17) | collective-permute-done | bytes 98336 | tf_op jit(solution)/shard_map/ppermute | solution.py:23
  38.9 12.9 %expand.4 = (f32[48,16]{1,0:T(8,128)}, bf16[2,32,48,128]{3,2,1,0:T(8,128)(2,1)}, bf16[2,32,48,128]{3,2,1,0:T(8,128)(2,1)}) custom-call(s32[864]{0:T(1024)} %reshape.556.words_ref, s32[4]{0:T(128)} %pad_add_fusion.1.groups_ref, bf16[4,48,1024]{2,1,0:T(8,128)(2,1)} %copy-done.16, bf16[4,48,1024]{2,1,0:T(8,128)(2,1)} %copy-done.20, bf16[1,4096]{1,0:T(2,128)(2,1)} %bitcast.101, ...), custom_call_target="tpu_custom_call" | custom-call | flops 6442450944 | bytes 16777216 | tf_op jit(solution)/shard_map/expand/pallas_call | solution.py:200
  53.5 12.9 %expand.5 = (f32[48,16]{1,0:T(8,128)}, bf16[2,32,48,128]{3,2,1,0:T(8,128)(2,1)}, bf16[2,32,48,128]{3,2,1,0:T(8,128)(2,1)}) custom-call(s32[864]{0:T(1024)} %reshape.556.words_ref, s32[4]{0:T(128)} %pad_add_fusion.1.groups_ref, bf16[4,48,1024]{2,1,0:T(8,128)(2,1)} %copy-done.17, bf16[4,48,1024]{2,1,0:T(8,128)(2,1)} %copy-done.22, bf16[1,4096]{1,0:T(2,128)(2,1)} %bitcast.102, ...), custom_call_target="tpu_custom_call" | custom-call | flops 6442450944 | bytes 16777216 | tf_op jit(solution)/shard_map/expand/pallas_call | solution.py:200
  68.4 2.4 activate.4
  72.7 13.6 %collective-permute-done.20.refs_1_ = bf16[2,32,48,128]{3,2,1,0:T(8,128)(2,1)S(1)} collective-permute-done((bf16[2,32,48,128]{3,2,1,0:T(8,128)(2,1)}, bf16[2,32,48,128]{3,2,1,0:T(8,128)(2,1)S(1)}, u32[]{:S(2)}, u32[]{:S(2)}) %collective-permute-start.20) | collective-permute-done | bytes 786464 | tf_op jit(solution)/shard_map/ppermute | solution.py:23
  86.3 2.4 activate.5
  90.0 4.7 %collective-permute-done.10.refs_1_ = bf16[32,48,128]{2,1,0:T(8,128)(2,1)S(1)} collective-permute-done((bf16[32,48,128]{2,1,0:T(8,128)(2,1)S(1)}, bf16[32,48,128]{2,1,0:T(8,128)(2,1)S(1)}, u32[]{:S(2)}, u32[]{:S(2)}) %collective-permute-start.10) | collective-permute-done | bytes 393248 | tf_op jit(solution)/shard_map/ppermute | solution.py:23
  95.5 9.0 %contract.4 = (bf16[48,4096]{1,0:T(8,128)(2,1)}, bf16[48,4096]{1,0:T(8,128)(2,1)}) custom-call(s32[864]{0:T(1024)} %reshape.556.words_ref, s32[4]{0:T(128)} %pad_add_fusion.1.groups_ref, bf16[32,48,128]{2,1,0:T(8,128)(2,1)} %copy-done.5, bf16[32,48,128]{2,1,0:T(8,128)(2,1)} %copy-done.29, f32[48,8]{1,0:T(8,128)} %copy-done.12, bf16[8,4096]{1,0:T(8,128)(2,1)} %bitcast.91, ...), custom_call_target="tpu_custom_call" | custom-call | flops 3221225472 | bytes 8388608 | tf_op jit(solution)/shard_map/contract/pallas_call | solution.py:316
  108.0 9.1 %contract.5 = (bf16[48,4096]{1,0:T(8,128)(2,1)}, bf16[48,4096]{1,0:T(8,128)(2,1)}) custom-call(s32[864]{0:T(1024)} %reshape.556.words_ref, s32[4]{0:T(128)} %pad_add_fusion.1.groups_ref, bf16[32,48,128]{2,1,0:T(8,128)(2,1)} %copy-done.4, bf16[32,48,128]{2,1,0:T(8,128)(2,1)} %copy-done.28, f32[48,8]{1,0:T(8,128)} %copy-done.10, bf16[8,4096]{1,0:T(8,128)(2,1)} %bitcast.92, ...), custom_call_target="tpu_custom_call" | custom-call | flops 3221225472 | bytes 8388608 | tf_op jit(solution)/shard_map/contract/pallas_call | solution.py:316
  119.6 4.4 %collective-permute-done.22 = bf16[48,4096]{1,0:T(8,128)(2,1)S(1)} collective-permute-done((bf16[48,4096]{1,0:T(8,128)(2,1)}, bf16[48,4096]{1,0:T(8,128)(2,1)S(1)}, u32[]{:S(2)}, u32[]{:S(2)}) %collective-permute-start.22) | collective-permute-done | bytes 393248 | tf_op jit(solution)/shard_map/ppermute | solution.py:23
  124.9 1.9 collective-permute-start.27
  131.4 2.3 collective-permute-done.27
  134.8 5.2 %collective-permute-done.24 = bf16[48,1024]{1,0:T(8,128)(2,1)S(1)} collective-permute-done((bf16[48,1024]{1,0:T(8,128)(2,1)S(1)}, bf16[48,1024]{1,0:T(8,128)(2,1)S(1)}, u32[]{:S(2)}, u32[]{:S(2)}) %collective-permute-start.24) | collective-permute-done | bytes 98336 | tf_op jit(solution)/shard_map/ppermute | solution.py:23
  140.8 2.6 %collective-permute-start.38 = (bf16[48,1024]{1,0:T(8,128)(2,1)S(1)}, bf16[48,1024]{1,0:T(8,128)(2,1)S(1)}, u32[]{:S(2)}, u32[]{:S(2)}) collective-permute-start(bf16[48,1024]{1,0:T(8,128)(2,1)S(1)} %fusion.19), channel_id=1, source_target_pairs={{0,6},{2,0},{4,2},{6,4},{1,7},{3,1},{5,3},{7,5},{8,14},{10,8},{12,... | collective-permute-start | bytes 294920 | tf_op jit(solution)/shard_map/ppermute | solution.py:23
  143.9 2.7 %collective-permute-done.36 = bf16[48,1024]{1,0:T(8,128)(2,1)S(1)} collective-permute-done((bf16[48,1024]{1,0:T(8,128)(2,1)S(1)}, bf16[48,1024]{1,0:T(8,128)(2,1)S(1)}, u32[]{:S(2)}, u32[]{:S(2)}) %collective-permute-start.36) | collective-permute-done | bytes 98336 | tf_op jit(solution)/shard_map/ppermute | solution.py:23
  146.6 2.5 collective-permute-done.37
  150.9 12.9 %expand.6 = (f32[48,16]{1,0:T(8,128)}, bf16[2,32,48,128]{3,2,1,0:T(8,128)(2,1)}, bf16[2,32,48,128]{3,2,1,0:T(8,128)(2,1)}) custom-call(s32[864]{0:T(1024)} %reshape.559.words_ref, s32[4]{0:T(128)} %pad_add_fusion.2.groups_ref, bf16[4,48,1024]{2,1,0:T(8,128)(2,1)} %copy-done.18, bf16[4,48,1024]{2,1,0:T(8,128)(2,1)} %copy-done.21, bf16[1,4096]{1,0:T(2,128)(2,1)} %bitcast.99, ...), custom_call_target="tpu_custom_call" | custom-call | flops 6442450944 | bytes 16777216 | tf_op jit(solution)/shard_map/expand/pallas_call | solution.py:200
  165.2 12.8 %expand.7 = (f32[48,16]{1,0:T(8,128)}, bf16[2,32,48,128]{3,2,1,0:T(8,128)(2,1)}, bf16[2,32,48,128]{3,2,1,0:T(8,128)(2,1)}) custom-call(s32[864]{0:T(1024)} %reshape.559.words_ref, s32[4]{0:T(128)} %pad_add_fusion.2.groups_ref, bf16[4,48,1024]{2,1,0:T(8,128)(2,1)} %copy-done.19, bf16[4,48,1024]{2,1,0:T(8,128)(2,1)} %copy-done.23, bf16[1,4096]{1,0:T(2,128)(2,1)} %bitcast.100, ...), custom_call_target="tpu_custom_call" | custom-call | flops 6442450944 | bytes 16777216 | tf_op jit(solution)/shard_map/expand/pallas_call | solution.py:200
  179.1 2.4 activate.6
  182.8 15.1 %collective-permute-done.40.refs_1_ = bf16[2,32,48,128]{3,2,1,0:T(8,128)(2,1)S(1)} collective-permute-done((bf16[2,32,48,128]{3,2,1,0:T(8,128)(2,1)}, bf16[2,32,48,128]{3,2,1,0:T(8,128)(2,1)S(1)}, u32[]{:S(2)}, u32[]{:S(2)}) %collective-permute-start.40) | collective-permute-done | bytes 786464 | tf_op jit(solution)/shard_map/ppermute | solution.py:23
  197.9 2.4 activate.7
  200.7 5.6 %collective-permute-done.31.refs_1_ = bf16[32,48,128]{2,1,0:T(8,128)(2,1)S(1)} collective-permute-done((bf16[32,48,128]{2,1,0:T(8,128)(2,1)S(1)}, bf16[32,48,128]{2,1,0:T(8,128)(2,1)S(1)}, u32[]{:S(2)}, u32[]{:S(2)}) %collective-permute-start.31) | collective-permute-done | bytes 393248 | tf_op jit(solution)/shard_map/ppermute | solution.py:23
  207.1 8.3 %contract.6 = (bf16[48,4096]{1,0:T(8,128)(2,1)}, bf16[48,4096]{1,0:T(8,128)(2,1)}) custom-call(s32[864]{0:T(1024)} %reshape.559.words_ref, s32[4]{0:T(128)} %pad_add_fusion.2.groups_ref, bf16[32,48,128]{2,1,0:T(8,128)(2,1)} %copy-done.6, bf16[32,48,128]{2,1,0:T(8,128)(2,1)} %copy-done.30, f32[48,8]{1,0:T(8,128)} %copy-done.14, bf16[8,4096]{1,0:T(8,128)(2,1)} %bitcast.93, ...), custom_call_target="tpu_custom_call" | custom-call | flops 3221225472 | bytes 8388608 | tf_op jit(solution)/shard_map/contract/pallas_call | solution.py:316
  216.9 8.3 %contract.7 = (bf16[48,4096]{1,0:T(8,128)(2,1)}, bf16[48,4096]{1,0:T(8,128)(2,1)}) custom-call(s32[864]{0:T(1024)} %reshape.559.words_ref, s32[4]{0:T(128)} %pad_add_fusion.2.groups_ref, bf16[32,48,128]{2,1,0:T(8,128)(2,1)} %copy-done.7, bf16[32,48,128]{2,1,0:T(8,128)(2,1)} %copy-done.31, f32[48,8]{1,0:T(8,128)} %copy-done.15, bf16[8,4096]{1,0:T(8,128)(2,1)} %bitcast.94, ...), custom_call_target="tpu_custom_call" | custom-call | flops 3221225472 | bytes 8388608 | tf_op jit(solution)/shard_map/contract/pallas_call | solution.py:316
  226.6 3.0 %collective-permute-start.33 = (bf16[48,1024]{1,0:T(8,128)(2,1)S(1)}, bf16[48,1024]{1,0:T(8,128)(2,1)S(1)}, u32[]{:S(2)}, u32[]{:S(2)}) collective-permute-start(bf16[48,1024]{1,0:T(8,128)(2,1)S(1)} %get-tuple-element.95), channel_id=1, source_target_pairs={{0,6},{2,0},{4,2},{6,4},{1,7},{3,1},{5,3},{7,5},{8,14},{10,8},{12,... | collective-permute-start | bytes 294920 | tf_op jit(solution)/shard_map/ppermute | solution.py:23
  230.9 4.1 %collective-permute-done.42 = bf16[48,4096]{1,0:T(8,128)(2,1)S(1)} collective-permute-done((bf16[48,4096]{1,0:T(8,128)(2,1)}, bf16[48,4096]{1,0:T(8,128)(2,1)S(1)}, u32[]{:S(2)}, u32[]{:S(2)}) %collective-permute-start.42) | collective-permute-done | bytes 393248 | tf_op jit(solution)/shard_map/ppermute | solution.py:23
  235.2 3.0 %collective-permute-start.43 = (bf16[48,1024]{1,0:T(8,128)(2,1)S(1)}, bf16[48,1024]{1,0:T(8,128)(2,1)S(1)}, u32[]{:S(2)}, u32[]{:S(2)}) collective-permute-start(bf16[48,1024]{1,0:T(8,128)(2,1)S(1)} %get-tuple-element.101), channel_id=1, source_target_pairs={{0,6},{2,0},{4,2},{6,4},{1,7},{3,1},{5,3},{7,5},{8,14},{10,8},{12,... | collective-permute-start | bytes 294920 | tf_op jit(solution)/shard_map/ppermute | solution.py:23
  240.2 7.8 %collective-permute-done.44 = bf16[48,1024]{1,0:T(8,128)(2,1)S(1)} collective-permute-done((bf16[48,1024]{1,0:T(8,128)(2,1)S(1)}, bf16[48,1024]{1,0:T(8,128)(2,1)S(1)}, u32[]{:S(2)}, u32[]{:S(2)}) %collective-permute-start.44) | collective-permute-done | bytes 98336 | tf_op jit(solution)/shard_map/ppermute | solution.py:23
  248.2 6.4 %collective-permute-start.46 = (bf16[96,1024]{1,0:T(8,128)(2,1)S(1)}, bf16[96,1024]{1,0:T(8,128)(2,1)S(1)}, u32[]{:S(2)}, u32[]{:S(2)}) collective-permute-start(bf16[96,1024]{1,0:T(8,128)(2,1)S(1)} %get-tuple-element.94), channel_id=1, source_target_pairs={{0,8},{8,0},{1,9},{9,1},{2,10},{10,2},{3,11},{11,3},{4,12},{12,4},... | collective-permute-start | bytes 589832 | tf_op jit(solution)/shard_map/ppermute | solution.py:23
  (213 shorter events, 62.0 us)
Async XLA Ops:
  4.3 34.5 %collective-permute-start.6 = (bf16[256,128,128]{2,1,0:T(8,128)(2,1)}, bf16[256,128,128]{2,1,0:T(8,128)(2,1)}, u32[]{:S(2)}, u32[]{:S(2)}) collective-permute-start(bf16[256,128,128]{2,1,0:T(8,128)(2,1)} %bitcast.68), channel_id=1, source_target_pairs={{0,8},{8,0},{1,9},{9,1},{2,10},{10,2},{3,11},{11,3},{4,12},{12,4},... | collective-permute-start | bytes 25165832 | tf_op jit(solution)/shard_map/ppermute | solution.py:23
  4.5 34.4 %collective-permute-start.7 = (bf16[256,128,128]{2,1,0:T(8,128)(2,1)}, bf16[256,128,128]{2,1,0:T(8,128)(2,1)}, u32[]{:S(2)}, u32[]{:S(2)}) collective-permute-start(bf16[256,128,128]{2,1,0:T(8,128)(2,1)} %bitcast.73), channel_id=1, source_target_pairs={{0,8},{8,0},{1,9},{9,1},{2,10},{10,2},{3,11},{11,3},{4,12},{12,4},... | collective-permute-start | bytes 25165832 | tf_op jit(solution)/shard_map/ppermute | solution.py:23
  4.8 85.2 %collective-permute-start.11 = (bf16[256,128,128]{2,1,0:T(8,128)(2,1)}, bf16[256,128,128]{2,1,0:T(8,128)(2,1)}, u32[]{:S(2)}, u32[]{:S(2)}) collective-permute-start(bf16[256,128,128]{2,1,0:T(8,128)(2,1)} %bitcast.78), channel_id=1, source_target_pairs={{0,8},{8,0},{1,9},{9,1},{2,10},{10,2},{3,11},{11,3},{4,12},{12,4},... | collective-permute-start | bytes 25165832 | tf_op jit(solution)/shard_map/ppermute | solution.py:23
  5.0 9.6 %collective-permute-start.2 = (bf16[48,1024]{1,0:T(8,128)(2,1)S(1)}, bf16[48,1024]{1,0:T(8,128)(2,1)S(1)}, u32[]{:S(2)}, u32[]{:S(2)}) collective-permute-start(bf16[48,1024]{1,0:T(8,128)(2,1)S(1)} %get-tuple-element.42), channel_id=1, source_target_pairs={{0,2},{2,4},{4,6},{6,0},{1,3},{3,5},{5,7},{7,1},{8,10},{10,12},{12... | collective-permute-start | bytes 294920 | tf_op jit(solution)/shard_map/ppermute | solution.py:23
  7.6 9.5 %collective-permute-start.3 = (bf16[48,1024]{1,0:T(8,128)(2,1)S(1)}, bf16[48,1024]{1,0:T(8,128)(2,1)S(1)}, u32[]{:S(2)}, u32[]{:S(2)}) collective-permute-start(bf16[48,1024]{1,0:T(8,128)(2,1)S(1)} %get-tuple-element.42), channel_id=1, source_target_pairs={{0,4},{2,6},{4,0},{6,2},{1,5},{3,7},{5,1},{7,3},{8,12},{10,14},{12... | collective-permute-start | bytes 294920 | tf_op jit(solution)/shard_map/ppermute | solution.py:23
  18.1 9.8 %collective-permute-start.17 = (bf16[48,1024]{1,0:T(8,128)(2,1)S(1)}, bf16[48,1024]{1,0:T(8,128)(2,1)S(1)}, u32[]{:S(2)}, u32[]{:S(2)}) collective-permute-start(bf16[48,1024]{1,0:T(8,128)(2,1)S(1)} %get-tuple-element.109), channel_id=1, source_target_pairs={{0,4},{2,6},{4,0},{6,2},{1,5},{3,7},{5,1},{7,3},{8,12},{10,14},{12... | collective-permute-start | bytes 294920 | tf_op jit(solution)/shard_map/ppermute | solution.py:23
  27.9 39.3 %collective-permute-start.9 = (bf16[24,32,128]{2,0,1:T(8,128)(2,1)S(1)}, bf16[24,32,128]{2,0,1:T(8,128)(2,1)S(1)}, u32[]{:S(2)}, u32[]{:S(2)}) collective-permute-start(bf16[24,32,128]{2,0,1:T(8,128)(2,1)S(1)} %select_bitcast_fusion.2), channel_id=1, source_target_pairs={{0,8},{8,0},{1,9},{9,1},{2,10},{10,2},{3,11},{11,3},{4,12},{12,4},... | collective-permute-start | bytes 589832 | tf_op jit(solution)/shard_map/ppermute | solution.py:23
  28.5 9.2 %collective-permute-start.5 = (bf16[4,48,1024]{2,1,0:T(8,128)(2,1)S(1)}, bf16[4,48,1024]{2,1,0:T(8,128)(2,1)S(1)}, u32[]{:S(2)}, u32[]{:S(2)}) collective-permute-start(bf16[4,48,1024]{2,1,0:T(8,128)(2,1)S(1)} %pad_maximum_fusion.1.refs_0_), channel_id=1, source_target_pairs={{0,1},{1,0},{2,3},{3,2},{4,5},{5,4},{6,7},{7,6},{8,9},{9,8},{10,11... | collective-permute-start | bytes 1179656 | tf_op jit(solution)/shard_map/ppermute | solution.py:23
  37.6 15.0 %collective-permute-start.19 = (bf16[4,48,1024]{2,1,0:T(8,128)(2,1)S(1)}, bf16[4,48,1024]{2,1,0:T(8,128)(2,1)S(1)}, u32[]{:S(2)}, u32[]{:S(2)}) collective-permute-start(bf16[4,48,1024]{2,1,0:T(8,128)(2,1)S(1)} %pad_maximum_fusion.2.refs_0_), channel_id=1, source_target_pairs={{0,1},{1,0},{2,3},{3,2},{4,5},{5,4},{6,7},{7,6},{8,9},{9,8},{10,11... | collective-permute-start | bytes 1179656 | tf_op jit(solution)/shard_map/ppermute | solution.py:23
  51.8 16.7 %collective-permute-start.8 = (bf16[2,32,48,128]{3,2,1,0:T(8,128)(2,1)}, bf16[2,32,48,128]{3,2,1,0:T(8,128)(2,1)S(1)}, u32[]{:S(2)}, u32[]{:S(2)}) collective-permute-start(bf16[2,32,48,128]{3,2,1,0:T(8,128)(2,1)} %get-tuple-element.50), channel_id=1, source_target_pairs={{0,1},{1,0},{2,3},{3,2},{4,5},{5,4},{6,7},{7,6},{8,9},{9,8},{10,11... | collective-permute-start | bytes 2359304 | tf_op jit(solution)/shard_map/ppermute | solution.py:23
  66.4 19.9 %collective-permute-start.20 = (bf16[2,32,48,128]{3,2,1,0:T(8,128)(2,1)}, bf16[2,32,48,128]{3,2,1,0:T(8,128)(2,1)S(1)}, u32[]{:S(2)}, u32[]{:S(2)}) collective-permute-start(bf16[2,32,48,128]{3,2,1,0:T(8,128)(2,1)} %get-tuple-element.58), channel_id=1, source_target_pairs={{0,1},{1,0},{2,3},{3,2},{4,5},{5,4},{6,7},{7,6},{8,9},{9,8},{10,11... | collective-permute-start | bytes 2359304 | tf_op jit(solution)/shard_map/ppermute | solution.py:23
  70.9 23.8 %collective-permute-start.10 = (bf16[32,48,128]{2,1,0:T(8,128)(2,1)S(1)}, bf16[32,48,128]{2,1,0:T(8,128)(2,1)S(1)}, u32[]{:S(2)}, u32[]{:S(2)}) collective-permute-start(bf16[32,48,128]{2,1,0:T(8,128)(2,1)S(1)} %get-tuple-element.52.refs_0_), channel_id=1, source_target_pairs={{0,1},{1,0},{2,3},{3,2},{4,5},{5,4},{6,7},{7,6},{8,9},{9,8},{10,11... | collective-permute-start | bytes 1179656 | tf_op jit(solution)/shard_map/ppermute | solution.py:23
  89.3 18.0 %collective-permute-start.21 = (bf16[32,48,128]{2,1,0:T(8,128)(2,1)S(1)}, bf16[32,48,128]{2,1,0:T(8,128)(2,1)S(1)}, u32[]{:S(2)}, u32[]{:S(2)}) collective-permute-start(bf16[32,48,128]{2,1,0:T(8,128)(2,1)S(1)} %get-tuple-element.60.refs_0_), channel_id=1, source_target_pairs={{0,1},{1,0},{2,3},{3,2},{4,5},{5,4},{6,7},{7,6},{8,9},{9,8},{10,11... | collective-permute-start | bytes 1179656 | tf_op jit(solution)/shard_map/ppermute | solution.py:23
  104.5 13.4 %collective-permute-start.12 = (bf16[48,4096]{1,0:T(8,128)(2,1)}, bf16[48,4096]{1,0:T(8,128)(2,1)S(1)}, u32[]{:S(2)}, u32[]{:S(2)}) collective-permute-start(bf16[48,4096]{1,0:T(8,128)(2,1)} %get-tuple-element.56), channel_id=1, source_target_pairs={{0,1},{1,0},{2,3},{3,2},{4,5},{5,4},{6,7},{7,6},{8,9},{9,8},{10,11... | collective-permute-start | bytes 1179656 | tf_op jit(solution)/shard_map/ppermute | solution.py:23
  124.9 8.8 %collective-permute-start.27 = (bf16[48,1024]{1,0:T(8,128)(2,1)S(1)}, bf16[48,1024]{1,0:T(8,128)(2,1)S(1)}, u32[]{:S(2)}, u32[]{:S(2)}) collective-permute-start(bf16[48,1024]{1,0:T(8,128)(2,1)S(1)} %fusion.23), channel_id=1, source_target_pairs={{0,4},{2,6},{4,0},{6,2},{1,5},{3,7},{5,1},{7,3},{8,12},{10,14},{12... | collective-permute-start | bytes 294920 | tf_op jit(solution)/shard_map/ppermute | solution.py:23
  128.6 11.4 %collective-permute-start.24 = (bf16[48,1024]{1,0:T(8,128)(2,1)S(1)}, bf16[48,1024]{1,0:T(8,128)(2,1)S(1)}, u32[]{:S(2)}, u32[]{:S(2)}) collective-permute-start(bf16[48,1024]{1,0:T(8,128)(2,1)S(1)} %get-tuple-element.108), channel_id=1, source_target_pairs={{0,4},{2,6},{4,0},{6,2},{1,5},{3,7},{5,1},{7,3},{8,12},{10,14},{12... | collective-permute-start | bytes 294920 | tf_op jit(solution)/shard_map/ppermute | solution.py:23
  131.4 8.5 %collective-permute-start.25 = (bf16[48,1024]{1,0:T(8,128)(2,1)S(1)}, bf16[48,1024]{1,0:T(8,128)(2,1)S(1)}, u32[]{:S(2)}, u32[]{:S(2)}) collective-permute-start(bf16[48,1024]{1,0:T(8,128)(2,1)S(1)} %get-tuple-element.107), channel_id=1, source_target_pairs={{0,2},{2,4},{4,6},{6,0},{1,3},{3,5},{5,7},{7,1},{8,10},{10,12},{12... | collective-permute-start | bytes 294920 | tf_op jit(solution)/shard_map/ppermute | solution.py:23
  133.8 16.3 %collective-permute-start.29 = (bf16[4,48,1024]{2,1,0:T(8,128)(2,1)S(1)}, bf16[4,48,1024]{2,1,0:T(8,128)(2,1)S(1)}, u32[]{:S(2)}, u32[]{:S(2)}) collective-permute-start(bf16[4,48,1024]{2,1,0:T(8,128)(2,1)S(1)} %pad_maximum_fusion.3.refs_0_), channel_id=1, source_target_pairs={{0,1},{1,0},{2,3},{3,2},{4,5},{5,4},{6,7},{7,6},{8,9},{9,8},{10,11... | collective-permute-start | bytes 1179656 | tf_op jit(solution)/shard_map/ppermute | solution.py:23
  140.1 8.9 %collective-permute-start.37 = (bf16[48,1024]{1,0:T(8,128)(2,1)S(1)}, bf16[48,1024]{1,0:T(8,128)(2,1)S(1)}, u32[]{:S(2)}, u32[]{:S(2)}) collective-permute-start(bf16[48,1024]{1,0:T(8,128)(2,1)S(1)} %fusion.19), channel_id=1, source_target_pairs={{0,4},{2,6},{4,0},{6,2},{1,5},{3,7},{5,1},{7,3},{8,12},{10,14},{12... | collective-permute-start | bytes 294920 | tf_op jit(solution)/shard_map/ppermute | solution.py:23
  140.8 8.3 %collective-permute-start.38 = (bf16[48,1024]{1,0:T(8,128)(2,1)S(1)}, bf16[48,1024]{1,0:T(8,128)(2,1)S(1)}, u32[]{:S(2)}, u32[]{:S(2)}) collective-permute-start(bf16[48,1024]{1,0:T(8,128)(2,1)S(1)} %fusion.19), channel_id=1, source_target_pairs={{0,6},{2,0},{4,2},{6,4},{1,7},{3,1},{5,3},{7,5},{8,14},{10,8},{12,... | collective-permute-start | bytes 294920 | tf_op jit(solution)/shard_map/ppermute | solution.py:23
  149.1 15.3 %collective-permute-start.39 = (bf16[4,48,1024]{2,1,0:T(8,128)(2,1)S(1)}, bf16[4,48,1024]{2,1,0:T(8,128)(2,1)S(1)}, u32[]{:S(2)}, u32[]{:S(2)}) collective-permute-start(bf16[4,48,1024]{2,1,0:T(8,128)(2,1)S(1)} %pad_maximum_fusion.4.refs_0_), channel_id=1, source_target_pairs={{0,1},{1,0},{2,3},{3,2},{4,5},{5,4},{6,7},{7,6},{8,9},{9,8},{10,11... | collective-permute-start | bytes 1179656 | tf_op jit(solution)/shard_map/ppermute | solution.py:23
  163.8 15.3 %collective-permute-start.30 = (bf16[2,32,48,128]{3,2,1,0:T(8,128)(2,1)}, bf16[2,32,48,128]{3,2,1,0:T(8,128)(2,1)S(1)}, u32[]{:S(2)}, u32[]{:S(2)}) collective-permute-start(bf16[2,32,48,128]{3,2,1,0:T(8,128)(2,1)} %get-tuple-element.65), channel_id=1, source_target_pairs={{0,1},{1,0},{2,3},{3,2},{4,5},{5,4},{6,7},{7,6},{8,9},{9,8},{10,11... | collective-permute-start | bytes 2359304 | tf_op jit(solution)/shard_map/ppermute | solution.py:23
  178.1 19.8 %collective-permute-start.40 = (bf16[2,32,48,128]{3,2,1,0:T(8,128)(2,1)}, bf16[2,32,48,128]{3,2,1,0:T(8,128)(2,1)S(1)}, u32[]{:S(2)}, u32[]{:S(2)}) collective-permute-start(bf16[2,32,48,128]{3,2,1,0:T(8,128)(2,1)} %get-tuple-element.72), channel_id=1, source_target_pairs={{0,1},{1,0},{2,3},{3,2},{4,5},{5,4},{6,7},{7,6},{8,9},{9,8},{10,11... | collective-permute-start | bytes 2359304 | tf_op jit(solution)/shard_map/ppermute | solution.py:23
  181.6 24.8 %collective-permute-start.31 = (bf16[32,48,128]{2,1,0:T(8,128)(2,1)S(1)}, bf16[32,48,128]{2,1,0:T(8,128)(2,1)S(1)}, u32[]{:S(2)}, u32[]{:S(2)}) collective-permute-start(bf16[32,48,128]{2,1,0:T(8,128)(2,1)S(1)} %get-tuple-element.67.refs_0_), channel_id=1, source_target_pairs={{0,1},{1,0},{2,3},{3,2},{4,5},{5,4},{6,7},{7,6},{8,9},{9,8},{10,11... | collective-permute-start | bytes 1179656 | tf_op jit(solution)/shard_map/ppermute | solution.py:23
  200.4 15.7 %collective-permute-start.41 = (bf16[32,48,128]{2,1,0:T(8,128)(2,1)S(1)}, bf16[32,48,128]{2,1,0:T(8,128)(2,1)S(1)}, u32[]{:S(2)}, u32[]{:S(2)}) collective-permute-start(bf16[32,48,128]{2,1,0:T(8,128)(2,1)S(1)} %get-tuple-element.74.refs_0_), channel_id=1, source_target_pairs={{0,1},{1,0},{2,3},{3,2},{4,5},{5,4},{6,7},{7,6},{8,9},{9,8},{10,11... | collective-permute-start | bytes 1179656 | tf_op jit(solution)/shard_map/ppermute | solution.py:23
  215.4 11.1 %collective-permute-start.32 = (bf16[48,4096]{1,0:T(8,128)(2,1)}, bf16[48,4096]{1,0:T(8,128)(2,1)S(1)}, u32[]{:S(2)}, u32[]{:S(2)}) collective-permute-start(bf16[48,4096]{1,0:T(8,128)(2,1)} %get-tuple-element.70), channel_id=1, source_target_pairs={{0,1},{1,0},{2,3},{3,2},{4,5},{5,4},{6,7},{7,6},{8,9},{9,8},{10,11... | collective-permute-start | bytes 1179656 | tf_op jit(solution)/shard_map/ppermute | solution.py:23
  225.2 9.8 %collective-permute-start.42 = (bf16[48,4096]{1,0:T(8,128)(2,1)}, bf16[48,4096]{1,0:T(8,128)(2,1)S(1)}, u32[]{:S(2)}, u32[]{:S(2)}) collective-permute-start(bf16[48,4096]{1,0:T(8,128)(2,1)} %get-tuple-element.77), channel_id=1, source_target_pairs={{0,1},{1,0},{2,3},{3,2},{4,5},{5,4},{6,7},{7,6},{8,9},{9,8},{10,11... | collective-permute-start | bytes 1179656 | tf_op jit(solution)/shard_map/ppermute | solution.py:23
  226.6 12.2 %collective-permute-start.33 = (bf16[48,1024]{1,0:T(8,128)(2,1)S(1)}, bf16[48,1024]{1,0:T(8,128)(2,1)S(1)}, u32[]{:S(2)}, u32[]{:S(2)}) collective-permute-start(bf16[48,1024]{1,0:T(8,128)(2,1)S(1)} %get-tuple-element.95), channel_id=1, source_target_pairs={{0,6},{2,0},{4,2},{6,4},{1,7},{3,1},{5,3},{7,5},{8,14},{10,8},{12,... | collective-permute-start | bytes 294920 | tf_op jit(solution)/shard_map/ppermute | solution.py:23
  229.6 10.5 %collective-permute-start.34 = (bf16[48,1024]{1,0:T(8,128)(2,1)S(1)}, bf16[48,1024]{1,0:T(8,128)(2,1)S(1)}, u32[]{:S(2)}, u32[]{:S(2)}) collective-permute-start(bf16[48,1024]{1,0:T(8,128)(2,1)S(1)} %get-tuple-element.97), channel_id=1, source_target_pairs={{0,4},{2,6},{4,0},{6,2},{1,5},{3,7},{5,1},{7,3},{8,12},{10,14},{12... | collective-permute-start | bytes 294920 | tf_op jit(solution)/shard_map/ppermute | solution.py:23
  229.6 10.5 %collective-permute-start.35 = (bf16[48,1024]{1,0:T(8,128)(2,1)S(1)}, bf16[48,1024]{1,0:T(8,128)(2,1)S(1)}, u32[]{:S(2)}, u32[]{:S(2)}) collective-permute-start(bf16[48,1024]{1,0:T(8,128)(2,1)S(1)} %get-tuple-element.96), channel_id=1, source_target_pairs={{0,2},{2,4},{4,6},{6,0},{1,3},{3,5},{5,7},{7,1},{8,10},{10,12},{12... | collective-permute-start | bytes 294920 | tf_op jit(solution)/shard_map/ppermute | solution.py:23
  238.2 9.9 %collective-permute-start.44 = (bf16[48,1024]{1,0:T(8,128)(2,1)S(1)}, bf16[48,1024]{1,0:T(8,128)(2,1)S(1)}, u32[]{:S(2)}, u32[]{:S(2)}) collective-permute-start(bf16[48,1024]{1,0:T(8,128)(2,1)S(1)} %get-tuple-element.103), channel_id=1, source_target_pairs={{0,4},{2,6},{4,0},{6,2},{1,5},{3,7},{5,1},{7,3},{8,12},{10,14},{12... | collective-permute-start | bytes 294920 | tf_op jit(solution)/shard_map/ppermute | solution.py:23
  238.8 9.3 %collective-permute-start.45 = (bf16[48,1024]{1,0:T(8,128)(2,1)S(1)}, bf16[48,1024]{1,0:T(8,128)(2,1)S(1)}, u32[]{:S(2)}, u32[]{:S(2)}) collective-permute-start(bf16[48,1024]{1,0:T(8,128)(2,1)S(1)} %get-tuple-element.102), channel_id=1, source_target_pairs={{0,2},{2,4},{4,6},{6,0},{1,3},{3,5},{5,7},{7,1},{8,10},{10,12},{12... | collective-permute-start | bytes 294920 | tf_op jit(solution)/shard_map/ppermute | solution.py:23
  (48 other events, 439.4 us)
